TPU v7x, 32 devices: a whole 2x2x4 slice. The times are simulated.
32 devices in a mesh: ctx: 8 (over z, y), pipe: 4 (over x, core).
Axes of the slice: x: 2, y: 2, z: 4, core: 2. Of those that a mesh axis runs over, the one named last changes fastest.
Arguments:
- queries: bfloat16 [4, 4096, 2048], P('pipe', 'ctx'), may hold values from -400 to 400
- keys: bfloat16 [4, 4096, 2048], P('pipe', 'ctx'), may hold values from -12 to 12
- values: bfloat16 [4, 4096, 2048], P('pipe', 'ctx'), may hold values from -15 to 15
- picks: int32 [4, 8, 16, 2], P('pipe'), may hold values from -1 to 6, as said below
Outputs:
- passed: bfloat16 [4, 4096, 2048], P('pipe', 'ctx')
Inputs may be any that keep to these rules, and one draw needn't show every extreme that they name: Each entry is -1 (no block) or a block earlier than its query block; a head's 2 entries differ unless -1; within one section and query block no block is named more than 4 times over all heads and picks, and this bound is reached; query block 0 names nothing and every later query block names its preceding block at least once.
All inputs are finite; a program needn't handle non-finite values.
Results may differ from a plain program's by a relative error of at most 0.0048.
Values may be sent and summed in bfloat16 or wider, within the bound.
No kernel may reach another device: no remote copies, remote signals or barrier semaphores. Data moves between devices by JAX's collectives and lax.ppermute only.
A program may use at most 128 MiB of HBM per device.

v0:
```python
import jax
import jax.numpy as jnp
from jax import lax
from jax.sharding import PartitionSpec as P

HEADS = 16
HD = 128
PICKS = 2


def passed_along(value, axis, steps):
    count = lax.axis_size(axis)
    pairs = [(source, (source + steps) % count) for source in range(count)]
    return lax.ppermute(value, axis, pairs)


def request_table(chosen, owners, slot_count):
    pick_count = chosen.shape[1]
    pick_ids = lax.iota(jnp.int32, pick_count)
    is_live = chosen >= 0
    earlier = pick_ids[None, :] < pick_ids[:, None]
    same_owner = (chosen[:, :, None] == chosen[:, None, :]) & earlier[None]
    pick_order = jnp.sum(same_owner.astype(jnp.int32), axis=2)
    head_ids = pick_ids // PICKS
    slot_ranks = lax.iota(jnp.int32, slot_count)
    matches = (
        is_live[:, None, None, :]
        & (chosen[:, None, None, :] == owners[None, :, None, None])
        & (pick_order[:, None, None, :] == slot_ranks[None, None, :, None])
    )
    was_found = jnp.any(matches, axis=3)
    head_table = jnp.sum(jnp.where(matches, head_ids[None, None, None, :], 0), axis=3)
    return (jnp.where(was_found, head_table, -1), pick_order)


def per_device(queries, keys, values, picks):
    ctx_width = lax.axis_size("ctx")
    rank_here = lax.axis_index("ctx")
    slot_count = max(1, PICKS * HEADS // ctx_width)
    block_rows = queries.shape[1]
    score_scale = HD ** (-0.5)
    every_pick = picks[0].reshape(ctx_width, HEADS * PICKS)
    chosen = lax.dynamic_slice_in_dim(every_pick, rank_here, 1, 0)
    pick_order = request_table(chosen, lax.iota(jnp.int32, ctx_width), slot_count)[1]
    asked_table = request_table(every_pick, rank_here.reshape(1), slot_count)[0]
    asked_heads = asked_table[:, 0, :]
    safe_asked = jnp.maximum(asked_heads, 0)
    query_heads = queries[0].reshape(block_rows, HEADS, HD).transpose(1, 0, 2)
    key_heads = keys[0].reshape(block_rows, HEADS, HD).transpose(1, 0, 2)
    value_heads = values[0].reshape(block_rows, HEADS, HD).transpose(1, 0, 2)
    is_live = chosen[0] >= 0
    flat_slot = jnp.where(is_live, chosen[0] * slot_count + pick_order[0], 0)
    remote_mask = jnp.repeat(is_live.reshape(HEADS, PICKS), block_rows, axis=1)
    row_index = lax.iota(jnp.int32, block_rows)
    causal = row_index[:, None] >= row_index[None, :]

    def masked_scores(query_head, key_rows, mask_row):
        raw_scores = lax.dot_general(
            query_head, key_rows, (((1,), (1,)), ((), ())), preferred_element_type=jnp.float32
        )
        allowed = jnp.concatenate(
            [causal, jnp.broadcast_to(mask_row[None, :], (block_rows, PICKS * block_rows))], axis=1
        )
        return jnp.where(allowed, raw_scores * score_scale, -jnp.inf)

    def row_stats(scores):
        row_top = jnp.max(scores, axis=1)
        row_total = jnp.sum(jnp.exp(scores - row_top[:, None]), axis=1)
        return (row_top, row_total)

    def weighted(scores, row_top, row_total, value_rows):
        prob_rows = (jnp.exp(scores - row_top[:, None]) / row_total[:, None]).astype(jnp.bfloat16)
        return jnp.dot(prob_rows, value_rows, preferred_element_type=jnp.float32).astype(
            jnp.bfloat16
        )

    send_both = jnp.concatenate([key_heads, value_heads], axis=2)[safe_asked]
    got_slots = lax.all_to_all(send_both, "ctx", split_axis=0, concat_axis=0, tiled=True)
    last_width = 2 * HD
    flat_slots = got_slots.reshape(ctx_width * slot_count, block_rows, last_width)
    remote_both = flat_slots[flat_slot].reshape(HEADS, PICKS * block_rows, last_width)
    all_keys = jnp.concatenate([key_heads, remote_both[:, :, :HD]], axis=1)
    all_values = jnp.concatenate([value_heads, remote_both[:, :, HD:]], axis=1)

    def per_head(head_items):
        query_head, key_rows, value_rows, mask_row = head_items
        scores = masked_scores(query_head, key_rows, mask_row)
        row_top, row_total = row_stats(scores)
        return weighted(scores, row_top, row_total, value_rows)

    outputs = lax.map(per_head, (query_heads, all_keys, all_values, remote_mask))
    merged = outputs.transpose(1, 0, 2).reshape(1, block_rows, HEADS * HD)
    merged = passed_along(merged, "pipe", 1)
    return merged


def solution(mesh):
    placed = (
        P("pipe", "ctx", None),
        P("pipe", "ctx", None),
        P("pipe", "ctx", None),
        P("pipe", None, None, None),
    )
    return jax.shard_map(
        per_device, mesh=mesh, in_specs=placed, out_specs=P("pipe", "ctx", None), check_vma=False
    )
```

profile of v0, /device:TPU:26, one launch (start us, length us, event | category | flops | bytes accessed | tf_op | source)
XLA Modules:
  0.0 346.2 jit_solution(9520784688046817269)
XLA Ops:
  1.7 3.9 %copy.44 = bf16[1,512,2048]{1,2,0:T(8,128)(2,1)} copy(bf16[1,512,2048]{2,1,0:T(8,128)(2,1)} %param.7) | data formatting | bytes 4194304 | tf_op args[1]
  5.6 2.9 copy.45
  8.5 4.0 %pad_maximum_fusion.2 = bf16[16,512,256]{1,2,0:T(8,128)(2,1)} fusion(bf16[16,512,128]{1,2,0:T(8,128)(2,1)S(1)} %bitcast.62, bf16[16,512,128]{1,2,0:T(8,128)(2,1)} %bitcast.64), kind=kLoop, calls=%fused_computation.24 | loop fusion | flops 8388608 | bytes 8388608 | tf_op jit(solution)/shard_map/concatenate | solution.py:77
  12.4 7.0 %gather_fusion = bf16[32,512,256]{1,2,0:T(8,128)(2,1)} fusion(bf16[16,512,256]{1,2,0:T(8,128)(2,1)} %pad_maximum_fusion.2, s32[1024]{0:T(1024)S(1)} %pad_clamp_fusion.1), kind=kCustom, calls=%fused_computation | custom fusion | bytes 16777344 | tf_op jit(solution)/shard_map/gather | solution.py:77
  19.4 12.1 %copy.51 = bf16[8,4,512,256]{3,2,1,0:T(8,128)(2,1)} copy(bf16[8,4,512,256]{2,3,1,0:T(8,128)(2,1)} %bitcast.61) | data formatting | bytes 16777216 | tf_op jit(solution)/shard_map/gather | solution.py:77
  31.6 6.0 %all-to-all-start = ((bf16[8,4,512,256]{3,2,1,0:T(8,128)(2,1)}), bf16[8,4,512,256]{3,2,1,0:T(8,128)(2,1)}, u32[]{:S(2)}, u32[]{:S(2)}) async-start(bf16[8,4,512,256]{3,2,1,0:T(8,128)(2,1)} %copy.51), calls=%async_computation | async-start | bytes 16777216 | tf_op jit(solution)/shard_map/all_to_all | solution.py:78
  37.5 3.9 %copy.52 = bf16[16,512,128]{2,1,0:T(8,128)(2,1)} copy(bf16[16,512,128]{1,2,0:T(8,128)(2,1)} %bitcast.65) | data formatting | bytes 4194304 | tf_op jit(solution)/shard_map/transpose | solution.py:49
  41.5 2.4 copy.53
  44.3 2.9 copy.43
  47.6 171.6 %all-to-all-done = bf16[8,4,512,256]{3,2,1,0:T(8,128)(2,1)} async-done(((bf16[8,4,512,256]{3,2,1,0:T(8,128)(2,1)}), bf16[8,4,512,256]{3,2,1,0:T(8,128)(2,1)}, u32[]{:S(2)}, u32[]{:S(2)}) %all-to-all-start) | async-done | bytes 8388640 | tf_op jit(solution)/shard_map/all_to_all | solution.py:78
  219.2 8.4 %gather_fusion.1 = bf16[32,512,256]{2,1,0:T(8,128)(2,1)} fusion(bf16[32,512,256]{2,1,0:T(8,128)(2,1)} %bitcast.9, s32[1024]{0:T(1024)S(1)} %pad_clamp_fusion), kind=kCustom, calls=%fused_computation.1 | custom fusion | bytes 16777344 | tf_op jit(solution)/shard_map/gather | solution.py:81
  227.5 4.0 %fusion.21 = (bf16[16,1024,128]{2,1,0:T(8,128)(2,1)S(1)}, bf16[16,1024,128]{2,1,0:T(8,128)(2,1)S(1)}) fusion(bf16[16,1024,256]{2,1,0:T(8,128)(2,1)} %bitcast.60), kind=kLoop, calls=%fused_computation.50 | loop fusion | bytes 16777216 | tf_op jit(solution)/shard_map/slice | solution.py:83
  232.2 4.9 %pad_maximum_fusion = (bf16[16,1536,128]{2,1,0:T(8,128)(2,1)}, bf16[16,1536,128]{2,1,0:T(8,128)(2,1)}) fusion(bf16[16,1024,128]{2,1,0:T(8,128)(2,1)S(1)} %get-tuple-element.98, bf16[16,512,128]{2,1,0:T(8,128)(2,1)S(1)} %copy-done, bf16[16,1024,128]{2,1,0:T(8,128)(2,1)S(1)} %get-tuple-element.97, bf16[16,512,128]{2,1,0:T(8,128)(2,1)S(1)} %copy-done.1), kind=kLoop, calls=%fused_computation.22 | loop fusion | flops 25165824 | bytes 25165824 | tf_op jit(solution)/shard_map/concatenate | solution.py:82
  237.1 76.8 %while.11 = (s32[]{:T(128)}, bf16[16,512,128]{2,1,0:T(8,128)(2,1)}, pred[16,1024]{1,0:T(8,128)(4,1)S(1)}, bf16[16,512,128]{1,2,0:T(8,128)(2,1)S(1)}, bf16[16,153...) while((s32[]{:T(128)}, bf16[16,512,128]{2,1,0:T(8,128)(2,1)}, ...), condition=%wide.region_7.8_spmd.clone, body=%wide.region_4.7_spmd.clone.sunk | while | flops 410057728 | bytes 11029082 | solution.py:91
  239.6 2.4 fusion.29
  242.1 1.7 fusion.27
  244.4 2.4 fusion.29
  246.9 1.7 fusion.27
  249.2 2.4 fusion.29
  251.7 1.7 fusion.27
  254.0 2.4 fusion.29
  256.5 1.7 fusion.27
  258.8 2.4 fusion.29
  261.3 1.7 fusion.27
  263.6 2.4 fusion.29
  266.1 1.7 fusion.27
  268.4 2.4 fusion.29
  270.9 1.7 fusion.27
  273.2 2.4 fusion.29
  275.7 1.7 fusion.27
  278.0 2.4 fusion.29
  280.5 1.7 fusion.27
  282.8 2.4 fusion.29
  285.3 1.7 fusion.27
  287.6 2.4 fusion.29
  290.1 1.7 fusion.27
  292.4 2.4 fusion.29
  294.9 1.7 fusion.27
  297.2 2.4 fusion.29
  299.7 1.7 fusion.27
  302.0 2.4 fusion.29
  304.5 1.7 fusion.27
  306.8 2.4 fusion.29
  309.3 1.7 fusion.27
  311.6 2.4 fusion.29
  313.9 2.9 copy.55
  316.9 2.3 reshape.238
  319.2 25.6 %collective-permute-done = bf16[1,512,2048]{2,1,0:T(8,128)(2,1)S(1)} collective-permute-done((bf16[1,512,2048]{2,1,0:T(8,128)(2,1)}, bf16[1,512,2048]{2,1,0:T(8,128)(2,1)S(1)}, u32[]{:S(2)}, u32[]{:S(2)}) %collective-permute-start) | collective-permute-done | bytes 2097184 | tf_op jit(solution)/shard_map/ppermute | solution.py:14
  (92 shorter events, 17.2 us)
Async XLA Ops:
  31.6 187.6 %all-to-all-start = ((bf16[8,4,512,256]{3,2,1,0:T(8,128)(2,1)}), bf16[8,4,512,256]{3,2,1,0:T(8,128)(2,1)}, u32[]{:S(2)}, u32[]{:S(2)}) async-start(bf16[8,4,512,256]{3,2,1,0:T(8,128)(2,1)} %copy.51), calls=%async_computation | async-start | bytes 16777216 | tf_op jit(solution)/shard_map/all_to_all | solution.py:78
  227.5 4.1 %copy-start = (bf16[16,512,128]{2,1,0:T(8,128)(2,1)S(1)}, bf16[16,512,128]{2,1,0:T(8,128)(2,1)}, u32[]{:S(2)}) copy-start(bf16[16,512,128]{2,1,0:T(8,128)(2,1)} %copy.52) | copy-start | bytes 6291460
  227.5 4.7 %copy-start.1 = (bf16[16,512,128]{2,1,0:T(8,128)(2,1)S(1)}, bf16[16,512,128]{2,1,0:T(8,128)(2,1)}, u32[]{:S(2)}) copy-start(bf16[16,512,128]{2,1,0:T(8,128)(2,1)} %copy.53) | copy-start | bytes 6291460
  319.2 25.7 %collective-permute-start = (bf16[1,512,2048]{2,1,0:T(8,128)(2,1)}, bf16[1,512,2048]{2,1,0:T(8,128)(2,1)S(1)}, u32[]{:S(2)}, u32[]{:S(2)}) collective-permute-start(bf16[1,512,2048]{2,1,0:T(8,128)(2,1)} %reshape.238), channel_id=1, source_target_pairs={{0,1},{1,2},{2,3},{3,0},{4,5},{5,6},{6,7},{7,4},{8,9},{9,10},{10,1... | collective-permute-start | bytes 6291464 | tf_op jit(solution)/shard_map/ppermute | solution.py:14
where the time goes:
time: 351 us; the launch traced here: 346 us
  waiting for transfers between devices  197 us (56%)
  matrix products  65.6 us (19%)
  local copies, waits for them, and re-layouts  56.5 us (16%)
  other arithmetic  20.5 us (6%)
  starting transfers between devices  6.02 us (2%)
    all_to_all x1, waiting for transfers between devices, per_device(): lax.all_to_all(send_both, 'ctx', split_axis=0, concat_axis=0, tiled=True)  172 us
    dot_general x16, matrix products, weighted(): jnp.dot(prob_rows, value_rows, preferred_element_type=jnp.float32)  38 us
    dot_general x16, matrix products, masked_scores(): lax.dot_general(query_head, key_rows, (((1,), (1,)), ((), ())), preferred...  27.6 us
    ppermute x1, waiting for transfers between devices, passed_along(): return lax.ppermute(value, axis, pairs)  25.6 us
    gather x2, local copies, waits for them, and re-layouts, per_device(): send_both = jnp.concatenate([key_heads, value_heads], axis=2)[safe_asked]  19.1 us
    unnamed x10, local copies, waits for them, and re-layouts  12.4 us
    reduce_sum x16, other arithmetic, row_stats(): row_total = jnp.sum(jnp.exp(scores - row_top[:, None]), axis=1)  9.17 us
    gather x1, local copies, waits for them, and re-layouts, per_device(): flat_slots[flat_slot].reshape(HEADS, PICKS * block_rows, last_width)  8.37 us
  transfers between devices with their start and end apart: 2, of which 2 were waited for; matrix products, arithmetic and copies ran while one was open for 3% of the time, Pallas kernels for 0%

commit v1 on v0

--- a/solution.py
+++ b/solution.py
@@ -1,11 +1,20 @@
+import functools
+import math
+
 import jax
 import jax.numpy as jnp
 from jax import lax
+from jax.experimental import pallas as pl
+from jax.experimental.pallas import tpu as pltpu
 from jax.sharding import PartitionSpec as P
 
 HEADS = 16
 HD = 128
 PICKS = 2
+EXP2_SCALE = HD ** -0.5 * math.log2(math.e)
+LANES = 128
+STAT_ROWS = 16
+VMEM_BYTES = 48 * 1024 * 1024
 
 
 def passed_along(value, axis, steps):
@@ -33,7 +42,344 @@
     return (jnp.where(was_found, head_table, -1), pick_order)
 
 
-def per_device(queries, keys, values, picks):
+def pack_kernel(plan_ref, *refs, copies, source_count):
+    sources = refs[:source_count]
+    outputs = refs[source_count:-1]
+    sems = refs[-1]
+    started = []
+    for number, (source, plan_at, target, place) in enumerate(copies):
+        head = jnp.maximum(plan_ref[plan_at], 0)
+        columns = pl.ds(pl.multiple_of(head * HD, HD), HD)
+        copy = pltpu.make_async_copy(
+            sources[source].at[:, columns], outputs[target].at[place], sems.at[number]
+        )
+        copy.start()
+        started.append(copy)
+    for copy in started:
+        copy.wait()
+
+
+def pack(plan, sources, copies, places):
+    rows = sources[0].shape[0]
+    return pl.pallas_call(
+        functools.partial(pack_kernel, copies=copies, source_count=len(sources)),
+        grid_spec=pltpu.PrefetchScalarGridSpec(
+            num_scalar_prefetch=1,
+            grid=(1,),
+            in_specs=[pl.BlockSpec(memory_space=pl.ANY)] * len(sources),
+            out_specs=[pl.BlockSpec(memory_space=pl.ANY)] * len(places),
+            scratch_shapes=[pltpu.SemaphoreType.DMA((len(copies),))],
+        ),
+        out_shape=[jax.ShapeDtypeStruct((count, rows, HD), jnp.bfloat16) for count in places],
+        compiler_params=pltpu.CompilerParams(vmem_limit_bytes=VMEM_BYTES),
+        cost_estimate=pl.CostEstimate(
+            flops=0, bytes_accessed=4 * rows * HD * len(copies), transcendentals=0
+        ),
+    )(plan, *sources)
+
+
+def diagonal():
+    shape = (LANES, LANES)
+    return lax.broadcasted_iota(jnp.int32, shape, 0) == lax.broadcasted_iota(jnp.int32, shape, 1)
+
+
+def raw_scores(query_rows, key_rows):
+    return lax.dot_general(
+        query_rows, key_rows, (((1,), (1,)), ((), ())), preferred_element_type=jnp.float32
+    )
+
+
+def with_ones(value_rows):
+    return jnp.concatenate([value_rows, jnp.ones_like(value_rows)], axis=1)
+
+
+def soft_part(score_parts, value_parts):
+    top = functools.reduce(
+        jnp.maximum, [jnp.max(scores, axis=1, keepdims=True) for scores in score_parts]
+    )
+    total = None
+    for scores, value_rows in zip(score_parts, value_parts):
+        weights = jnp.exp2((scores - top) * EXP2_SCALE).astype(jnp.bfloat16)
+        part = jnp.dot(weights, value_rows, preferred_element_type=jnp.float32)
+        total = part if total is None else total + part
+    sums = total[:, HD:]
+    return total[:, :HD] / sums, top * EXP2_SCALE + jnp.log2(sums)
+
+
+def across_lanes(column):
+    eye = diagonal()
+    return [
+        jnp.sum(jnp.where(eye, column[at : at + LANES], 0.0), axis=0, keepdims=True)
+        for at in range(0, column.shape[0], LANES)
+    ]
+
+
+def three_parts(stat_rows):
+    stats = jnp.concatenate(stat_rows, axis=0)
+    first = stats.astype(jnp.bfloat16).astype(jnp.float32)
+    second = (stats - first).astype(jnp.bfloat16).astype(jnp.float32)
+    third = stats - first - second
+    parts = jnp.concatenate([first, second, third], axis=0)
+    pad = jnp.zeros((STAT_ROWS - parts.shape[0], LANES), jnp.float32)
+    return jnp.concatenate([parts, pad], axis=0).astype(jnp.bfloat16)
+
+
+def attend_kernel(plan_ref, query_ref, key_ref, value_ref, out_ref, *, plan_at, tile):
+    head = plan_ref[plan_at + pl.program_id(0)]
+    rows = query_ref.shape[1]
+
+    @pl.when(head >= 0)
+    def _():
+        key_rows = key_ref[...]
+        value_rows = with_ones(value_ref[...])
+        stat_rows = []
+        for at in range(0, rows, tile):
+            scores = raw_scores(query_ref[0, at : at + tile, :], key_rows)
+            outputs, sums = soft_part([scores], [value_rows])
+            out_ref[0, at : at + tile, :] = outputs.astype(jnp.bfloat16)
+            stat_rows += across_lanes(sums)
+        out_ref[0, rows:, :] = three_parts(stat_rows)
+
+
+def attend(plan, plan_at, queries, keys, values):
+    slots, rows, _ = queries.shape
+    head_column = lambda slot, plan_ref: (0, jnp.maximum(plan_ref[plan_at + slot], 0))
+    return pl.pallas_call(
+        functools.partial(attend_kernel, plan_at=plan_at, tile=min(rows, 256)),
+        grid_spec=pltpu.PrefetchScalarGridSpec(
+            num_scalar_prefetch=1,
+            grid=(slots,),
+            in_specs=[
+                pl.BlockSpec((1, rows, HD), lambda slot, plan_ref: (slot, 0, 0)),
+                pl.BlockSpec((rows, HD), head_column),
+                pl.BlockSpec((rows, HD), head_column),
+            ],
+            out_specs=pl.BlockSpec((1, rows + STAT_ROWS, HD), lambda slot, plan_ref: (slot, 0, 0)),
+        ),
+        out_shape=jax.ShapeDtypeStruct((slots, rows + STAT_ROWS, HD), jnp.bfloat16),
+        compiler_params=pltpu.CompilerParams(vmem_limit_bytes=VMEM_BYTES),
+        cost_estimate=pl.CostEstimate(
+            flops=4 * slots * rows * rows * HD,
+            bytes_accessed=8 * slots * rows * HD,
+            transcendentals=slots * rows * rows,
+        ),
+    )(plan, queries, keys, values)
+
+
+def own_kernel(plan_ref, query_ref, key_ref, value_ref, near_ref, out_ref, *, plan_at, tile):
+    slot = plan_ref[plan_at + pl.program_id(0)]
+    rows = query_ref.shape[0]
+
+    def run(use_near):
+        value_rows = with_ones(value_ref[...])
+        if use_near:
+            near_keys = near_ref[0]
+            near_values = with_ones(near_ref[1])
+        stat_rows = []
+        for at in range(0, rows, tile):
+            reach = at + tile
+            query_rows = query_ref[at:reach, :]
+            scores = raw_scores(query_rows, key_ref[:reach, :])
+            shape = scores.shape
+            causal = lax.broadcasted_iota(jnp.int32, shape, 0) + at >= lax.broadcasted_iota(
+                jnp.int32, shape, 1
+            )
+            score_parts = [jnp.where(causal, scores, -jnp.inf)]
+            value_parts = [value_rows[:reach]]
+            if use_near:
+                score_parts.append(raw_scores(query_rows, near_keys))
+                value_parts.append(near_values)
+            outputs, sums = soft_part(score_parts, value_parts)
+            out_ref[0, at:reach, :] = outputs.astype(jnp.bfloat16)
+            stat_rows += across_lanes(sums)
+        out_ref[0, rows:, :] = three_parts(stat_rows)
+
+    @pl.when(slot >= 0)
+    def _():
+        run(True)
+
+    @pl.when(slot < 0)
+    def _():
+        run(False)
+
+
+def own_part(plan, plan_at, queries, keys, values, near):
+    rows = queries.shape[0]
+    column = lambda head, plan_ref: (0, head)
+    return pl.pallas_call(
+        functools.partial(own_kernel, plan_at=plan_at, tile=min(rows, 256)),
+        grid_spec=pltpu.PrefetchScalarGridSpec(
+            num_scalar_prefetch=1,
+            grid=(HEADS,),
+            in_specs=[
+                pl.BlockSpec((rows, HD), column),
+                pl.BlockSpec((rows, HD), column),
+                pl.BlockSpec((rows, HD), column),
+                pl.BlockSpec(
+                    (2, rows, HD),
+                    lambda head, plan_ref: (jnp.maximum(plan_ref[plan_at + head], 0), 0, 0),
+                ),
+            ],
+            out_specs=pl.BlockSpec((1, rows + STAT_ROWS, HD), lambda head, plan_ref: (head, 0, 0)),
+        ),
+        out_shape=jax.ShapeDtypeStruct((HEADS, rows + STAT_ROWS, HD), jnp.bfloat16),
+        compiler_params=pltpu.CompilerParams(vmem_limit_bytes=VMEM_BYTES),
+        cost_estimate=pl.CostEstimate(
+            flops=4 * HEADS * rows * rows * HD,
+            bytes_accessed=8 * HEADS * rows * HD,
+            transcendentals=HEADS * rows * rows,
+        ),
+    )(plan, queries, keys, values, near)
+
+
+def merge_kernel(plan_ref, own_ref, *refs, places):
+    parts, out_ref, held, sems = refs[: len(places)], refs[-3], refs[-2], refs[-1]
+    rows = out_ref.shape[0]
+    groups = rows // LANES
+    copies = [
+        pltpu.make_async_copy(part, held.at[pl.ds(place, part.shape[0])], sems.at[number])
+        for number, (part, place) in enumerate(zip(parts, places))
+    ]
+    for copy in copies:
+        copy.start()
+    for copy in copies:
+        copy.wait()
+
+    def stats_of(block):
+        stats = block.astype(jnp.float32)
+        return stats[:groups] + stats[groups : 2 * groups] + stats[2 * groups : 3 * groups]
+
+    def one_head(head, carry):
+        found = [plan_ref[head * PICKS + pick] for pick in range(PICKS)]
+        spots = [jnp.maximum(spot, 0) for spot in found]
+        sums = [stats_of(own_ref[head, rows:, :])]
+        for spot, safe in zip(found, spots):
+            sums.append(jnp.where(spot >= 0, stats_of(held[safe, rows:, :]), -jnp.inf))
+        top = functools.reduce(jnp.maximum, sums)
+        shares = [jnp.exp2(part - top) for part in sums]
+        whole = functools.reduce(jnp.add, shares)
+        shares = [share / whole for share in shares]
+        eye = diagonal()
+        columns = pl.ds(pl.multiple_of(head * HD, HD), HD)
+        for group in range(groups):
+            lines = pl.ds(group * LANES, LANES)
+            blocks = [own_ref[head, lines, :].astype(jnp.float32)]
+            for spot, safe in zip(found, spots):
+                block = held[safe, lines, :].astype(jnp.float32)
+                blocks.append(jnp.where(spot >= 0, block, 0.0))
+            mixed = None
+            for block, share in zip(blocks, shares):
+                spread = jnp.broadcast_to(share[group : group + 1, :], (LANES, LANES))
+                column = jnp.sum(jnp.where(eye, spread, 0.0), axis=1, keepdims=True)
+                term = block * column
+                mixed = term if mixed is None else mixed + term
+            out_ref[lines, columns] = mixed.astype(jnp.bfloat16)
+        return carry
+
+    lax.fori_loop(0, HEADS, one_head, 0)
+
+
+def merge(plan, own, parts, places, slot_total):
+    rows = own.shape[1] - STAT_ROWS
+    whole = lambda step, plan_ref: (0, 0, 0)
+    return pl.pallas_call(
+        functools.partial(merge_kernel, places=places),
+        grid_spec=pltpu.PrefetchScalarGridSpec(
+            num_scalar_prefetch=1,
+            grid=(1,),
+            in_specs=[pl.BlockSpec(own.shape, whole)]
+            + [pl.BlockSpec(memory_space=pl.ANY)] * len(parts),
+            out_specs=pl.BlockSpec((rows, HEADS * HD), lambda step, plan_ref: (0, 0)),
+            scratch_shapes=[
+                pltpu.VMEM((slot_total, rows + STAT_ROWS, HD), jnp.bfloat16),
+                pltpu.SemaphoreType.DMA((len(parts),)),
+            ],
+        ),
+        out_shape=jax.ShapeDtypeStruct((rows, HEADS * HD), jnp.bfloat16),
+        compiler_params=pltpu.CompilerParams(vmem_limit_bytes=VMEM_BYTES),
+        cost_estimate=pl.CostEstimate(
+            flops=6 * HEADS * rows * HD,
+            bytes_accessed=2 * (HEADS * 2 + slot_total) * rows * HD,
+            transcendentals=0,
+        ),
+    )(plan, own, *parts)
+
+
+def travelling_queries(queries, keys, values, picks):
+    width = lax.axis_size("ctx")
+    sections = lax.axis_size("pipe")
+    here = lax.axis_index("ctx")
+    slots = max(1, PICKS * HEADS // width)
+    queries, keys, values = queries[0], keys[0], values[0]
+
+    shifts = lax.iota(jnp.int32, width)
+    every_pick = picks[0].reshape(width, HEADS * PICKS)
+    table, every_order = request_table(every_pick, shifts, slots)
+    asking = here - shifts
+    ask = lax.dynamic_index_in_dim(table, here, 0, keepdims=False)[jnp.maximum(asking, 0)]
+    ask = jnp.where((asking >= 0)[:, None], ask, -1)
+    asked_by = here + shifts
+    asked = lax.dynamic_index_in_dim(table, here, 1, keepdims=False)
+    asked = asked[jnp.minimum(asked_by, width - 1)]
+    asked = jnp.where((asked_by < width)[:, None], asked, -1)
+    chosen = lax.dynamic_index_in_dim(every_pick, here, 0, keepdims=False)
+    order = lax.dynamic_index_in_dim(every_order, here, 0, keepdims=False)
+    is_near = (chosen >= 0) & (chosen == here - 1)
+    near_slot = jnp.max(jnp.where(is_near, order, -1).reshape(HEADS, PICKS), axis=1)
+    plan = jnp.concatenate([ask.reshape(-1), asked.reshape(-1), near_slot])
+    asked_at = width * slots
+    near_at = 2 * width * slots
+
+    before = passed_along(picks, "pipe", 1)[0].reshape(width, HEADS * PICKS)
+    before = lax.dynamic_index_in_dim(before, here, 0, keepdims=True)
+    before_order = request_table(before, shifts, slots)[1][0]
+    distance = here - before[0]
+    merge_plan = jnp.where(
+        (before[0] >= 0) & (distance >= 2), (distance - 2) * slots + before_order, -1
+    )
+
+    pieces = [(shift, 0, slots) for shift in piece_order(width)]
+    copies = []
+    for number, (shift, first, count) in enumerate(pieces):
+        copies += [(0, shift * slots + first + slot, number, slot) for slot in range(count)]
+    near_copies = []
+    for slot in range(slots):
+        near_copies += [
+            (0, asked_at + slots + slot, 0, 2 * slot),
+            (1, asked_at + slots + slot, 0, 2 * slot + 1),
+        ]
+    near_send = pack(plan, [keys, values], near_copies, [2 * slots])[0]
+    near = lax.ppermute(near_send, "ctx", [(at, at + 1) for at in range(width - 1)])
+    sends = pack(plan, [queries], copies, [count for _, _, count in pieces])
+
+    own = own_part(plan, near_at, queries, keys, values, near)
+    own = passed_along(own, "pipe", 1)
+
+    arrived, returned = [], []
+    for number, (shift, first, count) in enumerate(pieces):
+        send = sends[number]
+        if number >= 2:
+            send, arrived[number - 2] = lax.optimization_barrier((send, arrived[number - 2]))
+        pairs = [(at, at - shift) for at in range(shift, width)]
+        arrived.append(lax.ppermute(send, "ctx", pairs))
+    for number, (shift, first, count) in enumerate(pieces):
+        part = attend(plan, asked_at + shift * slots + first, arrived[number], keys, values)
+        pairs = [
+            (at * sections + section, (at + shift) * sections + (section + 1) % sections)
+            for at in range(width - shift)
+            for section in range(sections)
+        ]
+        returned.append(lax.ppermute(part, ("ctx", "pipe"), pairs))
+    places = [(shift - 2) * slots + first for shift, first, _ in pieces]
+    return merge(merge_plan, own, returned, places, (width - 2) * slots)[None]
+
+
+def piece_order(width):
+    middle = sorted(range(2, width - 1), key=lambda shift: abs(shift - width // 2))
+    return [width - 1] + middle
+
+
+def travelling_keys(queries, keys, values, picks):
     ctx_width = lax.axis_size("ctx")
     rank_here = lax.axis_index("ctx")
     slot_count = max(1, PICKS * HEADS // ctx_width)
@@ -55,13 +401,13 @@
     causal = row_index[:, None] >= row_index[None, :]
 
     def masked_scores(query_head, key_rows, mask_row):
-        raw_scores = lax.dot_general(
+        scores = lax.dot_general(
             query_head, key_rows, (((1,), (1,)), ((), ())), preferred_element_type=jnp.float32
         )
         allowed = jnp.concatenate(
             [causal, jnp.broadcast_to(mask_row[None, :], (block_rows, PICKS * block_rows))], axis=1
         )
-        return jnp.where(allowed, raw_scores * score_scale, -jnp.inf)
+        return jnp.where(allowed, scores * score_scale, -jnp.inf)
 
     def row_stats(scores):
         row_top = jnp.max(scores, axis=1)
@@ -90,8 +436,13 @@
 
     outputs = lax.map(per_head, (query_heads, all_keys, all_values, remote_mask))
     merged = outputs.transpose(1, 0, 2).reshape(1, block_rows, HEADS * HD)
-    merged = passed_along(merged, "pipe", 1)
-    return merged
+    return passed_along(merged, "pipe", 1)
+
+
+def per_device(queries, keys, values, picks):
+    few_shifts = lax.axis_size("ctx") <= 16
+    run = travelling_queries if few_shifts else travelling_keys
+    return run(queries, keys, values, picks)
 
 
 def solution(mesh):

time: 351 us -> 203 us (0.58)
  the two profiles are of different devices: /device:TPU:26 before, /device:TPU:18 now
where the time goes in v1:
time: 203 us; the launch traced here: 202 us
  waiting for transfers between devices  99.3 us (49%)
  starting transfers between devices  49.6 us (24%)
  Pallas kernels  44.3 us (22%)
  local copies, waits for them, and re-layouts  6.11 us (3%)
  other arithmetic  2.23 us (1%)
    ppermute x6, waiting for transfers between devices, travelling_queries(): returned.append(lax.ppermute(part, ('ctx', 'pipe'), pairs))  42.8 us
    ppermute x6, waiting for transfers between devices, travelling_queries(): arrived.append(lax.ppermute(send, 'ctx', pairs))  37.8 us
    ppermute x6, starting transfers between devices, travelling_queries(): returned.append(lax.ppermute(part, ('ctx', 'pipe'), pairs))  37.1 us
    ppermute x1, waiting for transfers between devices, travelling_queries(): lax.ppermute(near_send, 'ctx', [(at, at + 1) for at in range(width - 1)])  18.7 us
    pallas_call x1, Pallas kernels, own_part(): pl.pallas_call(functools.partial(own_kernel, plan_at=plan_at, tile=min(ro...  18.2 us
    pallas_call x6, Pallas kernels, attend(): pl.pallas_call(functools.partial(attend_kernel, plan_at=plan_at, tile=min...  14.8 us
    ppermute x6, starting transfers between devices, travelling_queries(): arrived.append(lax.ppermute(send, 'ctx', pairs))  8.97 us
    pallas_call x1, Pallas kernels, merge(): pl.pallas_call(functools.partial(merge_kernel, places=places), grid_spec=...  8.59 us
  transfers between devices with their start and end apart: 15, of which 5 were waited for; matrix products, arithmetic and copies ran while one was open for 0% of the time, Pallas kernels for 17%

profile of v1, /device:TPU:18, one launch (start us, length us, event | category | flops | bytes accessed | tf_op | source)
XLA Modules:
  0.0 201.9 jit_solution(8283893855178024559)
XLA Ops:
  0.0 0.8 copy.29
  0.9 0.1 copy.30
  1.0 0.3 convert_reduce_fusion
  1.3 0.6 and_reduce_fusion
  2.0 0.6 fusion
  2.6 0.1 constant_dynamic-slice_fusion.2
  2.8 0.1 copy.35
  2.9 0.1 copy.36
  3.0 0.6 gather_fusion.1
  3.6 0.1 select_n.78
  3.7 0.1 copy.34
  3.8 0.6 gather_fusion
  4.4 0.1 select_n.75
  4.5 0.1 select_n.80
  4.5 0.1 reduce_max.9
  4.8 1.6 copy-done
  6.4 1.6 copy-done.2
  7.9 1.0 shard_map.46
  8.9 3.6 %collective-permute-start.1 = (bf16[8,512,128]{2,1,0:T(8,128)(2,1)S(1)}, bf16[8,512,128]{2,1,0:T(8,128)(2,1)S(1)}, u32[]{:S(2)}, u32[]{:S(2)}) collective-permute-start(bf16[8,512,128]{2,1,0:T(8,128)(2,1)S(1)} %shard_map.46), channel_id=1, source_target_pairs={{0,4},{4,8},{8,12},{12,16},{16,20},{20,24},{24,28},{1,5},{5,9},{9,... | collective-permute-start | bytes 3145736 | tf_op jit(solution)/shard_map/ppermute | solution.py:352
  12.5 1.8 shard_map.48
  14.3 0.7 collective-permute-start.3
  15.0 3.1 %collective-permute-start.5 = (bf16[4,512,128]{2,1,0:T(8,128)(2,1)S(1)}, bf16[4,512,128]{2,1,0:T(8,128)(2,1)S(1)}, u32[]{:S(2)}, u32[]{:S(2)}) collective-permute-start(bf16[4,512,128]{2,1,0:T(8,128)(2,1)S(1)} %get-tuple-element.23), channel_id=1, source_target_pairs={{16,0},{20,4},{24,8},{28,12},{17,1},{21,5},{25,9},{29,13},{18,2},{... | collective-permute-start | bytes 1572872 | tf_op jit(solution)/shard_map/ppermute | solution.py:364
  18.1 18.7 %collective-permute-done.1.near_ref = bf16[8,512,128]{2,1,0:T(8,128)(2,1)S(1)} collective-permute-done((bf16[8,512,128]{2,1,0:T(8,128)(2,1)S(1)}, bf16[8,512,128]{2,1,0:T(8,128)(2,1)S(1)}, u32[]{:S(2)}, u32[]{:S(2)}) %collective-permute-start.1) | collective-permute-done | bytes 1048608 | tf_op jit(solution)/shard_map/ppermute | solution.py:352
  36.7 18.2 %shard_map.47 = bf16[16,528,128]{2,1,0:T(8,128)(2,1)} custom-call(s32[80]{0:T(128)S(1)} %pad_add_fusion.plan_ref, bf16[512,2048]{1,0:T(8,128)(2,1)S(1)} %bitcast.30, bf16[512,2048]{1,0:T(8,128)(2,1)S(1)} %bitcast.14, bf16[512,2048]{1,0:T(8,128)(2,1)} %bitcast.21, bf16[8,512,128]{2,1,0:T(8,128)(2,1)S(1)} %collective-permute-done.1.near_ref), custom_call_target="tpu_custom_call" | custom-call | flops 2147483648 | bytes 8388608 | tf_op jit(solution)/shard_map/pallas_call | solution.py:209
  54.9 1.9 collective-permute-start.7
  56.9 0.7 collective-permute-start.9
  57.6 34.0 %collective-permute-done.7.query_ref = bf16[4,512,128]{2,1,0:T(8,128)(2,1)S(1)} collective-permute-done((bf16[4,512,128]{2,1,0:T(8,128)(2,1)S(1)}, bf16[4,512,128]{2,1,0:T(8,128)(2,1)S(1)}, u32[]{:S(2)}, u32[]{:S(2)}) %collective-permute-start.7) | collective-permute-done | bytes 524320 | tf_op jit(solution)/shard_map/ppermute | solution.py:364
  91.6 1.9 collective-permute-start.11
  93.5 0.8 shard_map.50
  94.3 1.3 collective-permute-start.6
  95.6 0.7 collective-permute-start.13
  96.3 0.8 shard_map.49
  97.1 0.7 collective-permute-start.4
  97.8 4.5 %shard_map.51 = bf16[4,528,128]{2,1,0:T(8,128)(2,1)} custom-call(s32[80]{0:T(128)S(1)} %pad_add_fusion.plan_ref, bf16[4,512,128]{2,1,0:T(8,128)(2,1)S(1)} %collective-permute-done.7.query_ref, bf16[512,2048]{1,0:T(8,128)(2,1)S(1)} %bitcast.17, bf16[512,2048]{1,0:T(8,128)(2,1)S(1)} %bitcast.25), custom_call_target="tpu_custom_call" | custom-call | flops 536870912 | bytes 2097152 | tf_op jit(solution)/shard_map/pallas_call | solution.py:147
  102.4 2.1 %shard_map.52 = bf16[4,528,128]{2,1,0:T(8,128)(2,1)} custom-call(s32[80]{0:T(128)S(1)} %pad_add_fusion.plan_ref, bf16[4,512,128]{2,1,0:T(8,128)(2,1)S(1)} %collective-permute-done.9.query_ref, bf16[512,2048]{1,0:T(8,128)(2,1)S(1)} %bitcast.18, bf16[512,2048]{1,0:T(8,128)(2,1)S(1)} %bitcast.26), custom_call_target="tpu_custom_call" | custom-call | flops 536870912 | bytes 2097152 | tf_op jit(solution)/shard_map/pallas_call | solution.py:147
  104.4 3.8 %collective-permute-done.11.query_ref = bf16[4,512,128]{2,1,0:T(8,128)(2,1)S(1)} collective-permute-done((bf16[4,512,128]{2,1,0:T(8,128)(2,1)S(1)}, bf16[4,512,128]{2,1,0:T(8,128)(2,1)S(1)}, u32[]{:S(2)}, u32[]{:S(2)}) %collective-permute-start.11) | collective-permute-done | bytes 524320 | tf_op jit(solution)/shard_map/ppermute | solution.py:364
  108.2 4.5 %shard_map.53 = bf16[4,528,128]{2,1,0:T(8,128)(2,1)} custom-call(s32[80]{0:T(128)S(1)} %pad_add_fusion.plan_ref, bf16[4,512,128]{2,1,0:T(8,128)(2,1)S(1)} %collective-permute-done.11.query_ref, bf16[512,2048]{1,0:T(8,128)(2,1)S(1)} %bitcast.19, bf16[512,2048]{1,0:T(8,128)(2,1)S(1)} %bitcast.27), custom_call_target="tpu_custom_call" | custom-call | flops 536870912 | bytes 2097152 | tf_op jit(solution)/shard_map/pallas_call | solution.py:147
  112.8 1.5 collective-permute-start.10
  114.3 2.1 %shard_map.54 = bf16[4,528,128]{2,1,0:T(8,128)(2,1)} custom-call(s32[80]{0:T(128)S(1)} %pad_add_fusion.plan_ref, bf16[4,512,128]{2,1,0:T(8,128)(2,1)S(1)} %collective-permute-done.13.query_ref, bf16[512,2048]{1,0:T(8,128)(2,1)S(1)} %bitcast.20, bf16[512,2048]{1,0:T(8,128)(2,1)S(1)} %bitcast.28), custom_call_target="tpu_custom_call" | custom-call | flops 536870912 | bytes 2097152 | tf_op jit(solution)/shard_map/pallas_call | solution.py:147
  116.3 4.7 %collective-permute-start.8 = (bf16[4,528,128]{2,1,0:T(8,128)(2,1)}, bf16[4,528,128]{2,1,0:T(8,128)(2,1)}, u32[]{:S(2)}, u32[]{:S(2)}) collective-permute-start(bf16[4,528,128]{2,1,0:T(8,128)(2,1)} %shard_map.51), channel_id=1, source_target_pairs={{0,13},{1,14},{2,15},{3,12},{4,17},{5,18},{6,19},{7,16},{8,21},{9,... | collective-permute-start | bytes 1622024 | tf_op jit(solution)/shard_map/ppermute | solution.py:372
  121.1 1.5 collective-permute-start.14
  122.5 27.5 %collective-permute-start.12 = (bf16[4,528,128]{2,1,0:T(8,128)(2,1)}, bf16[4,528,128]{2,1,0:T(8,128)(2,1)}, u32[]{:S(2)}, u32[]{:S(2)}) collective-permute-start(bf16[4,528,128]{2,1,0:T(8,128)(2,1)} %shard_map.53), channel_id=1, source_target_pairs={{0,9},{1,10},{2,11},{3,8},{4,13},{5,14},{6,15},{7,12},{8,17},{9,18... | collective-permute-start | bytes 1622024 | tf_op jit(solution)/shard_map/ppermute | solution.py:372
  150.0 0.1 copy.28
  150.1 0.2 dynamic-slice_reduce_fusion
  150.3 0.2 convert_reduce_fusion.1
  150.5 4.2 %collective-permute-done.8.refs_2_ = bf16[4,528,128]{2,1,0:T(8,128)(2,1)} collective-permute-done((bf16[4,528,128]{2,1,0:T(8,128)(2,1)}, bf16[4,528,128]{2,1,0:T(8,128)(2,1)}, u32[]{:S(2)}, u32[]{:S(2)}) %collective-permute-start.8) | collective-permute-done | bytes 540704 | tf_op jit(solution)/shard_map/ppermute | solution.py:372
  154.7 38.6 %collective-permute-done.12.refs_4_ = bf16[4,528,128]{2,1,0:T(8,128)(2,1)} collective-permute-done((bf16[4,528,128]{2,1,0:T(8,128)(2,1)}, bf16[4,528,128]{2,1,0:T(8,128)(2,1)}, u32[]{:S(2)}, u32[]{:S(2)}) %collective-permute-start.12) | collective-permute-done | bytes 540704 | tf_op jit(solution)/shard_map/ppermute | solution.py:372
  193.3 8.6 %shard_map.55 = bf16[512,2048]{1,0:T(8,128)(2,1)} custom-call(s32[32]{0:T(128)S(1)} %and_select_fusion.3.plan_ref, bf16[16,528,128]{2,1,0:T(8,128)(2,1)S(1)} %collective-permute-done.2.own_ref, bf16[4,528,128]{2,1,0:T(8,128)(2,1)S(1)} %collective-permute-done.4.refs_0_, bf16[4,528,128]{2,1,0:T(8,128)(2,1)S(1)} %collective-permute-done.6.refs_1_, ...), custom_call_target="tpu_custom_call" | custom-call | flops 6291456 | bytes 7340032 | tf_op jit(solution)/shard_map/pallas_call | solution.py:285
  (39 shorter events, 0.5 us)
Async XLA Ops:
  4.8 1.6 copy-start
  6.4 1.6 copy-start.2
  7.9 4.5 %copy-start.4 = (bf16[1,512,2048]{2,1,0:T(8,128)(2,1)S(1)}, bf16[1,512,2048]{2,1,0:T(8,128)(2,1)}, u32[]{:S(2)}) copy-start(bf16[1,512,2048]{2,1,0:T(8,128)(2,1)} %param.4) | copy-start | bytes 6291460
  8.9 27.8 %copy-start.1 = (bf16[1,512,2048]{2,1,0:T(8,128)(2,1)S(1)}, bf16[1,512,2048]{2,1,0:T(8,128)(2,1)}, u32[]{:S(2)}) copy-start(bf16[1,512,2048]{2,1,0:T(8,128)(2,1)} %param.5) | copy-start | bytes 6291460
  8.9 27.8 %collective-permute-start.1 = (bf16[8,512,128]{2,1,0:T(8,128)(2,1)S(1)}, bf16[8,512,128]{2,1,0:T(8,128)(2,1)S(1)}, u32[]{:S(2)}, u32[]{:S(2)}) collective-permute-start(bf16[8,512,128]{2,1,0:T(8,128)(2,1)S(1)} %shard_map.46), channel_id=1, source_target_pairs={{0,4},{4,8},{8,12},{12,16},{16,20},{20,24},{24,28},{1,5},{5,9},{9,... | collective-permute-start | bytes 3145736 | tf_op jit(solution)/shard_map/ppermute | solution.py:352
  14.3 40.6 %collective-permute-start.3 = (bf16[4,512,128]{2,1,0:T(8,128)(2,1)S(1)}, bf16[4,512,128]{2,1,0:T(8,128)(2,1)S(1)}, u32[]{:S(2)}, u32[]{:S(2)}) collective-permute-start(bf16[4,512,128]{2,1,0:T(8,128)(2,1)S(1)} %get-tuple-element.20), channel_id=1, source_target_pairs={{28,0},{29,1},{30,2},{31,3}} | collective-permute-start | bytes 1572872 | tf_op jit(solution)/shard_map/ppermute | solution.py:364
  15.0 78.5 %copy-start.3 = (bf16[1,512,2048]{2,1,0:T(8,128)(2,1)S(1)}, bf16[1,512,2048]{2,1,0:T(8,128)(2,1)}, u32[]{:S(2)}) copy-start(bf16[1,512,2048]{2,1,0:T(8,128)(2,1)} %param.6) | copy-start | bytes 6291460
  15.0 41.9 %collective-permute-start.5 = (bf16[4,512,128]{2,1,0:T(8,128)(2,1)S(1)}, bf16[4,512,128]{2,1,0:T(8,128)(2,1)S(1)}, u32[]{:S(2)}, u32[]{:S(2)}) collective-permute-start(bf16[4,512,128]{2,1,0:T(8,128)(2,1)S(1)} %get-tuple-element.23), channel_id=1, source_target_pairs={{16,0},{20,4},{24,8},{28,12},{17,1},{21,5},{25,9},{29,13},{18,2},{... | collective-permute-start | bytes 1572872 | tf_op jit(solution)/shard_map/ppermute | solution.py:364
  54.9 138.4 %collective-permute-start.2 = (bf16[16,528,128]{2,1,0:T(8,128)(2,1)}, bf16[16,528,128]{2,1,0:T(8,128)(2,1)S(1)}, u32[]{:S(2)}, u32[]{:S(2)}) collective-permute-start(bf16[16,528,128]{2,1,0:T(8,128)(2,1)} %shard_map.47), channel_id=1, source_target_pairs={{0,1},{1,2},{2,3},{3,0},{4,5},{5,6},{6,7},{7,4},{8,9},{9,10},{10,1... | collective-permute-start | bytes 6488072 | tf_op jit(solution)/shard_map/ppermute | solution.py:23
  54.9 36.6 %collective-permute-start.7 = (bf16[4,512,128]{2,1,0:T(8,128)(2,1)S(1)}, bf16[4,512,128]{2,1,0:T(8,128)(2,1)S(1)}, u32[]{:S(2)}, u32[]{:S(2)}) collective-permute-start(bf16[4,512,128]{2,1,0:T(8,128)(2,1)S(1)} %get-tuple-element.26), channel_id=1, source_target_pairs={{12,0},{16,4},{20,8},{24,12},{28,16},{13,1},{17,5},{21,9},{25,13},... | collective-permute-start | bytes 1572872 | tf_op jit(solution)/shard_map/ppermute | solution.py:364
  56.9 38.7 %collective-permute-start.9 = (bf16[4,512,128]{2,1,0:T(8,128)(2,1)S(1)}, bf16[4,512,128]{2,1,0:T(8,128)(2,1)S(1)}, u32[]{:S(2)}, u32[]{:S(2)}) collective-permute-start(bf16[4,512,128]{2,1,0:T(8,128)(2,1)S(1)} %get-tuple-element.29), channel_id=1, source_target_pairs={{20,0},{24,4},{28,8},{21,1},{25,5},{29,9},{22,2},{26,6},{30,10},{2... | collective-permute-start | bytes 1572872 | tf_op jit(solution)/shard_map/ppermute | solution.py:364
  91.6 16.7 %collective-permute-start.11 = (bf16[4,512,128]{2,1,0:T(8,128)(2,1)S(1)}, bf16[4,512,128]{2,1,0:T(8,128)(2,1)S(1)}, u32[]{:S(2)}, u32[]{:S(2)}) collective-permute-start(bf16[4,512,128]{2,1,0:T(8,128)(2,1)S(1)} %get-tuple-element.31), channel_id=1, source_target_pairs={{8,0},{12,4},{16,8},{20,12},{24,16},{28,20},{9,1},{13,5},{17,9},{2... | collective-permute-start | bytes 1572872 | tf_op jit(solution)/shard_map/ppermute | solution.py:364
  94.3 26.7 %collective-permute-start.6 = (bf16[4,528,128]{2,1,0:T(8,128)(2,1)S(1)}, bf16[4,528,128]{2,1,0:T(8,128)(2,1)S(1)}, u32[]{:S(2)}, u32[]{:S(2)}) collective-permute-start(bf16[4,528,128]{2,1,0:T(8,128)(2,1)S(1)} %shard_map.50), channel_id=1, source_target_pairs={{0,17},{1,18},{2,19},{3,16},{4,21},{5,22},{6,23},{7,20},{8,25},{9,... | collective-permute-start | bytes 1622024 | tf_op jit(solution)/shard_map/ppermute | solution.py:372
  95.6 17.2 %collective-permute-start.13 = (bf16[4,512,128]{2,1,0:T(8,128)(2,1)S(1)}, bf16[4,512,128]{2,1,0:T(8,128)(2,1)S(1)}, u32[]{:S(2)}, u32[]{:S(2)}) collective-permute-start(bf16[4,512,128]{2,1,0:T(8,128)(2,1)S(1)} %get-tuple-element.32), channel_id=1, source_target_pairs={{24,0},{28,4},{25,1},{29,5},{26,2},{30,6},{27,3},{31,7}} | collective-permute-start | bytes 1572872 | tf_op jit(solution)/shard_map/ppermute | solution.py:364
  97.1 25.4 %collective-permute-start.4 = (bf16[4,528,128]{2,1,0:T(8,128)(2,1)S(1)}, bf16[4,528,128]{2,1,0:T(8,128)(2,1)S(1)}, u32[]{:S(2)}, u32[]{:S(2)}) collective-permute-start(bf16[4,528,128]{2,1,0:T(8,128)(2,1)S(1)} %shard_map.49), channel_id=1, source_target_pairs={{0,29},{1,30},{2,31},{3,28}} | collective-permute-start | bytes 1622024 | tf_op jit(solution)/shard_map/ppermute | solution.py:372
  102.4 5.9 %copy-start.5 = (s32[1,8,16,2]{2,3,1,0:T(2,128)S(1)}, s32[1,8,16,2]{2,3,1,0:T(2,128)}, u32[]{:S(2)}) copy-start(s32[1,8,16,2]{2,3,1,0:T(2,128)} %param.7) | copy-start | bytes 3076
  108.2 8.1 %collective-permute-start = (s32[1,8,16,2]{2,3,1,0:T(2,128)S(1)}, s32[1,8,16,2]{2,3,1,0:T(2,128)S(1)}, u32[]{:S(2)}, u32[]{:S(2)}) collective-permute-start(s32[1,8,16,2]{2,3,1,0:T(2,128)S(1)} %copy-done.5), channel_id=1, source_target_pairs={{0,1},{1,2},{2,3},{3,0},{4,5},{5,6},{6,7},{7,4},{8,9},{9,10},{10,1... | collective-permute-start | bytes 3080 | tf_op jit(solution)/shard_map/ppermute | solution.py:23
  112.8 37.7 %collective-permute-start.10 = (bf16[4,528,128]{2,1,0:T(8,128)(2,1)}, bf16[4,528,128]{2,1,0:T(8,128)(2,1)}, u32[]{:S(2)}, u32[]{:S(2)}) collective-permute-start(bf16[4,528,128]{2,1,0:T(8,128)(2,1)} %shard_map.52), channel_id=1, source_target_pairs={{0,21},{1,22},{2,23},{3,20},{4,25},{5,26},{6,27},{7,24},{8,29},{9,... | collective-permute-start | bytes 1622024 | tf_op jit(solution)/shard_map/ppermute | solution.py:372
  116.3 38.3 %collective-permute-start.8 = (bf16[4,528,128]{2,1,0:T(8,128)(2,1)}, bf16[4,528,128]{2,1,0:T(8,128)(2,1)}, u32[]{:S(2)}, u32[]{:S(2)}) collective-permute-start(bf16[4,528,128]{2,1,0:T(8,128)(2,1)} %shard_map.51), channel_id=1, source_target_pairs={{0,13},{1,14},{2,15},{3,12},{4,17},{5,18},{6,19},{7,16},{8,21},{9,... | collective-permute-start | bytes 1622024 | tf_op jit(solution)/shard_map/ppermute | solution.py:372
  121.1 33.6 %collective-permute-start.14 = (bf16[4,528,128]{2,1,0:T(8,128)(2,1)}, bf16[4,528,128]{2,1,0:T(8,128)(2,1)}, u32[]{:S(2)}, u32[]{:S(2)}) collective-permute-start(bf16[4,528,128]{2,1,0:T(8,128)(2,1)} %shard_map.54), channel_id=1, source_target_pairs={{0,25},{1,26},{2,27},{3,24},{4,29},{5,30},{6,31},{7,28}} | collective-permute-start | bytes 1622024 | tf_op jit(solution)/shard_map/ppermute | solution.py:372
  122.5 70.8 %collective-permute-start.12 = (bf16[4,528,128]{2,1,0:T(8,128)(2,1)}, bf16[4,528,128]{2,1,0:T(8,128)(2,1)}, u32[]{:S(2)}, u32[]{:S(2)}) collective-permute-start(bf16[4,528,128]{2,1,0:T(8,128)(2,1)} %shard_map.53), channel_id=1, source_target_pairs={{0,9},{1,10},{2,11},{3,8},{4,13},{5,14},{6,15},{7,12},{8,17},{9,18... | collective-permute-start | bytes 1622024 | tf_op jit(solution)/shard_map/ppermute | solution.py:372

commit v2 on v0

--- a/solution.py
+++ b/solution.py
@@ -1,11 +1,20 @@
+import functools
+import math
+
 import jax
 import jax.numpy as jnp
 from jax import lax
+from jax.experimental import pallas as pl
+from jax.experimental.pallas import tpu as pltpu
 from jax.sharding import PartitionSpec as P
 
 HEADS = 16
 HD = 128
 PICKS = 2
+EXP2_SCALE = HD ** -0.5 * math.log2(math.e)
+LANES = 128
+STAT_ROWS = 16
+VMEM_BYTES = 48 * 1024 * 1024
 
 
 def passed_along(value, axis, steps):
@@ -33,7 +42,433 @@
     return (jnp.where(was_found, head_table, -1), pick_order)
 
 
-def per_device(queries, keys, values, picks):
+def call(kernel, name_space, outputs, out_specs, scratch=(), flops=0, moved=0, exps=0):
+    return pl.pallas_call(
+        kernel,
+        in_specs=name_space,
+        out_specs=out_specs,
+        out_shape=outputs,
+        scratch_shapes=list(scratch),
+        compiler_params=pltpu.CompilerParams(vmem_limit_bytes=VMEM_BYTES),
+        cost_estimate=pl.CostEstimate(flops=20 * flops, bytes_accessed=moved, transcendentals=exps),
+    )
+
+
+SCALARS = pl.BlockSpec(memory_space=pltpu.SMEM)
+IN_HBM = pl.BlockSpec(memory_space=pltpu.HBM)
+IN_VMEM = pl.BlockSpec(memory_space=pltpu.VMEM)
+
+
+def list_heads(heads_ref, start, picks_ref, block, owner, slots):
+    width = picks_ref.shape[0]
+    for slot in range(slots):
+        heads_ref[start + slot] = -1
+    valid = (block >= 0) & (block < width) & (owner >= 0) & (owner < width)
+    row = jnp.clip(block, 0, width - 1)
+
+    def look(number, found):
+        pick, head = number // HEADS, number % HEADS
+        hit = valid & (picks_ref[row, pick, head] == owner)
+
+        @pl.when(hit)
+        def _():
+            heads_ref[start + found] = head
+
+        return found + hit.astype(jnp.int32)
+
+    lax.fori_loop(0, PICKS * HEADS, look, jnp.int32(0))
+
+
+def pack_kernel(here_ref, picks_ref, *refs, jobs, slots):
+    sources, outputs = refs[:3], refs[3 : 3 + len(jobs)]
+    heads_ref, sems = refs[-2], refs[-1]
+    here = here_ref[0]
+    listed = {}
+    for shift, first, count, is_near in jobs:
+        key = (shift, is_near)
+        if key not in listed:
+            listed[key] = len(listed) * slots
+            block, owner = (here + shift, here) if is_near else (here, here - shift)
+            list_heads(heads_ref, listed[key], picks_ref, block, owner, slots)
+    copies = []
+    for (shift, first, count, is_near), output in zip(jobs, outputs):
+        for slot in range(count):
+            head = jnp.maximum(heads_ref[listed[shift, is_near] + first + slot], 0)
+            columns = pl.ds(pl.multiple_of(head * HD, HD), HD)
+            for place, source in enumerate(sources[1:] if is_near else sources[:1]):
+                target = output.at[2 * slot + place if is_near else slot]
+                copy = pltpu.make_async_copy(
+                    source.at[:, columns], target, sems.at[len(copies)]
+                )
+                copy.start()
+                copies.append(copy)
+    for copy in copies:
+        copy.wait()
+
+
+def pack(here, picks, queries, keys, values, jobs, slots):
+    rows = queries.shape[0]
+    sizes = [2 * count if is_near else count for _, _, count, is_near in jobs]
+    return call(
+        functools.partial(pack_kernel, jobs=jobs, slots=slots),
+        [SCALARS, SCALARS, IN_HBM, IN_HBM, IN_HBM],
+        [jax.ShapeDtypeStruct((size, rows, HD), jnp.bfloat16) for size in sizes],
+        [IN_HBM] * len(sizes),
+        [pltpu.SMEM((len(jobs) * slots,), jnp.int32), pltpu.SemaphoreType.DMA((sum(sizes),))],
+        moved=4 * rows * HD * sum(sizes),
+    )(here, picks, queries, keys, values)
+
+
+def diagonal():
+    shape = (LANES, LANES)
+    return lax.broadcasted_iota(jnp.int32, shape, 0) == lax.broadcasted_iota(jnp.int32, shape, 1)
+
+
+def raw_scores(query_rows, key_rows):
+    return lax.dot_general(
+        query_rows, key_rows, (((1,), (1,)), ((), ())), preferred_element_type=jnp.float32
+    )
+
+
+def with_ones(value_rows):
+    return jnp.concatenate([value_rows, jnp.ones_like(value_rows)], axis=1)
+
+
+def soft_part(scores, value_rows):
+    top = jnp.max(scores, axis=1, keepdims=True)
+    weights = jnp.exp2((scores - top) * EXP2_SCALE).astype(jnp.bfloat16)
+    total = jnp.dot(weights, value_rows, preferred_element_type=jnp.float32)
+    sums = total[:, HD:]
+    return total[:, :HD] / sums, top * EXP2_SCALE + jnp.log2(sums)
+
+
+def across_lanes(column):
+    eye = diagonal()
+    return [
+        jnp.sum(jnp.where(eye, column[at : at + LANES], 0.0), axis=0, keepdims=True)
+        for at in range(0, column.shape[0], LANES)
+    ]
+
+
+def down_rows(line):
+    spread = jnp.broadcast_to(line, (LANES, LANES))
+    return jnp.sum(jnp.where(diagonal(), spread, 0.0), axis=1, keepdims=True)
+
+
+def three_parts(stats):
+    first = stats.astype(jnp.bfloat16).astype(jnp.float32)
+    second = (stats - first).astype(jnp.bfloat16).astype(jnp.float32)
+    third = stats - first - second
+    parts = jnp.concatenate([first, second, third], axis=0)
+    pad = jnp.zeros((STAT_ROWS - parts.shape[0], LANES), jnp.float32)
+    return jnp.concatenate([parts, pad], axis=0).astype(jnp.bfloat16)
+
+
+def stats_of(block, groups):
+    stats = block.astype(jnp.float32)
+    return stats[:groups] + stats[groups : 2 * groups] + stats[2 * groups : 3 * groups]
+
+
+def attend_rows(query_rows, key_rows, value_rows, tile):
+    outputs, lines = [], []
+    for at in range(0, query_rows.shape[0], tile):
+        part, sums = soft_part(raw_scores(query_rows[at : at + tile], key_rows), value_rows)
+        outputs.append(part)
+        lines += across_lanes(sums)
+    return jnp.concatenate(outputs, axis=0), jnp.concatenate(lines, axis=0)
+
+
+def head_columns(head):
+    return pl.ds(pl.multiple_of(head * HD, HD), HD)
+
+
+def attend_kernel(here_ref, picks_ref, key_ref, value_ref, *refs, group, slots):
+    heads_ref = refs[-1]
+    here = here_ref[0]
+    for number, (shift, first, count) in enumerate(group):
+        query_ref, out_ref = refs[number], refs[len(group) + number]
+        rows = query_ref.shape[1]
+        list_heads(heads_ref, 0, picks_ref, here + shift, here, slots)
+        for slot in range(count):
+            head = heads_ref[first + slot]
+
+            @pl.when(head >= 0)
+            def _():
+                columns = head_columns(head)
+                outputs, lines = attend_rows(
+                    query_ref[slot],
+                    key_ref[:, columns],
+                    with_ones(value_ref[:, columns]),
+                    min(rows, 256),
+                )
+                out_ref[slot, :rows, :] = outputs.astype(jnp.bfloat16)
+                out_ref[slot, rows:, :] = three_parts(lines)
+
+
+def attend(here, picks, keys, values, arrived, group, slots):
+    rows = keys.shape[0]
+    total = sum(count for _, _, count in group)
+    return call(
+        functools.partial(attend_kernel, group=group, slots=slots),
+        [SCALARS, SCALARS, IN_VMEM, IN_VMEM] + [IN_VMEM] * len(group),
+        [
+            jax.ShapeDtypeStruct((count, rows + STAT_ROWS, HD), jnp.bfloat16)
+            for _, _, count in group
+        ],
+        [IN_VMEM] * len(group),
+        [pltpu.SMEM((slots,), jnp.int32)],
+        flops=4 * total * rows * rows * HD,
+        moved=8 * total * rows * HD,
+        exps=total * rows * rows,
+    )(here, picks, keys, values, *arrived)
+
+
+def own_kernel(here_ref, query_ref, key_ref, value_ref, out_ref):
+    rows = query_ref.shape[0]
+    tile = min(rows, 256)
+
+    def one_head(head, carry):
+        columns = head_columns(head)
+        value_rows = with_ones(value_ref[:, columns])
+        lines = []
+        for at in range(0, rows, tile):
+            reach = at + tile
+            scores = raw_scores(query_ref[at:reach, columns], key_ref[:reach, columns])
+            row_ids = lax.broadcasted_iota(jnp.int32, scores.shape, 0) + at
+            seen = row_ids >= lax.broadcasted_iota(jnp.int32, scores.shape, 1)
+            outputs, sums = soft_part(jnp.where(seen, scores, -jnp.inf), value_rows[:reach])
+            out_ref[head, at:reach, :] = outputs.astype(jnp.bfloat16)
+            lines += across_lanes(sums)
+        out_ref[head, rows:, :] = three_parts(jnp.concatenate(lines, axis=0))
+        return carry
+
+    lax.fori_loop(0, HEADS, one_head, 0)
+
+
+def own_part(here, queries, keys, values):
+    rows = queries.shape[0]
+    return call(
+        own_kernel,
+        [SCALARS, IN_VMEM, IN_VMEM, IN_VMEM],
+        jax.ShapeDtypeStruct((HEADS, rows + STAT_ROWS, HD), jnp.bfloat16),
+        IN_VMEM,
+        flops=4 * HEADS * rows * rows * HD,
+        moved=8 * HEADS * rows * HD,
+        exps=HEADS * rows * rows,
+    )(here, queries, keys, values)
+
+
+def near_kernel(here_ref, picks_ref, query_ref, own_ref, *refs, shifts, slots):
+    near_refs, out_ref, heads_ref = refs[: len(shifts)], refs[-2], refs[-1]
+    rows = query_ref.shape[0]
+
+    def keep(head, carry):
+        out_ref[head] = own_ref[head]
+        return carry
+
+    lax.fori_loop(0, HEADS, keep, 0)
+    groups = rows // LANES
+    here = here_ref[0]
+    for shift, near_ref in zip(shifts, near_refs):
+        list_heads(heads_ref, 0, picks_ref, here, here - shift, slots)
+        for slot in range(slots):
+            head = heads_ref[slot]
+
+            @pl.when(head >= 0)
+            def _():
+                outputs, lines = attend_rows(
+                    query_ref[:, head_columns(head)],
+                    near_ref[2 * slot],
+                    with_ones(near_ref[2 * slot + 1]),
+                    min(rows, 256),
+                )
+                before = stats_of(out_ref[head, rows:, :], groups)
+                top = jnp.maximum(before, lines)
+                after = top + jnp.log2(jnp.exp2(before - top) + jnp.exp2(lines - top))
+                share = jnp.exp2(lines - after)
+                for group in range(groups):
+                    span = pl.ds(group * LANES, LANES)
+                    old = out_ref[head, span, :].astype(jnp.float32)
+                    new = outputs[group * LANES : (group + 1) * LANES]
+                    mixed = old + (new - old) * down_rows(share[group : group + 1, :])
+                    out_ref[head, span, :] = mixed.astype(jnp.bfloat16)
+                out_ref[head, rows:, :] = three_parts(after)
+
+
+def add_near(here, picks, queries, own, near, shifts, slots):
+    rows = queries.shape[0]
+    count = len(shifts) * slots
+    return call(
+        functools.partial(near_kernel, shifts=shifts, slots=slots),
+        [SCALARS, SCALARS, IN_VMEM, IN_VMEM] + [IN_VMEM] * len(shifts),
+        jax.ShapeDtypeStruct(own.shape, own.dtype),
+        IN_VMEM,
+        [pltpu.SMEM((slots,), jnp.int32)],
+        flops=4 * count * rows * rows * HD,
+        moved=12 * count * rows * HD,
+        exps=count * rows * rows,
+    )(here, picks, queries, own, *near)
+
+
+def merge_kernel(here_ref, picks_ref, own_ref, *refs, places, skipped, slots):
+    count = len(places)
+    parts, out_ref, held, spots_ref, found_ref, sems = refs[:count], *refs[count:]
+    rows = out_ref.shape[0]
+    groups = rows // LANES
+    width = picks_ref.shape[0]
+    here = here_ref[0]
+    copies = [
+        pltpu.make_async_copy(part, held.at[pl.ds(place, part.shape[0])], sems.at[number])
+        for number, (part, place) in enumerate(zip(parts, places))
+    ]
+    for copy in copies:
+        copy.start()
+    for owner in range(width):
+        found_ref[owner] = 0
+
+    def look(number, carry):
+        pick, head = number // HEADS, number % HEADS
+        owner = picks_ref[here, pick, head]
+        safe = jnp.maximum(owner, 0)
+        shift = here - safe
+        order = found_ref[safe]
+        found_ref[safe] = order + (owner >= 0).astype(jnp.int32)
+        is_held = owner >= 0
+        for left_out in skipped:
+            is_held = is_held & (shift != left_out)
+        spots_ref[head * PICKS + pick] = jnp.where(is_held, shift * slots + order, -1)
+        return carry
+
+    lax.fori_loop(0, PICKS * HEADS, look, 0)
+    for copy in copies:
+        copy.wait()
+
+    def one_head(head, carry):
+        found = [spots_ref[head * PICKS + pick] for pick in range(PICKS)]
+        spots = [jnp.maximum(spot, 0) for spot in found]
+        sums = [stats_of(own_ref[head, rows:, :], groups)]
+        for spot, safe in zip(found, spots):
+            sums.append(jnp.where(spot >= 0, stats_of(held[safe, rows:, :], groups), -jnp.inf))
+        top = functools.reduce(jnp.maximum, sums)
+        shares = [jnp.exp2(part - top) for part in sums]
+        whole = functools.reduce(jnp.add, shares)
+        shares = [share / whole for share in shares]
+        columns = head_columns(head)
+        for group in range(groups):
+            span = pl.ds(group * LANES, LANES)
+            mixed = own_ref[head, span, :].astype(jnp.float32)
+            mixed = mixed * down_rows(shares[0][group : group + 1, :])
+            for spot, safe, share in zip(found, spots, shares[1:]):
+                block = jnp.where(spot >= 0, held[safe, span, :].astype(jnp.float32), 0.0)
+                mixed = mixed + block * down_rows(share[group : group + 1, :])
+            out_ref[span, columns] = mixed.astype(jnp.bfloat16)
+        return carry
+
+    lax.fori_loop(0, HEADS, one_head, 0)
+
+
+def merge(here, picks, own, parts, places, skipped, slots):
+    rows = own.shape[1] - STAT_ROWS
+    width = picks.shape[0]
+    return call(
+        functools.partial(merge_kernel, places=places, skipped=skipped, slots=slots),
+        [SCALARS, SCALARS, IN_VMEM] + [pl.BlockSpec(memory_space=pl.ANY)] * len(parts),
+        jax.ShapeDtypeStruct((rows, HEADS * HD), jnp.bfloat16),
+        pl.BlockSpec((rows, HEADS * HD), lambda: (0, 0)),
+        [
+            pltpu.VMEM((width * slots, rows + STAT_ROWS, HD), jnp.bfloat16),
+            pltpu.SMEM((PICKS * HEADS,), jnp.int32),
+            pltpu.SMEM((width,), jnp.int32),
+            pltpu.SemaphoreType.DMA((len(parts),)),
+        ],
+        flops=6 * HEADS * rows * HD,
+        moved=2 * (HEADS * 2 + width * slots) * rows * HD,
+    )(here, picks, own, *parts)
+
+
+def after(value, *earlier):
+    return lax.optimization_barrier((value,) + earlier)[0]
+
+
+def groups_in_order(width, slots):
+    middle = width // 2
+    groups = []
+    for low in range(2, middle):
+        size = max(1, slots // 2) if low == middle - 1 else slots
+        for first in range(0, slots, size):
+            count = min(size, slots - first)
+            groups.append([(low, first, count), (width - low, first, count)])
+    return groups + [[(middle, 0, slots)]]
+
+
+def travelling_queries(queries, keys, values, picks):
+    width = lax.axis_size("ctx")
+    sections = lax.axis_size("pipe")
+    slots = max(1, PICKS * HEADS // width)
+    here = lax.axis_index("ctx").astype(jnp.int32).reshape(1)
+    queries, keys, values = queries[0], keys[0], values[0]
+    own_picks = picks[0].transpose(0, 2, 1)
+
+    groups = groups_in_order(width, slots)
+    near_shifts = (1, width - 1)
+    first_jobs = [(shift, 0, slots, True) for shift in near_shifts]
+    first_jobs += [piece + (False,) for piece in groups[0]]
+    later_jobs = [piece + (False,) for group in groups[1:] for piece in group]
+
+    def up(value, shift):
+        return lax.ppermute(value, "ctx", [(at, at + shift) for at in range(width - shift)])
+
+    def down(value, shift):
+        return lax.ppermute(value, "ctx", [(at, at - shift) for at in range(shift, width)])
+
+    def up_and_on(value, shift):
+        pairs = [
+            (at * sections + section, (at + shift) * sections + (section + 1) % sections)
+            for at in range(width - shift)
+            for section in range(sections)
+        ]
+        return lax.ppermute(value, ("ctx", "pipe"), pairs)
+
+    sends = dict(zip(first_jobs, pack(here, own_picks, queries, keys, values, first_jobs, slots)))
+    near = [up(sends[job], job[0]) for job in first_jobs if job[3]]
+    arrived = [down(sends[piece + (False,)], piece[0]) for piece in groups[0]]
+    before = passed_along(own_picks, "pipe", 1)
+    now = after(here, *[sends[job] for job in first_jobs])
+    sends |= zip(later_jobs, pack(now, own_picks, queries, keys, values, later_jobs, slots))
+
+    own = own_part(after(here, before, sends[later_jobs[0]]), queries, keys, values)
+    last, returned = own, {}
+    for number, group in enumerate(groups):
+        current = arrived
+        if number + 1 < len(groups):
+            waits = [last] + current
+            if number >= 2:
+                waits += [returned[piece] for piece in groups[number - 2]]
+            arrived = [
+                down(after(sends[piece + (False,)], *waits), piece[0])
+                for piece in groups[number + 1]
+            ]
+        waits = [last] + (near if number == 0 else [])
+        if number >= 2:
+            waits += [returned[piece] for piece in groups[number - 2]]
+        parts = attend(
+            after(here, *waits), own_picks, keys, values, current, tuple(group), slots
+        )
+        last = parts[0]
+        for piece, part in zip(group, parts):
+            if number >= 1:
+                part = after(part, *[returned[earlier] for earlier in groups[number - 1]])
+            returned[piece] = up_and_on(part, piece[0])
+        if number == 1:
+            own = add_near(after(here, last, *[returned[piece] for piece in groups[0]]), own_picks, queries, own, near, near_shifts, slots)
+            own_back = passed_along(own, "pipe", 1)
+            last = own
+    places = [shift * slots + first for shift, first, _ in returned]
+    parts = list(returned.values())
+    return merge(here, before, own_back, parts, places, near_shifts, slots)[None]
+
+
+def travelling_keys(queries, keys, values, picks):
     ctx_width = lax.axis_size("ctx")
     rank_here = lax.axis_index("ctx")
     slot_count = max(1, PICKS * HEADS // ctx_width)
@@ -55,13 +490,13 @@
     causal = row_index[:, None] >= row_index[None, :]
 
     def masked_scores(query_head, key_rows, mask_row):
-        raw_scores = lax.dot_general(
+        scores = lax.dot_general(
             query_head, key_rows, (((1,), (1,)), ((), ())), preferred_element_type=jnp.float32
         )
         allowed = jnp.concatenate(
             [causal, jnp.broadcast_to(mask_row[None, :], (block_rows, PICKS * block_rows))], axis=1
         )
-        return jnp.where(allowed, raw_scores * score_scale, -jnp.inf)
+        return jnp.where(allowed, scores * score_scale, -jnp.inf)
 
     def row_stats(scores):
         row_top = jnp.max(scores, axis=1)
@@ -90,8 +525,13 @@
 
     outputs = lax.map(per_head, (query_heads, all_keys, all_values, remote_mask))
     merged = outputs.transpose(1, 0, 2).reshape(1, block_rows, HEADS * HD)
-    merged = passed_along(merged, "pipe", 1)
-    return merged
+    return passed_along(merged, "pipe", 1)
+
+
+def per_device(queries, keys, values, picks):
+    few_shifts = 4 <= lax.axis_size("ctx") <= 16
+    run = travelling_queries if few_shifts else travelling_keys
+    return run(queries, keys, values, picks)
 
 
 def solution(mesh):

time: 351 us -> 180 us (0.51)
  waiting for transfers between devices: 197 us -> 88.9 us
  matrix products: 65.6 us -> 0 us
  local copies, waits for them, and re-layouts: 56.5 us -> 2.3 us
  Pallas kernels: 0 us -> 47 us
  starting transfers between devices: 6.02 us -> 38.3 us
  other arithmetic: 20.5 us -> 0 us
    all_to_all x1 -> x0, waiting for transfers between devices: 172 us -> none  [per_device(): lax.all_to_all(send_both, 'ctx', split_axis=0, concat_axis=0, tiled=True)]
    ppermute x0 -> x16, waiting for transfers between devices: none -> 88.9 us  [the longest x7 70.5 us: up_and_on(): return lax.ppermute(value, ('ctx', 'pipe'), pairs)]
    dot_general x32 -> x0, matrix products: 65.6 us -> none  [the longest x16 38 us: weighted(): jnp.dot(prob_rows, value_rows, preferred_element_type=jnp.float32)]
    pallas_call x0 -> x9, Pallas kernels: none -> 47 us  [the longest x1 16 us: own_part(): call(own_kernel, [SCALARS, IN_VMEM, IN_VMEM, IN_VMEM], jax.ShapeDtypeStru...]
    ppermute x0 -> x16, starting transfers between devices: none -> 38.3 us  [the longest x7 25 us: down(): lax.ppermute(value, 'ctx', [(at, at - shift) for at in range(shift, width)])]
    gather x3 -> x0, local copies, waits for them, and re-layouts: 27.5 us -> none  [the longest x2 19.1 us: per_device(): send_both = jnp.concatenate([key_heads, value_heads], axis=2)[safe_asked]]
    ppermute x1 -> x2, waiting for transfers between devices: 25.6 us -> 0.01 us  [passed_along(): return lax.ppermute(value, axis, pairs)]
    unnamed x10 -> x12, local copies, waits for them, and re-layouts: 12.4 us -> 2.3 us
  transfers between devices with their start and end apart: 2 -> 18, of which waited for: 2 -> 6; matrix products, arithmetic and copies ran while one was open for 3% -> 0% of each run, Pallas kernels for 0% -> 22%
where the time goes in v2:
time: 180 us; the launch traced here: 177 us
  waiting for transfers between devices  88.9 us (49%)
  Pallas kernels  47 us (26%)
  starting transfers between devices  38.3 us (21%)
  local copies, waits for them, and re-layouts  2.3 us (1%)
    ppermute x7, waiting for transfers between devices, up_and_on(): return lax.ppermute(value, ('ctx', 'pipe'), pairs)  70.5 us
    ppermute x7, starting transfers between devices, down(): lax.ppermute(value, 'ctx', [(at, at - shift) for at in range(shift, width)])  25 us
    ppermute x2, waiting for transfers between devices, up(): lax.ppermute(value, 'ctx', [(at, at + shift) for at in range(width - shif...  18.4 us
    pallas_call x1, Pallas kernels, own_part(): call(own_kernel, [SCALARS, IN_VMEM, IN_VMEM, IN_VMEM], jax.ShapeDtypeStru...  16 us
    ppermute x7, starting transfers between devices, up_and_on(): return lax.ppermute(value, ('ctx', 'pipe'), pairs)  9.16 us
    pallas_call x1, Pallas kernels, merge(): call(functools.partial(merge_kernel, places=places, skipped=skipped, slot...  8.01 us
    pallas_call x1, Pallas kernels, add_near(): call(functools.partial(near_kernel, shifts=shifts, slots=slots), [SCALARS...  7.92 us
    pallas_call x2, Pallas kernels, pack(): call(functools.partial(pack_kernel, jobs=jobs, slots=slots), [SCALARS, SC...  7.77 us
  transfers between devices with their start and end apart: 18, of which 6 were waited for; matrix products, arithmetic and copies ran while one was open for 0% of the time, Pallas kernels for 22%

profile of v2, /device:TPU:26, one launch (start us, length us, event | category | flops | bytes accessed | tf_op | source)
XLA Modules:
  0.0 177.0 jit_solution(11603175051460519449)
XLA Ops:
  0.0 0.0 collective-permute-start
  0.0 1.6 copy-done
  1.6 0.7 copy-done.4
  2.3 4.9 %shard_map.46 = (bf16[8,512,128]{2,1,0:T(8,128)(2,1)S(1)}, bf16[8,512,128]{2,1,0:T(8,128)(2,1)S(1)}, bf16[4,512,128]{2,1,0:T(8,128)(2,1)S(1)}, bf16[4,512,128]{2,1,0:T(8,128)(2,1)S(1)}) custom-call(s32[1]{0:T(128)} %bitcast.here_ref, s32[8,2,16]{2,1,0:T(2,128)S(1)} %bitcast.27, bf16[512,2048]{1,0:T(8,128)(2,1)S(1)} %bitcast.8, bf16[512,2048]{1,0:T(8,128)(2,1)} %bitcast.12, ...), custom_call_target="tpu_custom_call" | custom-call | bytes 6291456 | tf_op jit(solution)/shard_map/pallas_call | solution.py:112
  7.2 2.2 %collective-permute-start.3 = (bf16[4,512,128]{2,1,0:T(8,128)(2,1)S(1)}, bf16[4,512,128]{2,1,0:T(8,128)(2,1)S(1)}, u32[]{:S(2)}, u32[]{:S(2)}) collective-permute-start(bf16[4,512,128]{2,1,0:T(8,128)(2,1)S(1)} %get-tuple-element.39), channel_id=1, source_target_pairs={{8,0},{12,4},{16,8},{20,12},{24,16},{28,20},{9,1},{13,5},{17,9},{2... | collective-permute-start | bytes 1572872 | tf_op jit(solution)/shard_map/ppermute | solution.py:422
  9.5 1.3 collective-permute-start.4
  10.8 3.4 %collective-permute-start.1 = (bf16[8,512,128]{2,1,0:T(8,128)(2,1)S(1)}, bf16[8,512,128]{2,1,0:T(8,128)(2,1)S(1)}, u32[]{:S(2)}, u32[]{:S(2)}) collective-permute-start(bf16[8,512,128]{2,1,0:T(8,128)(2,1)S(1)} %get-tuple-element.37), channel_id=1, source_target_pairs={{0,4},{4,8},{8,12},{12,16},{16,20},{20,24},{24,28},{1,5},{5,9},{9,... | collective-permute-start | bytes 3145736 | tf_op jit(solution)/shard_map/ppermute | solution.py:419
  14.2 0.7 collective-permute-start.2
  14.9 2.9 %shard_map.47 = (bf16[2,512,128]{2,1,0:T(8,128)(2,1)S(1)}, bf16[2,512,128]{2,1,0:T(8,128)(2,1)S(1)}, bf16[2,512,128]{2,1,0:T(8,128)(2,1)S(1)}, bf16[2,512,128]{2,1,0:T(8,128)(2,1)S(1)}, bf16[4,512,128]{2,1,0:T(8,128)(2,1)S(1)}) custom-call(s32[1]{0:T(128)} %bitcast.here_ref, s32[8,2,16]{2,1,0:T(2,128)S(1)} %bitcast.28, bf16[512,2048]{1,0:T(8,128)(2,1)S(1)} %bitcast.9, ...), custom_call_target="tpu_custom_call" | custom-call | bytes 3145728 | tf_op jit(solution)/shard_map/pallas_call | solution.py:112
  17.8 0.0 collective-permute-done.picks_ref
  17.8 16.0 %shard_map.48.own_ref = bf16[16,528,128]{2,1,0:T(8,128)(2,1)} custom-call(s32[1]{0:T(128)} %bitcast.here_ref, bf16[512,2048]{1,0:T(8,128)(2,1)S(1)} %bitcast.10, bf16[512,2048]{1,0:T(8,128)(2,1)S(1)} %bitcast.14, bf16[512,2048]{1,0:T(8,128)(2,1)} %bitcast.21), custom_call_target="tpu_custom_call" | custom-call | flops 42949672960 | bytes 8388608 | tf_op jit(solution)/shard_map/pallas_call | solution.py:250
  33.8 0.0 collective-permute-done.3.refs_0_
  33.8 0.0 collective-permute-done.4.refs_1_
  33.8 2.8 %collective-permute-start.5 = (bf16[2,512,128]{2,1,0:T(8,128)(2,1)S(1)}, bf16[2,512,128]{2,1,0:T(8,128)(2,1)S(1)}, u32[]{:S(2)}, u32[]{:S(2)}) collective-permute-start(bf16[2,512,128]{2,1,0:T(8,128)(2,1)S(1)} %get-tuple-element.47), channel_id=1, source_target_pairs={{12,0},{16,4},{20,8},{24,12},{28,16},{13,1},{17,5},{21,9},{25,13},... | collective-permute-start | bytes 786440 | tf_op jit(solution)/shard_map/ppermute | solution.py:422
  36.6 4.8 %collective-permute-start.6 = (bf16[2,512,128]{2,1,0:T(8,128)(2,1)S(1)}, bf16[2,512,128]{2,1,0:T(8,128)(2,1)S(1)}, u32[]{:S(2)}, u32[]{:S(2)}) collective-permute-start(bf16[2,512,128]{2,1,0:T(8,128)(2,1)S(1)} %get-tuple-element.49), channel_id=1, source_target_pairs={{20,0},{24,4},{28,8},{21,1},{25,5},{29,9},{22,2},{26,6},{30,10},{2... | collective-permute-start | bytes 786440 | tf_op jit(solution)/shard_map/ppermute | solution.py:422
  41.4 18.4 %collective-permute-done.1.refs_0_ = bf16[8,512,128]{2,1,0:T(8,128)(2,1)S(1)} collective-permute-done((bf16[8,512,128]{2,1,0:T(8,128)(2,1)S(1)}, bf16[8,512,128]{2,1,0:T(8,128)(2,1)S(1)}, u32[]{:S(2)}, u32[]{:S(2)}) %collective-permute-start.1) | collective-permute-done | bytes 1048608 | tf_op jit(solution)/shard_map/ppermute | solution.py:419
  59.8 0.0 collective-permute-done.2.refs_1_
  59.8 2.7 %shard_map.49 = (bf16[4,528,128]{2,1,0:T(8,128)(2,1)S(1)}, bf16[4,528,128]{2,1,0:T(8,128)(2,1)S(1)}) custom-call(s32[1]{0:T(128)} %bitcast.here_ref, s32[8,2,16]{2,1,0:T(2,128)S(1)} %bitcast.29, bf16[512,2048]{1,0:T(8,128)(2,1)S(1)} %bitcast.15, bf16[512,2048]{1,0:T(8,128)(2,1)} %bitcast.22, bf16[4,512,128]{2,1,0:T(8,128)(2,1)S(1)} %collective-permute-done.3.refs_0_, ...), custom_call_target="tpu_custom_call" | custom-call | flops 21474836480 | bytes 4194304 | tf_op jit(solution)/shard_map/pallas_call | solution.py:211
  62.5 1.3 collective-permute-start.7
  63.8 0.0 collective-permute-done.5.refs_0_
  63.8 0.0 collective-permute-done.6.refs_1_
  63.8 1.3 collective-permute-start.12
  65.1 1.3 collective-permute-start.13
  66.4 0.0 copy-start.1
  66.4 1.4 collective-permute-start.8
  67.9 1.7 shard_map.50
  69.6 16.0 %collective-permute-done.8.refs_1_ = bf16[4,528,128]{2,1,0:T(8,128)(2,1)S(1)} collective-permute-done((bf16[4,528,128]{2,1,0:T(8,128)(2,1)S(1)}, bf16[4,528,128]{2,1,0:T(8,128)(2,1)S(1)}, u32[]{:S(2)}, u32[]{:S(2)}) %collective-permute-start.8) | collective-permute-done | bytes 540704 | tf_op jit(solution)/shard_map/ppermute | solution.py:430
  85.6 5.6 %collective-permute-done.7.refs_0_ = bf16[4,528,128]{2,1,0:T(8,128)(2,1)S(1)} collective-permute-done((bf16[4,528,128]{2,1,0:T(8,128)(2,1)S(1)}, bf16[4,528,128]{2,1,0:T(8,128)(2,1)S(1)}, u32[]{:S(2)}, u32[]{:S(2)}) %collective-permute-start.7) | collective-permute-done | bytes 540704 | tf_op jit(solution)/shard_map/ppermute | solution.py:430
  91.2 7.9 %shard_map.51 = bf16[16,528,128]{2,1,0:T(8,128)(2,1)} custom-call(s32[1]{0:T(128)} %bitcast.here_ref, s32[8,2,16]{2,1,0:T(2,128)S(1)} %bitcast.31, bf16[512,2048]{1,0:T(8,128)(2,1)S(1)} %bitcast.11, bf16[16,528,128]{2,1,0:T(8,128)(2,1)} %shard_map.48.own_ref, bf16[8,512,128]{2,1,0:T(8,128)(2,1)S(1)} %collective-permute-done.1.refs_0_, ...), custom_call_target="tpu_custom_call" | custom-call | flops 21474836480 | bytes 6291456 | tf_op jit(solution)/shard_map/pallas_call | solution.py:301
  99.2 0.0 collective-permute-start.9
  99.2 0.0 collective-permute-done.12.refs_0_
  99.2 0.0 collective-permute-done.13.refs_1_
  99.2 1.3 collective-permute-start.10
  100.5 1.3 collective-permute-start.11
  101.8 11.3 %collective-permute-start.16 = (bf16[4,512,128]{2,1,0:T(8,128)(2,1)S(1)}, bf16[4,512,128]{2,1,0:T(8,128)(2,1)S(1)}, u32[]{:S(2)}, u32[]{:S(2)}) collective-permute-start(bf16[4,512,128]{2,1,0:T(8,128)(2,1)S(1)} %get-tuple-element.67), channel_id=1, source_target_pairs={{16,0},{20,4},{24,8},{28,12},{17,1},{21,5},{25,9},{29,13},{18,2},{... | collective-permute-start | bytes 1572872 | tf_op jit(solution)/shard_map/ppermute | solution.py:422
  113.1 1.7 shard_map.52
  114.8 13.3 %collective-permute-done.10.refs_2_ = bf16[2,528,128]{2,1,0:T(8,128)(2,1)S(1)} collective-permute-done((bf16[2,528,128]{2,1,0:T(8,128)(2,1)S(1)}, bf16[2,528,128]{2,1,0:T(8,128)(2,1)S(1)}, u32[]{:S(2)}, u32[]{:S(2)}) %collective-permute-start.10) | collective-permute-done | bytes 270368 | tf_op jit(solution)/shard_map/ppermute | solution.py:430
  128.2 0.0 collective-permute-done.11.refs_3_
  128.2 1.3 collective-permute-start.14
  129.4 1.3 collective-permute-start.15
  130.7 0.0 collective-permute-done.16.refs_0_
  130.8 1.2 shard_map.53
  132.0 14.8 %collective-permute-done.14.refs_4_ = bf16[2,528,128]{2,1,0:T(8,128)(2,1)S(1)} collective-permute-done((bf16[2,528,128]{2,1,0:T(8,128)(2,1)S(1)}, bf16[2,528,128]{2,1,0:T(8,128)(2,1)S(1)}, u32[]{:S(2)}, u32[]{:S(2)}) %collective-permute-start.14) | collective-permute-done | bytes 270368 | tf_op jit(solution)/shard_map/ppermute | solution.py:430
  146.8 0.0 collective-permute-done.15.refs_5_
  146.8 1.3 collective-permute-start.17
  148.1 20.7 %collective-permute-done.17.refs_6_ = bf16[4,528,128]{2,1,0:T(8,128)(2,1)S(1)} collective-permute-done((bf16[4,528,128]{2,1,0:T(8,128)(2,1)S(1)}, bf16[4,528,128]{2,1,0:T(8,128)(2,1)S(1)}, u32[]{:S(2)}, u32[]{:S(2)}) %collective-permute-start.17) | collective-permute-done | bytes 540704 | tf_op jit(solution)/shard_map/ppermute | solution.py:430
  168.8 0.0 collective-permute-done.9.own_ref
  168.8 8.0 %shard_map.54 = bf16[512,2048]{1,0:T(8,128)(2,1)} custom-call(s32[1]{0:T(128)} %bitcast.here_ref, s32[8,2,16]{2,1,0:T(2,128)S(1)} %collective-permute-done.picks_ref, bf16[16,528,128]{2,1,0:T(8,128)(2,1)S(1)} %collective-permute-done.9.own_ref, bf16[4,528,128]{2,1,0:T(8,128)(2,1)S(1)} %collective-permute-done.7.refs_0_, ...), custom_call_target="tpu_custom_call" | custom-call | flops 125829120 | bytes 8388608 | tf_op jit(solution)/shard_map/pallas_call | solution.py:373
  (9 shorter events, 0.0 us)
Async XLA Ops:
  0.0 17.8 %collective-permute-start = (s32[8,2,16]{2,1,0:T(2,128)}, s32[8,2,16]{2,1,0:T(2,128)S(1)}, u32[]{:S(2)}, u32[]{:S(2)}) collective-permute-start(s32[8,2,16]{2,1,0:T(2,128)} %bitcast.26), channel_id=1, source_target_pairs={{0,1},{1,2},{2,3},{3,0},{4,5},{5,6},{6,7},{7,4},{8,9},{9,10},{10,1... | collective-permute-start | bytes 3080 | tf_op jit(solution)/shard_map/ppermute | solution.py:23
  0.0 1.6 copy-start
  1.6 0.7 copy-start.4
  2.3 12.6 %copy-start.2 = (bf16[1,512,2048]{2,1,0:T(8,128)(2,1)S(1)}, bf16[1,512,2048]{2,1,0:T(8,128)(2,1)}, u32[]{:S(2)}) copy-start(bf16[1,512,2048]{2,1,0:T(8,128)(2,1)} %param.5) | copy-start | bytes 6291460
  7.2 26.6 %collective-permute-start.3 = (bf16[4,512,128]{2,1,0:T(8,128)(2,1)S(1)}, bf16[4,512,128]{2,1,0:T(8,128)(2,1)S(1)}, u32[]{:S(2)}, u32[]{:S(2)}) collective-permute-start(bf16[4,512,128]{2,1,0:T(8,128)(2,1)S(1)} %get-tuple-element.39), channel_id=1, source_target_pairs={{8,0},{12,4},{16,8},{20,12},{24,16},{28,20},{9,1},{13,5},{17,9},{2... | collective-permute-start | bytes 1572872 | tf_op jit(solution)/shard_map/ppermute | solution.py:422
  9.5 24.3 %collective-permute-start.4 = (bf16[4,512,128]{2,1,0:T(8,128)(2,1)S(1)}, bf16[4,512,128]{2,1,0:T(8,128)(2,1)S(1)}, u32[]{:S(2)}, u32[]{:S(2)}) collective-permute-start(bf16[4,512,128]{2,1,0:T(8,128)(2,1)S(1)} %get-tuple-element.40), channel_id=1, source_target_pairs={{24,0},{28,4},{25,1},{29,5},{26,2},{30,6},{27,3},{31,7}} | collective-permute-start | bytes 1572872 | tf_op jit(solution)/shard_map/ppermute | solution.py:422
  10.8 49.0 %collective-permute-start.1 = (bf16[8,512,128]{2,1,0:T(8,128)(2,1)S(1)}, bf16[8,512,128]{2,1,0:T(8,128)(2,1)S(1)}, u32[]{:S(2)}, u32[]{:S(2)}) collective-permute-start(bf16[8,512,128]{2,1,0:T(8,128)(2,1)S(1)} %get-tuple-element.37), channel_id=1, source_target_pairs={{0,4},{4,8},{8,12},{12,16},{16,20},{20,24},{24,28},{1,5},{5,9},{9,... | collective-permute-start | bytes 3145736 | tf_op jit(solution)/shard_map/ppermute | solution.py:419
  14.2 45.6 %collective-permute-start.2 = (bf16[8,512,128]{2,1,0:T(8,128)(2,1)S(1)}, bf16[8,512,128]{2,1,0:T(8,128)(2,1)S(1)}, u32[]{:S(2)}, u32[]{:S(2)}) collective-permute-start(bf16[8,512,128]{2,1,0:T(8,128)(2,1)S(1)} %get-tuple-element.38), channel_id=1, source_target_pairs={{0,28},{1,29},{2,30},{3,31}} | collective-permute-start | bytes 3145736 | tf_op jit(solution)/shard_map/ppermute | solution.py:419
  33.8 34.1 %copy-start.3 = (bf16[1,512,2048]{2,1,0:T(8,128)(2,1)S(1)}, bf16[1,512,2048]{2,1,0:T(8,128)(2,1)}, u32[]{:S(2)}) copy-start(bf16[1,512,2048]{2,1,0:T(8,128)(2,1)} %param.6) | copy-start | bytes 6291460
  33.8 30.0 %collective-permute-start.5 = (bf16[2,512,128]{2,1,0:T(8,128)(2,1)S(1)}, bf16[2,512,128]{2,1,0:T(8,128)(2,1)S(1)}, u32[]{:S(2)}, u32[]{:S(2)}) collective-permute-start(bf16[2,512,128]{2,1,0:T(8,128)(2,1)S(1)} %get-tuple-element.47), channel_id=1, source_target_pairs={{12,0},{16,4},{20,8},{24,12},{28,16},{13,1},{17,5},{21,9},{25,13},... | collective-permute-start | bytes 786440 | tf_op jit(solution)/shard_map/ppermute | solution.py:422
  36.6 27.2 %collective-permute-start.6 = (bf16[2,512,128]{2,1,0:T(8,128)(2,1)S(1)}, bf16[2,512,128]{2,1,0:T(8,128)(2,1)S(1)}, u32[]{:S(2)}, u32[]{:S(2)}) collective-permute-start(bf16[2,512,128]{2,1,0:T(8,128)(2,1)S(1)} %get-tuple-element.49), channel_id=1, source_target_pairs={{20,0},{24,4},{28,8},{21,1},{25,5},{29,9},{22,2},{26,6},{30,10},{2... | collective-permute-start | bytes 786440 | tf_op jit(solution)/shard_map/ppermute | solution.py:422
  62.5 28.8 %collective-permute-start.7 = (bf16[4,528,128]{2,1,0:T(8,128)(2,1)S(1)}, bf16[4,528,128]{2,1,0:T(8,128)(2,1)S(1)}, u32[]{:S(2)}, u32[]{:S(2)}) collective-permute-start(bf16[4,528,128]{2,1,0:T(8,128)(2,1)S(1)} %get-tuple-element.45), channel_id=1, source_target_pairs={{0,9},{1,10},{2,11},{3,8},{4,13},{5,14},{6,15},{7,12},{8,17},{9,18... | collective-permute-start | bytes 1622024 | tf_op jit(solution)/shard_map/ppermute | solution.py:430
  63.8 35.4 %collective-permute-start.12 = (bf16[2,512,128]{2,1,0:T(8,128)(2,1)S(1)}, bf16[2,512,128]{2,1,0:T(8,128)(2,1)S(1)}, u32[]{:S(2)}, u32[]{:S(2)}) collective-permute-start(bf16[2,512,128]{2,1,0:T(8,128)(2,1)S(1)} %get-tuple-element.58), channel_id=1, source_target_pairs={{12,0},{16,4},{20,8},{24,12},{28,16},{13,1},{17,5},{21,9},{25,13},... | collective-permute-start | bytes 786440 | tf_op jit(solution)/shard_map/ppermute | solution.py:422
  65.1 34.1 %collective-permute-start.13 = (bf16[2,512,128]{2,1,0:T(8,128)(2,1)S(1)}, bf16[2,512,128]{2,1,0:T(8,128)(2,1)S(1)}, u32[]{:S(2)}, u32[]{:S(2)}) collective-permute-start(bf16[2,512,128]{2,1,0:T(8,128)(2,1)S(1)} %get-tuple-element.60), channel_id=1, source_target_pairs={{20,0},{24,4},{28,8},{21,1},{25,5},{29,9},{22,2},{26,6},{30,10},{2... | collective-permute-start | bytes 786440 | tf_op jit(solution)/shard_map/ppermute | solution.py:422
  66.4 24.8 %copy-start.1 = (bf16[1,512,2048]{2,1,0:T(8,128)(2,1)S(1)}, bf16[1,512,2048]{2,1,0:T(8,128)(2,1)}, u32[]{:S(2)}) copy-start(bf16[1,512,2048]{2,1,0:T(8,128)(2,1)} %param.4) | copy-start | bytes 6291460
  66.4 19.2 %collective-permute-start.8 = (bf16[4,528,128]{2,1,0:T(8,128)(2,1)S(1)}, bf16[4,528,128]{2,1,0:T(8,128)(2,1)S(1)}, u32[]{:S(2)}, u32[]{:S(2)}) collective-permute-start(bf16[4,528,128]{2,1,0:T(8,128)(2,1)S(1)} %get-tuple-element.51), channel_id=1, source_target_pairs={{0,25},{1,26},{2,27},{3,24},{4,29},{5,30},{6,31},{7,28}} | collective-permute-start | bytes 1622024 | tf_op jit(solution)/shard_map/ppermute | solution.py:430
  91.2 21.9 %copy-start.5 = (s32[1,8,16,2]{2,3,1,0:T(2,128)S(1)}, s32[1,8,16,2]{2,3,1,0:T(2,128)}, u32[]{:S(2)}) copy-start(s32[1,8,16,2]{2,3,1,0:T(2,128)} %param.7) | copy-start | bytes 3076
  99.2 69.7 %collective-permute-start.9 = (bf16[16,528,128]{2,1,0:T(8,128)(2,1)}, bf16[16,528,128]{2,1,0:T(8,128)(2,1)S(1)}, u32[]{:S(2)}, u32[]{:S(2)}) collective-permute-start(bf16[16,528,128]{2,1,0:T(8,128)(2,1)} %shard_map.51), channel_id=1, source_target_pairs={{0,1},{1,2},{2,3},{3,0},{4,5},{5,6},{6,7},{7,4},{8,9},{9,10},{10,1... | collective-permute-start | bytes 6488072 | tf_op jit(solution)/shard_map/ppermute | solution.py:23
  99.2 29.0 %collective-permute-start.10 = (bf16[2,528,128]{2,1,0:T(8,128)(2,1)S(1)}, bf16[2,528,128]{2,1,0:T(8,128)(2,1)S(1)}, u32[]{:S(2)}, u32[]{:S(2)}) collective-permute-start(bf16[2,528,128]{2,1,0:T(8,128)(2,1)S(1)} %get-tuple-element.53), channel_id=1, source_target_pairs={{0,13},{1,14},{2,15},{3,12},{4,17},{5,18},{6,19},{7,16},{8,21},{9,... | collective-permute-start | bytes 811016 | tf_op jit(solution)/shard_map/ppermute | solution.py:430
  100.5 27.7 %collective-permute-start.11 = (bf16[2,528,128]{2,1,0:T(8,128)(2,1)S(1)}, bf16[2,528,128]{2,1,0:T(8,128)(2,1)S(1)}, u32[]{:S(2)}, u32[]{:S(2)}) collective-permute-start(bf16[2,528,128]{2,1,0:T(8,128)(2,1)S(1)} %get-tuple-element.55), channel_id=1, source_target_pairs={{0,21},{1,22},{2,23},{3,20},{4,25},{5,26},{6,27},{7,24},{8,29},{9,... | collective-permute-start | bytes 811016 | tf_op jit(solution)/shard_map/ppermute | solution.py:430
  101.8 29.0 %collective-permute-start.16 = (bf16[4,512,128]{2,1,0:T(8,128)(2,1)S(1)}, bf16[4,512,128]{2,1,0:T(8,128)(2,1)S(1)}, u32[]{:S(2)}, u32[]{:S(2)}) collective-permute-start(bf16[4,512,128]{2,1,0:T(8,128)(2,1)S(1)} %get-tuple-element.67), channel_id=1, source_target_pairs={{16,0},{20,4},{24,8},{28,12},{17,1},{21,5},{25,9},{29,13},{18,2},{... | collective-permute-start | bytes 1572872 | tf_op jit(solution)/shard_map/ppermute | solution.py:422
  128.2 18.6 %collective-permute-start.14 = (bf16[2,528,128]{2,1,0:T(8,128)(2,1)S(1)}, bf16[2,528,128]{2,1,0:T(8,128)(2,1)S(1)}, u32[]{:S(2)}, u32[]{:S(2)}) collective-permute-start(bf16[2,528,128]{2,1,0:T(8,128)(2,1)S(1)} %get-tuple-element.62), channel_id=1, source_target_pairs={{0,13},{1,14},{2,15},{3,12},{4,17},{5,18},{6,19},{7,16},{8,21},{9,... | collective-permute-start | bytes 811016 | tf_op jit(solution)/shard_map/ppermute | solution.py:430
  129.4 17.4 %collective-permute-start.15 = (bf16[2,528,128]{2,1,0:T(8,128)(2,1)S(1)}, bf16[2,528,128]{2,1,0:T(8,128)(2,1)S(1)}, u32[]{:S(2)}, u32[]{:S(2)}) collective-permute-start(bf16[2,528,128]{2,1,0:T(8,128)(2,1)S(1)} %get-tuple-element.64), channel_id=1, source_target_pairs={{0,21},{1,22},{2,23},{3,20},{4,25},{5,26},{6,27},{7,24},{8,29},{9,... | collective-permute-start | bytes 811016 | tf_op jit(solution)/shard_map/ppermute | solution.py:430
  146.8 22.0 %collective-permute-start.17 = (bf16[4,528,128]{2,1,0:T(8,128)(2,1)S(1)}, bf16[4,528,128]{2,1,0:T(8,128)(2,1)S(1)}, u32[]{:S(2)}, u32[]{:S(2)}) collective-permute-start(bf16[4,528,128]{2,1,0:T(8,128)(2,1)S(1)} %shard_map.53), channel_id=1, source_target_pairs={{0,17},{1,18},{2,19},{3,16},{4,21},{5,22},{6,23},{7,20},{8,25},{9,... | collective-permute-start | bytes 1622024 | tf_op jit(solution)/shard_map/ppermute | solution.py:430

commit v3 on v2

--- a/solution.py
+++ b/solution.py
@@ -50,13 +50,27 @@
         out_shape=outputs,
         scratch_shapes=list(scratch),
         compiler_params=pltpu.CompilerParams(vmem_limit_bytes=VMEM_BYTES),
-        cost_estimate=pl.CostEstimate(flops=20 * flops, bytes_accessed=moved, transcendentals=exps),
+        cost_estimate=pl.CostEstimate(flops=flops, bytes_accessed=moved, transcendentals=exps),
     )
 
 
 SCALARS = pl.BlockSpec(memory_space=pltpu.SMEM)
 IN_HBM = pl.BlockSpec(memory_space=pltpu.HBM)
 IN_VMEM = pl.BlockSpec(memory_space=pltpu.VMEM)
+
+
+def tick_kernel(here_ref, out_ref):
+    out_ref[0] = here_ref[0]
+
+
+def tick(here, *earlier, flops=10**12):
+    return call(
+        tick_kernel,
+        [SCALARS],
+        jax.ShapeDtypeStruct((1,), jnp.int32),
+        SCALARS,
+        flops=flops,
+    )(after(here, *earlier))
 
 
 def list_heads(heads_ref, start, picks_ref, block, owner, slots):
@@ -139,13 +153,14 @@
     weights = jnp.exp2((scores - top) * EXP2_SCALE).astype(jnp.bfloat16)
     total = jnp.dot(weights, value_rows, preferred_element_type=jnp.float32)
     sums = total[:, HD:]
-    return total[:, :HD] / sums, top * EXP2_SCALE + jnp.log2(sums)
+    return total[:, :HD] * pl.reciprocal(sums), top * EXP2_SCALE, sums
 
 
 def across_lanes(column):
     eye = diagonal()
+    spread = jnp.broadcast_to(column, (column.shape[0], LANES))
     return [
-        jnp.sum(jnp.where(eye, column[at : at + LANES], 0.0), axis=0, keepdims=True)
+        jnp.sum(jnp.where(eye, spread[at : at + LANES], 0.0), axis=0, keepdims=True)
         for at in range(0, column.shape[0], LANES)
     ]
 
@@ -169,13 +184,19 @@
     return stats[:groups] + stats[groups : 2 * groups] + stats[2 * groups : 3 * groups]
 
 
+def log_sums(tops, sums):
+    top_lines = [line for top in tops for line in across_lanes(top)]
+    sum_lines = [line for part in sums for line in across_lanes(part)]
+    return jnp.concatenate(top_lines, axis=0) + jnp.log2(jnp.concatenate(sum_lines, axis=0))
+
+
 def attend_rows(query_rows, key_rows, value_rows, tile):
-    outputs, lines = [], []
-    for at in range(0, query_rows.shape[0], tile):
-        part, sums = soft_part(raw_scores(query_rows[at : at + tile], key_rows), value_rows)
-        outputs.append(part)
-        lines += across_lanes(sums)
-    return jnp.concatenate(outputs, axis=0), jnp.concatenate(lines, axis=0)
+    found = [
+        soft_part(raw_scores(query_rows[at : at + tile], key_rows), value_rows)
+        for at in range(0, query_rows.shape[0], tile)
+    ]
+    outputs, tops, sums = zip(*found)
+    return jnp.concatenate(outputs, axis=0), log_sums(tops, sums)
 
 
 def head_columns(head):
@@ -190,19 +211,12 @@
         rows = query_ref.shape[1]
         list_heads(heads_ref, 0, picks_ref, here + shift, here, slots)
         for slot in range(count):
-            head = heads_ref[first + slot]
-
-            @pl.when(head >= 0)
-            def _():
-                columns = head_columns(head)
-                outputs, lines = attend_rows(
-                    query_ref[slot],
-                    key_ref[:, columns],
-                    with_ones(value_ref[:, columns]),
-                    min(rows, 256),
-                )
-                out_ref[slot, :rows, :] = outputs.astype(jnp.bfloat16)
-                out_ref[slot, rows:, :] = three_parts(lines)
+            columns = head_columns(jnp.maximum(heads_ref[first + slot], 0))
+            outputs, lines = attend_rows(
+                query_ref[slot], key_ref[:, columns], with_ones(value_ref[:, columns]), min(rows, 256)
+            )
+            out_ref[slot, :rows, :] = outputs.astype(jnp.bfloat16)
+            out_ref[slot, rows:, :] = three_parts(lines)
 
 
 def attend(here, picks, keys, values, arrived, group, slots):
@@ -230,19 +244,20 @@
     def one_head(head, carry):
         columns = head_columns(head)
         value_rows = with_ones(value_ref[:, columns])
-        lines = []
+        tops, all_sums = [], []
         for at in range(0, rows, tile):
             reach = at + tile
             scores = raw_scores(query_ref[at:reach, columns], key_ref[:reach, columns])
             row_ids = lax.broadcasted_iota(jnp.int32, scores.shape, 0) + at
             seen = row_ids >= lax.broadcasted_iota(jnp.int32, scores.shape, 1)
-            outputs, sums = soft_part(jnp.where(seen, scores, -jnp.inf), value_rows[:reach])
+            outputs, top, sums = soft_part(jnp.where(seen, scores, -jnp.inf), value_rows[:reach])
             out_ref[head, at:reach, :] = outputs.astype(jnp.bfloat16)
-            lines += across_lanes(sums)
-        out_ref[head, rows:, :] = three_parts(jnp.concatenate(lines, axis=0))
+            tops.append(top)
+            all_sums.append(sums)
+        out_ref[head, rows:, :] = three_parts(log_sums(tops, all_sums))
         return carry
 
-    lax.fori_loop(0, HEADS, one_head, 0)
+    lax.fori_loop(0, HEADS, one_head, 0, unroll=4)
 
 
 def own_part(here, queries, keys, values):
@@ -310,80 +325,142 @@
     )(here, picks, queries, own, *near)
 
 
-def merge_kernel(here_ref, picks_ref, own_ref, *refs, places, skipped, slots):
-    count = len(places)
-    parts, out_ref, held, spots_ref, found_ref, sems = refs[:count], *refs[count:]
-    rows = out_ref.shape[0]
-    groups = rows // LANES
-    width = picks_ref.shape[0]
-    here = here_ref[0]
-    copies = [
-        pltpu.make_async_copy(part, held.at[pl.ds(place, part.shape[0])], sems.at[number])
-        for number, (part, place) in enumerate(zip(parts, places))
-    ]
-    for copy in copies:
-        copy.start()
-    for owner in range(width):
+def find_spots(spots_ref, found_ref, picks_ref, here, shifts, slots):
+    for owner in range(picks_ref.shape[0]):
         found_ref[owner] = 0
 
     def look(number, carry):
         pick, head = number // HEADS, number % HEADS
         owner = picks_ref[here, pick, head]
         safe = jnp.maximum(owner, 0)
-        shift = here - safe
         order = found_ref[safe]
         found_ref[safe] = order + (owner >= 0).astype(jnp.int32)
-        is_held = owner >= 0
-        for left_out in skipped:
-            is_held = is_held & (shift != left_out)
-        spots_ref[head * PICKS + pick] = jnp.where(is_held, shift * slots + order, -1)
+        spot = jnp.int32(-1)
+        for place, shift in enumerate(shifts):
+            spot = jnp.where(here - safe == shift, place * slots + order, spot)
+        spots_ref[head * PICKS + pick] = jnp.where(owner >= 0, spot, -1)
         return carry
 
     lax.fori_loop(0, PICKS * HEADS, look, 0)
+
+
+def merge_kernel(here_ref, picks_ref, *refs, places, shifts, slots):
+    count = len(places)
+    parts = refs[: count + 1]
+    out_ref, sums_ref, held, spots_ref, found_ref, sems = refs[count + 1 :]
+    groups = sums_ref.shape[1]
+    rows = groups * LANES
+    copies = [
+        pltpu.make_async_copy(part, held.at[pl.ds(place, part.shape[0])], sems.at[number])
+        for number, (part, place) in enumerate(zip(parts, (0,) + places))
+    ]
+    for copy in copies:
+        copy.start()
+    find_spots(spots_ref, found_ref, picks_ref, here_ref[0], shifts, slots)
     for copy in copies:
         copy.wait()
 
     def one_head(head, carry):
         found = [spots_ref[head * PICKS + pick] for pick in range(PICKS)]
-        spots = [jnp.maximum(spot, 0) for spot in found]
-        sums = [stats_of(own_ref[head, rows:, :], groups)]
-        for spot, safe in zip(found, spots):
-            sums.append(jnp.where(spot >= 0, stats_of(held[safe, rows:, :], groups), -jnp.inf))
+        spots = [head] + [jnp.where(spot >= 0, HEADS + spot, head) for spot in found]
+        sums = [stats_of(held[spot, rows:, :], groups) for spot in spots]
+        for pick, spot in enumerate(found):
+            sums[1 + pick] = jnp.where(spot >= 0, sums[1 + pick], -jnp.inf)
         top = functools.reduce(jnp.maximum, sums)
         shares = [jnp.exp2(part - top) for part in sums]
         whole = functools.reduce(jnp.add, shares)
-        shares = [share / whole for share in shares]
-        columns = head_columns(head)
+        sums_ref[head] = top + jnp.log2(whole)
         for group in range(groups):
             span = pl.ds(group * LANES, LANES)
-            mixed = own_ref[head, span, :].astype(jnp.float32)
-            mixed = mixed * down_rows(shares[0][group : group + 1, :])
-            for spot, safe, share in zip(found, spots, shares[1:]):
-                block = jnp.where(spot >= 0, held[safe, span, :].astype(jnp.float32), 0.0)
-                mixed = mixed + block * down_rows(share[group : group + 1, :])
-            out_ref[span, columns] = mixed.astype(jnp.bfloat16)
+            own = held[head, span, :].astype(jnp.float32)
+            mixed = own
+            for spot, share in zip(spots[1:], shares[1:]):
+                weight = down_rows((share / whole)[group : group + 1, :])
+                mixed = mixed + (held[spot, span, :].astype(jnp.float32) - own) * weight
+            out_ref[head, span, :] = mixed
         return carry
 
-    lax.fori_loop(0, HEADS, one_head, 0)
-
-
-def merge(here, picks, own, parts, places, skipped, slots):
+    lax.fori_loop(0, HEADS, one_head, 0, unroll=2)
+
+
+def merge(here, picks, own, parts, places, shifts, slots):
     rows = own.shape[1] - STAT_ROWS
     width = picks.shape[0]
+    total = HEADS + len(shifts) * slots
     return call(
-        functools.partial(merge_kernel, places=places, skipped=skipped, slots=slots),
-        [SCALARS, SCALARS, IN_VMEM] + [pl.BlockSpec(memory_space=pl.ANY)] * len(parts),
-        jax.ShapeDtypeStruct((rows, HEADS * HD), jnp.bfloat16),
-        pl.BlockSpec((rows, HEADS * HD), lambda: (0, 0)),
+        functools.partial(
+            merge_kernel, places=tuple(HEADS + place for place in places), shifts=shifts, slots=slots
+        ),
+        [SCALARS, SCALARS] + [pl.BlockSpec(memory_space=pl.ANY)] * (1 + len(parts)),
         [
-            pltpu.VMEM((width * slots, rows + STAT_ROWS, HD), jnp.bfloat16),
+            jax.ShapeDtypeStruct((HEADS, rows, HD), jnp.float32),
+            jax.ShapeDtypeStruct((HEADS, rows // LANES, LANES), jnp.float32),
+        ],
+        [IN_VMEM, IN_VMEM],
+        [
+            pltpu.VMEM((total, rows + STAT_ROWS, HD), jnp.bfloat16),
             pltpu.SMEM((PICKS * HEADS,), jnp.int32),
             pltpu.SMEM((width,), jnp.int32),
-            pltpu.SemaphoreType.DMA((len(parts),)),
+            pltpu.SemaphoreType.DMA((1 + len(parts),)),
         ],
         flops=6 * HEADS * rows * HD,
-        moved=2 * (HEADS * 2 + width * slots) * rows * HD,
+        moved=2 * (HEADS * 2 + total) * rows * HD,
     )(here, picks, own, *parts)
+
+
+def finish_kernel(
+    here_ref, picks_ref, mixed_ref, sums_ref, part_ref, out_ref, spots_ref, found_ref, *, shift, slots
+):
+    groups = sums_ref.shape[1]
+    rows = groups * LANES
+    step = pl.program_id(0)
+    per_step = HEADS // pl.num_programs(0)
+
+    @pl.when(step == 0)
+    def _():
+        find_spots(spots_ref, found_ref, picks_ref, here_ref[0], (shift,), slots)
+
+    for place in range(per_step):
+        head = step * per_step + place
+        spot = jnp.maximum(spots_ref[head * PICKS], spots_ref[head * PICKS + 1])
+        columns = pl.ds(place * HD, HD)
+
+        @pl.when(spot < 0)
+        def _():
+            out_ref[:, columns] = mixed_ref[head].astype(jnp.bfloat16)
+
+        @pl.when(spot >= 0)
+        def _():
+            before = sums_ref[head]
+            added = stats_of(part_ref[spot, rows:, :], groups)
+            share = 1.0 / (1.0 + jnp.exp2(before - added))
+            for group in range(groups):
+                span = pl.ds(group * LANES, LANES)
+                old = mixed_ref[head, span, :]
+                new = part_ref[spot, span, :].astype(jnp.float32)
+                mixed = old + (new - old) * down_rows(share[group : group + 1, :])
+                out_ref[span, columns] = mixed.astype(jnp.bfloat16)
+
+
+def finish(here, picks, mixed, sums, part, shift, slots):
+    heads, rows, _ = mixed.shape
+    width = picks.shape[0]
+    steps = 4
+    return pl.pallas_call(
+        functools.partial(finish_kernel, shift=shift, slots=slots),
+        grid=(steps,),
+        in_specs=[SCALARS, SCALARS, IN_VMEM, IN_VMEM, IN_VMEM],
+        out_specs=pl.BlockSpec((rows, heads // steps * HD), lambda step: (0, step)),
+        out_shape=jax.ShapeDtypeStruct((rows, heads * HD), jnp.bfloat16),
+        scratch_shapes=[
+            pltpu.SMEM((PICKS * HEADS,), jnp.int32),
+            pltpu.SMEM((width,), jnp.int32),
+        ],
+        compiler_params=pltpu.CompilerParams(vmem_limit_bytes=VMEM_BYTES),
+        cost_estimate=pl.CostEstimate(
+            flops=2 * heads * rows * HD, bytes_accessed=8 * heads * rows * HD, transcendentals=0
+        ),
+    )(here, picks, mixed, sums, part)
 
 
 def after(value, *earlier):
@@ -392,9 +469,9 @@
 
 def groups_in_order(width, slots):
     middle = width // 2
-    groups = []
-    for low in range(2, middle):
-        size = max(1, slots // 2) if low == middle - 1 else slots
+    groups = [[(1, 0, slots)], [(shift, 0, slots) for shift in (width - 2, width - 1)]]
+    for low in range(3, middle):
+        size = max(1, slots // 2)
         for first in range(0, slots, size):
             count = min(size, slots - first)
             groups.append([(low, first, count), (width - low, first, count)])
@@ -410,10 +487,10 @@
     own_picks = picks[0].transpose(0, 2, 1)
 
     groups = groups_in_order(width, slots)
-    near_shifts = (1, width - 1)
+    near_shifts = (2,)
     first_jobs = [(shift, 0, slots, True) for shift in near_shifts]
-    first_jobs += [piece + (False,) for piece in groups[0]]
-    later_jobs = [piece + (False,) for group in groups[1:] for piece in group]
+    first_jobs += [piece + (False,) for group in groups[:2] for piece in group]
+    later_jobs = [piece + (False,) for group in groups[2:] for piece in group]
 
     def up(value, shift):
         return lax.ppermute(value, "ctx", [(at, at + shift) for at in range(width - shift)])
@@ -431,41 +508,73 @@
 
     sends = dict(zip(first_jobs, pack(here, own_picks, queries, keys, values, first_jobs, slots)))
     near = [up(sends[job], job[0]) for job in first_jobs if job[3]]
-    arrived = [down(sends[piece + (False,)], piece[0]) for piece in groups[0]]
+    arrived = {
+        piece: down(sends[piece + (False,)], piece[0]) for group in groups[:2] for piece in group
+    }
     before = passed_along(own_picks, "pipe", 1)
     now = after(here, *[sends[job] for job in first_jobs])
     sends |= zip(later_jobs, pack(now, own_picks, queries, keys, values, later_jobs, slots))
 
+    def attend_group(token, group):
+        return dict(
+            zip(
+                group,
+                attend(
+                    token,
+                    own_picks,
+                    keys,
+                    values,
+                    [arrived[piece] for piece in group],
+                    tuple(group),
+                    slots,
+                ),
+            )
+        )
+
+    def ask_for(group, *earlier):
+        for piece in group:
+            arrived[piece] = down(after(sends[piece + (False,)], *earlier), piece[0])
+
+    def send_back(parts, *earlier):
+        for piece, part in parts.items():
+            returned[piece] = up_and_on(after(part, *earlier) if earlier else part, piece[0])
+
+    def those(found, group):
+        return [found[piece] for piece in group]
+
+    returned = {}
     own = own_part(after(here, before, sends[later_jobs[0]]), queries, keys, values)
-    last, returned = own, {}
-    for number, group in enumerate(groups):
-        current = arrived
-        if number + 1 < len(groups):
-            waits = [last] + current
-            if number >= 2:
-                waits += [returned[piece] for piece in groups[number - 2]]
-            arrived = [
-                down(after(sends[piece + (False,)], *waits), piece[0])
-                for piece in groups[number + 1]
-            ]
-        waits = [last] + (near if number == 0 else [])
-        if number >= 2:
-            waits += [returned[piece] for piece in groups[number - 2]]
-        parts = attend(
-            after(here, *waits), own_picks, keys, values, current, tuple(group), slots
-        )
-        last = parts[0]
-        for piece, part in zip(group, parts):
-            if number >= 1:
-                part = after(part, *[returned[earlier] for earlier in groups[number - 1]])
-            returned[piece] = up_and_on(part, piece[0])
-        if number == 1:
-            own = add_near(after(here, last, *[returned[piece] for piece in groups[0]]), own_picks, queries, own, near, near_shifts, slots)
-            own_back = passed_along(own, "pipe", 1)
-            last = own
-    places = [shift * slots + first for shift, first, _ in returned]
-    parts = list(returned.values())
-    return merge(here, before, own_back, parts, places, near_shifts, slots)[None]
+    parts = attend_group(after(here, own), groups[0])
+    send_back(parts)
+    parts_next = attend_group(after(here, *parts.values(), *near), groups[1])
+    send_back(parts_next)
+    ask_for(groups[2], *parts_next.values(), *arrived.values())
+    now = tick(here, *parts_next.values())
+    own = add_near(now, own_picks, queries, own, near, near_shifts, slots)
+    before_last = groups[0] + groups[1]
+    for number in range(2, len(groups)):
+        group = groups[number]
+        waits = [own] if number == 2 else []
+        waits += [own_back] if number == len(groups) - 1 else []
+        parts = attend_group(after(now, *waits), group)
+        now = tick(now, *parts.values(), flops=0)
+        if number == 2:
+            ask_for(groups[number + 1], *parts.values(), *those(arrived, group))
+        send_back(parts, *those(returned, before_last))
+        if number == 2:
+            own_back = passed_along(after(own, *those(returned, before_last)), "pipe", 1)
+        now = tick(now, *those(returned, before_last))
+        before_last = group
+        if 2 <= number < len(groups) - 2:
+            ask_for(groups[number + 2], now, *those(arrived, groups[number + 1]))
+
+    final = groups[-1][0]
+    merged_shifts = tuple(shift for shift in range(1, width) if shift not in (2, final[0]))
+    pieces = [piece for piece in returned if piece != final]
+    places = [merged_shifts.index(shift) * slots + first for shift, first, _ in pieces]
+    parts = [returned[piece] for piece in pieces]
+    mixed, sums = merge(now, before, own_back, parts, places, merged_shifts, slots)
+    return finish(now, before, mixed, sums, returned[final], final[0], slots)[None]
 
 
 def travelling_keys(queries, keys, values, picks):
@@ -529,7 +638,7 @@
 
 
 def per_device(queries, keys, values, picks):
-    few_shifts = 4 <= lax.axis_size("ctx") <= 16
+    few_shifts = 8 <= lax.axis_size("ctx") <= 16
     run = travelling_queries if few_shifts else travelling_keys
     return run(queries, keys, values, picks)
 

time: 180 us -> 180 us (level)
  the two profiles are of different devices: /device:TPU:26 before, /device:TPU:22 now
where the time goes in v3:
time: 180 us
  Pallas kernels  73.8 us (41%)
  starting transfers between devices  59.1 us (33%)
  waiting for transfers between devices  39.5 us (22%)
  local copies, waits for them, and re-layouts  6.8 us (4%)
    ppermute x8, starting transfers between devices, down(): lax.ppermute(value, 'ctx', [(at, at - shift) for at in range(shift, width)])  40.7 us
    pallas_call x5, Pallas kernels, attend(): call(functools.partial(attend_kernel, group=group, slots=slots), [SCALARS...  26.2 us
    ppermute x2, waiting for transfers between devices, passed_along(): return lax.ppermute(value, axis, pairs)  25.6 us
    ppermute x8, starting transfers between devices, up_and_on(): return lax.ppermute(value, ('ctx', 'pipe'), pairs)  14.6 us
    pallas_call x1, Pallas kernels, own_part(): call(own_kernel, [SCALARS, IN_VMEM, IN_VMEM, IN_VMEM], jax.ShapeDtypeStru...  10.7 us
    pallas_call x1, Pallas kernels, merge(): call(functools.partial(merge_kernel, places=tuple((HEADS + place for plac...  8.73 us
    ppermute x8, waiting for transfers between devices, down(): lax.ppermute(value, 'ctx', [(at, at - shift) for at in range(shift, width)])  8.24 us
    pallas_call x1, Pallas kernels, add_near(): call(functools.partial(near_kernel, shifts=shifts, slots=slots), [SCALARS...  8.2 us
  transfers between devices with their start and end apart: 19, of which 3 were waited for; matrix products, arithmetic and copies ran while one was open for 0% of the time, Pallas kernels for 35%

profile of v3, /device:TPU:22, one launch (start us, length us, event | category | flops | bytes accessed | tf_op | source)
XLA Modules:
  0.0 179.5 jit_solution(11829177642422224514)
XLA Ops:
  0.0 1.6 copy-done.3
  1.6 0.7 copy-done.8
  2.3 4.3 %shard_map.46 = (bf16[8,512,128]{2,1,0:T(8,128)(2,1)S(1)}, bf16[4,512,128]{2,1,0:T(8,128)(2,1)S(1)}, bf16[4,512,128]{2,1,0:T(8,128)(2,1)S(1)}, bf16[4,512,128]{2,1,0:T(8,128)(2,1)S(1)}) custom-call(s32[1]{0:T(128)} %bitcast.here_ref, s32[8,2,16]{2,1,0:T(2,128)S(1)} %bitcast.28, bf16[512,2048]{1,0:T(8,128)(2,1)S(1)} %bitcast.24, bf16[512,2048]{1,0:T(8,128)(2,1)} %bitcast.8, ...), custom_call_target="tpu_custom_call" | custom-call | bytes 5242880 | tf_op jit(solution)/shard_map/pallas_call | solution.py:126
  6.6 3.6 %collective-permute-start.2 = (bf16[8,512,128]{2,1,0:T(8,128)(2,1)S(1)}, bf16[8,512,128]{2,1,0:T(8,128)(2,1)S(1)}, u32[]{:S(2)}, u32[]{:S(2)}) collective-permute-start(bf16[8,512,128]{2,1,0:T(8,128)(2,1)S(1)} %get-tuple-element.46), channel_id=1, source_target_pairs={{0,8},{4,12},{8,16},{12,20},{16,24},{20,28},{1,9},{5,13},{9,17},{1... | collective-permute-start | bytes 3145736 | tf_op jit(solution)/shard_map/ppermute | solution.py:496
  10.2 2.4 %collective-permute-start.1 = (bf16[4,512,128]{2,1,0:T(8,128)(2,1)S(1)}, bf16[4,512,128]{2,1,0:T(8,128)(2,1)S(1)}, u32[]{:S(2)}, u32[]{:S(2)}) collective-permute-start(bf16[4,512,128]{2,1,0:T(8,128)(2,1)S(1)} %get-tuple-element.47), channel_id=1, source_target_pairs={{4,0},{8,4},{12,8},{16,12},{20,16},{24,20},{28,24},{5,1},{9,5},{13... | collective-permute-start | bytes 1572872 | tf_op jit(solution)/shard_map/ppermute | solution.py:499
  12.6 0.7 collective-permute-start.3
  13.3 0.7 collective-permute-start.4
  14.0 0.1 collective-permute-start
  14.1 3.5 %shard_map.47 = (bf16[2,512,128]{2,1,0:T(8,128)(2,1)}, bf16[2,512,128]{2,1,0:T(8,128)(2,1)}, bf16[2,512,128]{2,1,0:T(8,128)(2,1)}, bf16[2,512,128]{2,1,0:T(8,128)(2,1)}, bf16[4,512,128]{2,1,0:T(8,128)(2,1)}) custom-call(s32[1]{0:T(128)} %bitcast.here_ref, s32[8,2,16]{2,1,0:T(2,128)S(1)} %bitcast.30, bf16[512,2048]{1,0:T(8,128)(2,1)S(1)} %bitcast.25, ...), custom_call_target="tpu_custom_call" | custom-call | bytes 3145728 | tf_op jit(solution)/shard_map/pallas_call | solution.py:126
  17.7 0.0 copy-start.1
  17.7 10.7 %shard_map.48.own_ref = bf16[16,528,128]{2,1,0:T(8,128)(2,1)} custom-call(s32[1]{0:T(128)} %bitcast.here_ref, bf16[512,2048]{1,0:T(8,128)(2,1)S(1)} %bitcast.26, bf16[512,2048]{1,0:T(8,128)(2,1)S(1)} %bitcast.10, bf16[512,2048]{1,0:T(8,128)(2,1)} %bitcast.18), custom_call_target="tpu_custom_call" | custom-call | flops 2147483648 | bytes 8388608 | tf_op jit(solution)/shard_map/pallas_call | solution.py:265
  28.4 3.7 %shard_map.49 = bf16[4,528,128]{2,1,0:T(8,128)(2,1)} custom-call(s32[1]{0:T(128)} %bitcast.here_ref, s32[8,2,16]{2,1,0:T(2,128)S(1)} %bitcast.31, bf16[512,2048]{1,0:T(8,128)(2,1)S(1)} %bitcast.11, bf16[512,2048]{1,0:T(8,128)(2,1)S(1)} %bitcast.20, bf16[4,512,128]{2,1,0:T(8,128)(2,1)S(1)} %collective-permute-done.1.refs_0_), custom_call_target="tpu_custom_call" | custom-call | flops 536870912 | bytes 2097152 | tf_op jit(solution)/shard_map/pallas_call | solution.py:225
  32.1 5.2 %collective-permute-start.7 = (bf16[4,528,128]{2,1,0:T(8,128)(2,1)}, bf16[4,528,128]{2,1,0:T(8,128)(2,1)}, u32[]{:S(2)}, u32[]{:S(2)}) collective-permute-start(bf16[4,528,128]{2,1,0:T(8,128)(2,1)} %shard_map.49), channel_id=1, source_target_pairs={{0,5},{1,6},{2,7},{3,4},{4,9},{5,10},{6,11},{7,8},{8,13},{9,14},{1... | collective-permute-start | bytes 1622024 | tf_op jit(solution)/shard_map/ppermute | solution.py:507
  37.3 0.0 copy-start.6
  37.3 1.0 copy-done.6
  38.3 6.8 %shard_map.50 = (bf16[4,528,128]{2,1,0:T(8,128)(2,1)}, bf16[4,528,128]{2,1,0:T(8,128)(2,1)}) custom-call(s32[1]{0:T(128)} %bitcast.here_ref, s32[8,2,16]{2,1,0:T(2,128)S(1)} %bitcast.32, bf16[512,2048]{1,0:T(8,128)(2,1)S(1)} %bitcast.12, bf16[512,2048]{1,0:T(8,128)(2,1)} %bitcast.19, bf16[4,512,128]{2,1,0:T(8,128)(2,1)S(1)} %collective-permute-done.3.refs_0_, ...), custom_call_target="tpu_custom_call" | custom-call | flops 1073741824 | bytes 4194304 | tf_op jit(solution)/shard_map/pallas_call | solution.py:225
  45.1 1.5 collective-permute-start.8
  46.6 1.5 collective-permute-start.9
  48.1 2.0 %collective-permute-start.5 = (bf16[2,512,128]{2,1,0:T(8,128)(2,1)}, bf16[2,512,128]{2,1,0:T(8,128)(2,1)}, u32[]{:S(2)}, u32[]{:S(2)}) collective-permute-start(bf16[2,512,128]{2,1,0:T(8,128)(2,1)} %get-tuple-element.59), channel_id=1, source_target_pairs={{12,0},{16,4},{20,8},{24,12},{28,16},{13,1},{17,5},{21,9},{25,13},... | collective-permute-start | bytes 786440 | tf_op jit(solution)/shard_map/ppermute | solution.py:499
  50.1 7.6 %collective-permute-start.6 = (bf16[2,512,128]{2,1,0:T(8,128)(2,1)}, bf16[2,512,128]{2,1,0:T(8,128)(2,1)}, u32[]{:S(2)}, u32[]{:S(2)}) collective-permute-start(bf16[2,512,128]{2,1,0:T(8,128)(2,1)} %get-tuple-element.61), channel_id=1, source_target_pairs={{20,0},{24,4},{28,8},{21,1},{25,5},{29,9},{22,2},{26,6},{30,10},{2... | collective-permute-start | bytes 786440 | tf_op jit(solution)/shard_map/ppermute | solution.py:499
  57.7 0.5 shard_map.51.here_ref
  58.3 1.1 copy-done.4
  59.3 0.3 copy-done.7
  59.6 8.2 %shard_map.52 = bf16[16,528,128]{2,1,0:T(8,128)(2,1)} custom-call(s32[1]{0:T(128)} %shard_map.51.here_ref, s32[8,2,16]{2,1,0:T(2,128)S(1)} %bitcast.33, bf16[512,2048]{1,0:T(8,128)(2,1)S(1)} %bitcast.27, bf16[16,528,128]{2,1,0:T(8,128)(2,1)} %shard_map.48.own_ref, bf16[8,512,128]{2,1,0:T(8,128)(2,1)S(1)} %copy-done.7), custom_call_target="tpu_custom_call" | custom-call | flops 536870912 | bytes 3145728 | tf_op jit(solution)/shard_map/pallas_call | solution.py:316
  67.8 5.5 %shard_map.53 = (bf16[2,528,128]{2,1,0:T(8,128)(2,1)}, bf16[2,528,128]{2,1,0:T(8,128)(2,1)}) custom-call(s32[1]{0:T(128)} %shard_map.51.here_ref, s32[8,2,16]{2,1,0:T(2,128)S(1)} %bitcast.34, bf16[512,2048]{1,0:T(8,128)(2,1)S(1)} %bitcast.13, bf16[512,2048]{1,0:T(8,128)(2,1)S(1)} %bitcast.21, bf16[2,512,128]{2,1,0:T(8,128)(2,1)} %collective-permute-done.5.refs_0_, ...), custom_call_target="tpu_custom_call" | custom-call | flops 536870912 | bytes 2097152 | tf_op jit(solution)/shard_map/pallas_call | solution.py:225
  73.3 1.1 shard_map.54.here_ref
  74.4 2.0 %collective-permute-start.10 = (bf16[2,512,128]{2,1,0:T(8,128)(2,1)}, bf16[2,512,128]{2,1,0:T(8,128)(2,1)}, u32[]{:S(2)}, u32[]{:S(2)}) collective-permute-start(bf16[2,512,128]{2,1,0:T(8,128)(2,1)} %get-tuple-element.67), channel_id=1, source_target_pairs={{12,0},{16,4},{20,8},{24,12},{28,16},{13,1},{17,5},{21,9},{25,13},... | collective-permute-start | bytes 786440 | tf_op jit(solution)/shard_map/ppermute | solution.py:499
  76.4 5.4 %collective-permute-start.11 = (bf16[2,512,128]{2,1,0:T(8,128)(2,1)}, bf16[2,512,128]{2,1,0:T(8,128)(2,1)}, u32[]{:S(2)}, u32[]{:S(2)}) collective-permute-start(bf16[2,512,128]{2,1,0:T(8,128)(2,1)} %get-tuple-element.69), channel_id=1, source_target_pairs={{20,0},{24,4},{28,8},{21,1},{25,5},{29,9},{22,2},{26,6},{30,10},{2... | collective-permute-start | bytes 786440 | tf_op jit(solution)/shard_map/ppermute | solution.py:499
  81.9 1.3 collective-permute-start.12
  83.2 1.3 collective-permute-start.13
  84.5 1.1 shard_map.55.here_ref
  85.6 8.2 %collective-permute-done.11.refs_1_ = bf16[2,512,128]{2,1,0:T(8,128)(2,1)} collective-permute-done((bf16[2,512,128]{2,1,0:T(8,128)(2,1)}, bf16[2,512,128]{2,1,0:T(8,128)(2,1)}, u32[]{:S(2)}, u32[]{:S(2)}) %collective-permute-start.11) | collective-permute-done | bytes 262176 | tf_op jit(solution)/shard_map/ppermute | solution.py:499
  93.8 19.9 %collective-permute-start.15 = (bf16[4,512,128]{2,1,0:T(8,128)(2,1)}, bf16[4,512,128]{2,1,0:T(8,128)(2,1)}, u32[]{:S(2)}, u32[]{:S(2)}) collective-permute-start(bf16[4,512,128]{2,1,0:T(8,128)(2,1)} %get-tuple-element.79), channel_id=1, source_target_pairs={{16,0},{20,4},{24,8},{28,12},{17,1},{21,5},{25,9},{29,13},{18,2},{... | collective-permute-start | bytes 1572872 | tf_op jit(solution)/shard_map/ppermute | solution.py:499
  113.7 5.4 %shard_map.56 = (bf16[2,528,128]{2,1,0:T(8,128)(2,1)}, bf16[2,528,128]{2,1,0:T(8,128)(2,1)}) custom-call(s32[1]{0:T(128)} %shard_map.55.here_ref, s32[8,2,16]{2,1,0:T(2,128)S(1)} %bitcast.35, bf16[512,2048]{1,0:T(8,128)(2,1)S(1)} %bitcast.14, bf16[512,2048]{1,0:T(8,128)(2,1)S(1)} %bitcast.22, bf16[2,512,128]{2,1,0:T(8,128)(2,1)} %collective-permute-done.10.refs_0_, ...), custom_call_target="tpu_custom_call" | custom-call | flops 536870912 | bytes 2097152 | tf_op jit(solution)/shard_map/pallas_call | solution.py:225
  119.2 1.1 shard_map.57.here_ref
  120.2 0.1 collective-permute-start.14
  120.3 1.3 collective-permute-start.17
  121.6 1.3 collective-permute-start.16
  122.9 1.1 shard_map.58.here_ref
  124.1 25.6 %collective-permute-done.14.refs_0_ = bf16[16,528,128]{2,1,0:T(8,128)(2,1)} collective-permute-done((bf16[16,528,128]{2,1,0:T(8,128)(2,1)}, bf16[16,528,128]{2,1,0:T(8,128)(2,1)}, u32[]{:S(2)}, u32[]{:S(2)}) %collective-permute-start.14) | collective-permute-done | bytes 2162720 | tf_op jit(solution)/shard_map/ppermute | solution.py:23
  149.7 4.7 %shard_map.59 = bf16[4,528,128]{2,1,0:T(8,128)(2,1)} custom-call(s32[1]{0:T(128)} %shard_map.58.here_ref, s32[8,2,16]{2,1,0:T(2,128)S(1)} %bitcast.36, bf16[512,2048]{1,0:T(8,128)(2,1)S(1)} %bitcast.15, bf16[512,2048]{1,0:T(8,128)(2,1)S(1)} %bitcast.23, bf16[4,512,128]{2,1,0:T(8,128)(2,1)} %collective-permute-done.15.refs_0_), custom_call_target="tpu_custom_call" | custom-call | flops 536870912 | bytes 2097152 | tf_op jit(solution)/shard_map/pallas_call | solution.py:225
  154.4 1.1 shard_map.60.here_ref
  155.5 1.3 collective-permute-start.18
  156.8 1.2 shard_map.61.here_ref
  158.0 8.7 %shard_map.62 = (f32[16,512,128]{2,1,0:T(8,128)}, f32[16,4,128]{2,1,0:T(4,128)S(1)}) custom-call(s32[1]{0:T(128)} %shard_map.61.here_ref, s32[8,2,16]{2,1,0:T(2,128)S(1)} %copy-done.12, bf16[16,528,128]{2,1,0:T(8,128)(2,1)} %collective-permute-done.14.refs_0_, bf16[4,528,128]{2,1,0:T(8,128)(2,1)} %collective-permute-done.7.refs_1_, ...), custom_call_target="tpu_custom_call" | custom-call | flops 6291456 | bytes 8912896 | tf_op jit(solution)/shard_map/pallas_call | solution.py:390
  166.8 5.7 %collective-permute-done.18.part_ref = bf16[4,528,128]{2,1,0:T(8,128)(2,1)} collective-permute-done((bf16[4,528,128]{2,1,0:T(8,128)(2,1)}, bf16[4,528,128]{2,1,0:T(8,128)(2,1)}, u32[]{:S(2)}, u32[]{:S(2)}) %collective-permute-start.18) | collective-permute-done | bytes 540704 | tf_op jit(solution)/shard_map/ppermute | solution.py:507
  172.5 2.2 %copy-done.5 = f32[16,512,128]{2,1,0:T(8,128)S(1)} copy-done((f32[16,512,128]{2,1,0:T(8,128)S(1)}, f32[16,512,128]{2,1,0:T(8,128)}, u32[]{:S(2)}) %copy-start.5) | copy-done | bytes 4194328
  174.6 4.9 %shard_map.63 = bf16[512,2048]{1,0:T(8,128)(2,1)} custom-call(s32[1]{0:T(128)} %shard_map.61.here_ref, s32[8,2,16]{2,1,0:T(2,128)S(1)} %copy-done.12, f32[16,512,128]{2,1,0:T(8,128)S(1)} %copy-done.5, f32[16,4,128]{2,1,0:T(4,128)S(1)} %get-tuple-element.85.sums_ref, bf16[4,528,128]{2,1,0:T(8,128)(2,1)} %collective-permute-done.18.part_ref), custom_call_target="tpu_custom_call" | custom-call | flops 2097152 | bytes 8388608 | tf_op jit(solution)/shard_map/pallas_call | solution.py:449
  (34 shorter events, 0.1 us)
Async XLA Ops:
  0.0 1.6 copy-start.3
  1.6 0.7 copy-start.8
  2.3 11.7 %copy-start.9 = (s32[1,8,16,2]{2,3,1,0:T(2,128)S(1)}, s32[1,8,16,2]{2,3,1,0:T(2,128)}, u32[]{:S(2)}) copy-start(s32[1,8,16,2]{2,3,1,0:T(2,128)} %param.7) | copy-start | bytes 3076
  2.3 11.8 %copy-start = (bf16[1,512,2048]{2,1,0:T(8,128)(2,1)S(1)}, bf16[1,512,2048]{2,1,0:T(8,128)(2,1)}, u32[]{:S(2)}) copy-start(bf16[1,512,2048]{2,1,0:T(8,128)(2,1)} %param.5) | copy-start | bytes 6291460
  6.6 30.7 %collective-permute-start.2 = (bf16[8,512,128]{2,1,0:T(8,128)(2,1)S(1)}, bf16[8,512,128]{2,1,0:T(8,128)(2,1)S(1)}, u32[]{:S(2)}, u32[]{:S(2)}) collective-permute-start(bf16[8,512,128]{2,1,0:T(8,128)(2,1)S(1)} %get-tuple-element.46), channel_id=1, source_target_pairs={{0,8},{4,12},{8,16},{12,20},{16,24},{20,28},{1,9},{5,13},{9,17},{1... | collective-permute-start | bytes 3145736 | tf_op jit(solution)/shard_map/ppermute | solution.py:496
  10.2 18.2 %collective-permute-start.1 = (bf16[4,512,128]{2,1,0:T(8,128)(2,1)S(1)}, bf16[4,512,128]{2,1,0:T(8,128)(2,1)S(1)}, u32[]{:S(2)}, u32[]{:S(2)}) collective-permute-start(bf16[4,512,128]{2,1,0:T(8,128)(2,1)S(1)} %get-tuple-element.47), channel_id=1, source_target_pairs={{4,0},{8,4},{12,8},{16,12},{20,16},{24,20},{28,24},{5,1},{9,5},{13... | collective-permute-start | bytes 1572872 | tf_op jit(solution)/shard_map/ppermute | solution.py:499
  12.6 25.7 %collective-permute-start.3 = (bf16[4,512,128]{2,1,0:T(8,128)(2,1)S(1)}, bf16[4,512,128]{2,1,0:T(8,128)(2,1)S(1)}, u32[]{:S(2)}, u32[]{:S(2)}) collective-permute-start(bf16[4,512,128]{2,1,0:T(8,128)(2,1)S(1)} %get-tuple-element.48), channel_id=1, source_target_pairs={{24,0},{28,4},{25,1},{29,5},{26,2},{30,6},{27,3},{31,7}} | collective-permute-start | bytes 1572872 | tf_op jit(solution)/shard_map/ppermute | solution.py:499
  13.3 25.0 %collective-permute-start.4 = (bf16[4,512,128]{2,1,0:T(8,128)(2,1)S(1)}, bf16[4,512,128]{2,1,0:T(8,128)(2,1)S(1)}, u32[]{:S(2)}, u32[]{:S(2)}) collective-permute-start(bf16[4,512,128]{2,1,0:T(8,128)(2,1)S(1)} %get-tuple-element.49), channel_id=1, source_target_pairs={{28,0},{29,1},{30,2},{31,3}} | collective-permute-start | bytes 1572872 | tf_op jit(solution)/shard_map/ppermute | solution.py:499
  14.0 3.6 %collective-permute-start = (s32[8,2,16]{2,1,0:T(2,128)S(1)}, s32[8,2,16]{2,1,0:T(2,128)S(1)}, u32[]{:S(2)}, u32[]{:S(2)}) collective-permute-start(s32[8,2,16]{2,1,0:T(2,128)S(1)} %bitcast.29), channel_id=1, source_target_pairs={{0,1},{1,2},{2,3},{3,0},{4,5},{5,6},{6,7},{7,4},{8,9},{9,10},{10,1... | collective-permute-start | bytes 3080 | tf_op jit(solution)/shard_map/ppermute | solution.py:23
  17.7 10.7 %copy-start.11 = (s32[8,2,16]{2,1,0:T(2,128)}, s32[8,2,16]{2,1,0:T(2,128)S(1)}, u32[]{:S(2)}) copy-start(s32[8,2,16]{2,1,0:T(2,128)S(1)} %collective-permute-done.picks_ref) | copy-start | bytes 3076
  17.7 10.7 %copy-start.1 = (bf16[1,512,2048]{2,1,0:T(8,128)(2,1)S(1)}, bf16[1,512,2048]{2,1,0:T(8,128)(2,1)}, u32[]{:S(2)}) copy-start(bf16[1,512,2048]{2,1,0:T(8,128)(2,1)} %param.6) | copy-start | bytes 6291460
  32.1 49.8 %collective-permute-start.7 = (bf16[4,528,128]{2,1,0:T(8,128)(2,1)}, bf16[4,528,128]{2,1,0:T(8,128)(2,1)}, u32[]{:S(2)}, u32[]{:S(2)}) collective-permute-start(bf16[4,528,128]{2,1,0:T(8,128)(2,1)} %shard_map.49), channel_id=1, source_target_pairs={{0,5},{1,6},{2,7},{3,4},{4,9},{5,10},{6,11},{7,8},{8,13},{9,14},{1... | collective-permute-start | bytes 1622024 | tf_op jit(solution)/shard_map/ppermute | solution.py:507
  37.3 1.0 copy-start.6
  45.1 36.7 %collective-permute-start.8 = (bf16[4,528,128]{2,1,0:T(8,128)(2,1)}, bf16[4,528,128]{2,1,0:T(8,128)(2,1)}, u32[]{:S(2)}, u32[]{:S(2)}) collective-permute-start(bf16[4,528,128]{2,1,0:T(8,128)(2,1)} %get-tuple-element.55), channel_id=1, source_target_pairs={{0,25},{1,26},{2,27},{3,24},{4,29},{5,30},{6,31},{7,28}} | collective-permute-start | bytes 1622024 | tf_op jit(solution)/shard_map/ppermute | solution.py:507
  46.6 35.3 %collective-permute-start.9 = (bf16[4,528,128]{2,1,0:T(8,128)(2,1)}, bf16[4,528,128]{2,1,0:T(8,128)(2,1)}, u32[]{:S(2)}, u32[]{:S(2)}) collective-permute-start(bf16[4,528,128]{2,1,0:T(8,128)(2,1)} %get-tuple-element.56), channel_id=1, source_target_pairs={{0,29},{1,30},{2,31},{3,28}} | collective-permute-start | bytes 1622024 | tf_op jit(solution)/shard_map/ppermute | solution.py:507
  48.1 19.7 %collective-permute-start.5 = (bf16[2,512,128]{2,1,0:T(8,128)(2,1)}, bf16[2,512,128]{2,1,0:T(8,128)(2,1)}, u32[]{:S(2)}, u32[]{:S(2)}) collective-permute-start(bf16[2,512,128]{2,1,0:T(8,128)(2,1)} %get-tuple-element.59), channel_id=1, source_target_pairs={{12,0},{16,4},{20,8},{24,12},{28,16},{13,1},{17,5},{21,9},{25,13},... | collective-permute-start | bytes 786440 | tf_op jit(solution)/shard_map/ppermute | solution.py:499
  50.1 17.7 %collective-permute-start.6 = (bf16[2,512,128]{2,1,0:T(8,128)(2,1)}, bf16[2,512,128]{2,1,0:T(8,128)(2,1)}, u32[]{:S(2)}, u32[]{:S(2)}) collective-permute-start(bf16[2,512,128]{2,1,0:T(8,128)(2,1)} %get-tuple-element.61), channel_id=1, source_target_pairs={{20,0},{24,4},{28,8},{21,1},{25,5},{29,9},{22,2},{26,6},{30,10},{2... | collective-permute-start | bytes 786440 | tf_op jit(solution)/shard_map/ppermute | solution.py:499
  57.7 1.6 copy-start.4
  57.7 1.9 %copy-start.7 = (bf16[8,512,128]{2,1,0:T(8,128)(2,1)S(1)}, bf16[8,512,128]{2,1,0:T(8,128)(2,1)}, u32[]{:S(2)}) copy-start(bf16[8,512,128]{2,1,0:T(8,128)(2,1)} %copy-done.6) | copy-start | bytes 3145732
  57.7 1.9 %copy-start.10 = (s32[1,8,16,2]{2,3,1,0:T(2,128)S(1)}, s32[1,8,16,2]{2,3,1,0:T(2,128)}, u32[]{:S(2)}) copy-start(s32[1,8,16,2]{2,3,1,0:T(2,128)} %param.7) | copy-start | bytes 3076
  59.6 8.2 %copy-start.2 = (bf16[1,512,2048]{2,1,0:T(8,128)(2,1)S(1)}, bf16[1,512,2048]{2,1,0:T(8,128)(2,1)}, u32[]{:S(2)}) copy-start(bf16[1,512,2048]{2,1,0:T(8,128)(2,1)} %param.6) | copy-start | bytes 6291460
  74.4 11.2 %collective-permute-start.10 = (bf16[2,512,128]{2,1,0:T(8,128)(2,1)}, bf16[2,512,128]{2,1,0:T(8,128)(2,1)}, u32[]{:S(2)}, u32[]{:S(2)}) collective-permute-start(bf16[2,512,128]{2,1,0:T(8,128)(2,1)} %get-tuple-element.67), channel_id=1, source_target_pairs={{12,0},{16,4},{20,8},{24,12},{28,16},{13,1},{17,5},{21,9},{25,13},... | collective-permute-start | bytes 786440 | tf_op jit(solution)/shard_map/ppermute | solution.py:499
  76.4 17.4 %collective-permute-start.11 = (bf16[2,512,128]{2,1,0:T(8,128)(2,1)}, bf16[2,512,128]{2,1,0:T(8,128)(2,1)}, u32[]{:S(2)}, u32[]{:S(2)}) collective-permute-start(bf16[2,512,128]{2,1,0:T(8,128)(2,1)} %get-tuple-element.69), channel_id=1, source_target_pairs={{20,0},{24,4},{28,8},{21,1},{25,5},{29,9},{22,2},{26,6},{30,10},{2... | collective-permute-start | bytes 786440 | tf_op jit(solution)/shard_map/ppermute | solution.py:499
  81.9 38.5 %collective-permute-start.12 = (bf16[2,528,128]{2,1,0:T(8,128)(2,1)}, bf16[2,528,128]{2,1,0:T(8,128)(2,1)}, u32[]{:S(2)}, u32[]{:S(2)}) collective-permute-start(bf16[2,528,128]{2,1,0:T(8,128)(2,1)} %get-tuple-element.73), channel_id=1, source_target_pairs={{0,13},{1,14},{2,15},{3,12},{4,17},{5,18},{6,19},{7,16},{8,21},{9,... | collective-permute-start | bytes 811016 | tf_op jit(solution)/shard_map/ppermute | solution.py:507
  83.2 37.2 %collective-permute-start.13 = (bf16[2,528,128]{2,1,0:T(8,128)(2,1)}, bf16[2,528,128]{2,1,0:T(8,128)(2,1)}, u32[]{:S(2)}, u32[]{:S(2)}) collective-permute-start(bf16[2,528,128]{2,1,0:T(8,128)(2,1)} %get-tuple-element.74), channel_id=1, source_target_pairs={{0,21},{1,22},{2,23},{3,20},{4,25},{5,26},{6,27},{7,24},{8,29},{9,... | collective-permute-start | bytes 811016 | tf_op jit(solution)/shard_map/ppermute | solution.py:507
  93.8 55.9 %collective-permute-start.15 = (bf16[4,512,128]{2,1,0:T(8,128)(2,1)}, bf16[4,512,128]{2,1,0:T(8,128)(2,1)}, u32[]{:S(2)}, u32[]{:S(2)}) collective-permute-start(bf16[4,512,128]{2,1,0:T(8,128)(2,1)} %get-tuple-element.79), channel_id=1, source_target_pairs={{16,0},{20,4},{24,8},{28,12},{17,1},{21,5},{25,9},{29,13},{18,2},{... | collective-permute-start | bytes 1572872 | tf_op jit(solution)/shard_map/ppermute | solution.py:499
  120.2 29.4 %collective-permute-start.14 = (bf16[16,528,128]{2,1,0:T(8,128)(2,1)}, bf16[16,528,128]{2,1,0:T(8,128)(2,1)}, u32[]{:S(2)}, u32[]{:S(2)}) collective-permute-start(bf16[16,528,128]{2,1,0:T(8,128)(2,1)} %shard_map.52), channel_id=1, source_target_pairs={{0,1},{1,2},{2,3},{3,0},{4,5},{5,6},{6,7},{7,4},{8,9},{9,10},{10,1... | collective-permute-start | bytes 6488072 | tf_op jit(solution)/shard_map/ppermute | solution.py:23
  120.3 34.0 %collective-permute-start.17 = (bf16[2,528,128]{2,1,0:T(8,128)(2,1)}, bf16[2,528,128]{2,1,0:T(8,128)(2,1)}, u32[]{:S(2)}, u32[]{:S(2)}) collective-permute-start(bf16[2,528,128]{2,1,0:T(8,128)(2,1)} %get-tuple-element.82), channel_id=1, source_target_pairs={{0,21},{1,22},{2,23},{3,20},{4,25},{5,26},{6,27},{7,24},{8,29},{9,... | collective-permute-start | bytes 811016 | tf_op jit(solution)/shard_map/ppermute | solution.py:507
  121.6 32.7 %collective-permute-start.16 = (bf16[2,528,128]{2,1,0:T(8,128)(2,1)}, bf16[2,528,128]{2,1,0:T(8,128)(2,1)}, u32[]{:S(2)}, u32[]{:S(2)}) collective-permute-start(bf16[2,528,128]{2,1,0:T(8,128)(2,1)} %get-tuple-element.81), channel_id=1, source_target_pairs={{0,13},{1,14},{2,15},{3,12},{4,17},{5,18},{6,19},{7,16},{8,21},{9,... | collective-permute-start | bytes 811016 | tf_op jit(solution)/shard_map/ppermute | solution.py:507
  155.5 17.0 %collective-permute-start.18 = (bf16[4,528,128]{2,1,0:T(8,128)(2,1)}, bf16[4,528,128]{2,1,0:T(8,128)(2,1)}, u32[]{:S(2)}, u32[]{:S(2)}) collective-permute-start(bf16[4,528,128]{2,1,0:T(8,128)(2,1)} %shard_map.59), channel_id=1, source_target_pairs={{0,17},{1,18},{2,19},{3,16},{4,21},{5,22},{6,23},{7,20},{8,25},{9,... | collective-permute-start | bytes 1622024 | tf_op jit(solution)/shard_map/ppermute | solution.py:507
  156.8 1.2 copy-start.12
  172.5 2.2 %copy-start.5 = (f32[16,512,128]{2,1,0:T(8,128)S(1)}, f32[16,512,128]{2,1,0:T(8,128)}, u32[]{:S(2)}) copy-start(f32[16,512,128]{2,1,0:T(8,128)} %get-tuple-element.84.mixed_ref) | copy-start | bytes 12582916

commit v4 on v3

--- a/solution.py
+++ b/solution.py
@@ -14,7 +14,8 @@
 EXP2_SCALE = HD ** -0.5 * math.log2(math.e)
 LANES = 128
 STAT_ROWS = 16
-VMEM_BYTES = 48 * 1024 * 1024
+VMEM_BYTES = 24 * 1024 * 1024
+HIGH_COST = 10**12
 
 
 def passed_along(value, axis, steps):
@@ -63,34 +64,30 @@
     out_ref[0] = here_ref[0]
 
 
-def tick(here, *earlier, flops=10**12):
+def tick(here, *earlier):
     return call(
         tick_kernel,
         [SCALARS],
         jax.ShapeDtypeStruct((1,), jnp.int32),
         SCALARS,
-        flops=flops,
+        flops=HIGH_COST,
     )(after(here, *earlier))
 
 
 def list_heads(heads_ref, start, picks_ref, block, owner, slots):
     width = picks_ref.shape[0]
+    spare = heads_ref.shape[0] - 1
     for slot in range(slots):
         heads_ref[start + slot] = -1
     valid = (block >= 0) & (block < width) & (owner >= 0) & (owner < width)
     row = jnp.clip(block, 0, width - 1)
-
-    def look(number, found):
-        pick, head = number // HEADS, number % HEADS
-        hit = valid & (picks_ref[row, pick, head] == owner)
-
-        @pl.when(hit)
-        def _():
-            heads_ref[start + found] = head
-
-        return found + hit.astype(jnp.int32)
-
-    lax.fori_loop(0, PICKS * HEADS, look, jnp.int32(0))
+    wanted = jnp.where(valid, owner, -2)
+    found = jnp.int32(0)
+    for pick in range(PICKS):
+        for head in range(HEADS):
+            hit = picks_ref[row, pick, head] == wanted
+            heads_ref[jnp.where(hit, start + found, spare)] = head
+            found = found + hit.astype(jnp.int32)
 
 
 def pack_kernel(here_ref, picks_ref, *refs, jobs, slots):
@@ -128,7 +125,7 @@
         [SCALARS, SCALARS, IN_HBM, IN_HBM, IN_HBM],
         [jax.ShapeDtypeStruct((size, rows, HD), jnp.bfloat16) for size in sizes],
         [IN_HBM] * len(sizes),
-        [pltpu.SMEM((len(jobs) * slots,), jnp.int32), pltpu.SemaphoreType.DMA((sum(sizes),))],
+        [pltpu.SMEM((len(jobs) * slots + 1,), jnp.int32), pltpu.SemaphoreType.DMA((sum(sizes),))],
         moved=4 * rows * HD * sum(sizes),
     )(here, picks, queries, keys, values)
 
@@ -213,7 +210,7 @@
         for slot in range(count):
             columns = head_columns(jnp.maximum(heads_ref[first + slot], 0))
             outputs, lines = attend_rows(
-                query_ref[slot], key_ref[:, columns], with_ones(value_ref[:, columns]), min(rows, 256)
+                query_ref[slot], key_ref[:, columns], with_ones(value_ref[:, columns]), rows
             )
             out_ref[slot, :rows, :] = outputs.astype(jnp.bfloat16)
             out_ref[slot, rows:, :] = three_parts(lines)
@@ -230,7 +227,7 @@
             for _, _, count in group
         ],
         [IN_VMEM] * len(group),
-        [pltpu.SMEM((slots,), jnp.int32)],
+        [pltpu.SMEM((slots + 1,), jnp.int32)],
         flops=4 * total * rows * rows * HD,
         moved=8 * total * rows * HD,
         exps=total * rows * rows,
@@ -273,86 +270,60 @@
     )(here, queries, keys, values)
 
 
-def near_kernel(here_ref, picks_ref, query_ref, own_ref, *refs, shifts, slots):
-    near_refs, out_ref, heads_ref = refs[: len(shifts)], refs[-2], refs[-1]
+def near_kernel(here_ref, picks_ref, query_ref, own_ref, near_ref, out_ref, heads_ref, *, shift, slots):
     rows = query_ref.shape[0]
-
-    def keep(head, carry):
+    here = here_ref[0]
+    list_heads(heads_ref, 0, picks_ref, here, here - shift, slots)
+    for head in range(HEADS):
         out_ref[head] = own_ref[head]
-        return carry
-
-    lax.fori_loop(0, HEADS, keep, 0)
-    groups = rows // LANES
-    here = here_ref[0]
-    for shift, near_ref in zip(shifts, near_refs):
-        list_heads(heads_ref, 0, picks_ref, here, here - shift, slots)
-        for slot in range(slots):
-            head = heads_ref[slot]
-
-            @pl.when(head >= 0)
-            def _():
-                outputs, lines = attend_rows(
-                    query_ref[:, head_columns(head)],
-                    near_ref[2 * slot],
-                    with_ones(near_ref[2 * slot + 1]),
-                    min(rows, 256),
-                )
-                before = stats_of(out_ref[head, rows:, :], groups)
-                top = jnp.maximum(before, lines)
-                after = top + jnp.log2(jnp.exp2(before - top) + jnp.exp2(lines - top))
-                share = jnp.exp2(lines - after)
-                for group in range(groups):
-                    span = pl.ds(group * LANES, LANES)
-                    old = out_ref[head, span, :].astype(jnp.float32)
-                    new = outputs[group * LANES : (group + 1) * LANES]
-                    mixed = old + (new - old) * down_rows(share[group : group + 1, :])
-                    out_ref[head, span, :] = mixed.astype(jnp.bfloat16)
-                out_ref[head, rows:, :] = three_parts(after)
-
-
-def add_near(here, picks, queries, own, near, shifts, slots):
+    for slot in range(slots):
+        columns = head_columns(jnp.maximum(heads_ref[slot], 0))
+        outputs, lines = attend_rows(
+            query_ref[:, columns], near_ref[2 * slot], with_ones(near_ref[2 * slot + 1]), rows
+        )
+        out_ref[HEADS + slot, :rows, :] = outputs.astype(jnp.bfloat16)
+        out_ref[HEADS + slot, rows:, :] = three_parts(lines)
+
+
+def add_near(here, picks, queries, own, near, shift, slots):
     rows = queries.shape[0]
-    count = len(shifts) * slots
     return call(
-        functools.partial(near_kernel, shifts=shifts, slots=slots),
-        [SCALARS, SCALARS, IN_VMEM, IN_VMEM] + [IN_VMEM] * len(shifts),
-        jax.ShapeDtypeStruct(own.shape, own.dtype),
+        functools.partial(near_kernel, shift=shift, slots=slots),
+        [SCALARS, SCALARS, IN_VMEM, IN_VMEM, IN_VMEM],
+        jax.ShapeDtypeStruct((HEADS + slots,) + own.shape[1:], own.dtype),
         IN_VMEM,
-        [pltpu.SMEM((slots,), jnp.int32)],
-        flops=4 * count * rows * rows * HD,
-        moved=12 * count * rows * HD,
-        exps=count * rows * rows,
-    )(here, picks, queries, own, *near)
+        [pltpu.SMEM((slots + 1,), jnp.int32)],
+        flops=HIGH_COST,
+        moved=12 * slots * rows * HD,
+        exps=slots * rows * rows,
+    )(here, picks, queries, own, near)
 
 
 def find_spots(spots_ref, found_ref, picks_ref, here, shifts, slots):
     for owner in range(picks_ref.shape[0]):
         found_ref[owner] = 0
 
-    def look(number, carry):
-        pick, head = number // HEADS, number % HEADS
-        owner = picks_ref[here, pick, head]
-        safe = jnp.maximum(owner, 0)
-        order = found_ref[safe]
-        found_ref[safe] = order + (owner >= 0).astype(jnp.int32)
-        spot = jnp.int32(-1)
-        for place, shift in enumerate(shifts):
-            spot = jnp.where(here - safe == shift, place * slots + order, spot)
-        spots_ref[head * PICKS + pick] = jnp.where(owner >= 0, spot, -1)
-        return carry
-
-    lax.fori_loop(0, PICKS * HEADS, look, 0)
+    for pick in range(PICKS):
+        for head in range(HEADS):
+            owner = picks_ref[here, pick, head]
+            safe = jnp.maximum(owner, 0)
+            order = found_ref[safe]
+            found_ref[safe] = order + (owner >= 0).astype(jnp.int32)
+            spot = jnp.int32(-1)
+            for place, shift in enumerate(shifts):
+                spot = jnp.where(here - safe == shift, place * slots + order, spot)
+            spots_ref[head * PICKS + pick] = jnp.where(owner >= 0, spot, -1)
 
 
 def merge_kernel(here_ref, picks_ref, *refs, places, shifts, slots):
     count = len(places)
-    parts = refs[: count + 1]
-    out_ref, sums_ref, held, spots_ref, found_ref, sems = refs[count + 1 :]
+    parts = refs[:count]
+    out_ref, sums_ref, held, spots_ref, found_ref, sems = refs[count:]
     groups = sums_ref.shape[1]
     rows = groups * LANES
     copies = [
         pltpu.make_async_copy(part, held.at[pl.ds(place, part.shape[0])], sems.at[number])
-        for number, (part, place) in enumerate(zip(parts, (0,) + places))
+        for number, (part, place) in enumerate(zip(parts, places))
     ]
     for copy in copies:
         copy.start()
@@ -383,15 +354,13 @@
     lax.fori_loop(0, HEADS, one_head, 0, unroll=2)
 
 
-def merge(here, picks, own, parts, places, shifts, slots):
-    rows = own.shape[1] - STAT_ROWS
+def merge(here, picks, parts, places, shifts, slots):
+    rows = parts[0].shape[1] - STAT_ROWS
     width = picks.shape[0]
     total = HEADS + len(shifts) * slots
     return call(
-        functools.partial(
-            merge_kernel, places=tuple(HEADS + place for place in places), shifts=shifts, slots=slots
-        ),
-        [SCALARS, SCALARS] + [pl.BlockSpec(memory_space=pl.ANY)] * (1 + len(parts)),
+        functools.partial(merge_kernel, places=tuple(places), shifts=shifts, slots=slots),
+        [SCALARS, SCALARS] + [pl.BlockSpec(memory_space=pl.ANY)] * len(parts),
         [
             jax.ShapeDtypeStruct((HEADS, rows, HD), jnp.float32),
             jax.ShapeDtypeStruct((HEADS, rows // LANES, LANES), jnp.float32),
@@ -401,11 +370,11 @@
             pltpu.VMEM((total, rows + STAT_ROWS, HD), jnp.bfloat16),
             pltpu.SMEM((PICKS * HEADS,), jnp.int32),
             pltpu.SMEM((width,), jnp.int32),
-            pltpu.SemaphoreType.DMA((1 + len(parts),)),
+            pltpu.SemaphoreType.DMA((len(parts),)),
         ],
-        flops=6 * HEADS * rows * HD,
+        flops=HIGH_COST,
         moved=2 * (HEADS * 2 + total) * rows * HD,
-    )(here, picks, own, *parts)
+    )(here, picks, *parts)
 
 
 def finish_kernel(
@@ -546,34 +515,38 @@
     own = own_part(after(here, before, sends[later_jobs[0]]), queries, keys, values)
     parts = attend_group(after(here, own), groups[0])
     send_back(parts)
-    parts_next = attend_group(after(here, *parts.values(), *near), groups[1])
-    send_back(parts_next)
-    ask_for(groups[2], *parts_next.values(), *arrived.values())
-    now = tick(here, *parts_next.values())
-    own = add_near(now, own_picks, queries, own, near, near_shifts, slots)
+    parts = attend_group(after(here, *parts.values(), *near), groups[1])
+    send_back(parts)
+    ask_for(groups[2], *parts.values(), *arrived.values())
+    now = after(here, *parts.values())
     before_last = groups[0] + groups[1]
     for number in range(2, len(groups)):
         group = groups[number]
-        waits = [own] if number == 2 else []
-        waits += [own_back] if number == len(groups) - 1 else []
-        parts = attend_group(after(now, *waits), group)
-        now = tick(now, *parts.values(), flops=0)
+        if number == len(groups) - 1:
+            now = tick(now, *those(returned, groups[number - 2]))
+            now = after(now, own_back)
+        parts = attend_group(now, group)
         if number == 2:
             ask_for(groups[number + 1], *parts.values(), *those(arrived, group))
         send_back(parts, *those(returned, before_last))
+        now = after(now, *parts.values())
         if number == 2:
-            own_back = passed_along(after(own, *those(returned, before_last)), "pipe", 1)
-        now = tick(now, *those(returned, before_last))
-        before_last = group
+            now = after(now, *those(returned, before_last))
+            own = add_near(now, own_picks, queries, own, near[0], near_shifts[0], slots)
+            own_back = passed_along(own, "pipe", 1)
+            now = after(now, own)
         if 2 <= number < len(groups) - 2:
             ask_for(groups[number + 2], now, *those(arrived, groups[number + 1]))
+        before_last = group
+    now = after(now, *those(returned, groups[-2]))
 
     final = groups[-1][0]
-    merged_shifts = tuple(shift for shift in range(1, width) if shift not in (2, final[0]))
+    others = [shift for shift in range(1, width) if shift not in near_shifts + final[:1]]
+    merged_shifts = near_shifts + tuple(others)
     pieces = [piece for piece in returned if piece != final]
-    places = [merged_shifts.index(shift) * slots + first for shift, first, _ in pieces]
-    parts = [returned[piece] for piece in pieces]
-    mixed, sums = merge(now, before, own_back, parts, places, merged_shifts, slots)
+    places = [HEADS + merged_shifts.index(shift) * slots + first for shift, first, _ in pieces]
+    parts = [own_back] + [returned[piece] for piece in pieces]
+    mixed, sums = merge(now, before, parts, [0] + places, merged_shifts, slots)
     return finish(now, before, mixed, sums, returned[final], final[0], slots)[None]
 
 

time: 180 us -> 159 us (0.88)
  the two profiles are of different devices: /device:TPU:22 before, /device:TPU:26 now
where the time goes in v4:
time: 159 us
  waiting for transfers between devices  53.9 us (34%)
  starting transfers between devices  51.4 us (32%)
  Pallas kernels  45.2 us (28%)
  local copies, waits for them, and re-layouts  7.71 us (5%)
    ppermute x8, starting transfers between devices, down(): lax.ppermute(value, 'ctx', [(at, at - shift) for at in range(shift, width)])  37.3 us
    ppermute x8, waiting for transfers between devices, up_and_on(): return lax.ppermute(value, ('ctx', 'pipe'), pairs)  24.5 us
    ppermute x2, waiting for transfers between devices, passed_along(): return lax.ppermute(value, axis, pairs)  21.2 us
    pallas_call x5, Pallas kernels, attend(): call(functools.partial(attend_kernel, group=group, slots=slots), [SCALARS...  17.8 us
    ppermute x8, starting transfers between devices, up_and_on(): return lax.ppermute(value, ('ctx', 'pipe'), pairs)  12.1 us
    unnamed x26, local copies, waits for them, and re-layouts  7.71 us
    ppermute x8, waiting for transfers between devices, down(): lax.ppermute(value, 'ctx', [(at, at - shift) for at in range(shift, width)])  7.7 us
    pallas_call x1, Pallas kernels, own_part(): call(own_kernel, [SCALARS, IN_VMEM, IN_VMEM, IN_VMEM], jax.ShapeDtypeStru...  7.62 us
  transfers between devices with their start and end apart: 19, of which 7 were waited for; matrix products, arithmetic and copies ran while one was open for 0% of the time, Pallas kernels for 24%

profile of v4, /device:TPU:26, one launch (start us, length us, event | category | flops | bytes accessed | tf_op | source)
XLA Modules:
  0.0 158.5 jit_solution(5738574018235910186)
XLA Ops:
  0.0 1.6 %copy-done = bf16[1,512,2048]{2,1,0:T(8,128)(2,1)S(1)} copy-done((bf16[1,512,2048]{2,1,0:T(8,128)(2,1)S(1)}, bf16[1,512,2048]{2,1,0:T(8,128)(2,1)}, u32[]{:S(2)}) %copy-start) | copy-done | bytes 2097176
  1.6 1.6 %copy-done.2 = bf16[1,512,2048]{2,1,0:T(8,128)(2,1)S(1)} copy-done((bf16[1,512,2048]{2,1,0:T(8,128)(2,1)S(1)}, bf16[1,512,2048]{2,1,0:T(8,128)(2,1)}, u32[]{:S(2)}) %copy-start.2) | copy-done | bytes 2097176
  3.2 1.6 %copy-done.4 = bf16[1,512,2048]{2,1,0:T(8,128)(2,1)S(1)} copy-done((bf16[1,512,2048]{2,1,0:T(8,128)(2,1)S(1)}, bf16[1,512,2048]{2,1,0:T(8,128)(2,1)}, u32[]{:S(2)}) %copy-start.4) | copy-done | bytes 2097176
  4.8 0.7 copy-done.5
  5.5 2.1 %shard_map.46 = (bf16[8,512,128]{2,1,0:T(8,128)(2,1)S(1)}, bf16[4,512,128]{2,1,0:T(8,128)(2,1)S(1)}, bf16[4,512,128]{2,1,0:T(8,128)(2,1)S(1)}, bf16[4,512,128]{2,1,0:T(8,128)(2,1)S(1)}) custom-call(s32[1]{0:T(128)} %bitcast.here_ref, s32[8,2,16]{2,1,0:T(2,128)S(1)} %bitcast.28, bf16[512,2048]{1,0:T(8,128)(2,1)S(1)} %bitcast.24, ...), custom_call_target="tpu_custom_call" | custom-call | bytes 5242880 | tf_op jit(solution)/shard_map/pallas_call | solution.py:123
  7.5 1.3 collective-permute-start.2
  8.8 5.5 %collective-permute-start.1 = (bf16[4,512,128]{2,1,0:T(8,128)(2,1)S(1)}, bf16[4,512,128]{2,1,0:T(8,128)(2,1)S(1)}, u32[]{:S(2)}, u32[]{:S(2)}) collective-permute-start(bf16[4,512,128]{2,1,0:T(8,128)(2,1)S(1)} %get-tuple-element.46), channel_id=1, source_target_pairs={{4,0},{8,4},{12,8},{16,12},{20,16},{24,20},{28,24},{5,1},{9,5},{13... | collective-permute-start | bytes 1572872 | tf_op jit(solution)/shard_map/ppermute | solution.py:468
  14.3 1.3 collective-permute-start.3
  15.7 0.7 collective-permute-start.4
  16.4 0.1 collective-permute-start
  16.4 2.3 %shard_map.47 = (bf16[2,512,128]{2,1,0:T(8,128)(2,1)S(1)}, bf16[2,512,128]{2,1,0:T(8,128)(2,1)S(1)}, bf16[2,512,128]{2,1,0:T(8,128)(2,1)}, bf16[2,512,128]{2,1,0:T(8,128)(2,1)}, bf16[4,512,128]{2,1,0:T(8,128)(2,1)}) custom-call(s32[1]{0:T(128)} %bitcast.here_ref, s32[8,2,16]{2,1,0:T(2,128)S(1)} %bitcast.30, bf16[512,2048]{1,0:T(8,128)(2,1)S(1)} %bitcast.25, ...), custom_call_target="tpu_custom_call" | custom-call | bytes 3145728 | tf_op jit(solution)/shard_map/pallas_call | solution.py:123
  18.7 0.8 collective-permute-done.picks_ref
  19.5 0.6 copy-done.7
  20.1 7.6 %shard_map.48.own_ref = bf16[16,528,128]{2,1,0:T(8,128)(2,1)S(1)} custom-call(s32[1]{0:T(128)} %bitcast.here_ref, bf16[512,2048]{1,0:T(8,128)(2,1)S(1)} %bitcast.26, bf16[512,2048]{1,0:T(8,128)(2,1)S(1)} %bitcast.10, bf16[512,2048]{1,0:T(8,128)(2,1)S(1)} %bitcast.18), custom_call_target="tpu_custom_call" | custom-call | flops 2147483648 | bytes 8388608 | tf_op jit(solution)/shard_map/pallas_call | solution.py:262
  27.7 0.0 copy-start.6
  27.7 0.0 collective-permute-done.1.refs_0_
  27.8 2.6 %shard_map.49 = bf16[4,528,128]{2,1,0:T(8,128)(2,1)S(1)} custom-call(s32[1]{0:T(128)} %bitcast.here_ref, s32[8,2,16]{2,1,0:T(2,128)S(1)} %bitcast.31, bf16[512,2048]{1,0:T(8,128)(2,1)S(1)} %bitcast.11, bf16[512,2048]{1,0:T(8,128)(2,1)S(1)} %bitcast.19, bf16[4,512,128]{2,1,0:T(8,128)(2,1)S(1)} %collective-permute-done.1.refs_0_), custom_call_target="tpu_custom_call" | custom-call | flops 536870912 | bytes 2097152 | tf_op jit(solution)/shard_map/pallas_call | solution.py:222
  30.4 3.5 %collective-permute-start.7 = (bf16[4,528,128]{2,1,0:T(8,128)(2,1)S(1)}, bf16[4,528,128]{2,1,0:T(8,128)(2,1)S(1)}, u32[]{:S(2)}, u32[]{:S(2)}) collective-permute-start(bf16[4,528,128]{2,1,0:T(8,128)(2,1)S(1)} %shard_map.49), channel_id=1, source_target_pairs={{0,5},{1,6},{2,7},{3,4},{4,9},{5,10},{6,11},{7,8},{8,13},{9,14},{1... | collective-permute-start | bytes 1622024 | tf_op jit(solution)/shard_map/ppermute | solution.py:476
  33.9 0.5 collective-permute-done.2.near_ref
  34.3 2.1 %collective-permute-done.3.refs_0_ = bf16[4,512,128]{2,1,0:T(8,128)(2,1)S(1)} collective-permute-done((bf16[4,512,128]{2,1,0:T(8,128)(2,1)S(1)}, bf16[4,512,128]{2,1,0:T(8,128)(2,1)S(1)}, u32[]{:S(2)}, u32[]{:S(2)}) %collective-permute-start.3) | collective-permute-done | bytes 524320 | tf_op jit(solution)/shard_map/ppermute | solution.py:468
  36.5 3.9 %shard_map.50 = (bf16[4,528,128]{2,1,0:T(8,128)(2,1)S(1)}, bf16[4,528,128]{2,1,0:T(8,128)(2,1)S(1)}) custom-call(s32[1]{0:T(128)} %bitcast.here_ref, s32[8,2,16]{2,1,0:T(2,128)S(1)} %bitcast.32, bf16[512,2048]{1,0:T(8,128)(2,1)S(1)} %bitcast.12, bf16[512,2048]{1,0:T(8,128)(2,1)S(1)} %bitcast.20, bf16[4,512,128]{2,1,0:T(8,128)(2,1)S(1)} %collective-permute-done.3.refs_0_, ...), custom_call_target="tpu_custom_call" | custom-call | flops 1073741824 | bytes 4194304 | tf_op jit(solution)/shard_map/pallas_call | solution.py:222
  40.4 1.3 collective-permute-start.8
  41.7 0.7 collective-permute-start.9
  42.4 1.3 collective-permute-start.5
  43.7 6.3 %collective-permute-start.6 = (bf16[2,512,128]{2,1,0:T(8,128)(2,1)S(1)}, bf16[2,512,128]{2,1,0:T(8,128)(2,1)S(1)}, u32[]{:S(2)}, u32[]{:S(2)}) collective-permute-start(bf16[2,512,128]{2,1,0:T(8,128)(2,1)S(1)} %get-tuple-element.59), channel_id=1, source_target_pairs={{20,0},{24,4},{28,8},{21,1},{25,5},{29,9},{22,2},{26,6},{30,10},{2... | collective-permute-start | bytes 786440 | tf_op jit(solution)/shard_map/ppermute | solution.py:468
  50.0 5.6 %collective-permute-done.6.refs_1_ = bf16[2,512,128]{2,1,0:T(8,128)(2,1)S(1)} collective-permute-done((bf16[2,512,128]{2,1,0:T(8,128)(2,1)S(1)}, bf16[2,512,128]{2,1,0:T(8,128)(2,1)S(1)}, u32[]{:S(2)}, u32[]{:S(2)}) %collective-permute-start.6) | collective-permute-done | bytes 262176 | tf_op jit(solution)/shard_map/ppermute | solution.py:468
  55.6 3.3 %shard_map.51 = (bf16[2,528,128]{2,1,0:T(8,128)(2,1)}, bf16[2,528,128]{2,1,0:T(8,128)(2,1)}) custom-call(s32[1]{0:T(128)} %bitcast.here_ref, s32[8,2,16]{2,1,0:T(2,128)S(1)} %bitcast.33, bf16[512,2048]{1,0:T(8,128)(2,1)S(1)} %bitcast.13, bf16[512,2048]{1,0:T(8,128)(2,1)S(1)} %bitcast.21, bf16[2,512,128]{2,1,0:T(8,128)(2,1)S(1)} %collective-permute-done.5.refs_0_, ...), custom_call_target="tpu_custom_call" | custom-call | flops 536870912 | bytes 2097152 | tf_op jit(solution)/shard_map/pallas_call | solution.py:222
  58.9 5.8 %collective-permute-start.10 = (bf16[2,512,128]{2,1,0:T(8,128)(2,1)}, bf16[2,512,128]{2,1,0:T(8,128)(2,1)}, u32[]{:S(2)}, u32[]{:S(2)}) collective-permute-start(bf16[2,512,128]{2,1,0:T(8,128)(2,1)} %get-tuple-element.66), channel_id=1, source_target_pairs={{12,0},{16,4},{20,8},{24,12},{28,16},{13,1},{17,5},{21,9},{25,13},... | collective-permute-start | bytes 786440 | tf_op jit(solution)/shard_map/ppermute | solution.py:468
  64.7 6.6 %collective-permute-start.11 = (bf16[2,512,128]{2,1,0:T(8,128)(2,1)}, bf16[2,512,128]{2,1,0:T(8,128)(2,1)}, u32[]{:S(2)}, u32[]{:S(2)}) collective-permute-start(bf16[2,512,128]{2,1,0:T(8,128)(2,1)} %get-tuple-element.68), channel_id=1, source_target_pairs={{20,0},{24,4},{28,8},{21,1},{25,5},{29,9},{22,2},{26,6},{30,10},{2... | collective-permute-start | bytes 786440 | tf_op jit(solution)/shard_map/ppermute | solution.py:468
  71.3 0.8 copy-done.9
  72.1 0.8 copy-done.11
  72.9 1.3 collective-permute-start.12
  74.2 1.5 collective-permute-start.13
  75.7 4.1 %shard_map.52 = bf16[20,528,128]{2,1,0:T(8,128)(2,1)} custom-call(s32[1]{0:T(128)} %bitcast.here_ref, s32[8,2,16]{2,1,0:T(2,128)S(1)} %bitcast.34, bf16[512,2048]{1,0:T(8,128)(2,1)S(1)} %bitcast.27, bf16[16,528,128]{2,1,0:T(8,128)(2,1)S(1)} %shard_map.48.own_ref, bf16[8,512,128]{2,1,0:T(8,128)(2,1)S(1)} %collective-permute-done.2.near_ref), custom_call_target="tpu_custom_call" | custom-call | flops 999999995904 | bytes 3145728 | tf_op jit(solution)/shard_map/pallas_call | solution.py:290
  79.8 0.7 collective-permute-start.14
  80.5 9.7 %collective-permute-start.15 = (bf16[4,512,128]{2,1,0:T(8,128)(2,1)}, bf16[4,512,128]{2,1,0:T(8,128)(2,1)}, u32[]{:S(2)}, u32[]{:S(2)}) collective-permute-start(bf16[4,512,128]{2,1,0:T(8,128)(2,1)} %get-tuple-element.77), channel_id=1, source_target_pairs={{16,0},{20,4},{24,8},{28,12},{17,1},{21,5},{25,9},{29,13},{18,2},{... | collective-permute-start | bytes 1572872 | tf_op jit(solution)/shard_map/ppermute | solution.py:468
  90.3 3.7 %shard_map.53 = (bf16[2,528,128]{2,1,0:T(8,128)(2,1)}, bf16[2,528,128]{2,1,0:T(8,128)(2,1)}) custom-call(s32[1]{0:T(128)} %bitcast.here_ref, s32[8,2,16]{2,1,0:T(2,128)S(1)} %bitcast.35, bf16[512,2048]{1,0:T(8,128)(2,1)S(1)} %bitcast.14, bf16[512,2048]{1,0:T(8,128)(2,1)S(1)} %bitcast.22, bf16[2,512,128]{2,1,0:T(8,128)(2,1)} %collective-permute-done.10.refs_0_, ...), custom_call_target="tpu_custom_call" | custom-call | flops 536870912 | bytes 2097152 | tf_op jit(solution)/shard_map/pallas_call | solution.py:222
  93.9 3.7 %collective-permute-done.12.refs_4_ = bf16[2,528,128]{2,1,0:T(8,128)(2,1)} collective-permute-done((bf16[2,528,128]{2,1,0:T(8,128)(2,1)}, bf16[2,528,128]{2,1,0:T(8,128)(2,1)}, u32[]{:S(2)}, u32[]{:S(2)}) %collective-permute-start.12) | collective-permute-done | bytes 270368 | tf_op jit(solution)/shard_map/ppermute | solution.py:476
  97.6 1.3 collective-permute-start.17
  98.9 1.3 collective-permute-start.16
  100.2 0.5 shard_map.54.here_ref
  100.8 0.0 copy-start.10
  100.8 20.4 %collective-permute-done.14.refs_0_ = bf16[20,528,128]{2,1,0:T(8,128)(2,1)} collective-permute-done((bf16[20,528,128]{2,1,0:T(8,128)(2,1)}, bf16[20,528,128]{2,1,0:T(8,128)(2,1)}, u32[]{:S(2)}, u32[]{:S(2)}) %collective-permute-start.14) | collective-permute-done | bytes 2703392 | tf_op jit(solution)/shard_map/ppermute | solution.py:24
  121.2 4.4 %shard_map.55 = bf16[4,528,128]{2,1,0:T(8,128)(2,1)} custom-call(s32[1]{0:T(128)} %shard_map.54.here_ref, s32[8,2,16]{2,1,0:T(2,128)S(1)} %bitcast.36, bf16[512,2048]{1,0:T(8,128)(2,1)S(1)} %bitcast.15, bf16[512,2048]{1,0:T(8,128)(2,1)S(1)} %bitcast.23, bf16[4,512,128]{2,1,0:T(8,128)(2,1)} %collective-permute-done.15.refs_0_), custom_call_target="tpu_custom_call" | custom-call | flops 536870912 | bytes 2097152 | tf_op jit(solution)/shard_map/pallas_call | solution.py:222
  125.6 1.3 collective-permute-start.18
  126.9 6.4 %shard_map.56 = (f32[16,512,128]{2,1,0:T(8,128)S(1)}, f32[16,4,128]{2,1,0:T(4,128)S(1)}) custom-call(s32[1]{0:T(128)} %shard_map.54.here_ref, s32[8,2,16]{2,1,0:T(2,128)S(1)} %copy-done.8, bf16[20,528,128]{2,1,0:T(8,128)(2,1)} %collective-permute-done.14.refs_0_, bf16[4,528,128]{2,1,0:T(8,128)(2,1)S(1)} %copy-done.10, ...), custom_call_target="tpu_custom_call" | custom-call | flops 999999995904 | bytes 9437184 | tf_op jit(solution)/shard_map/pallas_call | solution.py:361
  133.3 20.8 %collective-permute-done.18.part_ref = bf16[4,528,128]{2,1,0:T(8,128)(2,1)} collective-permute-done((bf16[4,528,128]{2,1,0:T(8,128)(2,1)}, bf16[4,528,128]{2,1,0:T(8,128)(2,1)}, u32[]{:S(2)}, u32[]{:S(2)}) %collective-permute-start.18) | collective-permute-done | bytes 540704 | tf_op jit(solution)/shard_map/ppermute | solution.py:476
  154.1 4.4 %shard_map.57 = bf16[512,2048]{1,0:T(8,128)(2,1)} custom-call(s32[1]{0:T(128)} %shard_map.54.here_ref, s32[8,2,16]{2,1,0:T(2,128)S(1)} %copy-done.8, f32[16,512,128]{2,1,0:T(8,128)S(1)} %get-tuple-element.82.mixed_ref, f32[16,4,128]{2,1,0:T(4,128)S(1)} %get-tuple-element.83.sums_ref, bf16[4,528,128]{2,1,0:T(8,128)(2,1)} %collective-permute-done.18.part_ref), custom_call_target="tpu_custom_call" | custom-call | flops 2097152 | bytes 8388608 | tf_op jit(solution)/shard_map/pallas_call | solution.py:418
  (28 shorter events, 0.1 us)
Async XLA Ops:
  0.0 1.6 %copy-start = (bf16[1,512,2048]{2,1,0:T(8,128)(2,1)S(1)}, bf16[1,512,2048]{2,1,0:T(8,128)(2,1)}, u32[]{:S(2)}) copy-start(bf16[1,512,2048]{2,1,0:T(8,128)(2,1)} %param.5) | copy-start | bytes 6291460
  1.6 1.6 %copy-start.2 = (bf16[1,512,2048]{2,1,0:T(8,128)(2,1)S(1)}, bf16[1,512,2048]{2,1,0:T(8,128)(2,1)}, u32[]{:S(2)}) copy-start(bf16[1,512,2048]{2,1,0:T(8,128)(2,1)} %param.6) | copy-start | bytes 6291460
  3.2 1.6 %copy-start.4 = (bf16[1,512,2048]{2,1,0:T(8,128)(2,1)S(1)}, bf16[1,512,2048]{2,1,0:T(8,128)(2,1)}, u32[]{:S(2)}) copy-start(bf16[1,512,2048]{2,1,0:T(8,128)(2,1)} %param.4) | copy-start | bytes 6291460
  4.8 0.7 copy-start.5
  7.5 26.8 %collective-permute-start.2 = (bf16[8,512,128]{2,1,0:T(8,128)(2,1)S(1)}, bf16[8,512,128]{2,1,0:T(8,128)(2,1)S(1)}, u32[]{:S(2)}, u32[]{:S(2)}) collective-permute-start(bf16[8,512,128]{2,1,0:T(8,128)(2,1)S(1)} %get-tuple-element.45), channel_id=1, source_target_pairs={{0,8},{4,12},{8,16},{12,20},{16,24},{20,28},{1,9},{5,13},{9,17},{1... | collective-permute-start | bytes 3145736 | tf_op jit(solution)/shard_map/ppermute | solution.py:465
  8.8 18.9 %collective-permute-start.1 = (bf16[4,512,128]{2,1,0:T(8,128)(2,1)S(1)}, bf16[4,512,128]{2,1,0:T(8,128)(2,1)S(1)}, u32[]{:S(2)}, u32[]{:S(2)}) collective-permute-start(bf16[4,512,128]{2,1,0:T(8,128)(2,1)S(1)} %get-tuple-element.46), channel_id=1, source_target_pairs={{4,0},{8,4},{12,8},{16,12},{20,16},{24,20},{28,24},{5,1},{9,5},{13... | collective-permute-start | bytes 1572872 | tf_op jit(solution)/shard_map/ppermute | solution.py:468
  14.3 22.1 %collective-permute-start.3 = (bf16[4,512,128]{2,1,0:T(8,128)(2,1)S(1)}, bf16[4,512,128]{2,1,0:T(8,128)(2,1)S(1)}, u32[]{:S(2)}, u32[]{:S(2)}) collective-permute-start(bf16[4,512,128]{2,1,0:T(8,128)(2,1)S(1)} %get-tuple-element.47), channel_id=1, source_target_pairs={{24,0},{28,4},{25,1},{29,5},{26,2},{30,6},{27,3},{31,7}} | collective-permute-start | bytes 1572872 | tf_op jit(solution)/shard_map/ppermute | solution.py:468
  15.7 20.8 %collective-permute-start.4 = (bf16[4,512,128]{2,1,0:T(8,128)(2,1)S(1)}, bf16[4,512,128]{2,1,0:T(8,128)(2,1)S(1)}, u32[]{:S(2)}, u32[]{:S(2)}) collective-permute-start(bf16[4,512,128]{2,1,0:T(8,128)(2,1)S(1)} %get-tuple-element.48), channel_id=1, source_target_pairs={{28,0},{29,1},{30,2},{31,3}} | collective-permute-start | bytes 1572872 | tf_op jit(solution)/shard_map/ppermute | solution.py:468
  16.4 3.1 %collective-permute-start = (s32[8,2,16]{2,1,0:T(2,128)S(1)}, s32[8,2,16]{2,1,0:T(2,128)S(1)}, u32[]{:S(2)}, u32[]{:S(2)}) collective-permute-start(s32[8,2,16]{2,1,0:T(2,128)S(1)} %bitcast.29), channel_id=1, source_target_pairs={{0,1},{1,2},{2,3},{3,0},{4,5},{5,6},{6,7},{7,4},{8,9},{9,10},{10,1... | collective-permute-start | bytes 3080 | tf_op jit(solution)/shard_map/ppermute | solution.py:24
  19.5 0.6 copy-start.7
  20.1 7.7 %copy-start.1 = (bf16[1,512,2048]{2,1,0:T(8,128)(2,1)S(1)}, bf16[1,512,2048]{2,1,0:T(8,128)(2,1)}, u32[]{:S(2)}) copy-start(bf16[1,512,2048]{2,1,0:T(8,128)(2,1)} %param.5) | copy-start | bytes 6291460
  20.1 7.7 %copy-start.3 = (bf16[1,512,2048]{2,1,0:T(8,128)(2,1)S(1)}, bf16[1,512,2048]{2,1,0:T(8,128)(2,1)}, u32[]{:S(2)}) copy-start(bf16[1,512,2048]{2,1,0:T(8,128)(2,1)} %param.6) | copy-start | bytes 6291460
  27.7 8.7 %copy-start.6 = (s32[1,8,16,2]{2,3,1,0:T(2,128)S(1)}, s32[1,8,16,2]{2,3,1,0:T(2,128)}, u32[]{:S(2)}) copy-start(s32[1,8,16,2]{2,3,1,0:T(2,128)} %param.7) | copy-start | bytes 3076
  30.4 40.9 %collective-permute-start.7 = (bf16[4,528,128]{2,1,0:T(8,128)(2,1)S(1)}, bf16[4,528,128]{2,1,0:T(8,128)(2,1)S(1)}, u32[]{:S(2)}, u32[]{:S(2)}) collective-permute-start(bf16[4,528,128]{2,1,0:T(8,128)(2,1)S(1)} %shard_map.49), channel_id=1, source_target_pairs={{0,5},{1,6},{2,7},{3,4},{4,9},{5,10},{6,11},{7,8},{8,13},{9,14},{1... | collective-permute-start | bytes 1622024 | tf_op jit(solution)/shard_map/ppermute | solution.py:476
  40.4 31.7 %collective-permute-start.8 = (bf16[4,528,128]{2,1,0:T(8,128)(2,1)S(1)}, bf16[4,528,128]{2,1,0:T(8,128)(2,1)S(1)}, u32[]{:S(2)}, u32[]{:S(2)}) collective-permute-start(bf16[4,528,128]{2,1,0:T(8,128)(2,1)S(1)} %get-tuple-element.54), channel_id=1, source_target_pairs={{0,25},{1,26},{2,27},{3,24},{4,29},{5,30},{6,31},{7,28}} | collective-permute-start | bytes 1622024 | tf_op jit(solution)/shard_map/ppermute | solution.py:476
  41.7 30.4 %collective-permute-start.9 = (bf16[4,528,128]{2,1,0:T(8,128)(2,1)S(1)}, bf16[4,528,128]{2,1,0:T(8,128)(2,1)S(1)}, u32[]{:S(2)}, u32[]{:S(2)}) collective-permute-start(bf16[4,528,128]{2,1,0:T(8,128)(2,1)S(1)} %get-tuple-element.55), channel_id=1, source_target_pairs={{0,29},{1,30},{2,31},{3,28}} | collective-permute-start | bytes 1622024 | tf_op jit(solution)/shard_map/ppermute | solution.py:476
  42.4 7.6 %collective-permute-start.5 = (bf16[2,512,128]{2,1,0:T(8,128)(2,1)S(1)}, bf16[2,512,128]{2,1,0:T(8,128)(2,1)S(1)}, u32[]{:S(2)}, u32[]{:S(2)}) collective-permute-start(bf16[2,512,128]{2,1,0:T(8,128)(2,1)S(1)} %get-tuple-element.57), channel_id=1, source_target_pairs={{12,0},{16,4},{20,8},{24,12},{28,16},{13,1},{17,5},{21,9},{25,13},... | collective-permute-start | bytes 786440 | tf_op jit(solution)/shard_map/ppermute | solution.py:468
  43.7 11.9 %collective-permute-start.6 = (bf16[2,512,128]{2,1,0:T(8,128)(2,1)S(1)}, bf16[2,512,128]{2,1,0:T(8,128)(2,1)S(1)}, u32[]{:S(2)}, u32[]{:S(2)}) collective-permute-start(bf16[2,512,128]{2,1,0:T(8,128)(2,1)S(1)} %get-tuple-element.59), channel_id=1, source_target_pairs={{20,0},{24,4},{28,8},{21,1},{25,5},{29,9},{22,2},{26,6},{30,10},{2... | collective-permute-start | bytes 786440 | tf_op jit(solution)/shard_map/ppermute | solution.py:468
  58.9 21.7 %collective-permute-start.10 = (bf16[2,512,128]{2,1,0:T(8,128)(2,1)}, bf16[2,512,128]{2,1,0:T(8,128)(2,1)}, u32[]{:S(2)}, u32[]{:S(2)}) collective-permute-start(bf16[2,512,128]{2,1,0:T(8,128)(2,1)} %get-tuple-element.66), channel_id=1, source_target_pairs={{12,0},{16,4},{20,8},{24,12},{28,16},{13,1},{17,5},{21,9},{25,13},... | collective-permute-start | bytes 786440 | tf_op jit(solution)/shard_map/ppermute | solution.py:468
  64.7 15.8 %collective-permute-start.11 = (bf16[2,512,128]{2,1,0:T(8,128)(2,1)}, bf16[2,512,128]{2,1,0:T(8,128)(2,1)}, u32[]{:S(2)}, u32[]{:S(2)}) collective-permute-start(bf16[2,512,128]{2,1,0:T(8,128)(2,1)} %get-tuple-element.68), channel_id=1, source_target_pairs={{20,0},{24,4},{28,8},{21,1},{25,5},{29,9},{22,2},{26,6},{30,10},{2... | collective-permute-start | bytes 786440 | tf_op jit(solution)/shard_map/ppermute | solution.py:468
  71.3 0.8 copy-start.9
  72.1 0.8 copy-start.11
  72.9 24.7 %collective-permute-start.12 = (bf16[2,528,128]{2,1,0:T(8,128)(2,1)}, bf16[2,528,128]{2,1,0:T(8,128)(2,1)}, u32[]{:S(2)}, u32[]{:S(2)}) collective-permute-start(bf16[2,528,128]{2,1,0:T(8,128)(2,1)} %get-tuple-element.72), channel_id=1, source_target_pairs={{0,13},{1,14},{2,15},{3,12},{4,17},{5,18},{6,19},{7,16},{8,21},{9,... | collective-permute-start | bytes 811016 | tf_op jit(solution)/shard_map/ppermute | solution.py:476
  74.2 23.4 %collective-permute-start.13 = (bf16[2,528,128]{2,1,0:T(8,128)(2,1)}, bf16[2,528,128]{2,1,0:T(8,128)(2,1)}, u32[]{:S(2)}, u32[]{:S(2)}) collective-permute-start(bf16[2,528,128]{2,1,0:T(8,128)(2,1)} %get-tuple-element.73), channel_id=1, source_target_pairs={{0,21},{1,22},{2,23},{3,20},{4,25},{5,26},{6,27},{7,24},{8,29},{9,... | collective-permute-start | bytes 811016 | tf_op jit(solution)/shard_map/ppermute | solution.py:476
  79.8 41.4 %collective-permute-start.14 = (bf16[20,528,128]{2,1,0:T(8,128)(2,1)}, bf16[20,528,128]{2,1,0:T(8,128)(2,1)}, u32[]{:S(2)}, u32[]{:S(2)}) collective-permute-start(bf16[20,528,128]{2,1,0:T(8,128)(2,1)} %shard_map.52), channel_id=1, source_target_pairs={{0,1},{1,2},{2,3},{3,0},{4,5},{5,6},{6,7},{7,4},{8,9},{9,10},{10,1... | collective-permute-start | bytes 8110088 | tf_op jit(solution)/shard_map/ppermute | solution.py:24
  80.5 40.7 %collective-permute-start.15 = (bf16[4,512,128]{2,1,0:T(8,128)(2,1)}, bf16[4,512,128]{2,1,0:T(8,128)(2,1)}, u32[]{:S(2)}, u32[]{:S(2)}) collective-permute-start(bf16[4,512,128]{2,1,0:T(8,128)(2,1)} %get-tuple-element.77), channel_id=1, source_target_pairs={{16,0},{20,4},{24,8},{28,12},{17,1},{21,5},{25,9},{29,13},{18,2},{... | collective-permute-start | bytes 1572872 | tf_op jit(solution)/shard_map/ppermute | solution.py:468
  97.6 27.9 %collective-permute-start.17 = (bf16[2,528,128]{2,1,0:T(8,128)(2,1)}, bf16[2,528,128]{2,1,0:T(8,128)(2,1)}, u32[]{:S(2)}, u32[]{:S(2)}) collective-permute-start(bf16[2,528,128]{2,1,0:T(8,128)(2,1)} %get-tuple-element.80), channel_id=1, source_target_pairs={{0,21},{1,22},{2,23},{3,20},{4,25},{5,26},{6,27},{7,24},{8,29},{9,... | collective-permute-start | bytes 811016 | tf_op jit(solution)/shard_map/ppermute | solution.py:476
  98.9 26.7 %collective-permute-start.16 = (bf16[2,528,128]{2,1,0:T(8,128)(2,1)}, bf16[2,528,128]{2,1,0:T(8,128)(2,1)}, u32[]{:S(2)}, u32[]{:S(2)}) collective-permute-start(bf16[2,528,128]{2,1,0:T(8,128)(2,1)} %get-tuple-element.79), channel_id=1, source_target_pairs={{0,13},{1,14},{2,15},{3,12},{4,17},{5,18},{6,19},{7,16},{8,21},{9,... | collective-permute-start | bytes 811016 | tf_op jit(solution)/shard_map/ppermute | solution.py:476
  100.8 26.1 %copy-start.8 = (s32[8,2,16]{2,1,0:T(2,128)S(1)}, s32[8,2,16]{2,1,0:T(2,128)}, u32[]{:S(2)}) copy-start(s32[8,2,16]{2,1,0:T(2,128)} %copy-done.7) | copy-start | bytes 3076
  100.8 26.1 %copy-start.10 = (bf16[4,528,128]{2,1,0:T(8,128)(2,1)S(1)}, bf16[4,528,128]{2,1,0:T(8,128)(2,1)}, u32[]{:S(2)}) copy-start(bf16[4,528,128]{2,1,0:T(8,128)(2,1)} %copy-done.9) | copy-start | bytes 1622020
  100.8 26.1 %copy-start.12 = (bf16[4,528,128]{2,1,0:T(8,128)(2,1)S(1)}, bf16[4,528,128]{2,1,0:T(8,128)(2,1)}, u32[]{:S(2)}) copy-start(bf16[4,528,128]{2,1,0:T(8,128)(2,1)} %copy-done.11) | copy-start | bytes 1622020
  125.6 28.5 %collective-permute-start.18 = (bf16[4,528,128]{2,1,0:T(8,128)(2,1)}, bf16[4,528,128]{2,1,0:T(8,128)(2,1)}, u32[]{:S(2)}, u32[]{:S(2)}) collective-permute-start(bf16[4,528,128]{2,1,0:T(8,128)(2,1)} %shard_map.55), channel_id=1, source_target_pairs={{0,17},{1,18},{2,19},{3,16},{4,21},{5,22},{6,23},{7,20},{8,25},{9,... | collective-permute-start | bytes 1622024 | tf_op jit(solution)/shard_map/ppermute | solution.py:476

commit v5 on v4

--- a/solution.py
+++ b/solution.py
@@ -15,6 +15,7 @@
 LANES = 128
 STAT_ROWS = 16
 VMEM_BYTES = 24 * 1024 * 1024
+ALL_VMEM_BYTES = 62 * 1024 * 1024
 HIGH_COST = 10**12
 
 
@@ -43,14 +44,16 @@
     return (jnp.where(was_found, head_table, -1), pick_order)
 
 
-def call(kernel, name_space, outputs, out_specs, scratch=(), flops=0, moved=0, exps=0):
+def call(
+    kernel, name_space, outputs, out_specs, scratch=(), flops=0, moved=0, exps=0, vmem=VMEM_BYTES
+):
     return pl.pallas_call(
         kernel,
         in_specs=name_space,
         out_specs=out_specs,
         out_shape=outputs,
         scratch_shapes=list(scratch),
-        compiler_params=pltpu.CompilerParams(vmem_limit_bytes=VMEM_BYTES),
+        compiler_params=pltpu.CompilerParams(vmem_limit_bytes=vmem),
         cost_estimate=pl.CostEstimate(flops=flops, bytes_accessed=moved, transcendentals=exps),
     )
 
@@ -127,6 +130,7 @@
         [IN_HBM] * len(sizes),
         [pltpu.SMEM((len(jobs) * slots + 1,), jnp.int32), pltpu.SemaphoreType.DMA((sum(sizes),))],
         moved=4 * rows * HD * sum(sizes),
+        vmem=ALL_VMEM_BYTES,
     )(here, picks, queries, keys, values)
 
 
@@ -216,7 +220,7 @@
             out_ref[slot, rows:, :] = three_parts(lines)
 
 
-def attend(here, picks, keys, values, arrived, group, slots):
+def attend(here, picks, keys, values, arrived, group, slots, is_anchor):
     rows = keys.shape[0]
     total = sum(count for _, _, count in group)
     return call(
@@ -228,7 +232,7 @@
         ],
         [IN_VMEM] * len(group),
         [pltpu.SMEM((slots + 1,), jnp.int32)],
-        flops=4 * total * rows * rows * HD,
+        flops=HIGH_COST if is_anchor else 4 * total * rows * rows * HD,
         moved=8 * total * rows * HD,
         exps=total * rows * rows,
     )(here, picks, keys, values, *arrived)
@@ -484,7 +488,7 @@
     now = after(here, *[sends[job] for job in first_jobs])
     sends |= zip(later_jobs, pack(now, own_picks, queries, keys, values, later_jobs, slots))
 
-    def attend_group(token, group):
+    def attend_group(token, group, is_anchor=False):
         return dict(
             zip(
                 group,
@@ -496,6 +500,7 @@
                     [arrived[piece] for piece in group],
                     tuple(group),
                     slots,
+                    is_anchor,
                 ),
             )
         )
@@ -513,11 +518,12 @@
 
     returned = {}
     own = own_part(after(here, before, sends[later_jobs[0]]), queries, keys, values)
+    ask_for(groups[2][:1], own, *those(arrived, groups[0]))
     parts = attend_group(after(here, own), groups[0])
     send_back(parts)
-    parts = attend_group(after(here, *parts.values(), *near), groups[1])
+    ask_for(groups[2][1:], *parts.values(), *near, *those(arrived, groups[1]))
+    parts = attend_group(after(here, *parts.values(), *near), groups[1], is_anchor=True)
     send_back(parts)
-    ask_for(groups[2], *parts.values(), *arrived.values())
     now = after(here, *parts.values())
     before_last = groups[0] + groups[1]
     for number in range(2, len(groups)):
@@ -525,9 +531,9 @@
         if number == len(groups) - 1:
             now = tick(now, *those(returned, groups[number - 2]))
             now = after(now, own_back)
-        parts = attend_group(now, group)
         if number == 2:
-            ask_for(groups[number + 1], *parts.values(), *those(arrived, group))
+            ask_for(groups[number + 1], now, *those(arrived, group))
+        parts = attend_group(now, group, is_anchor=number == 2)
         send_back(parts, *those(returned, before_last))
         now = after(now, *parts.values())
         if number == 2:

time: 159 us -> 284 us (1.79); the launches traced: 159 us -> 281 us
  Pallas kernels: 45.2 us -> 176 us
  waiting for transfers between devices: 53.9 us -> 41.3 us
  starting transfers between devices: 51.4 us -> 58.6 us
  local copies, waits for them, and re-layouts: 7.71 us -> 4.78 us
    pallas_call x2, Pallas kernels: 4.31 us -> 132 us  [pack(): call(functools.partial(pack_kernel, jobs=jobs, slots=slots), [SCALARS, SC...]
    ppermute x8, waiting for transfers between devices: 7.7 us -> 0.02 us  [down(): lax.ppermute(value, 'ctx', [(at, at - shift) for at in range(shift, width)])]
    ppermute x8, starting transfers between devices: 37.3 us -> 44 us  [down(): lax.ppermute(value, 'ctx', [(at, at - shift) for at in range(shift, width)])]
    ppermute x2, waiting for transfers between devices: 21.2 us -> 17.8 us  [passed_along(): return lax.ppermute(value, axis, pairs)]
    unnamed x26 -> x14, local copies, waits for them, and re-layouts: 7.71 us -> 4.78 us
  transfers between devices with their start and end apart: 19 -> 19, of which waited for: 7 -> 4; matrix products, arithmetic and copies ran while one was open for 0% -> 0% of each run, Pallas kernels for 24% -> 32%
where the time goes in v5:
time: 284 us; the launch traced here: 281 us
  Pallas kernels  176 us (62%)
  starting transfers between devices  58.6 us (21%)
  waiting for transfers between devices  41.3 us (15%)
  local copies, waits for them, and re-layouts  4.78 us (2%)
    pallas_call x2, Pallas kernels, pack(): call(functools.partial(pack_kernel, jobs=jobs, slots=slots), [SCALARS, SC...  132 us
    ppermute x8, starting transfers between devices, down(): lax.ppermute(value, 'ctx', [(at, at - shift) for at in range(shift, width)])  44 us
    ppermute x8, waiting for transfers between devices, up_and_on(): return lax.ppermute(value, ('ctx', 'pipe'), pairs)  23.5 us
    pallas_call x5, Pallas kernels, attend(): call(functools.partial(attend_kernel, group=group, slots=slots), [SCALARS...  20.3 us
    ppermute x2, waiting for transfers between devices, passed_along(): return lax.ppermute(value, axis, pairs)  17.8 us
    ppermute x8, starting transfers between devices, up_and_on(): return lax.ppermute(value, ('ctx', 'pipe'), pairs)  13.3 us
    pallas_call x1, Pallas kernels, own_part(): call(own_kernel, [SCALARS, IN_VMEM, IN_VMEM, IN_VMEM], jax.ShapeDtypeStru...  7.62 us
    pallas_call x1, Pallas kernels, merge(): call(functools.partial(merge_kernel, places=tuple(places), shifts=shifts,...  6.97 us
  transfers between devices with their start and end apart: 19, of which 4 were waited for; matrix products, arithmetic and copies ran while one was open for 0% of the time, Pallas kernels for 32%

profile of v5, /device:TPU:26, one launch (start us, length us, event | category | flops | bytes accessed | tf_op | source)
XLA Modules:
  0.0 280.7 jit_solution(10143591184510072076)
XLA Ops:
  0.0 82.0 %shard_map.46 = (bf16[8,512,128]{2,1,0:T(8,128)(2,1)}, bf16[4,512,128]{2,1,0:T(8,128)(2,1)}, bf16[4,512,128]{2,1,0:T(8,128)(2,1)}, bf16[4,512,128]{2,1,0:T(8,128)(2,1)}) custom-call(s32[1]{0:T(128)} %bitcast.here_ref, s32[8,2,16]{2,1,0:T(2,128)} %bitcast.28, bf16[512,2048]{1,0:T(8,128)(2,1)} %bitcast.24, bf16[512,2048]{1,0:T(8,128)(2,1)} %bitcast.8, ...), custom_call_target="tpu_custom_call" | custom-call | bytes 5242880 | tf_op jit(solution)/shard_map/pallas_call | solution.py:126
  82.0 1.3 collective-permute-start.2
  83.3 5.5 %collective-permute-start.1 = (bf16[4,512,128]{2,1,0:T(8,128)(2,1)}, bf16[4,512,128]{2,1,0:T(8,128)(2,1)S(1)}, u32[]{:S(2)}, u32[]{:S(2)}) collective-permute-start(bf16[4,512,128]{2,1,0:T(8,128)(2,1)} %get-tuple-element.46), channel_id=1, source_target_pairs={{4,0},{8,4},{12,8},{16,12},{20,16},{24,20},{28,24},{5,1},{9,5},{13... | collective-permute-start | bytes 1572872 | tf_op jit(solution)/shard_map/ppermute | solution.py:472
  88.8 2.1 collective-permute-start.3
  90.9 1.5 collective-permute-start.4
  92.4 0.0 collective-permute-start
  92.4 49.9 %shard_map.47 = (bf16[2,512,128]{2,1,0:T(8,128)(2,1)}, bf16[2,512,128]{2,1,0:T(8,128)(2,1)}, bf16[2,512,128]{2,1,0:T(8,128)(2,1)}, bf16[2,512,128]{2,1,0:T(8,128)(2,1)}, bf16[4,512,128]{2,1,0:T(8,128)(2,1)}) custom-call(s32[1]{0:T(128)} %bitcast.here_ref, s32[8,2,16]{2,1,0:T(2,128)} %bitcast.29, bf16[512,2048]{1,0:T(8,128)(2,1)} %bitcast.25, ...), custom_call_target="tpu_custom_call" | custom-call | bytes 3145728 | tf_op jit(solution)/shard_map/pallas_call | solution.py:126
  142.3 0.0 collective-permute-done.picks_ref
  142.4 0.0 copy-start
  142.4 1.6 copy-done
  144.0 1.6 copy-done.2
  145.5 1.6 copy-done.4
  147.1 7.6 %shard_map.48.own_ref = bf16[16,528,128]{2,1,0:T(8,128)(2,1)S(1)} custom-call(s32[1]{0:T(128)} %bitcast.here_ref, bf16[512,2048]{1,0:T(8,128)(2,1)S(1)} %bitcast.26, bf16[512,2048]{1,0:T(8,128)(2,1)S(1)} %bitcast.10, bf16[512,2048]{1,0:T(8,128)(2,1)S(1)} %bitcast.18), custom_call_target="tpu_custom_call" | custom-call | flops 2147483648 | bytes 8388608 | tf_op jit(solution)/shard_map/pallas_call | solution.py:266
  154.8 0.0 collective-permute-done.1.refs_0_
  154.8 2.4 collective-permute-start.5
  157.2 3.3 %shard_map.49 = bf16[4,528,128]{2,1,0:T(8,128)(2,1)} custom-call(s32[1]{0:T(128)} %bitcast.here_ref, s32[8,2,16]{2,1,0:T(2,128)S(1)} %bitcast.31, bf16[512,2048]{1,0:T(8,128)(2,1)S(1)} %bitcast.11, bf16[512,2048]{1,0:T(8,128)(2,1)S(1)} %bitcast.19, bf16[4,512,128]{2,1,0:T(8,128)(2,1)S(1)} %collective-permute-done.1.refs_0_), custom_call_target="tpu_custom_call" | custom-call | flops 536870912 | bytes 2097152 | tf_op jit(solution)/shard_map/pallas_call | solution.py:226
  160.5 3.9 %collective-permute-start.7 = (bf16[4,528,128]{2,1,0:T(8,128)(2,1)}, bf16[4,528,128]{2,1,0:T(8,128)(2,1)}, u32[]{:S(2)}, u32[]{:S(2)}) collective-permute-start(bf16[4,528,128]{2,1,0:T(8,128)(2,1)} %shard_map.49), channel_id=1, source_target_pairs={{0,5},{1,6},{2,7},{3,4},{4,9},{5,10},{6,11},{7,8},{8,13},{9,14},{1... | collective-permute-start | bytes 1622024 | tf_op jit(solution)/shard_map/ppermute | solution.py:480
  164.5 0.0 collective-permute-done.3.refs_0_
  164.5 0.0 collective-permute-done.2.near_ref
  164.5 2.0 collective-permute-start.6
  166.5 5.2 %shard_map.50 = (bf16[4,528,128]{2,1,0:T(8,128)(2,1)}, bf16[4,528,128]{2,1,0:T(8,128)(2,1)}) custom-call(s32[1]{0:T(128)} %bitcast.here_ref, s32[8,2,16]{2,1,0:T(2,128)S(1)} %bitcast.32, bf16[512,2048]{1,0:T(8,128)(2,1)S(1)} %bitcast.12, bf16[512,2048]{1,0:T(8,128)(2,1)S(1)} %bitcast.20, bf16[4,512,128]{2,1,0:T(8,128)(2,1)} %collective-permute-done.3.refs_0_, ...), custom_call_target="tpu_custom_call" | custom-call | flops 999999995904 | bytes 4194304 | tf_op jit(solution)/shard_map/pallas_call | solution.py:226
  171.8 1.3 collective-permute-start.8
  173.1 1.5 collective-permute-start.9
  174.5 0.0 collective-permute-done.5.refs_0_
  174.5 0.0 collective-permute-done.6.refs_1_
  174.5 2.1 collective-permute-start.10
  176.6 8.3 %collective-permute-start.11 = (bf16[2,512,128]{2,1,0:T(8,128)(2,1)}, bf16[2,512,128]{2,1,0:T(8,128)(2,1)}, u32[]{:S(2)}, u32[]{:S(2)}) collective-permute-start(bf16[2,512,128]{2,1,0:T(8,128)(2,1)} %get-tuple-element.68), channel_id=1, source_target_pairs={{20,0},{24,4},{28,8},{21,1},{25,5},{29,9},{22,2},{26,6},{30,10},{2... | collective-permute-start | bytes 786440 | tf_op jit(solution)/shard_map/ppermute | solution.py:472
  184.9 3.6 %shard_map.51 = (bf16[2,528,128]{2,1,0:T(8,128)(2,1)}, bf16[2,528,128]{2,1,0:T(8,128)(2,1)}) custom-call(s32[1]{0:T(128)} %bitcast.here_ref, s32[8,2,16]{2,1,0:T(2,128)S(1)} %bitcast.33, bf16[512,2048]{1,0:T(8,128)(2,1)S(1)} %bitcast.13, bf16[512,2048]{1,0:T(8,128)(2,1)S(1)} %bitcast.21, bf16[2,512,128]{2,1,0:T(8,128)(2,1)} %collective-permute-done.5.refs_0_, ...), custom_call_target="tpu_custom_call" | custom-call | flops 999999995904 | bytes 2097152 | tf_op jit(solution)/shard_map/pallas_call | solution.py:226
  188.6 0.0 collective-permute-done.7.refs_1_
  188.6 2.6 collective-permute-done.8.refs_2_
  191.2 1.3 collective-permute-start.12
  192.5 1.5 collective-permute-start.13
  194.0 4.1 %shard_map.52 = bf16[20,528,128]{2,1,0:T(8,128)(2,1)} custom-call(s32[1]{0:T(128)} %bitcast.here_ref, s32[8,2,16]{2,1,0:T(2,128)S(1)} %bitcast.34, bf16[512,2048]{1,0:T(8,128)(2,1)S(1)} %bitcast.27, bf16[16,528,128]{2,1,0:T(8,128)(2,1)S(1)} %shard_map.48.own_ref, bf16[8,512,128]{2,1,0:T(8,128)(2,1)S(1)} %collective-permute-done.2.near_ref), custom_call_target="tpu_custom_call" | custom-call | flops 999999995904 | bytes 3145728 | tf_op jit(solution)/shard_map/pallas_call | solution.py:294
  198.1 0.0 collective-permute-start.14
  198.1 20.0 %collective-permute-start.15 = (bf16[4,512,128]{2,1,0:T(8,128)(2,1)}, bf16[4,512,128]{2,1,0:T(8,128)(2,1)}, u32[]{:S(2)}, u32[]{:S(2)}) collective-permute-start(bf16[4,512,128]{2,1,0:T(8,128)(2,1)} %get-tuple-element.77), channel_id=1, source_target_pairs={{16,0},{20,4},{24,8},{28,12},{17,1},{21,5},{25,9},{29,13},{18,2},{... | collective-permute-start | bytes 1572872 | tf_op jit(solution)/shard_map/ppermute | solution.py:472
  218.1 3.6 %shard_map.53 = (bf16[2,528,128]{2,1,0:T(8,128)(2,1)}, bf16[2,528,128]{2,1,0:T(8,128)(2,1)}) custom-call(s32[1]{0:T(128)} %bitcast.here_ref, s32[8,2,16]{2,1,0:T(2,128)S(1)} %bitcast.35, bf16[512,2048]{1,0:T(8,128)(2,1)S(1)} %bitcast.14, bf16[512,2048]{1,0:T(8,128)(2,1)S(1)} %bitcast.22, bf16[2,512,128]{2,1,0:T(8,128)(2,1)} %collective-permute-done.10.refs_0_, ...), custom_call_target="tpu_custom_call" | custom-call | flops 536870912 | bytes 2097152 | tf_op jit(solution)/shard_map/pallas_call | solution.py:226
  221.8 1.3 collective-permute-start.17
  223.1 1.3 collective-permute-start.16
  224.4 0.5 shard_map.54.here_ref
  224.9 17.8 %collective-permute-done.14.refs_0_ = bf16[20,528,128]{2,1,0:T(8,128)(2,1)} collective-permute-done((bf16[20,528,128]{2,1,0:T(8,128)(2,1)}, bf16[20,528,128]{2,1,0:T(8,128)(2,1)}, u32[]{:S(2)}, u32[]{:S(2)}) %collective-permute-start.14) | collective-permute-done | bytes 2703392 | tf_op jit(solution)/shard_map/ppermute | solution.py:25
  242.7 0.0 collective-permute-done.15.refs_0_
  242.7 4.4 %shard_map.55 = bf16[4,528,128]{2,1,0:T(8,128)(2,1)} custom-call(s32[1]{0:T(128)} %shard_map.54.here_ref, s32[8,2,16]{2,1,0:T(2,128)S(1)} %bitcast.36, bf16[512,2048]{1,0:T(8,128)(2,1)S(1)} %bitcast.15, bf16[512,2048]{1,0:T(8,128)(2,1)S(1)} %bitcast.23, bf16[4,512,128]{2,1,0:T(8,128)(2,1)} %collective-permute-done.15.refs_0_), custom_call_target="tpu_custom_call" | custom-call | flops 536870912 | bytes 2097152 | tf_op jit(solution)/shard_map/pallas_call | solution.py:226
  247.1 0.0 collective-permute-done.17.refs_7_
  247.1 0.3 collective-permute-done.16.refs_6_
  247.5 1.3 collective-permute-start.18
  248.8 7.0 %shard_map.56 = (f32[16,512,128]{2,1,0:T(8,128)S(1)}, f32[16,4,128]{2,1,0:T(4,128)S(1)}) custom-call(s32[1]{0:T(128)} %shard_map.54.here_ref, s32[8,2,16]{2,1,0:T(2,128)S(1)} %collective-permute-done.picks_ref, bf16[20,528,128]{2,1,0:T(8,128)(2,1)} %collective-permute-done.14.refs_0_, bf16[4,528,128]{2,1,0:T(8,128)(2,1)} %collective-permute-done.7.refs_1_, ...), custom_call_target="tpu_custom_call" | custom-call | flops 999999995904 | bytes 9437184 | tf_op jit(solution)/shard_map/pallas_call | solution.py:365
  255.7 20.6 %collective-permute-done.18.part_ref = bf16[4,528,128]{2,1,0:T(8,128)(2,1)} collective-permute-done((bf16[4,528,128]{2,1,0:T(8,128)(2,1)}, bf16[4,528,128]{2,1,0:T(8,128)(2,1)}, u32[]{:S(2)}, u32[]{:S(2)}) %collective-permute-start.18) | collective-permute-done | bytes 540704 | tf_op jit(solution)/shard_map/ppermute | solution.py:480
  276.3 4.4 %shard_map.57 = bf16[512,2048]{1,0:T(8,128)(2,1)} custom-call(s32[1]{0:T(128)} %shard_map.54.here_ref, s32[8,2,16]{2,1,0:T(2,128)S(1)} %collective-permute-done.picks_ref, f32[16,512,128]{2,1,0:T(8,128)S(1)} %get-tuple-element.82.mixed_ref, f32[16,4,128]{2,1,0:T(4,128)S(1)} %get-tuple-element.83.sums_ref, bf16[4,528,128]{2,1,0:T(8,128)(2,1)} %collective-permute-done.18.part_ref), custom_call_target="tpu_custom_call" | custom-call | flops 2097152 | bytes 8388608 | tf_op jit(solution)/shard_map/pallas_call | solution.py:422
  (16 shorter events, 0.0 us)
Async XLA Ops:
  0.0 92.4 %copy-start.5 = (s32[1,8,16,2]{2,3,1,0:T(2,128)S(1)}, s32[1,8,16,2]{2,3,1,0:T(2,128)}, u32[]{:S(2)}) copy-start(s32[1,8,16,2]{2,3,1,0:T(2,128)} %param.7) | copy-start | bytes 3076
  82.0 82.5 %collective-permute-start.2 = (bf16[8,512,128]{2,1,0:T(8,128)(2,1)}, bf16[8,512,128]{2,1,0:T(8,128)(2,1)S(1)}, u32[]{:S(2)}, u32[]{:S(2)}) collective-permute-start(bf16[8,512,128]{2,1,0:T(8,128)(2,1)} %get-tuple-element.45), channel_id=1, source_target_pairs={{0,8},{4,12},{8,16},{12,20},{16,24},{20,28},{1,9},{5,13},{9,17},{1... | collective-permute-start | bytes 3145736 | tf_op jit(solution)/shard_map/ppermute | solution.py:469
  83.3 71.5 %collective-permute-start.1 = (bf16[4,512,128]{2,1,0:T(8,128)(2,1)}, bf16[4,512,128]{2,1,0:T(8,128)(2,1)S(1)}, u32[]{:S(2)}, u32[]{:S(2)}) collective-permute-start(bf16[4,512,128]{2,1,0:T(8,128)(2,1)} %get-tuple-element.46), channel_id=1, source_target_pairs={{4,0},{8,4},{12,8},{16,12},{20,16},{24,20},{28,24},{5,1},{9,5},{13... | collective-permute-start | bytes 1572872 | tf_op jit(solution)/shard_map/ppermute | solution.py:472
  88.8 75.7 %collective-permute-start.3 = (bf16[4,512,128]{2,1,0:T(8,128)(2,1)}, bf16[4,512,128]{2,1,0:T(8,128)(2,1)}, u32[]{:S(2)}, u32[]{:S(2)}) collective-permute-start(bf16[4,512,128]{2,1,0:T(8,128)(2,1)} %get-tuple-element.47), channel_id=1, source_target_pairs={{24,0},{28,4},{25,1},{29,5},{26,2},{30,6},{27,3},{31,7}} | collective-permute-start | bytes 1572872 | tf_op jit(solution)/shard_map/ppermute | solution.py:472
  90.9 73.5 %collective-permute-start.4 = (bf16[4,512,128]{2,1,0:T(8,128)(2,1)}, bf16[4,512,128]{2,1,0:T(8,128)(2,1)}, u32[]{:S(2)}, u32[]{:S(2)}) collective-permute-start(bf16[4,512,128]{2,1,0:T(8,128)(2,1)} %get-tuple-element.48), channel_id=1, source_target_pairs={{28,0},{29,1},{30,2},{31,3}} | collective-permute-start | bytes 1572872 | tf_op jit(solution)/shard_map/ppermute | solution.py:472
  92.4 50.0 %collective-permute-start = (s32[8,2,16]{2,1,0:T(2,128)S(1)}, s32[8,2,16]{2,1,0:T(2,128)S(1)}, u32[]{:S(2)}, u32[]{:S(2)}) collective-permute-start(s32[8,2,16]{2,1,0:T(2,128)S(1)} %bitcast.30), channel_id=1, source_target_pairs={{0,1},{1,2},{2,3},{3,0},{4,5},{5,6},{6,7},{7,4},{8,9},{9,10},{10,1... | collective-permute-start | bytes 3080 | tf_op jit(solution)/shard_map/ppermute | solution.py:25
  142.4 1.6 copy-start
  143.9 1.6 copy-start.2
  145.5 1.6 copy-start.4
  147.1 10.0 %copy-start.1 = (bf16[1,512,2048]{2,1,0:T(8,128)(2,1)S(1)}, bf16[1,512,2048]{2,1,0:T(8,128)(2,1)}, u32[]{:S(2)}) copy-start(bf16[1,512,2048]{2,1,0:T(8,128)(2,1)} %param.5) | copy-start | bytes 6291460
  147.1 10.0 %copy-start.3 = (bf16[1,512,2048]{2,1,0:T(8,128)(2,1)S(1)}, bf16[1,512,2048]{2,1,0:T(8,128)(2,1)}, u32[]{:S(2)}) copy-start(bf16[1,512,2048]{2,1,0:T(8,128)(2,1)} %param.6) | copy-start | bytes 6291460
  147.1 10.1 %copy-start.6 = (s32[1,8,16,2]{2,3,1,0:T(2,128)S(1)}, s32[1,8,16,2]{2,3,1,0:T(2,128)}, u32[]{:S(2)}) copy-start(s32[1,8,16,2]{2,3,1,0:T(2,128)} %param.7) | copy-start | bytes 3076
  154.8 19.8 %collective-permute-start.5 = (bf16[2,512,128]{2,1,0:T(8,128)(2,1)}, bf16[2,512,128]{2,1,0:T(8,128)(2,1)}, u32[]{:S(2)}, u32[]{:S(2)}) collective-permute-start(bf16[2,512,128]{2,1,0:T(8,128)(2,1)} %get-tuple-element.57), channel_id=1, source_target_pairs={{12,0},{16,4},{20,8},{24,12},{28,16},{13,1},{17,5},{21,9},{25,13},... | collective-permute-start | bytes 786440 | tf_op jit(solution)/shard_map/ppermute | solution.py:472
  160.5 28.0 %collective-permute-start.7 = (bf16[4,528,128]{2,1,0:T(8,128)(2,1)}, bf16[4,528,128]{2,1,0:T(8,128)(2,1)}, u32[]{:S(2)}, u32[]{:S(2)}) collective-permute-start(bf16[4,528,128]{2,1,0:T(8,128)(2,1)} %shard_map.49), channel_id=1, source_target_pairs={{0,5},{1,6},{2,7},{3,4},{4,9},{5,10},{6,11},{7,8},{8,13},{9,14},{1... | collective-permute-start | bytes 1622024 | tf_op jit(solution)/shard_map/ppermute | solution.py:480
  164.5 10.0 %collective-permute-start.6 = (bf16[2,512,128]{2,1,0:T(8,128)(2,1)}, bf16[2,512,128]{2,1,0:T(8,128)(2,1)}, u32[]{:S(2)}, u32[]{:S(2)}) collective-permute-start(bf16[2,512,128]{2,1,0:T(8,128)(2,1)} %get-tuple-element.59), channel_id=1, source_target_pairs={{20,0},{24,4},{28,8},{21,1},{25,5},{29,9},{22,2},{26,6},{30,10},{2... | collective-permute-start | bytes 786440 | tf_op jit(solution)/shard_map/ppermute | solution.py:472
  171.8 19.4 %collective-permute-start.8 = (bf16[4,528,128]{2,1,0:T(8,128)(2,1)}, bf16[4,528,128]{2,1,0:T(8,128)(2,1)}, u32[]{:S(2)}, u32[]{:S(2)}) collective-permute-start(bf16[4,528,128]{2,1,0:T(8,128)(2,1)} %get-tuple-element.54), channel_id=1, source_target_pairs={{0,25},{1,26},{2,27},{3,24},{4,29},{5,30},{6,31},{7,28}} | collective-permute-start | bytes 1622024 | tf_op jit(solution)/shard_map/ppermute | solution.py:480
  173.1 18.1 %collective-permute-start.9 = (bf16[4,528,128]{2,1,0:T(8,128)(2,1)}, bf16[4,528,128]{2,1,0:T(8,128)(2,1)}, u32[]{:S(2)}, u32[]{:S(2)}) collective-permute-start(bf16[4,528,128]{2,1,0:T(8,128)(2,1)} %get-tuple-element.55), channel_id=1, source_target_pairs={{0,29},{1,30},{2,31},{3,28}} | collective-permute-start | bytes 1622024 | tf_op jit(solution)/shard_map/ppermute | solution.py:480
  174.5 23.6 %collective-permute-start.10 = (bf16[2,512,128]{2,1,0:T(8,128)(2,1)}, bf16[2,512,128]{2,1,0:T(8,128)(2,1)}, u32[]{:S(2)}, u32[]{:S(2)}) collective-permute-start(bf16[2,512,128]{2,1,0:T(8,128)(2,1)} %get-tuple-element.66), channel_id=1, source_target_pairs={{12,0},{16,4},{20,8},{24,12},{28,16},{13,1},{17,5},{21,9},{25,13},... | collective-permute-start | bytes 786440 | tf_op jit(solution)/shard_map/ppermute | solution.py:472
  176.6 21.5 %collective-permute-start.11 = (bf16[2,512,128]{2,1,0:T(8,128)(2,1)}, bf16[2,512,128]{2,1,0:T(8,128)(2,1)}, u32[]{:S(2)}, u32[]{:S(2)}) collective-permute-start(bf16[2,512,128]{2,1,0:T(8,128)(2,1)} %get-tuple-element.68), channel_id=1, source_target_pairs={{20,0},{24,4},{28,8},{21,1},{25,5},{29,9},{22,2},{26,6},{30,10},{2... | collective-permute-start | bytes 786440 | tf_op jit(solution)/shard_map/ppermute | solution.py:472
  191.2 30.6 %collective-permute-start.12 = (bf16[2,528,128]{2,1,0:T(8,128)(2,1)}, bf16[2,528,128]{2,1,0:T(8,128)(2,1)}, u32[]{:S(2)}, u32[]{:S(2)}) collective-permute-start(bf16[2,528,128]{2,1,0:T(8,128)(2,1)} %get-tuple-element.72), channel_id=1, source_target_pairs={{0,13},{1,14},{2,15},{3,12},{4,17},{5,18},{6,19},{7,16},{8,21},{9,... | collective-permute-start | bytes 811016 | tf_op jit(solution)/shard_map/ppermute | solution.py:480
  192.5 29.3 %collective-permute-start.13 = (bf16[2,528,128]{2,1,0:T(8,128)(2,1)}, bf16[2,528,128]{2,1,0:T(8,128)(2,1)}, u32[]{:S(2)}, u32[]{:S(2)}) collective-permute-start(bf16[2,528,128]{2,1,0:T(8,128)(2,1)} %get-tuple-element.73), channel_id=1, source_target_pairs={{0,21},{1,22},{2,23},{3,20},{4,25},{5,26},{6,27},{7,24},{8,29},{9,... | collective-permute-start | bytes 811016 | tf_op jit(solution)/shard_map/ppermute | solution.py:480
  198.1 44.6 %collective-permute-start.14 = (bf16[20,528,128]{2,1,0:T(8,128)(2,1)}, bf16[20,528,128]{2,1,0:T(8,128)(2,1)}, u32[]{:S(2)}, u32[]{:S(2)}) collective-permute-start(bf16[20,528,128]{2,1,0:T(8,128)(2,1)} %shard_map.52), channel_id=1, source_target_pairs={{0,1},{1,2},{2,3},{3,0},{4,5},{5,6},{6,7},{7,4},{8,9},{9,10},{10,1... | collective-permute-start | bytes 8110088 | tf_op jit(solution)/shard_map/ppermute | solution.py:25
  198.1 44.6 %collective-permute-start.15 = (bf16[4,512,128]{2,1,0:T(8,128)(2,1)}, bf16[4,512,128]{2,1,0:T(8,128)(2,1)}, u32[]{:S(2)}, u32[]{:S(2)}) collective-permute-start(bf16[4,512,128]{2,1,0:T(8,128)(2,1)} %get-tuple-element.77), channel_id=1, source_target_pairs={{16,0},{20,4},{24,8},{28,12},{17,1},{21,5},{25,9},{29,13},{18,2},{... | collective-permute-start | bytes 1572872 | tf_op jit(solution)/shard_map/ppermute | solution.py:472
  221.8 25.3 %collective-permute-start.17 = (bf16[2,528,128]{2,1,0:T(8,128)(2,1)}, bf16[2,528,128]{2,1,0:T(8,128)(2,1)}, u32[]{:S(2)}, u32[]{:S(2)}) collective-permute-start(bf16[2,528,128]{2,1,0:T(8,128)(2,1)} %get-tuple-element.80), channel_id=1, source_target_pairs={{0,21},{1,22},{2,23},{3,20},{4,25},{5,26},{6,27},{7,24},{8,29},{9,... | collective-permute-start | bytes 811016 | tf_op jit(solution)/shard_map/ppermute | solution.py:480
  223.1 24.4 %collective-permute-start.16 = (bf16[2,528,128]{2,1,0:T(8,128)(2,1)}, bf16[2,528,128]{2,1,0:T(8,128)(2,1)}, u32[]{:S(2)}, u32[]{:S(2)}) collective-permute-start(bf16[2,528,128]{2,1,0:T(8,128)(2,1)} %get-tuple-element.79), channel_id=1, source_target_pairs={{0,13},{1,14},{2,15},{3,12},{4,17},{5,18},{6,19},{7,16},{8,21},{9,... | collective-permute-start | bytes 811016 | tf_op jit(solution)/shard_map/ppermute | solution.py:480
  247.5 28.8 %collective-permute-start.18 = (bf16[4,528,128]{2,1,0:T(8,128)(2,1)}, bf16[4,528,128]{2,1,0:T(8,128)(2,1)}, u32[]{:S(2)}, u32[]{:S(2)}) collective-permute-start(bf16[4,528,128]{2,1,0:T(8,128)(2,1)} %shard_map.55), channel_id=1, source_target_pairs={{0,17},{1,18},{2,19},{3,16},{4,21},{5,22},{6,23},{7,20},{8,25},{9,... | collective-permute-start | bytes 1622024 | tf_op jit(solution)/shard_map/ppermute | solution.py:480

commit v6 on v5

--- a/solution.py
+++ b/solution.py
@@ -120,17 +120,17 @@
         copy.wait()
 
 
-def pack(here, picks, queries, keys, values, jobs, slots):
+def pack(here, picks, queries, keys, values, jobs, slots, vmem=VMEM_BYTES):
     rows = queries.shape[0]
     sizes = [2 * count if is_near else count for _, _, count, is_near in jobs]
     return call(
         functools.partial(pack_kernel, jobs=jobs, slots=slots),
         [SCALARS, SCALARS, IN_HBM, IN_HBM, IN_HBM],
         [jax.ShapeDtypeStruct((size, rows, HD), jnp.bfloat16) for size in sizes],
-        [IN_HBM] * len(sizes),
+        [IN_VMEM] * len(sizes),
         [pltpu.SMEM((len(jobs) * slots + 1,), jnp.int32), pltpu.SemaphoreType.DMA((sum(sizes),))],
         moved=4 * rows * HD * sum(sizes),
-        vmem=ALL_VMEM_BYTES,
+        vmem=vmem,
     )(here, picks, queries, keys, values)
 
 
@@ -274,33 +274,31 @@
     )(here, queries, keys, values)
 
 
-def near_kernel(here_ref, picks_ref, query_ref, own_ref, near_ref, out_ref, heads_ref, *, shift, slots):
+def near_kernel(here_ref, picks_ref, query_ref, near_ref, out_ref, heads_ref, *, shift, slots):
     rows = query_ref.shape[0]
     here = here_ref[0]
     list_heads(heads_ref, 0, picks_ref, here, here - shift, slots)
-    for head in range(HEADS):
-        out_ref[head] = own_ref[head]
     for slot in range(slots):
         columns = head_columns(jnp.maximum(heads_ref[slot], 0))
         outputs, lines = attend_rows(
             query_ref[:, columns], near_ref[2 * slot], with_ones(near_ref[2 * slot + 1]), rows
         )
-        out_ref[HEADS + slot, :rows, :] = outputs.astype(jnp.bfloat16)
-        out_ref[HEADS + slot, rows:, :] = three_parts(lines)
-
-
-def add_near(here, picks, queries, own, near, shift, slots):
+        out_ref[slot, :rows, :] = outputs.astype(jnp.bfloat16)
+        out_ref[slot, rows:, :] = three_parts(lines)
+
+
+def near_part(here, picks, queries, near, shift, slots):
     rows = queries.shape[0]
     return call(
         functools.partial(near_kernel, shift=shift, slots=slots),
-        [SCALARS, SCALARS, IN_VMEM, IN_VMEM, IN_VMEM],
-        jax.ShapeDtypeStruct((HEADS + slots,) + own.shape[1:], own.dtype),
+        [SCALARS, SCALARS, IN_VMEM, IN_VMEM],
+        jax.ShapeDtypeStruct((slots, rows + STAT_ROWS, HD), jnp.bfloat16),
         IN_VMEM,
         [pltpu.SMEM((slots + 1,), jnp.int32)],
         flops=HIGH_COST,
         moved=12 * slots * rows * HD,
         exps=slots * rows * rows,
-    )(here, picks, queries, own, near)
+    )(here, picks, queries, near)
 
 
 def find_spots(spots_ref, found_ref, picks_ref, here, shifts, slots):
@@ -479,7 +477,10 @@
         ]
         return lax.ppermute(value, ("ctx", "pipe"), pairs)
 
-    sends = dict(zip(first_jobs, pack(here, own_picks, queries, keys, values, first_jobs, slots)))
+    packed = pack(
+        here, own_picks, queries, keys, values, first_jobs, slots, vmem=ALL_VMEM_BYTES
+    )
+    sends = dict(zip(first_jobs, packed))
     near = [up(sends[job], job[0]) for job in first_jobs if job[3]]
     arrived = {
         piece: down(sends[piece + (False,)], piece[0]) for group in groups[:2] for piece in group
@@ -518,6 +519,7 @@
 
     returned = {}
     own = own_part(after(here, before, sends[later_jobs[0]]), queries, keys, values)
+    own_back = passed_along(own, "pipe", 1)
     ask_for(groups[2][:1], own, *those(arrived, groups[0]))
     parts = attend_group(after(here, own), groups[0])
     send_back(parts)
@@ -530,17 +532,18 @@
         group = groups[number]
         if number == len(groups) - 1:
             now = tick(now, *those(returned, groups[number - 2]))
-            now = after(now, own_back)
+            now = after(now, near_back)
         if number == 2:
             ask_for(groups[number + 1], now, *those(arrived, group))
+            now = after(now, own_back)
         parts = attend_group(now, group, is_anchor=number == 2)
         send_back(parts, *those(returned, before_last))
         now = after(now, *parts.values())
         if number == 2:
             now = after(now, *those(returned, before_last))
-            own = add_near(now, own_picks, queries, own, near[0], near_shifts[0], slots)
-            own_back = passed_along(own, "pipe", 1)
-            now = after(now, own)
+            beside = near_part(now, own_picks, queries, near[0], near_shifts[0], slots)
+            near_back = passed_along(beside, "pipe", 1)
+            now = after(now, beside)
         if 2 <= number < len(groups) - 2:
             ask_for(groups[number + 2], now, *those(arrived, groups[number + 1]))
         before_last = group
@@ -551,8 +554,8 @@
     merged_shifts = near_shifts + tuple(others)
     pieces = [piece for piece in returned if piece != final]
     places = [HEADS + merged_shifts.index(shift) * slots + first for shift, first, _ in pieces]
-    parts = [own_back] + [returned[piece] for piece in pieces]
-    mixed, sums = merge(now, before, parts, [0] + places, merged_shifts, slots)
+    parts = [own_back, near_back] + [returned[piece] for piece in pieces]
+    mixed, sums = merge(now, before, parts, [0, HEADS] + places, merged_shifts, slots)
     return finish(now, before, mixed, sums, returned[final], final[0], slots)[None]
 
 

time: 284 us -> 155 us (0.55)
  Pallas kernels: 176 us -> 51.7 us
  starting transfers between devices: 58.6 us -> 54 us
    pallas_call x2, Pallas kernels: 132 us -> 7.8 us  [pack(): call(functools.partial(pack_kernel, jobs=jobs, slots=slots), [SCALARS, SC...]
    ppermute x8, starting transfers between devices: 44 us -> 28 us  [down(): lax.ppermute(value, 'ctx', [(at, at - shift) for at in range(shift, width)])]
    ppermute x2 -> x3, starting transfers between devices: 0.01 us -> 12 us  [passed_along(): return lax.ppermute(value, axis, pairs)]
    ppermute x2 -> x3, waiting for transfers between devices: 17.8 us -> 6.69 us  [passed_along(): return lax.ppermute(value, axis, pairs)]
    ppermute x8, waiting for transfers between devices: 23.5 us -> 31.5 us  [up_and_on(): return lax.ppermute(value, ('ctx', 'pipe'), pairs)]
    ppermute x8, waiting for transfers between devices: 0.02 us -> 4.12 us  [down(): lax.ppermute(value, 'ctx', [(at, at - shift) for at in range(shift, width)])]
  transfers between devices with their start and end apart: 19 -> 20, of which waited for: 4 -> 6; matrix products, arithmetic and copies ran while one was open for 0% -> 0% of each run, Pallas kernels for 32% -> 27%
where the time goes in v6:
time: 155 us; the launch traced here: 154 us
  starting transfers between devices  54 us (35%)
  Pallas kernels  51.7 us (33%)
  waiting for transfers between devices  42.3 us (27%)
  local copies, waits for them, and re-layouts  5.37 us (3%)
    ppermute x8, waiting for transfers between devices, up_and_on(): return lax.ppermute(value, ('ctx', 'pipe'), pairs)  31.5 us
    ppermute x8, starting transfers between devices, down(): lax.ppermute(value, 'ctx', [(at, at - shift) for at in range(shift, width)])  28 us
    pallas_call x5, Pallas kernels, attend(): call(functools.partial(attend_kernel, group=group, slots=slots), [SCALARS...  19.7 us
    ppermute x8, starting transfers between devices, up_and_on(): return lax.ppermute(value, ('ctx', 'pipe'), pairs)  12.7 us
    ppermute x3, starting transfers between devices, passed_along(): return lax.ppermute(value, axis, pairs)  12 us
    pallas_call x1, Pallas kernels, own_part(): call(own_kernel, [SCALARS, IN_VMEM, IN_VMEM, IN_VMEM], jax.ShapeDtypeStru...  8.95 us
    pallas_call x2, Pallas kernels, pack(): call(functools.partial(pack_kernel, jobs=jobs, slots=slots), [SCALARS, SC...  7.8 us
    pallas_call x1, Pallas kernels, merge(): call(functools.partial(merge_kernel, places=tuple(places), shifts=shifts,...  6.91 us
  transfers between devices with their start and end apart: 20, of which 6 were waited for; matrix products, arithmetic and copies ran while one was open for 0% of the time, Pallas kernels for 27%

profile of v6, /device:TPU:26, one launch (start us, length us, event | category | flops | bytes accessed | tf_op | source)
XLA Modules:
  0.0 153.6 jit_solution(145574279941903365)
XLA Ops:
  0.0 5.0 %shard_map.46 = (bf16[8,512,128]{2,1,0:T(8,128)(2,1)}, bf16[4,512,128]{2,1,0:T(8,128)(2,1)}, bf16[4,512,128]{2,1,0:T(8,128)(2,1)}, bf16[4,512,128]{2,1,0:T(8,128)(2,1)}) custom-call(s32[1]{0:T(128)} %bitcast.here_ref, s32[8,2,16]{2,1,0:T(2,128)} %bitcast.28, bf16[512,2048]{1,0:T(8,128)(2,1)} %bitcast.24, bf16[512,2048]{1,0:T(8,128)(2,1)} %bitcast.8, ...), custom_call_target="tpu_custom_call" | custom-call | bytes 5242880 | tf_op jit(solution)/shard_map/pallas_call | solution.py:126
  5.0 1.3 collective-permute-start.2
  6.3 5.3 %collective-permute-start.1 = (bf16[4,512,128]{2,1,0:T(8,128)(2,1)}, bf16[4,512,128]{2,1,0:T(8,128)(2,1)S(1)}, u32[]{:S(2)}, u32[]{:S(2)}) collective-permute-start(bf16[4,512,128]{2,1,0:T(8,128)(2,1)} %get-tuple-element.47), channel_id=1, source_target_pairs={{4,0},{8,4},{12,8},{16,12},{20,16},{24,20},{28,24},{5,1},{9,5},{13... | collective-permute-start | bytes 1572872 | tf_op jit(solution)/shard_map/ppermute | solution.py:470
  11.6 1.3 collective-permute-start.3
  13.0 0.7 collective-permute-start.4
  13.7 0.1 collective-permute-start
  13.7 0.0 copy-start
  13.8 1.6 %copy-done = bf16[1,512,2048]{2,1,0:T(8,128)(2,1)S(1)} copy-done((bf16[1,512,2048]{2,1,0:T(8,128)(2,1)S(1)}, bf16[1,512,2048]{2,1,0:T(8,128)(2,1)}, u32[]{:S(2)}) %copy-start) | copy-done | bytes 2097176
  15.3 1.6 %copy-done.2 = bf16[1,512,2048]{2,1,0:T(8,128)(2,1)S(1)} copy-done((bf16[1,512,2048]{2,1,0:T(8,128)(2,1)S(1)}, bf16[1,512,2048]{2,1,0:T(8,128)(2,1)}, u32[]{:S(2)}) %copy-start.2) | copy-done | bytes 2097176
  16.9 1.6 %copy-done.4 = bf16[1,512,2048]{2,1,0:T(8,128)(2,1)S(1)} copy-done((bf16[1,512,2048]{2,1,0:T(8,128)(2,1)S(1)}, bf16[1,512,2048]{2,1,0:T(8,128)(2,1)}, u32[]{:S(2)}) %copy-start.4) | copy-done | bytes 2097176
  18.5 2.8 %shard_map.47 = (bf16[2,512,128]{2,1,0:T(8,128)(2,1)}, bf16[2,512,128]{2,1,0:T(8,128)(2,1)}, bf16[2,512,128]{2,1,0:T(8,128)(2,1)}, bf16[2,512,128]{2,1,0:T(8,128)(2,1)}, bf16[4,512,128]{2,1,0:T(8,128)(2,1)}) custom-call(s32[1]{0:T(128)} %bitcast.here_ref, s32[8,2,16]{2,1,0:T(2,128)S(1)} %bitcast.30, bf16[512,2048]{1,0:T(8,128)(2,1)S(1)} %bitcast.25, ...), custom_call_target="tpu_custom_call" | custom-call | bytes 3145728 | tf_op jit(solution)/shard_map/pallas_call | solution.py:126
  21.3 0.0 collective-permute-done.picks_ref
  21.3 0.6 copy-done.6
  21.9 9.0 %shard_map.48 = bf16[16,528,128]{2,1,0:T(8,128)(2,1)} custom-call(s32[1]{0:T(128)} %bitcast.here_ref, bf16[512,2048]{1,0:T(8,128)(2,1)S(1)} %bitcast.26, bf16[512,2048]{1,0:T(8,128)(2,1)S(1)} %bitcast.10, bf16[512,2048]{1,0:T(8,128)(2,1)S(1)} %bitcast.18), custom_call_target="tpu_custom_call" | custom-call | flops 2147483648 | bytes 8388608 | tf_op jit(solution)/shard_map/pallas_call | solution.py:266
  30.9 0.6 collective-permute-start.5
  31.5 0.0 collective-permute-done.1.refs_0_
  31.5 2.6 %collective-permute-start.6 = (bf16[2,512,128]{2,1,0:T(8,128)(2,1)}, bf16[2,512,128]{2,1,0:T(8,128)(2,1)}, u32[]{:S(2)}, u32[]{:S(2)}) collective-permute-start(bf16[2,512,128]{2,1,0:T(8,128)(2,1)} %get-tuple-element.59), channel_id=1, source_target_pairs={{12,0},{16,4},{20,8},{24,12},{28,16},{13,1},{17,5},{21,9},{25,13},... | collective-permute-start | bytes 786440 | tf_op jit(solution)/shard_map/ppermute | solution.py:470
  34.1 3.4 %shard_map.49 = bf16[4,528,128]{2,1,0:T(8,128)(2,1)} custom-call(s32[1]{0:T(128)} %bitcast.here_ref, s32[8,2,16]{2,1,0:T(2,128)S(1)} %bitcast.31, bf16[512,2048]{1,0:T(8,128)(2,1)S(1)} %bitcast.11, bf16[512,2048]{1,0:T(8,128)(2,1)S(1)} %bitcast.19, bf16[4,512,128]{2,1,0:T(8,128)(2,1)S(1)} %collective-permute-done.1.refs_0_), custom_call_target="tpu_custom_call" | custom-call | flops 536870912 | bytes 2097152 | tf_op jit(solution)/shard_map/pallas_call | solution.py:226
  37.5 3.3 %collective-permute-start.8 = (bf16[4,528,128]{2,1,0:T(8,128)(2,1)}, bf16[4,528,128]{2,1,0:T(8,128)(2,1)}, u32[]{:S(2)}, u32[]{:S(2)}) collective-permute-start(bf16[4,528,128]{2,1,0:T(8,128)(2,1)} %shard_map.49), channel_id=1, source_target_pairs={{0,5},{1,6},{2,7},{3,4},{4,9},{5,10},{6,11},{7,8},{8,13},{9,14},{1... | collective-permute-start | bytes 1622024 | tf_op jit(solution)/shard_map/ppermute | solution.py:478
  40.8 0.0 collective-permute-done.4.refs_1_
  40.8 0.0 collective-permute-done.2.near_ref
  40.8 2.0 %collective-permute-start.7 = (bf16[2,512,128]{2,1,0:T(8,128)(2,1)}, bf16[2,512,128]{2,1,0:T(8,128)(2,1)}, u32[]{:S(2)}, u32[]{:S(2)}) collective-permute-start(bf16[2,512,128]{2,1,0:T(8,128)(2,1)} %get-tuple-element.61), channel_id=1, source_target_pairs={{20,0},{24,4},{28,8},{21,1},{25,5},{29,9},{22,2},{26,6},{30,10},{2... | collective-permute-start | bytes 786440 | tf_op jit(solution)/shard_map/ppermute | solution.py:470
  42.8 4.7 %shard_map.50 = (bf16[4,528,128]{2,1,0:T(8,128)(2,1)}, bf16[4,528,128]{2,1,0:T(8,128)(2,1)}) custom-call(s32[1]{0:T(128)} %bitcast.here_ref, s32[8,2,16]{2,1,0:T(2,128)S(1)} %bitcast.32, bf16[512,2048]{1,0:T(8,128)(2,1)S(1)} %bitcast.12, bf16[512,2048]{1,0:T(8,128)(2,1)S(1)} %bitcast.20, bf16[4,512,128]{2,1,0:T(8,128)(2,1)S(1)} %collective-permute-done.3.refs_0_, ...), custom_call_target="tpu_custom_call" | custom-call | flops 999999995904 | bytes 4194304 | tf_op jit(solution)/shard_map/pallas_call | solution.py:226
  47.6 1.3 collective-permute-start.9
  48.9 1.5 collective-permute-start.10
  50.3 2.9 %collective-permute-start.11 = (bf16[2,512,128]{2,1,0:T(8,128)(2,1)}, bf16[2,512,128]{2,1,0:T(8,128)(2,1)}, u32[]{:S(2)}, u32[]{:S(2)}) collective-permute-start(bf16[2,512,128]{2,1,0:T(8,128)(2,1)} %get-tuple-element.68), channel_id=1, source_target_pairs={{12,0},{16,4},{20,8},{24,12},{28,16},{13,1},{17,5},{21,9},{25,13},... | collective-permute-start | bytes 786440 | tf_op jit(solution)/shard_map/ppermute | solution.py:470
  53.2 6.7 %collective-permute-done.5.refs_0_ = bf16[16,528,128]{2,1,0:T(8,128)(2,1)} collective-permute-done((bf16[16,528,128]{2,1,0:T(8,128)(2,1)}, bf16[16,528,128]{2,1,0:T(8,128)(2,1)}, u32[]{:S(2)}, u32[]{:S(2)}) %collective-permute-start.5) | collective-permute-done | bytes 2162720 | tf_op jit(solution)/shard_map/ppermute | solution.py:25
  59.9 2.0 %collective-permute-start.12 = (bf16[2,512,128]{2,1,0:T(8,128)(2,1)}, bf16[2,512,128]{2,1,0:T(8,128)(2,1)}, u32[]{:S(2)}, u32[]{:S(2)}) collective-permute-start(bf16[2,512,128]{2,1,0:T(8,128)(2,1)} %get-tuple-element.70), channel_id=1, source_target_pairs={{20,0},{24,4},{28,8},{21,1},{25,5},{29,9},{22,2},{26,6},{30,10},{2... | collective-permute-start | bytes 786440 | tf_op jit(solution)/shard_map/ppermute | solution.py:470
  61.9 3.6 %shard_map.51 = (bf16[2,528,128]{2,1,0:T(8,128)(2,1)}, bf16[2,528,128]{2,1,0:T(8,128)(2,1)}) custom-call(s32[1]{0:T(128)} %bitcast.here_ref, s32[8,2,16]{2,1,0:T(2,128)S(1)} %bitcast.33, bf16[512,2048]{1,0:T(8,128)(2,1)S(1)} %bitcast.13, bf16[512,2048]{1,0:T(8,128)(2,1)S(1)} %bitcast.21, bf16[2,512,128]{2,1,0:T(8,128)(2,1)} %collective-permute-done.6.refs_0_, ...), custom_call_target="tpu_custom_call" | custom-call | flops 999999995904 | bytes 2097152 | tf_op jit(solution)/shard_map/pallas_call | solution.py:226
  65.5 0.0 collective-permute-done.8.refs_2_
  65.5 0.9 collective-permute-done.9.refs_3_
  66.4 1.3 collective-permute-start.14
  67.7 1.5 collective-permute-start.13
  69.2 3.3 %shard_map.52 = bf16[4,528,128]{2,1,0:T(8,128)(2,1)} custom-call(s32[1]{0:T(128)} %bitcast.here_ref, s32[8,2,16]{2,1,0:T(2,128)S(1)} %bitcast.34, bf16[512,2048]{1,0:T(8,128)(2,1)S(1)} %bitcast.27, bf16[8,512,128]{2,1,0:T(8,128)(2,1)S(1)} %collective-permute-done.2.near_ref), custom_call_target="tpu_custom_call" | custom-call | flops 999999995904 | bytes 3145728 | tf_op jit(solution)/shard_map/pallas_call | solution.py:292
  72.5 11.4 %collective-permute-start.15 = (bf16[4,528,128]{2,1,0:T(8,128)(2,1)}, bf16[4,528,128]{2,1,0:T(8,128)(2,1)}, u32[]{:S(2)}, u32[]{:S(2)}) collective-permute-start(bf16[4,528,128]{2,1,0:T(8,128)(2,1)} %shard_map.52), channel_id=1, source_target_pairs={{0,1},{1,2},{2,3},{3,0},{4,5},{5,6},{6,7},{7,4},{8,9},{9,10},{10,1... | collective-permute-start | bytes 1622024 | tf_op jit(solution)/shard_map/ppermute | solution.py:25
  83.9 11.2 %collective-permute-start.16 = (bf16[4,512,128]{2,1,0:T(8,128)(2,1)}, bf16[4,512,128]{2,1,0:T(8,128)(2,1)}, u32[]{:S(2)}, u32[]{:S(2)}) collective-permute-start(bf16[4,512,128]{2,1,0:T(8,128)(2,1)} %get-tuple-element.79), channel_id=1, source_target_pairs={{16,0},{20,4},{24,8},{28,12},{17,1},{21,5},{25,9},{29,13},{18,2},{... | collective-permute-start | bytes 1572872 | tf_op jit(solution)/shard_map/ppermute | solution.py:470
  95.1 3.6 %shard_map.53 = (bf16[2,528,128]{2,1,0:T(8,128)(2,1)}, bf16[2,528,128]{2,1,0:T(8,128)(2,1)}) custom-call(s32[1]{0:T(128)} %bitcast.here_ref, s32[8,2,16]{2,1,0:T(2,128)S(1)} %bitcast.35, bf16[512,2048]{1,0:T(8,128)(2,1)S(1)} %bitcast.14, bf16[512,2048]{1,0:T(8,128)(2,1)S(1)} %bitcast.22, bf16[2,512,128]{2,1,0:T(8,128)(2,1)} %collective-permute-done.11.refs_0_, ...), custom_call_target="tpu_custom_call" | custom-call | flops 536870912 | bytes 2097152 | tf_op jit(solution)/shard_map/pallas_call | solution.py:226
  98.7 1.3 collective-permute-start.18
  100.0 1.3 collective-permute-start.17
  101.3 0.5 shard_map.54.here_ref
  101.9 4.1 %collective-permute-done.16.refs_0_ = bf16[4,512,128]{2,1,0:T(8,128)(2,1)} collective-permute-done((bf16[4,512,128]{2,1,0:T(8,128)(2,1)}, bf16[4,512,128]{2,1,0:T(8,128)(2,1)}, u32[]{:S(2)}, u32[]{:S(2)}) %collective-permute-start.16) | collective-permute-done | bytes 524320 | tf_op jit(solution)/shard_map/ppermute | solution.py:470
  106.0 4.4 %shard_map.55 = bf16[4,528,128]{2,1,0:T(8,128)(2,1)} custom-call(s32[1]{0:T(128)} %shard_map.54.here_ref, s32[8,2,16]{2,1,0:T(2,128)S(1)} %bitcast.36, bf16[512,2048]{1,0:T(8,128)(2,1)S(1)} %bitcast.15, bf16[512,2048]{1,0:T(8,128)(2,1)S(1)} %bitcast.23, bf16[4,512,128]{2,1,0:T(8,128)(2,1)} %collective-permute-done.16.refs_0_), custom_call_target="tpu_custom_call" | custom-call | flops 536870912 | bytes 2097152 | tf_op jit(solution)/shard_map/pallas_call | solution.py:226
  110.3 3.1 %collective-permute-done.18.refs_8_ = bf16[2,528,128]{2,1,0:T(8,128)(2,1)} collective-permute-done((bf16[2,528,128]{2,1,0:T(8,128)(2,1)}, bf16[2,528,128]{2,1,0:T(8,128)(2,1)}, u32[]{:S(2)}, u32[]{:S(2)}) %collective-permute-start.18) | collective-permute-done | bytes 270368 | tf_op jit(solution)/shard_map/ppermute | solution.py:478
  113.4 11.5 %collective-permute-done.17.refs_7_ = bf16[2,528,128]{2,1,0:T(8,128)(2,1)} collective-permute-done((bf16[2,528,128]{2,1,0:T(8,128)(2,1)}, bf16[2,528,128]{2,1,0:T(8,128)(2,1)}, u32[]{:S(2)}, u32[]{:S(2)}) %collective-permute-start.17) | collective-permute-done | bytes 270368 | tf_op jit(solution)/shard_map/ppermute | solution.py:478
  124.9 1.3 collective-permute-start.19
  126.2 6.9 %shard_map.56 = (f32[16,512,128]{2,1,0:T(8,128)S(1)}, f32[16,4,128]{2,1,0:T(4,128)S(1)}) custom-call(s32[1]{0:T(128)} %shard_map.54.here_ref, s32[8,2,16]{2,1,0:T(2,128)S(1)} %copy-done.7, bf16[16,528,128]{2,1,0:T(8,128)(2,1)} %collective-permute-done.5.refs_0_, bf16[4,528,128]{2,1,0:T(8,128)(2,1)} %collective-permute-done.15.refs_1_, ...), custom_call_target="tpu_custom_call" | custom-call | flops 999999995904 | bytes 9437184 | tf_op jit(solution)/shard_map/pallas_call | solution.py:363
  133.1 16.0 %collective-permute-done.19.part_ref = bf16[4,528,128]{2,1,0:T(8,128)(2,1)} collective-permute-done((bf16[4,528,128]{2,1,0:T(8,128)(2,1)}, bf16[4,528,128]{2,1,0:T(8,128)(2,1)}, u32[]{:S(2)}, u32[]{:S(2)}) %collective-permute-start.19) | collective-permute-done | bytes 540704 | tf_op jit(solution)/shard_map/ppermute | solution.py:478
  149.1 4.5 %shard_map.57 = bf16[512,2048]{1,0:T(8,128)(2,1)} custom-call(s32[1]{0:T(128)} %shard_map.54.here_ref, s32[8,2,16]{2,1,0:T(2,128)S(1)} %copy-done.7, f32[16,512,128]{2,1,0:T(8,128)S(1)} %get-tuple-element.84.mixed_ref, f32[16,4,128]{2,1,0:T(4,128)S(1)} %get-tuple-element.85.sums_ref, bf16[4,528,128]{2,1,0:T(8,128)(2,1)} %collective-permute-done.19.part_ref), custom_call_target="tpu_custom_call" | custom-call | flops 2097152 | bytes 8388608 | tf_op jit(solution)/shard_map/pallas_call | solution.py:420
  (20 shorter events, 0.0 us)
Async XLA Ops:
  0.0 13.7 %copy-start.5 = (s32[1,8,16,2]{2,3,1,0:T(2,128)S(1)}, s32[1,8,16,2]{2,3,1,0:T(2,128)}, u32[]{:S(2)}) copy-start(s32[1,8,16,2]{2,3,1,0:T(2,128)} %param.7) | copy-start | bytes 3076
  5.0 35.8 %collective-permute-start.2 = (bf16[8,512,128]{2,1,0:T(8,128)(2,1)}, bf16[8,512,128]{2,1,0:T(8,128)(2,1)S(1)}, u32[]{:S(2)}, u32[]{:S(2)}) collective-permute-start(bf16[8,512,128]{2,1,0:T(8,128)(2,1)} %get-tuple-element.46), channel_id=1, source_target_pairs={{0,8},{4,12},{8,16},{12,20},{16,24},{20,28},{1,9},{5,13},{9,17},{1... | collective-permute-start | bytes 3145736 | tf_op jit(solution)/shard_map/ppermute | solution.py:467
  6.3 25.2 %collective-permute-start.1 = (bf16[4,512,128]{2,1,0:T(8,128)(2,1)}, bf16[4,512,128]{2,1,0:T(8,128)(2,1)S(1)}, u32[]{:S(2)}, u32[]{:S(2)}) collective-permute-start(bf16[4,512,128]{2,1,0:T(8,128)(2,1)} %get-tuple-element.47), channel_id=1, source_target_pairs={{4,0},{8,4},{12,8},{16,12},{20,16},{24,20},{28,24},{5,1},{9,5},{13... | collective-permute-start | bytes 1572872 | tf_op jit(solution)/shard_map/ppermute | solution.py:470
  11.6 25.8 %collective-permute-start.3 = (bf16[4,512,128]{2,1,0:T(8,128)(2,1)}, bf16[4,512,128]{2,1,0:T(8,128)(2,1)S(1)}, u32[]{:S(2)}, u32[]{:S(2)}) collective-permute-start(bf16[4,512,128]{2,1,0:T(8,128)(2,1)} %get-tuple-element.48), channel_id=1, source_target_pairs={{24,0},{28,4},{25,1},{29,5},{26,2},{30,6},{27,3},{31,7}} | collective-permute-start | bytes 1572872 | tf_op jit(solution)/shard_map/ppermute | solution.py:470
  13.0 27.8 %collective-permute-start.4 = (bf16[4,512,128]{2,1,0:T(8,128)(2,1)}, bf16[4,512,128]{2,1,0:T(8,128)(2,1)S(1)}, u32[]{:S(2)}, u32[]{:S(2)}) collective-permute-start(bf16[4,512,128]{2,1,0:T(8,128)(2,1)} %get-tuple-element.49), channel_id=1, source_target_pairs={{28,0},{29,1},{30,2},{31,3}} | collective-permute-start | bytes 1572872 | tf_op jit(solution)/shard_map/ppermute | solution.py:470
  13.7 7.6 %collective-permute-start = (s32[8,2,16]{2,1,0:T(2,128)S(1)}, s32[8,2,16]{2,1,0:T(2,128)S(1)}, u32[]{:S(2)}, u32[]{:S(2)}) collective-permute-start(s32[8,2,16]{2,1,0:T(2,128)S(1)} %bitcast.29), channel_id=1, source_target_pairs={{0,1},{1,2},{2,3},{3,0},{4,5},{5,6},{6,7},{7,4},{8,9},{9,10},{10,1... | collective-permute-start | bytes 3080 | tf_op jit(solution)/shard_map/ppermute | solution.py:25
  13.7 1.6 %copy-start = (bf16[1,512,2048]{2,1,0:T(8,128)(2,1)S(1)}, bf16[1,512,2048]{2,1,0:T(8,128)(2,1)}, u32[]{:S(2)}) copy-start(bf16[1,512,2048]{2,1,0:T(8,128)(2,1)} %param.5) | copy-start | bytes 6291460
  15.3 1.6 %copy-start.2 = (bf16[1,512,2048]{2,1,0:T(8,128)(2,1)S(1)}, bf16[1,512,2048]{2,1,0:T(8,128)(2,1)}, u32[]{:S(2)}) copy-start(bf16[1,512,2048]{2,1,0:T(8,128)(2,1)} %param.6) | copy-start | bytes 6291460
  16.9 1.6 %copy-start.4 = (bf16[1,512,2048]{2,1,0:T(8,128)(2,1)S(1)}, bf16[1,512,2048]{2,1,0:T(8,128)(2,1)}, u32[]{:S(2)}) copy-start(bf16[1,512,2048]{2,1,0:T(8,128)(2,1)} %param.4) | copy-start | bytes 6291460
  21.3 0.6 copy-start.6
  21.9 12.2 %copy-start.1 = (bf16[1,512,2048]{2,1,0:T(8,128)(2,1)S(1)}, bf16[1,512,2048]{2,1,0:T(8,128)(2,1)}, u32[]{:S(2)}) copy-start(bf16[1,512,2048]{2,1,0:T(8,128)(2,1)} %param.5) | copy-start | bytes 6291460
  21.9 12.2 %copy-start.3 = (bf16[1,512,2048]{2,1,0:T(8,128)(2,1)S(1)}, bf16[1,512,2048]{2,1,0:T(8,128)(2,1)}, u32[]{:S(2)}) copy-start(bf16[1,512,2048]{2,1,0:T(8,128)(2,1)} %param.6) | copy-start | bytes 6291460
  30.9 29.0 %collective-permute-start.5 = (bf16[16,528,128]{2,1,0:T(8,128)(2,1)}, bf16[16,528,128]{2,1,0:T(8,128)(2,1)}, u32[]{:S(2)}, u32[]{:S(2)}) collective-permute-start(bf16[16,528,128]{2,1,0:T(8,128)(2,1)} %shard_map.48), channel_id=1, source_target_pairs={{0,1},{1,2},{2,3},{3,0},{4,5},{5,6},{6,7},{7,4},{8,9},{9,10},{10,1... | collective-permute-start | bytes 6488072 | tf_op jit(solution)/shard_map/ppermute | solution.py:25
  31.5 17.3 %collective-permute-start.6 = (bf16[2,512,128]{2,1,0:T(8,128)(2,1)}, bf16[2,512,128]{2,1,0:T(8,128)(2,1)}, u32[]{:S(2)}, u32[]{:S(2)}) collective-permute-start(bf16[2,512,128]{2,1,0:T(8,128)(2,1)} %get-tuple-element.59), channel_id=1, source_target_pairs={{12,0},{16,4},{20,8},{24,12},{28,16},{13,1},{17,5},{21,9},{25,13},... | collective-permute-start | bytes 786440 | tf_op jit(solution)/shard_map/ppermute | solution.py:470
  37.5 28.0 %collective-permute-start.8 = (bf16[4,528,128]{2,1,0:T(8,128)(2,1)}, bf16[4,528,128]{2,1,0:T(8,128)(2,1)}, u32[]{:S(2)}, u32[]{:S(2)}) collective-permute-start(bf16[4,528,128]{2,1,0:T(8,128)(2,1)} %shard_map.49), channel_id=1, source_target_pairs={{0,5},{1,6},{2,7},{3,4},{4,9},{5,10},{6,11},{7,8},{8,13},{9,14},{1... | collective-permute-start | bytes 1622024 | tf_op jit(solution)/shard_map/ppermute | solution.py:478
  40.8 9.5 %collective-permute-start.7 = (bf16[2,512,128]{2,1,0:T(8,128)(2,1)}, bf16[2,512,128]{2,1,0:T(8,128)(2,1)}, u32[]{:S(2)}, u32[]{:S(2)}) collective-permute-start(bf16[2,512,128]{2,1,0:T(8,128)(2,1)} %get-tuple-element.61), channel_id=1, source_target_pairs={{20,0},{24,4},{28,8},{21,1},{25,5},{29,9},{22,2},{26,6},{30,10},{2... | collective-permute-start | bytes 786440 | tf_op jit(solution)/shard_map/ppermute | solution.py:470
  47.6 18.8 %collective-permute-start.9 = (bf16[4,528,128]{2,1,0:T(8,128)(2,1)}, bf16[4,528,128]{2,1,0:T(8,128)(2,1)}, u32[]{:S(2)}, u32[]{:S(2)}) collective-permute-start(bf16[4,528,128]{2,1,0:T(8,128)(2,1)} %get-tuple-element.55), channel_id=1, source_target_pairs={{0,25},{1,26},{2,27},{3,24},{4,29},{5,30},{6,31},{7,28}} | collective-permute-start | bytes 1622024 | tf_op jit(solution)/shard_map/ppermute | solution.py:478
  48.9 17.6 %collective-permute-start.10 = (bf16[4,528,128]{2,1,0:T(8,128)(2,1)}, bf16[4,528,128]{2,1,0:T(8,128)(2,1)}, u32[]{:S(2)}, u32[]{:S(2)}) collective-permute-start(bf16[4,528,128]{2,1,0:T(8,128)(2,1)} %get-tuple-element.56), channel_id=1, source_target_pairs={{0,29},{1,30},{2,31},{3,28}} | collective-permute-start | bytes 1622024 | tf_op jit(solution)/shard_map/ppermute | solution.py:478
  50.3 33.5 %collective-permute-start.11 = (bf16[2,512,128]{2,1,0:T(8,128)(2,1)}, bf16[2,512,128]{2,1,0:T(8,128)(2,1)}, u32[]{:S(2)}, u32[]{:S(2)}) collective-permute-start(bf16[2,512,128]{2,1,0:T(8,128)(2,1)} %get-tuple-element.68), channel_id=1, source_target_pairs={{12,0},{16,4},{20,8},{24,12},{28,16},{13,1},{17,5},{21,9},{25,13},... | collective-permute-start | bytes 786440 | tf_op jit(solution)/shard_map/ppermute | solution.py:470
  59.9 24.0 %collective-permute-start.12 = (bf16[2,512,128]{2,1,0:T(8,128)(2,1)}, bf16[2,512,128]{2,1,0:T(8,128)(2,1)}, u32[]{:S(2)}, u32[]{:S(2)}) collective-permute-start(bf16[2,512,128]{2,1,0:T(8,128)(2,1)} %get-tuple-element.70), channel_id=1, source_target_pairs={{20,0},{24,4},{28,8},{21,1},{25,5},{29,9},{22,2},{26,6},{30,10},{2... | collective-permute-start | bytes 786440 | tf_op jit(solution)/shard_map/ppermute | solution.py:470
  66.4 32.3 %collective-permute-start.14 = (bf16[2,528,128]{2,1,0:T(8,128)(2,1)}, bf16[2,528,128]{2,1,0:T(8,128)(2,1)}, u32[]{:S(2)}, u32[]{:S(2)}) collective-permute-start(bf16[2,528,128]{2,1,0:T(8,128)(2,1)} %get-tuple-element.75), channel_id=1, source_target_pairs={{0,21},{1,22},{2,23},{3,20},{4,25},{5,26},{6,27},{7,24},{8,29},{9,... | collective-permute-start | bytes 811016 | tf_op jit(solution)/shard_map/ppermute | solution.py:478
  67.7 31.0 %collective-permute-start.13 = (bf16[2,528,128]{2,1,0:T(8,128)(2,1)}, bf16[2,528,128]{2,1,0:T(8,128)(2,1)}, u32[]{:S(2)}, u32[]{:S(2)}) collective-permute-start(bf16[2,528,128]{2,1,0:T(8,128)(2,1)} %get-tuple-element.74), channel_id=1, source_target_pairs={{0,13},{1,14},{2,15},{3,12},{4,17},{5,18},{6,19},{7,16},{8,21},{9,... | collective-permute-start | bytes 811016 | tf_op jit(solution)/shard_map/ppermute | solution.py:478
  72.5 29.4 %collective-permute-start.15 = (bf16[4,528,128]{2,1,0:T(8,128)(2,1)}, bf16[4,528,128]{2,1,0:T(8,128)(2,1)}, u32[]{:S(2)}, u32[]{:S(2)}) collective-permute-start(bf16[4,528,128]{2,1,0:T(8,128)(2,1)} %shard_map.52), channel_id=1, source_target_pairs={{0,1},{1,2},{2,3},{3,0},{4,5},{5,6},{6,7},{7,4},{8,9},{9,10},{10,1... | collective-permute-start | bytes 1622024 | tf_op jit(solution)/shard_map/ppermute | solution.py:25
  83.9 22.1 %collective-permute-start.16 = (bf16[4,512,128]{2,1,0:T(8,128)(2,1)}, bf16[4,512,128]{2,1,0:T(8,128)(2,1)}, u32[]{:S(2)}, u32[]{:S(2)}) collective-permute-start(bf16[4,512,128]{2,1,0:T(8,128)(2,1)} %get-tuple-element.79), channel_id=1, source_target_pairs={{16,0},{20,4},{24,8},{28,12},{17,1},{21,5},{25,9},{29,13},{18,2},{... | collective-permute-start | bytes 1572872 | tf_op jit(solution)/shard_map/ppermute | solution.py:470
  98.7 14.7 %collective-permute-start.18 = (bf16[2,528,128]{2,1,0:T(8,128)(2,1)}, bf16[2,528,128]{2,1,0:T(8,128)(2,1)}, u32[]{:S(2)}, u32[]{:S(2)}) collective-permute-start(bf16[2,528,128]{2,1,0:T(8,128)(2,1)} %get-tuple-element.82), channel_id=1, source_target_pairs={{0,21},{1,22},{2,23},{3,20},{4,25},{5,26},{6,27},{7,24},{8,29},{9,... | collective-permute-start | bytes 811016 | tf_op jit(solution)/shard_map/ppermute | solution.py:478
  100.0 24.8 %collective-permute-start.17 = (bf16[2,528,128]{2,1,0:T(8,128)(2,1)}, bf16[2,528,128]{2,1,0:T(8,128)(2,1)}, u32[]{:S(2)}, u32[]{:S(2)}) collective-permute-start(bf16[2,528,128]{2,1,0:T(8,128)(2,1)} %get-tuple-element.81), channel_id=1, source_target_pairs={{0,13},{1,14},{2,15},{3,12},{4,17},{5,18},{6,19},{7,16},{8,21},{9,... | collective-permute-start | bytes 811016 | tf_op jit(solution)/shard_map/ppermute | solution.py:478
  101.9 24.3 %copy-start.7 = (s32[8,2,16]{2,1,0:T(2,128)S(1)}, s32[8,2,16]{2,1,0:T(2,128)}, u32[]{:S(2)}) copy-start(s32[8,2,16]{2,1,0:T(2,128)} %copy-done.6) | copy-start | bytes 3076
  124.9 24.3 %collective-permute-start.19 = (bf16[4,528,128]{2,1,0:T(8,128)(2,1)}, bf16[4,528,128]{2,1,0:T(8,128)(2,1)}, u32[]{:S(2)}, u32[]{:S(2)}) collective-permute-start(bf16[4,528,128]{2,1,0:T(8,128)(2,1)} %shard_map.55), channel_id=1, source_target_pairs={{0,17},{1,18},{2,19},{3,16},{4,21},{5,22},{6,23},{7,20},{8,25},{9,... | collective-permute-start | bytes 1622024 | tf_op jit(solution)/shard_map/ppermute | solution.py:478

commit v7 on v6

--- a/solution.py
+++ b/solution.py
@@ -15,7 +15,6 @@
 LANES = 128
 STAT_ROWS = 16
 VMEM_BYTES = 24 * 1024 * 1024
-ALL_VMEM_BYTES = 62 * 1024 * 1024
 HIGH_COST = 10**12
 
 
@@ -45,7 +44,7 @@
 
 
 def call(
-    kernel, name_space, outputs, out_specs, scratch=(), flops=0, moved=0, exps=0, vmem=VMEM_BYTES
+    kernel, name_space, outputs, out_specs, scratch=(), flops=0, moved=0, exps=0
 ):
     return pl.pallas_call(
         kernel,
@@ -53,7 +52,7 @@
         out_specs=out_specs,
         out_shape=outputs,
         scratch_shapes=list(scratch),
-        compiler_params=pltpu.CompilerParams(vmem_limit_bytes=vmem),
+        compiler_params=pltpu.CompilerParams(vmem_limit_bytes=VMEM_BYTES),
         cost_estimate=pl.CostEstimate(flops=flops, bytes_accessed=moved, transcendentals=exps),
     )
 
@@ -94,7 +93,9 @@
 
 
 def pack_kernel(here_ref, picks_ref, *refs, jobs, slots):
-    sources, outputs = refs[:3], refs[3 : 3 + len(jobs)]
+    is_near = jobs[0][3]
+    sources = refs[: 1 + is_near]
+    outputs = refs[1 + is_near : 1 + is_near + len(jobs)]
     heads_ref, sems = refs[-2], refs[-1]
     here = here_ref[0]
     listed = {}
@@ -109,7 +110,7 @@
         for slot in range(count):
             head = jnp.maximum(heads_ref[listed[shift, is_near] + first + slot], 0)
             columns = pl.ds(pl.multiple_of(head * HD, HD), HD)
-            for place, source in enumerate(sources[1:] if is_near else sources[:1]):
+            for place, source in enumerate(sources):
                 target = output.at[2 * slot + place if is_near else slot]
                 copy = pltpu.make_async_copy(
                     source.at[:, columns], target, sems.at[len(copies)]
@@ -120,18 +121,17 @@
         copy.wait()
 
 
-def pack(here, picks, queries, keys, values, jobs, slots, vmem=VMEM_BYTES):
-    rows = queries.shape[0]
-    sizes = [2 * count if is_near else count for _, _, count, is_near in jobs]
+def pack(here, picks, sources, jobs, slots):
+    rows = sources[0].shape[0]
+    sizes = [len(sources) * count for _, _, count, _ in jobs]
     return call(
         functools.partial(pack_kernel, jobs=jobs, slots=slots),
-        [SCALARS, SCALARS, IN_HBM, IN_HBM, IN_HBM],
+        [SCALARS, SCALARS] + [IN_VMEM] * len(sources),
         [jax.ShapeDtypeStruct((size, rows, HD), jnp.bfloat16) for size in sizes],
         [IN_VMEM] * len(sizes),
         [pltpu.SMEM((len(jobs) * slots + 1,), jnp.int32), pltpu.SemaphoreType.DMA((sum(sizes),))],
         moved=4 * rows * HD * sum(sizes),
-        vmem=vmem,
-    )(here, picks, queries, keys, values)
+    )(here, picks, *sources)
 
 
 def diagonal():
@@ -238,12 +238,12 @@
     )(here, picks, keys, values, *arrived)
 
 
-def own_kernel(here_ref, query_ref, key_ref, value_ref, out_ref):
+def own_heads(query_ref, key_ref, value_ref, out_ref, heads):
     rows = query_ref.shape[0]
     tile = min(rows, 256)
 
-    def one_head(head, carry):
-        columns = head_columns(head)
+    def one_head(place, carry):
+        columns = head_columns(heads[0] + place)
         value_rows = with_ones(value_ref[:, columns])
         tops, all_sums = [], []
         for at in range(0, rows, tile):
@@ -252,53 +252,61 @@
             row_ids = lax.broadcasted_iota(jnp.int32, scores.shape, 0) + at
             seen = row_ids >= lax.broadcasted_iota(jnp.int32, scores.shape, 1)
             outputs, top, sums = soft_part(jnp.where(seen, scores, -jnp.inf), value_rows[:reach])
-            out_ref[head, at:reach, :] = outputs.astype(jnp.bfloat16)
+            out_ref[place, at:reach, :] = outputs.astype(jnp.bfloat16)
             tops.append(top)
             all_sums.append(sums)
-        out_ref[head, rows:, :] = three_parts(log_sums(tops, all_sums))
+        out_ref[place, rows:, :] = three_parts(log_sums(tops, all_sums))
         return carry
 
-    lax.fori_loop(0, HEADS, one_head, 0, unroll=4)
-
-
-def own_part(here, queries, keys, values):
+    lax.fori_loop(0, len(heads), one_head, 0, unroll=4)
+
+
+def own_kernel(here_ref, query_ref, key_ref, value_ref, out_ref, *, heads):
+    own_heads(query_ref, key_ref, value_ref, out_ref, heads)
+
+
+def own_part(here, queries, keys, values, heads):
     rows = queries.shape[0]
     return call(
-        own_kernel,
+        functools.partial(own_kernel, heads=heads),
         [SCALARS, IN_VMEM, IN_VMEM, IN_VMEM],
-        jax.ShapeDtypeStruct((HEADS, rows + STAT_ROWS, HD), jnp.bfloat16),
+        jax.ShapeDtypeStruct((len(heads), rows + STAT_ROWS, HD), jnp.bfloat16),
         IN_VMEM,
-        flops=4 * HEADS * rows * rows * HD,
-        moved=8 * HEADS * rows * HD,
-        exps=HEADS * rows * rows,
+        flops=4 * len(heads) * rows * rows * HD,
+        moved=8 * len(heads) * rows * HD,
+        exps=len(heads) * rows * rows,
     )(here, queries, keys, values)
 
 
-def near_kernel(here_ref, picks_ref, query_ref, near_ref, out_ref, heads_ref, *, shift, slots):
+def near_kernel(
+    here_ref, picks_ref, query_ref, key_ref, value_ref, near_ref, out_ref, heads_ref, *, heads, shift, slots
+):
     rows = query_ref.shape[0]
     here = here_ref[0]
     list_heads(heads_ref, 0, picks_ref, here, here - shift, slots)
+    own_heads(query_ref, key_ref, value_ref, out_ref, heads)
     for slot in range(slots):
         columns = head_columns(jnp.maximum(heads_ref[slot], 0))
         outputs, lines = attend_rows(
             query_ref[:, columns], near_ref[2 * slot], with_ones(near_ref[2 * slot + 1]), rows
         )
-        out_ref[slot, :rows, :] = outputs.astype(jnp.bfloat16)
-        out_ref[slot, rows:, :] = three_parts(lines)
-
-
-def near_part(here, picks, queries, near, shift, slots):
+        out_ref[len(heads) + slot, :rows, :] = outputs.astype(jnp.bfloat16)
+        out_ref[len(heads) + slot, rows:, :] = three_parts(lines)
+
+
+def near_part(here, picks, queries, keys, values, near, heads, shift, slots):
     rows = queries.shape[0]
+    total = len(heads) + slots
     return call(
-        functools.partial(near_kernel, shift=shift, slots=slots),
-        [SCALARS, SCALARS, IN_VMEM, IN_VMEM],
-        jax.ShapeDtypeStruct((slots, rows + STAT_ROWS, HD), jnp.bfloat16),
+        functools.partial(near_kernel, heads=heads, shift=shift, slots=slots),
+        [SCALARS, SCALARS, IN_VMEM, IN_VMEM, IN_VMEM, IN_VMEM],
+        jax.ShapeDtypeStruct((total, rows + STAT_ROWS, HD), jnp.bfloat16),
         IN_VMEM,
         [pltpu.SMEM((slots + 1,), jnp.int32)],
         flops=HIGH_COST,
-        moved=12 * slots * rows * HD,
-        exps=slots * rows * rows,
-    )(here, picks, queries, near)
+        moved=12 * total * rows * HD,
+        exps=total * rows * rows,
+    )(here, picks, queries, keys, values, near)
 
 
 def find_spots(spots_ref, found_ref, picks_ref, here, shifts, slots):
@@ -374,7 +382,7 @@
             pltpu.SMEM((width,), jnp.int32),
             pltpu.SemaphoreType.DMA((len(parts),)),
         ],
-        flops=HIGH_COST,
+        flops=6 * HEADS * rows * HD,
         moved=2 * (HEADS * 2 + total) * rows * HD,
     )(here, picks, *parts)
 
@@ -458,10 +466,9 @@
     own_picks = picks[0].transpose(0, 2, 1)
 
     groups = groups_in_order(width, slots)
-    near_shifts = (2,)
-    first_jobs = [(shift, 0, slots, True) for shift in near_shifts]
-    first_jobs += [piece + (False,) for group in groups[:2] for piece in group]
-    later_jobs = [piece + (False,) for group in groups[2:] for piece in group]
+    near_shift = 2
+    near_jobs = [(near_shift, 0, slots, True)]
+    query_jobs = [piece + (False,) for group in groups for piece in group]
 
     def up(value, shift):
         return lax.ppermute(value, "ctx", [(at, at + shift) for at in range(width - shift)])
@@ -477,17 +484,15 @@
         ]
         return lax.ppermute(value, ("ctx", "pipe"), pairs)
 
-    packed = pack(
-        here, own_picks, queries, keys, values, first_jobs, slots, vmem=ALL_VMEM_BYTES
-    )
-    sends = dict(zip(first_jobs, packed))
-    near = [up(sends[job], job[0]) for job in first_jobs if job[3]]
+    near_send = pack(here, own_picks, [keys, values], near_jobs, slots)[0]
+    near = up(near_send, near_shift)
+    now = after(here, near_send)
+    packed = pack(now, own_picks, [queries], query_jobs, slots)
+    sends = {job[:3]: send for job, send in zip(query_jobs, packed)}
     arrived = {
-        piece: down(sends[piece + (False,)], piece[0]) for group in groups[:2] for piece in group
+        piece: down(sends[piece], piece[0]) for group in groups[:2] for piece in group
     }
     before = passed_along(own_picks, "pipe", 1)
-    now = after(here, *[sends[job] for job in first_jobs])
-    sends |= zip(later_jobs, pack(now, own_picks, queries, keys, values, later_jobs, slots))
 
     def attend_group(token, group, is_anchor=False):
         return dict(
@@ -508,54 +513,58 @@
 
     def ask_for(group, *earlier):
         for piece in group:
-            arrived[piece] = down(after(sends[piece + (False,)], *earlier), piece[0])
-
-    def send_back(parts, *earlier):
+            arrived[piece] = down(after(sends[piece], *earlier), piece[0])
+
+    def send_back(parts):
         for piece, part in parts.items():
-            returned[piece] = up_and_on(after(part, *earlier) if earlier else part, piece[0])
+            if len(returned) >= 3:
+                part = after(part, list(returned.values())[-3])
+            returned[piece] = up_and_on(part, piece[0])
 
     def those(found, group):
         return [found[piece] for piece in group]
 
     returned = {}
-    own = own_part(after(here, before, sends[later_jobs[0]]), queries, keys, values)
+    first_heads, other_heads = range(HEADS // 2), range(HEADS // 2, HEADS)
+    own = own_part(
+        after(here, before, sends[groups[0][0]]), queries, keys, values, first_heads
+    )
     own_back = passed_along(own, "pipe", 1)
     ask_for(groups[2][:1], own, *those(arrived, groups[0]))
     parts = attend_group(after(here, own), groups[0])
     send_back(parts)
-    ask_for(groups[2][1:], *parts.values(), *near, *those(arrived, groups[1]))
-    parts = attend_group(after(here, *parts.values(), *near), groups[1], is_anchor=True)
+    ask_for(groups[2][1:], *parts.values(), near, *those(arrived, groups[1]))
+    parts = attend_group(after(here, near, *parts.values()), groups[1], is_anchor=True)
     send_back(parts)
     now = after(here, *parts.values())
-    before_last = groups[0] + groups[1]
     for number in range(2, len(groups)):
         group = groups[number]
         if number == len(groups) - 1:
-            now = tick(now, *those(returned, groups[number - 2]))
-            now = after(now, near_back)
+            now = tick(now, list(returned.values())[-4])
         if number == 2:
             ask_for(groups[number + 1], now, *those(arrived, group))
             now = after(now, own_back)
         parts = attend_group(now, group, is_anchor=number == 2)
-        send_back(parts, *those(returned, before_last))
+        send_back(parts)
         now = after(now, *parts.values())
         if number == 2:
-            now = after(now, *those(returned, before_last))
-            beside = near_part(now, own_picks, queries, near[0], near_shifts[0], slots)
-            near_back = passed_along(beside, "pipe", 1)
+            now = after(now, list(returned.values())[-4])
+            beside = near_part(
+                now, own_picks, queries, keys, values, near, other_heads, near_shift, slots
+            )
+            beside_back = passed_along(after(beside, *those(arrived, groups[3])), "pipe", 1)
             now = after(now, beside)
         if 2 <= number < len(groups) - 2:
             ask_for(groups[number + 2], now, *those(arrived, groups[number + 1]))
-        before_last = group
-    now = after(now, *those(returned, groups[-2]))
+    now = tick(now)
 
     final = groups[-1][0]
-    others = [shift for shift in range(1, width) if shift not in near_shifts + final[:1]]
-    merged_shifts = near_shifts + tuple(others)
+    others = [shift for shift in range(1, width) if shift not in (near_shift, final[0])]
+    merged_shifts = (near_shift,) + tuple(others)
     pieces = [piece for piece in returned if piece != final]
     places = [HEADS + merged_shifts.index(shift) * slots + first for shift, first, _ in pieces]
-    parts = [own_back, near_back] + [returned[piece] for piece in pieces]
-    mixed, sums = merge(now, before, parts, [0, HEADS] + places, merged_shifts, slots)
+    parts = [own_back, beside_back] + [returned[piece] for piece in pieces]
+    mixed, sums = merge(now, before, parts, [0, len(first_heads)] + places, merged_shifts, slots)
     return finish(now, before, mixed, sums, returned[final], final[0], slots)[None]
 
 

time: 155 us -> 153 us (0.987)
  the two profiles are of different devices: /device:TPU:26 before, /device:TPU:28 now
where the time goes in v7:
time: 153 us; the launch traced here: 152 us
  Pallas kernels  49.9 us (33%)
  waiting for transfers between devices  49.4 us (32%)
  starting transfers between devices  48.7 us (32%)
  local copies, waits for them, and re-layouts  3.91 us (3%)
    ppermute x8, starting transfers between devices, down(): lax.ppermute(value, 'ctx', [(at, at - shift) for at in range(shift, width)])  35.8 us
    ppermute x8, waiting for transfers between devices, up_and_on(): return lax.ppermute(value, ('ctx', 'pipe'), pairs)  21.3 us
    pallas_call x5, Pallas kernels, attend(): call(functools.partial(attend_kernel, group=group, slots=slots), [SCALARS...  19.7 us
    ppermute x8, waiting for transfers between devices, down(): lax.ppermute(value, 'ctx', [(at, at - shift) for at in range(shift, width)])  15 us
    ppermute x3, waiting for transfers between devices, passed_along(): return lax.ppermute(value, axis, pairs)  13 us
    ppermute x8, starting transfers between devices, up_and_on(): return lax.ppermute(value, ('ctx', 'pipe'), pairs)  10.3 us
    pallas_call x1, Pallas kernels, near_part(): call(functools.partial(near_kernel, heads=heads, shift=shift, slots=slots...  7.51 us
    pallas_call x1, Pallas kernels, merge(): call(functools.partial(merge_kernel, places=tuple(places), shifts=shifts,...  6.93 us
  transfers between devices with their start and end apart: 20, of which 8 were waited for; matrix products, arithmetic and copies ran while one was open for 0% of the time, Pallas kernels for 29%

profile of v7, /device:TPU:28, one launch (start us, length us, event | category | flops | bytes accessed | tf_op | source)
XLA Modules:
  0.0 152.0 jit_solution(7622784055175436584)
XLA Ops:
  0.0 1.6 %copy-done = bf16[1,512,2048]{2,1,0:T(8,128)(2,1)S(1)} copy-done((bf16[1,512,2048]{2,1,0:T(8,128)(2,1)S(1)}, bf16[1,512,2048]{2,1,0:T(8,128)(2,1)}, u32[]{:S(2)}) %copy-start) | copy-done | bytes 2097176
  1.6 1.6 %copy-done.2 = bf16[1,512,2048]{2,1,0:T(8,128)(2,1)S(1)} copy-done((bf16[1,512,2048]{2,1,0:T(8,128)(2,1)S(1)}, bf16[1,512,2048]{2,1,0:T(8,128)(2,1)}, u32[]{:S(2)}) %copy-start.2) | copy-done | bytes 2097176
  3.2 0.7 copy-done.5
  3.9 1.2 shard_map.46
  5.0 0.0 copy-start.6
  5.1 0.0 copy-start.1
  5.1 1.4 collective-permute-start
  6.5 3.7 %shard_map.47 = (bf16[4,512,128]{2,1,0:T(8,128)(2,1)S(1)}, bf16[4,512,128]{2,1,0:T(8,128)(2,1)S(1)}, bf16[4,512,128]{2,1,0:T(8,128)(2,1)S(1)}, bf16[2,512,128]{2...) custom-call(s32[1]{0:T(128)} %bitcast.here_ref, ...), custom_call_target="tpu_custom_call" | custom-call | bytes 6291456 | tf_op jit(solution)/shard_map/pallas_call | solution.py:127
  10.2 2.4 %collective-permute-start.2 = (bf16[4,512,128]{2,1,0:T(8,128)(2,1)S(1)}, bf16[4,512,128]{2,1,0:T(8,128)(2,1)S(1)}, u32[]{:S(2)}, u32[]{:S(2)}) collective-permute-start(bf16[4,512,128]{2,1,0:T(8,128)(2,1)S(1)} %get-tuple-element.45), channel_id=1, source_target_pairs={{4,0},{8,4},{12,8},{16,12},{20,16},{24,20},{28,24},{5,1},{9,5},{13... | collective-permute-start | bytes 1572872 | tf_op jit(solution)/shard_map/ppermute | solution.py:477
  12.7 4.4 %collective-permute-start.3 = (bf16[4,512,128]{2,1,0:T(8,128)(2,1)S(1)}, bf16[4,512,128]{2,1,0:T(8,128)(2,1)S(1)}, u32[]{:S(2)}, u32[]{:S(2)}) collective-permute-start(bf16[4,512,128]{2,1,0:T(8,128)(2,1)S(1)} %get-tuple-element.49), channel_id=1, source_target_pairs={{24,0},{28,4},{25,1},{29,5},{26,2},{30,6},{27,3},{31,7}} | collective-permute-start | bytes 1572872 | tf_op jit(solution)/shard_map/ppermute | solution.py:477
  17.0 1.3 collective-permute-start.4
  18.4 0.1 collective-permute-start.1
  18.5 3.1 %collective-permute-done.1.picks_ref = s32[8,2,16]{2,1,0:T(2,128)S(1)} collective-permute-done((s32[8,2,16]{2,1,0:T(2,128)S(1)}, s32[8,2,16]{2,1,0:T(2,128)S(1)}, u32[]{:S(2)}, u32[]{:S(2)}) %collective-permute-start.1) | collective-permute-done | bytes 1056 | tf_op jit(solution)/shard_map/ppermute | solution.py:24
  21.5 4.8 %shard_map.48 = bf16[8,528,128]{2,1,0:T(8,128)(2,1)} custom-call(s32[1]{0:T(128)} %bitcast.here_ref, bf16[512,2048]{1,0:T(8,128)(2,1)S(1)} %bitcast.25, bf16[512,2048]{1,0:T(8,128)(2,1)S(1)} %bitcast.9, bf16[512,2048]{1,0:T(8,128)(2,1)S(1)} %bitcast.17), custom_call_target="tpu_custom_call" | custom-call | flops 1073741824 | bytes 4194304 | tf_op jit(solution)/shard_map/pallas_call | solution.py:270
  26.3 0.0 collective-permute-start.5
  26.3 0.0 collective-permute-done.2.refs_0_
  26.3 4.4 %collective-permute-start.6 = (bf16[2,512,128]{2,1,0:T(8,128)(2,1)}, bf16[2,512,128]{2,1,0:T(8,128)(2,1)}, u32[]{:S(2)}, u32[]{:S(2)}) collective-permute-start(bf16[2,512,128]{2,1,0:T(8,128)(2,1)} %get-tuple-element.56), channel_id=1, source_target_pairs={{12,0},{16,4},{20,8},{24,12},{28,16},{13,1},{17,5},{21,9},{25,13},... | collective-permute-start | bytes 786440 | tf_op jit(solution)/shard_map/ppermute | solution.py:477
  30.7 3.4 %shard_map.49 = bf16[4,528,128]{2,1,0:T(8,128)(2,1)} custom-call(s32[1]{0:T(128)} %bitcast.here_ref, s32[8,2,16]{2,1,0:T(2,128)S(1)} %bitcast.30, bf16[512,2048]{1,0:T(8,128)(2,1)S(1)} %bitcast.10, bf16[512,2048]{1,0:T(8,128)(2,1)S(1)} %bitcast.18, bf16[4,512,128]{2,1,0:T(8,128)(2,1)S(1)} %collective-permute-done.2.refs_0_), custom_call_target="tpu_custom_call" | custom-call | flops 536870912 | bytes 2097152 | tf_op jit(solution)/shard_map/pallas_call | solution.py:226
  34.1 1.3 collective-permute-start.11
  35.3 5.3 %collective-permute-done.4.refs_1_ = bf16[4,512,128]{2,1,0:T(8,128)(2,1)S(1)} collective-permute-done((bf16[4,512,128]{2,1,0:T(8,128)(2,1)S(1)}, bf16[4,512,128]{2,1,0:T(8,128)(2,1)S(1)}, u32[]{:S(2)}, u32[]{:S(2)}) %collective-permute-start.4) | collective-permute-done | bytes 524320 | tf_op jit(solution)/shard_map/ppermute | solution.py:477
  40.7 2.0 %collective-permute-start.7 = (bf16[2,512,128]{2,1,0:T(8,128)(2,1)}, bf16[2,512,128]{2,1,0:T(8,128)(2,1)}, u32[]{:S(2)}, u32[]{:S(2)}) collective-permute-start(bf16[2,512,128]{2,1,0:T(8,128)(2,1)} %get-tuple-element.58), channel_id=1, source_target_pairs={{20,0},{24,4},{28,8},{21,1},{25,5},{29,9},{22,2},{26,6},{30,10},{2... | collective-permute-start | bytes 786440 | tf_op jit(solution)/shard_map/ppermute | solution.py:477
  42.7 4.7 %shard_map.50 = (bf16[4,528,128]{2,1,0:T(8,128)(2,1)}, bf16[4,528,128]{2,1,0:T(8,128)(2,1)}) custom-call(s32[1]{0:T(128)} %bitcast.here_ref, s32[8,2,16]{2,1,0:T(2,128)S(1)} %bitcast.31, bf16[512,2048]{1,0:T(8,128)(2,1)S(1)} %bitcast.11, bf16[512,2048]{1,0:T(8,128)(2,1)S(1)} %bitcast.19, bf16[4,512,128]{2,1,0:T(8,128)(2,1)S(1)} %collective-permute-done.3.refs_0_, ...), custom_call_target="tpu_custom_call" | custom-call | flops 999999995904 | bytes 4194304 | tf_op jit(solution)/shard_map/pallas_call | solution.py:226
  47.4 1.3 collective-permute-start.8
  48.7 1.3 collective-permute-start.15
  50.0 2.1 %collective-permute-done.6.refs_0_ = bf16[2,512,128]{2,1,0:T(8,128)(2,1)} collective-permute-done((bf16[2,512,128]{2,1,0:T(8,128)(2,1)}, bf16[2,512,128]{2,1,0:T(8,128)(2,1)}, u32[]{:S(2)}, u32[]{:S(2)}) %collective-permute-start.6) | collective-permute-done | bytes 262176 | tf_op jit(solution)/shard_map/ppermute | solution.py:477
  52.1 3.9 %collective-permute-done.7.refs_1_ = bf16[2,512,128]{2,1,0:T(8,128)(2,1)} collective-permute-done((bf16[2,512,128]{2,1,0:T(8,128)(2,1)}, bf16[2,512,128]{2,1,0:T(8,128)(2,1)}, u32[]{:S(2)}, u32[]{:S(2)}) %collective-permute-start.7) | collective-permute-done | bytes 262176 | tf_op jit(solution)/shard_map/ppermute | solution.py:477
  55.9 10.7 %collective-permute-start.9 = (bf16[2,512,128]{2,1,0:T(8,128)(2,1)}, bf16[2,512,128]{2,1,0:T(8,128)(2,1)}, u32[]{:S(2)}, u32[]{:S(2)}) collective-permute-start(bf16[2,512,128]{2,1,0:T(8,128)(2,1)} %get-tuple-element.65), channel_id=1, source_target_pairs={{12,0},{16,4},{20,8},{24,12},{28,16},{13,1},{17,5},{21,9},{25,13},... | collective-permute-start | bytes 786440 | tf_op jit(solution)/shard_map/ppermute | solution.py:477
  66.6 2.0 %collective-permute-start.10 = (bf16[2,512,128]{2,1,0:T(8,128)(2,1)}, bf16[2,512,128]{2,1,0:T(8,128)(2,1)}, u32[]{:S(2)}, u32[]{:S(2)}) collective-permute-start(bf16[2,512,128]{2,1,0:T(8,128)(2,1)} %get-tuple-element.67), channel_id=1, source_target_pairs={{20,0},{24,4},{28,8},{21,1},{25,5},{29,9},{22,2},{26,6},{30,10},{2... | collective-permute-start | bytes 786440 | tf_op jit(solution)/shard_map/ppermute | solution.py:477
  68.6 3.6 %shard_map.51 = (bf16[2,528,128]{2,1,0:T(8,128)(2,1)}, bf16[2,528,128]{2,1,0:T(8,128)(2,1)}) custom-call(s32[1]{0:T(128)} %bitcast.here_ref, s32[8,2,16]{2,1,0:T(2,128)S(1)} %bitcast.32, bf16[512,2048]{1,0:T(8,128)(2,1)S(1)} %bitcast.12, bf16[512,2048]{1,0:T(8,128)(2,1)S(1)} %bitcast.20, bf16[2,512,128]{2,1,0:T(8,128)(2,1)} %collective-permute-done.6.refs_0_, ...), custom_call_target="tpu_custom_call" | custom-call | flops 999999995904 | bytes 2097152 | tf_op jit(solution)/shard_map/pallas_call | solution.py:226
  72.2 1.3 collective-permute-start.12
  73.5 0.0 collective-permute-done.8.refs_3_
  73.5 1.3 collective-permute-start.16
  74.8 7.5 %shard_map.52 = bf16[12,528,128]{2,1,0:T(8,128)(2,1)} custom-call(s32[1]{0:T(128)} %bitcast.here_ref, s32[8,2,16]{2,1,0:T(2,128)S(1)} %bitcast.33, bf16[512,2048]{1,0:T(8,128)(2,1)S(1)} %bitcast.26, bf16[512,2048]{1,0:T(8,128)(2,1)S(1)} %bitcast.13, bf16[512,2048]{1,0:T(8,128)(2,1)S(1)} %bitcast.21, bf16[8,512,128]{2,1,0:T(8,128)(2,1)S(1)} %collective-permute-done.near_ref), custom_call_target="tpu_custom_call" | custom-call | flops 999999995904 | bytes 9437184 | tf_op jit(solution)/shard_map/pallas_call | solution.py:300
  82.4 8.7 %collective-permute-start.13 = (bf16[4,512,128]{2,1,0:T(8,128)(2,1)}, bf16[4,512,128]{2,1,0:T(8,128)(2,1)}, u32[]{:S(2)}, u32[]{:S(2)}) collective-permute-start(bf16[4,512,128]{2,1,0:T(8,128)(2,1)} %get-tuple-element.74), channel_id=1, source_target_pairs={{16,0},{20,4},{24,8},{28,12},{17,1},{21,5},{25,9},{29,13},{18,2},{... | collective-permute-start | bytes 1572872 | tf_op jit(solution)/shard_map/ppermute | solution.py:477
  91.0 3.6 %shard_map.53 = (bf16[2,528,128]{2,1,0:T(8,128)(2,1)}, bf16[2,528,128]{2,1,0:T(8,128)(2,1)}) custom-call(s32[1]{0:T(128)} %bitcast.here_ref, s32[8,2,16]{2,1,0:T(2,128)S(1)} %bitcast.34, bf16[512,2048]{1,0:T(8,128)(2,1)S(1)} %bitcast.14, bf16[512,2048]{1,0:T(8,128)(2,1)S(1)} %bitcast.22, bf16[2,512,128]{2,1,0:T(8,128)(2,1)} %collective-permute-done.9.refs_0_, ...), custom_call_target="tpu_custom_call" | custom-call | flops 536870912 | bytes 2097152 | tf_op jit(solution)/shard_map/pallas_call | solution.py:226
  94.6 0.5 shard_map.54.here_ref
  95.2 1.3 collective-permute-start.18
  96.5 1.3 collective-permute-start.17
  97.8 1.0 collective-permute-start.14
  98.8 3.7 %collective-permute-done.13.refs_0_ = bf16[4,512,128]{2,1,0:T(8,128)(2,1)} collective-permute-done((bf16[4,512,128]{2,1,0:T(8,128)(2,1)}, bf16[4,512,128]{2,1,0:T(8,128)(2,1)}, u32[]{:S(2)}, u32[]{:S(2)}) %collective-permute-start.13) | collective-permute-done | bytes 524320 | tf_op jit(solution)/shard_map/ppermute | solution.py:477
  102.6 4.4 %shard_map.55 = bf16[4,528,128]{2,1,0:T(8,128)(2,1)} custom-call(s32[1]{0:T(128)} %shard_map.54.here_ref, s32[8,2,16]{2,1,0:T(2,128)S(1)} %bitcast.35, bf16[512,2048]{1,0:T(8,128)(2,1)S(1)} %bitcast.15, bf16[512,2048]{1,0:T(8,128)(2,1)S(1)} %bitcast.23, bf16[4,512,128]{2,1,0:T(8,128)(2,1)} %collective-permute-done.13.refs_0_), custom_call_target="tpu_custom_call" | custom-call | flops 536870912 | bytes 2097152 | tf_op jit(solution)/shard_map/pallas_call | solution.py:226
  106.9 1.3 collective-permute-start.19
  108.2 1.2 shard_map.56.here_ref
  109.4 4.8 %collective-permute-done.18.refs_8_ = bf16[2,528,128]{2,1,0:T(8,128)(2,1)} collective-permute-done((bf16[2,528,128]{2,1,0:T(8,128)(2,1)}, bf16[2,528,128]{2,1,0:T(8,128)(2,1)}, u32[]{:S(2)}, u32[]{:S(2)}) %collective-permute-start.18) | collective-permute-done | bytes 270368 | tf_op jit(solution)/shard_map/ppermute | solution.py:485
  114.2 10.0 %collective-permute-done.14.refs_1_ = bf16[12,528,128]{2,1,0:T(8,128)(2,1)} collective-permute-done((bf16[12,528,128]{2,1,0:T(8,128)(2,1)}, bf16[12,528,128]{2,1,0:T(8,128)(2,1)}, u32[]{:S(2)}, u32[]{:S(2)}) %collective-permute-start.14) | collective-permute-done | bytes 1622048 | tf_op jit(solution)/shard_map/ppermute | solution.py:24
  124.1 6.9 %shard_map.57 = (f32[16,512,128]{2,1,0:T(8,128)S(1)}, f32[16,4,128]{2,1,0:T(4,128)S(1)}) custom-call(s32[1]{0:T(128)} %shard_map.56.here_ref, s32[8,2,16]{2,1,0:T(2,128)S(1)} %copy-done.9, bf16[8,528,128]{2,1,0:T(8,128)(2,1)} %collective-permute-done.5.refs_0_, bf16[12,528,128]{2,1,0:T(8,128)(2,1)} %collective-permute-done.14.refs_1_, ...), custom_call_target="tpu_custom_call" | custom-call | flops 6291456 | bytes 9437184 | tf_op jit(solution)/shard_map/pallas_call | solution.py:371
  131.0 16.6 %collective-permute-done.19.part_ref = bf16[4,528,128]{2,1,0:T(8,128)(2,1)} collective-permute-done((bf16[4,528,128]{2,1,0:T(8,128)(2,1)}, bf16[4,528,128]{2,1,0:T(8,128)(2,1)}, u32[]{:S(2)}, u32[]{:S(2)}) %collective-permute-start.19) | collective-permute-done | bytes 540704 | tf_op jit(solution)/shard_map/ppermute | solution.py:485
  147.6 4.4 %shard_map.58 = bf16[512,2048]{1,0:T(8,128)(2,1)} custom-call(s32[1]{0:T(128)} %shard_map.56.here_ref, s32[8,2,16]{2,1,0:T(2,128)S(1)} %copy-done.9, f32[16,512,128]{2,1,0:T(8,128)S(1)} %get-tuple-element.80.mixed_ref, f32[16,4,128]{2,1,0:T(4,128)S(1)} %get-tuple-element.81.sums_ref, bf16[4,528,128]{2,1,0:T(8,128)(2,1)} %collective-permute-done.19.part_ref), custom_call_target="tpu_custom_call" | custom-call | flops 2097152 | bytes 8388608 | tf_op jit(solution)/shard_map/pallas_call | solution.py:428
  (25 shorter events, 0.1 us)
Async XLA Ops:
  0.0 1.6 %copy-start = (bf16[1,512,2048]{2,1,0:T(8,128)(2,1)S(1)}, bf16[1,512,2048]{2,1,0:T(8,128)(2,1)}, u32[]{:S(2)}) copy-start(bf16[1,512,2048]{2,1,0:T(8,128)(2,1)} %param.5) | copy-start | bytes 6291460
  1.6 1.6 %copy-start.2 = (bf16[1,512,2048]{2,1,0:T(8,128)(2,1)S(1)}, bf16[1,512,2048]{2,1,0:T(8,128)(2,1)}, u32[]{:S(2)}) copy-start(bf16[1,512,2048]{2,1,0:T(8,128)(2,1)} %param.6) | copy-start | bytes 6291460
  3.2 0.7 copy-start.5
  3.9 2.6 %copy-start.4 = (bf16[1,512,2048]{2,1,0:T(8,128)(2,1)S(1)}, bf16[1,512,2048]{2,1,0:T(8,128)(2,1)}, u32[]{:S(2)}) copy-start(bf16[1,512,2048]{2,1,0:T(8,128)(2,1)} %param.4) | copy-start | bytes 6291460
  3.9 17.6 %copy-start.3 = (bf16[1,512,2048]{2,1,0:T(8,128)(2,1)S(1)}, bf16[1,512,2048]{2,1,0:T(8,128)(2,1)}, u32[]{:S(2)}) copy-start(bf16[1,512,2048]{2,1,0:T(8,128)(2,1)} %param.6) | copy-start | bytes 6291460
  5.0 13.3 %copy-start.6 = (s32[1,8,16,2]{2,3,1,0:T(2,128)S(1)}, s32[1,8,16,2]{2,3,1,0:T(2,128)}, u32[]{:S(2)}) copy-start(s32[1,8,16,2]{2,3,1,0:T(2,128)} %param.7) | copy-start | bytes 3076
  5.1 16.5 %copy-start.1 = (bf16[1,512,2048]{2,1,0:T(8,128)(2,1)S(1)}, bf16[1,512,2048]{2,1,0:T(8,128)(2,1)}, u32[]{:S(2)}) copy-start(bf16[1,512,2048]{2,1,0:T(8,128)(2,1)} %param.5) | copy-start | bytes 6291460
  5.1 35.6 %collective-permute-start = (bf16[8,512,128]{2,1,0:T(8,128)(2,1)S(1)}, bf16[8,512,128]{2,1,0:T(8,128)(2,1)S(1)}, u32[]{:S(2)}, u32[]{:S(2)}) collective-permute-start(bf16[8,512,128]{2,1,0:T(8,128)(2,1)S(1)} %shard_map.46), channel_id=1, source_target_pairs={{0,8},{4,12},{8,16},{12,20},{16,24},{20,28},{1,9},{5,13},{9,17},{1... | collective-permute-start | bytes 3145736 | tf_op jit(solution)/shard_map/ppermute | solution.py:474
  10.2 16.1 %collective-permute-start.2 = (bf16[4,512,128]{2,1,0:T(8,128)(2,1)S(1)}, bf16[4,512,128]{2,1,0:T(8,128)(2,1)S(1)}, u32[]{:S(2)}, u32[]{:S(2)}) collective-permute-start(bf16[4,512,128]{2,1,0:T(8,128)(2,1)S(1)} %get-tuple-element.45), channel_id=1, source_target_pairs={{4,0},{8,4},{12,8},{16,12},{20,16},{24,20},{28,24},{5,1},{9,5},{13... | collective-permute-start | bytes 1572872 | tf_op jit(solution)/shard_map/ppermute | solution.py:477
  12.7 21.4 %collective-permute-start.3 = (bf16[4,512,128]{2,1,0:T(8,128)(2,1)S(1)}, bf16[4,512,128]{2,1,0:T(8,128)(2,1)S(1)}, u32[]{:S(2)}, u32[]{:S(2)}) collective-permute-start(bf16[4,512,128]{2,1,0:T(8,128)(2,1)S(1)} %get-tuple-element.49), channel_id=1, source_target_pairs={{24,0},{28,4},{25,1},{29,5},{26,2},{30,6},{27,3},{31,7}} | collective-permute-start | bytes 1572872 | tf_op jit(solution)/shard_map/ppermute | solution.py:477
  17.0 23.6 %collective-permute-start.4 = (bf16[4,512,128]{2,1,0:T(8,128)(2,1)S(1)}, bf16[4,512,128]{2,1,0:T(8,128)(2,1)S(1)}, u32[]{:S(2)}, u32[]{:S(2)}) collective-permute-start(bf16[4,512,128]{2,1,0:T(8,128)(2,1)S(1)} %get-tuple-element.50), channel_id=1, source_target_pairs={{28,0},{29,1},{30,2},{31,3}} | collective-permute-start | bytes 1572872 | tf_op jit(solution)/shard_map/ppermute | solution.py:477
  18.4 3.1 %collective-permute-start.1 = (s32[8,2,16]{2,1,0:T(2,128)S(1)}, s32[8,2,16]{2,1,0:T(2,128)S(1)}, u32[]{:S(2)}, u32[]{:S(2)}) collective-permute-start(s32[8,2,16]{2,1,0:T(2,128)S(1)} %bitcast.29), channel_id=1, source_target_pairs={{0,1},{1,2},{2,3},{3,0},{4,5},{5,6},{6,7},{7,4},{8,9},{9,10},{10,1... | collective-permute-start | bytes 3080 | tf_op jit(solution)/shard_map/ppermute | solution.py:24
  21.5 4.8 %copy-start.8 = (s32[8,2,16]{2,1,0:T(2,128)}, s32[8,2,16]{2,1,0:T(2,128)S(1)}, u32[]{:S(2)}) copy-start(s32[8,2,16]{2,1,0:T(2,128)S(1)} %collective-permute-done.1.picks_ref) | copy-start | bytes 3076
  26.3 22.3 %collective-permute-start.5 = (bf16[8,528,128]{2,1,0:T(8,128)(2,1)}, bf16[8,528,128]{2,1,0:T(8,128)(2,1)}, u32[]{:S(2)}, u32[]{:S(2)}) collective-permute-start(bf16[8,528,128]{2,1,0:T(8,128)(2,1)} %shard_map.48), channel_id=1, source_target_pairs={{0,1},{1,2},{2,3},{3,0},{4,5},{5,6},{6,7},{7,4},{8,9},{9,10},{10,1... | collective-permute-start | bytes 3244040 | tf_op jit(solution)/shard_map/ppermute | solution.py:24
  26.3 25.7 %collective-permute-start.6 = (bf16[2,512,128]{2,1,0:T(8,128)(2,1)}, bf16[2,512,128]{2,1,0:T(8,128)(2,1)}, u32[]{:S(2)}, u32[]{:S(2)}) collective-permute-start(bf16[2,512,128]{2,1,0:T(8,128)(2,1)} %get-tuple-element.56), channel_id=1, source_target_pairs={{12,0},{16,4},{20,8},{24,12},{28,16},{13,1},{17,5},{21,9},{25,13},... | collective-permute-start | bytes 786440 | tf_op jit(solution)/shard_map/ppermute | solution.py:477
  34.1 38.2 %collective-permute-start.11 = (bf16[4,528,128]{2,1,0:T(8,128)(2,1)}, bf16[4,528,128]{2,1,0:T(8,128)(2,1)}, u32[]{:S(2)}, u32[]{:S(2)}) collective-permute-start(bf16[4,528,128]{2,1,0:T(8,128)(2,1)} %shard_map.49), channel_id=1, source_target_pairs={{0,5},{1,6},{2,7},{3,4},{4,9},{5,10},{6,11},{7,8},{8,13},{9,14},{1... | collective-permute-start | bytes 1622024 | tf_op jit(solution)/shard_map/ppermute | solution.py:485
  40.7 15.2 %collective-permute-start.7 = (bf16[2,512,128]{2,1,0:T(8,128)(2,1)}, bf16[2,512,128]{2,1,0:T(8,128)(2,1)}, u32[]{:S(2)}, u32[]{:S(2)}) collective-permute-start(bf16[2,512,128]{2,1,0:T(8,128)(2,1)} %get-tuple-element.58), channel_id=1, source_target_pairs={{20,0},{24,4},{28,8},{21,1},{25,5},{29,9},{22,2},{26,6},{30,10},{2... | collective-permute-start | bytes 786440 | tf_op jit(solution)/shard_map/ppermute | solution.py:477
  47.4 26.2 %collective-permute-start.8 = (bf16[4,528,128]{2,1,0:T(8,128)(2,1)}, bf16[4,528,128]{2,1,0:T(8,128)(2,1)}, u32[]{:S(2)}, u32[]{:S(2)}) collective-permute-start(bf16[4,528,128]{2,1,0:T(8,128)(2,1)} %get-tuple-element.51), channel_id=1, source_target_pairs={{0,25},{1,26},{2,27},{3,24},{4,29},{5,30},{6,31},{7,28}} | collective-permute-start | bytes 1622024 | tf_op jit(solution)/shard_map/ppermute | solution.py:485
  48.7 46.5 %collective-permute-start.15 = (bf16[4,528,128]{2,1,0:T(8,128)(2,1)}, bf16[4,528,128]{2,1,0:T(8,128)(2,1)}, u32[]{:S(2)}, u32[]{:S(2)}) collective-permute-start(bf16[4,528,128]{2,1,0:T(8,128)(2,1)} %get-tuple-element.52), channel_id=1, source_target_pairs={{0,29},{1,30},{2,31},{3,28}} | collective-permute-start | bytes 1622024 | tf_op jit(solution)/shard_map/ppermute | solution.py:485
  55.9 26.4 %collective-permute-start.9 = (bf16[2,512,128]{2,1,0:T(8,128)(2,1)}, bf16[2,512,128]{2,1,0:T(8,128)(2,1)}, u32[]{:S(2)}, u32[]{:S(2)}) collective-permute-start(bf16[2,512,128]{2,1,0:T(8,128)(2,1)} %get-tuple-element.65), channel_id=1, source_target_pairs={{12,0},{16,4},{20,8},{24,12},{28,16},{13,1},{17,5},{21,9},{25,13},... | collective-permute-start | bytes 786440 | tf_op jit(solution)/shard_map/ppermute | solution.py:477
  66.6 15.8 %collective-permute-start.10 = (bf16[2,512,128]{2,1,0:T(8,128)(2,1)}, bf16[2,512,128]{2,1,0:T(8,128)(2,1)}, u32[]{:S(2)}, u32[]{:S(2)}) collective-permute-start(bf16[2,512,128]{2,1,0:T(8,128)(2,1)} %get-tuple-element.67), channel_id=1, source_target_pairs={{20,0},{24,4},{28,8},{21,1},{25,5},{29,9},{22,2},{26,6},{30,10},{2... | collective-permute-start | bytes 786440 | tf_op jit(solution)/shard_map/ppermute | solution.py:477
  72.2 22.4 %collective-permute-start.12 = (bf16[2,528,128]{2,1,0:T(8,128)(2,1)}, bf16[2,528,128]{2,1,0:T(8,128)(2,1)}, u32[]{:S(2)}, u32[]{:S(2)}) collective-permute-start(bf16[2,528,128]{2,1,0:T(8,128)(2,1)} %get-tuple-element.71), channel_id=1, source_target_pairs={{0,13},{1,14},{2,15},{3,12},{4,17},{5,18},{6,19},{7,16},{8,21},{9,... | collective-permute-start | bytes 811016 | tf_op jit(solution)/shard_map/ppermute | solution.py:485
  73.5 33.4 %collective-permute-start.16 = (bf16[2,528,128]{2,1,0:T(8,128)(2,1)}, bf16[2,528,128]{2,1,0:T(8,128)(2,1)}, u32[]{:S(2)}, u32[]{:S(2)}) collective-permute-start(bf16[2,528,128]{2,1,0:T(8,128)(2,1)} %get-tuple-element.77), channel_id=1, source_target_pairs={{0,21},{1,22},{2,23},{3,20},{4,25},{5,26},{6,27},{7,24},{8,29},{9,... | collective-permute-start | bytes 811016 | tf_op jit(solution)/shard_map/ppermute | solution.py:485
  82.4 20.2 %collective-permute-start.13 = (bf16[4,512,128]{2,1,0:T(8,128)(2,1)}, bf16[4,512,128]{2,1,0:T(8,128)(2,1)}, u32[]{:S(2)}, u32[]{:S(2)}) collective-permute-start(bf16[4,512,128]{2,1,0:T(8,128)(2,1)} %get-tuple-element.74), channel_id=1, source_target_pairs={{16,0},{20,4},{24,8},{28,12},{17,1},{21,5},{25,9},{29,13},{18,2},{... | collective-permute-start | bytes 1572872 | tf_op jit(solution)/shard_map/ppermute | solution.py:477
  94.6 7.9 %copy-start.7 = (s32[1,8,16,2]{2,3,1,0:T(2,128)S(1)}, s32[1,8,16,2]{2,3,1,0:T(2,128)}, u32[]{:S(2)}) copy-start(s32[1,8,16,2]{2,3,1,0:T(2,128)} %param.7) | copy-start | bytes 3076
  95.2 19.0 %collective-permute-start.18 = (bf16[2,528,128]{2,1,0:T(8,128)(2,1)}, bf16[2,528,128]{2,1,0:T(8,128)(2,1)}, u32[]{:S(2)}, u32[]{:S(2)}) collective-permute-start(bf16[2,528,128]{2,1,0:T(8,128)(2,1)} %get-tuple-element.79), channel_id=1, source_target_pairs={{0,21},{1,22},{2,23},{3,20},{4,25},{5,26},{6,27},{7,24},{8,29},{9,... | collective-permute-start | bytes 811016 | tf_op jit(solution)/shard_map/ppermute | solution.py:485
  96.5 17.7 %collective-permute-start.17 = (bf16[2,528,128]{2,1,0:T(8,128)(2,1)}, bf16[2,528,128]{2,1,0:T(8,128)(2,1)}, u32[]{:S(2)}, u32[]{:S(2)}) collective-permute-start(bf16[2,528,128]{2,1,0:T(8,128)(2,1)} %get-tuple-element.78), channel_id=1, source_target_pairs={{0,13},{1,14},{2,15},{3,12},{4,17},{5,18},{6,19},{7,16},{8,21},{9,... | collective-permute-start | bytes 811016 | tf_op jit(solution)/shard_map/ppermute | solution.py:485
  97.8 26.3 %collective-permute-start.14 = (bf16[12,528,128]{2,1,0:T(8,128)(2,1)}, bf16[12,528,128]{2,1,0:T(8,128)(2,1)}, u32[]{:S(2)}, u32[]{:S(2)}) collective-permute-start(bf16[12,528,128]{2,1,0:T(8,128)(2,1)} %shard_map.52), channel_id=1, source_target_pairs={{0,1},{1,2},{2,3},{3,0},{4,5},{5,6},{6,7},{7,4},{8,9},{9,10},{10,1... | collective-permute-start | bytes 4866056 | tf_op jit(solution)/shard_map/ppermute | solution.py:24
  106.9 40.7 %collective-permute-start.19 = (bf16[4,528,128]{2,1,0:T(8,128)(2,1)}, bf16[4,528,128]{2,1,0:T(8,128)(2,1)}, u32[]{:S(2)}, u32[]{:S(2)}) collective-permute-start(bf16[4,528,128]{2,1,0:T(8,128)(2,1)} %shard_map.55), channel_id=1, source_target_pairs={{0,17},{1,18},{2,19},{3,16},{4,21},{5,22},{6,23},{7,20},{8,25},{9,... | collective-permute-start | bytes 1622024 | tf_op jit(solution)/shard_map/ppermute | solution.py:485
  108.2 15.9 %copy-start.9 = (s32[8,2,16]{2,1,0:T(2,128)S(1)}, s32[8,2,16]{2,1,0:T(2,128)}, u32[]{:S(2)}) copy-start(s32[8,2,16]{2,1,0:T(2,128)} %copy-done.8) | copy-start | bytes 3076

commit v8 on v7

--- a/solution.py
+++ b/solution.py
@@ -238,12 +238,12 @@
     )(here, picks, keys, values, *arrived)
 
 
-def own_heads(query_ref, key_ref, value_ref, out_ref, heads):
+def own_kernel(here_ref, query_ref, key_ref, value_ref, out_ref):
     rows = query_ref.shape[0]
     tile = min(rows, 256)
 
-    def one_head(place, carry):
-        columns = head_columns(heads[0] + place)
+    def one_head(head, carry):
+        columns = head_columns(head)
         value_rows = with_ones(value_ref[:, columns])
         tops, all_sums = [], []
         for at in range(0, rows, tile):
@@ -252,61 +252,53 @@
             row_ids = lax.broadcasted_iota(jnp.int32, scores.shape, 0) + at
             seen = row_ids >= lax.broadcasted_iota(jnp.int32, scores.shape, 1)
             outputs, top, sums = soft_part(jnp.where(seen, scores, -jnp.inf), value_rows[:reach])
-            out_ref[place, at:reach, :] = outputs.astype(jnp.bfloat16)
+            out_ref[head, at:reach, :] = outputs.astype(jnp.bfloat16)
             tops.append(top)
             all_sums.append(sums)
-        out_ref[place, rows:, :] = three_parts(log_sums(tops, all_sums))
+        out_ref[head, rows:, :] = three_parts(log_sums(tops, all_sums))
         return carry
 
-    lax.fori_loop(0, len(heads), one_head, 0, unroll=4)
-
-
-def own_kernel(here_ref, query_ref, key_ref, value_ref, out_ref, *, heads):
-    own_heads(query_ref, key_ref, value_ref, out_ref, heads)
-
-
-def own_part(here, queries, keys, values, heads):
+    lax.fori_loop(0, HEADS, one_head, 0, unroll=4)
+
+
+def own_part(here, queries, keys, values):
     rows = queries.shape[0]
     return call(
-        functools.partial(own_kernel, heads=heads),
+        own_kernel,
         [SCALARS, IN_VMEM, IN_VMEM, IN_VMEM],
-        jax.ShapeDtypeStruct((len(heads), rows + STAT_ROWS, HD), jnp.bfloat16),
+        jax.ShapeDtypeStruct((HEADS, rows + STAT_ROWS, HD), jnp.bfloat16),
         IN_VMEM,
-        flops=4 * len(heads) * rows * rows * HD,
-        moved=8 * len(heads) * rows * HD,
-        exps=len(heads) * rows * rows,
+        flops=4 * HEADS * rows * rows * HD,
+        moved=8 * HEADS * rows * HD,
+        exps=HEADS * rows * rows,
     )(here, queries, keys, values)
 
 
-def near_kernel(
-    here_ref, picks_ref, query_ref, key_ref, value_ref, near_ref, out_ref, heads_ref, *, heads, shift, slots
-):
+def near_kernel(here_ref, picks_ref, query_ref, near_ref, out_ref, heads_ref, *, shift, slots):
     rows = query_ref.shape[0]
     here = here_ref[0]
     list_heads(heads_ref, 0, picks_ref, here, here - shift, slots)
-    own_heads(query_ref, key_ref, value_ref, out_ref, heads)
     for slot in range(slots):
         columns = head_columns(jnp.maximum(heads_ref[slot], 0))
         outputs, lines = attend_rows(
             query_ref[:, columns], near_ref[2 * slot], with_ones(near_ref[2 * slot + 1]), rows
         )
-        out_ref[len(heads) + slot, :rows, :] = outputs.astype(jnp.bfloat16)
-        out_ref[len(heads) + slot, rows:, :] = three_parts(lines)
-
-
-def near_part(here, picks, queries, keys, values, near, heads, shift, slots):
+        out_ref[slot, :rows, :] = outputs.astype(jnp.bfloat16)
+        out_ref[slot, rows:, :] = three_parts(lines)
+
+
+def near_part(here, picks, queries, near, shift, slots):
     rows = queries.shape[0]
-    total = len(heads) + slots
     return call(
-        functools.partial(near_kernel, heads=heads, shift=shift, slots=slots),
-        [SCALARS, SCALARS, IN_VMEM, IN_VMEM, IN_VMEM, IN_VMEM],
-        jax.ShapeDtypeStruct((total, rows + STAT_ROWS, HD), jnp.bfloat16),
+        functools.partial(near_kernel, shift=shift, slots=slots),
+        [SCALARS, SCALARS, IN_VMEM, IN_VMEM],
+        jax.ShapeDtypeStruct((slots, rows + STAT_ROWS, HD), jnp.bfloat16),
         IN_VMEM,
         [pltpu.SMEM((slots + 1,), jnp.int32)],
-        flops=HIGH_COST,
-        moved=12 * total * rows * HD,
-        exps=total * rows * rows,
-    )(here, picks, queries, keys, values, near)
+        flops=4 * slots * rows * rows * HD,
+        moved=12 * slots * rows * HD,
+        exps=slots * rows * rows,
+    )(here, picks, queries, near)
 
 
 def find_spots(spots_ref, found_ref, picks_ref, here, shifts, slots):
@@ -328,7 +320,7 @@
 def merge_kernel(here_ref, picks_ref, *refs, places, shifts, slots):
     count = len(places)
     parts = refs[:count]
-    out_ref, sums_ref, held, spots_ref, found_ref, sems = refs[count:]
+    result_ref, out_ref, sums_ref, held, spots_ref, found_ref, sems = refs[count:]
     groups = sums_ref.shape[1]
     rows = groups * LANES
     copies = [
@@ -359,6 +351,7 @@
                 weight = down_rows((share / whole)[group : group + 1, :])
                 mixed = mixed + (held[spot, span, :].astype(jnp.float32) - own) * weight
             out_ref[head, span, :] = mixed
+            result_ref[span, head_columns(head)] = mixed.astype(jnp.bfloat16)
         return carry
 
     lax.fori_loop(0, HEADS, one_head, 0, unroll=2)
@@ -372,10 +365,11 @@
         functools.partial(merge_kernel, places=tuple(places), shifts=shifts, slots=slots),
         [SCALARS, SCALARS] + [pl.BlockSpec(memory_space=pl.ANY)] * len(parts),
         [
+            jax.ShapeDtypeStruct((rows, HEADS * HD), jnp.bfloat16),
             jax.ShapeDtypeStruct((HEADS, rows, HD), jnp.float32),
             jax.ShapeDtypeStruct((HEADS, rows // LANES, LANES), jnp.float32),
         ],
-        [IN_VMEM, IN_VMEM],
+        [IN_VMEM, IN_VMEM, IN_VMEM],
         [
             pltpu.VMEM((total, rows + STAT_ROWS, HD), jnp.bfloat16),
             pltpu.SMEM((PICKS * HEADS,), jnp.int32),
@@ -388,58 +382,58 @@
 
 
 def finish_kernel(
-    here_ref, picks_ref, mixed_ref, sums_ref, part_ref, out_ref, spots_ref, found_ref, *, shift, slots
+    here_ref, picks_ref, mixed_ref, sums_ref, part_ref, old_ref, out_ref, heads_ref, held, sems, *, shift, slots
 ):
+    del old_ref
     groups = sums_ref.shape[1]
     rows = groups * LANES
-    step = pl.program_id(0)
-    per_step = HEADS // pl.num_programs(0)
-
-    @pl.when(step == 0)
-    def _():
-        find_spots(spots_ref, found_ref, picks_ref, here_ref[0], (shift,), slots)
-
-    for place in range(per_step):
-        head = step * per_step + place
-        spot = jnp.maximum(spots_ref[head * PICKS], spots_ref[head * PICKS + 1])
-        columns = pl.ds(place * HD, HD)
-
-        @pl.when(spot < 0)
+    here = here_ref[0]
+    list_heads(heads_ref, 0, picks_ref, here, here - shift, slots)
+
+    def patch(slot):
+        columns = head_columns(jnp.maximum(heads_ref[slot], 0))
+        return pltpu.make_async_copy(held.at[slot], out_ref.at[:, columns], sems.at[slot])
+
+    for slot in range(slots):
+
+        @pl.when(heads_ref[slot] >= 0)
         def _():
-            out_ref[:, columns] = mixed_ref[head].astype(jnp.bfloat16)
-
-        @pl.when(spot >= 0)
-        def _():
-            before = sums_ref[head]
-            added = stats_of(part_ref[spot, rows:, :], groups)
-            share = 1.0 / (1.0 + jnp.exp2(before - added))
+            head = heads_ref[slot]
+            added = stats_of(part_ref[slot, rows:, :], groups)
+            share = 1.0 / (1.0 + jnp.exp2(sums_ref[head] - added))
             for group in range(groups):
                 span = pl.ds(group * LANES, LANES)
                 old = mixed_ref[head, span, :]
-                new = part_ref[spot, span, :].astype(jnp.float32)
+                new = part_ref[slot, span, :].astype(jnp.float32)
                 mixed = old + (new - old) * down_rows(share[group : group + 1, :])
-                out_ref[span, columns] = mixed.astype(jnp.bfloat16)
-
-
-def finish(here, picks, mixed, sums, part, shift, slots):
+                held[slot, span, :] = mixed.astype(jnp.bfloat16)
+            patch(slot).start()
+
+    for slot in range(slots):
+
+        @pl.when(heads_ref[slot] >= 0)
+        def _():
+            patch(slot).wait()
+
+
+def finish(here, picks, result, mixed, sums, part, shift, slots):
     heads, rows, _ = mixed.shape
-    width = picks.shape[0]
-    steps = 4
     return pl.pallas_call(
         functools.partial(finish_kernel, shift=shift, slots=slots),
-        grid=(steps,),
-        in_specs=[SCALARS, SCALARS, IN_VMEM, IN_VMEM, IN_VMEM],
-        out_specs=pl.BlockSpec((rows, heads // steps * HD), lambda step: (0, step)),
-        out_shape=jax.ShapeDtypeStruct((rows, heads * HD), jnp.bfloat16),
+        in_specs=[SCALARS, SCALARS, IN_VMEM, IN_VMEM, IN_VMEM, IN_HBM],
+        out_specs=IN_HBM,
+        out_shape=jax.ShapeDtypeStruct(result.shape, result.dtype),
         scratch_shapes=[
-            pltpu.SMEM((PICKS * HEADS,), jnp.int32),
-            pltpu.SMEM((width,), jnp.int32),
+            pltpu.SMEM((slots + 1,), jnp.int32),
+            pltpu.VMEM((slots, rows, HD), jnp.bfloat16),
+            pltpu.SemaphoreType.DMA((slots,)),
         ],
+        input_output_aliases={5: 0},
         compiler_params=pltpu.CompilerParams(vmem_limit_bytes=VMEM_BYTES),
         cost_estimate=pl.CostEstimate(
-            flops=2 * heads * rows * HD, bytes_accessed=8 * heads * rows * HD, transcendentals=0
+            flops=2 * slots * rows * HD, bytes_accessed=8 * slots * rows * HD, transcendentals=0
         ),
-    )(here, picks, mixed, sums, part)
+    )(here, picks, mixed, sums, part, result)
 
 
 def after(value, *earlier):
@@ -448,13 +442,13 @@
 
 def groups_in_order(width, slots):
     middle = width // 2
-    groups = [[(1, 0, slots)], [(shift, 0, slots) for shift in (width - 2, width - 1)]]
+    groups = [[(middle, 0, slots)], [(shift, 0, slots) for shift in (1, width - 1)]]
     for low in range(3, middle):
         size = max(1, slots // 2)
         for first in range(0, slots, size):
             count = min(size, slots - first)
             groups.append([(low, first, count), (width - low, first, count)])
-    return groups + [[(middle, 0, slots)]]
+    return groups + [[(width - 2, 0, slots)]]
 
 
 def travelling_queries(queries, keys, values, picks):
@@ -486,13 +480,12 @@
 
     near_send = pack(here, own_picks, [keys, values], near_jobs, slots)[0]
     near = up(near_send, near_shift)
-    now = after(here, near_send)
-    packed = pack(now, own_picks, [queries], query_jobs, slots)
-    sends = {job[:3]: send for job, send in zip(query_jobs, packed)}
-    arrived = {
-        piece: down(sends[piece], piece[0]) for group in groups[:2] for piece in group
-    }
-    before = passed_along(own_picks, "pipe", 1)
+    sends, now = {}, after(here, near_send)
+    for jobs in (query_jobs[:1], query_jobs[1:]):
+        packed = pack(now, own_picks, [queries], jobs, slots)
+        sends |= {job[:3]: send for job, send in zip(jobs, packed)}
+        now = after(now, *packed)
+    arrived = {}
 
     def attend_group(token, group, is_anchor=False):
         return dict(
@@ -513,7 +506,8 @@
 
     def ask_for(group, *earlier):
         for piece in group:
-            arrived[piece] = down(after(sends[piece], *earlier), piece[0])
+            send = after(sends[piece], *earlier) if earlier else sends[piece]
+            arrived[piece] = down(send, piece[0])
 
     def send_back(parts):
         for piece, part in parts.items():
@@ -525,37 +519,31 @@
         return [found[piece] for piece in group]
 
     returned = {}
-    first_heads, other_heads = range(HEADS // 2), range(HEADS // 2, HEADS)
-    own = own_part(
-        after(here, before, sends[groups[0][0]]), queries, keys, values, first_heads
-    )
+    ask_for(groups[0])
+    own = own_part(now, queries, keys, values)
     own_back = passed_along(own, "pipe", 1)
-    ask_for(groups[2][:1], own, *those(arrived, groups[0]))
-    parts = attend_group(after(here, own), groups[0])
-    send_back(parts)
-    ask_for(groups[2][1:], *parts.values(), near, *those(arrived, groups[1]))
-    parts = attend_group(after(here, near, *parts.values()), groups[1], is_anchor=True)
-    send_back(parts)
-    now = after(here, *parts.values())
-    for number in range(2, len(groups)):
-        group = groups[number]
+    ask_for(groups[1], own)
+    now = after(here, own)
+    for number, group in enumerate(groups):
+        if number == 0:
+            ask_for(groups[2][:1], now, *those(arrived, group))
+        elif number == 1:
+            ask_for(groups[2][1:], now, *those(arrived, group))
+        elif number + 1 < len(groups):
+            ask_for(groups[number + 1], now, *those(arrived, group))
+        if number == 2:
+            now = after(now, own_back)
         if number == len(groups) - 1:
-            now = tick(now, list(returned.values())[-4])
-        if number == 2:
-            ask_for(groups[number + 1], now, *those(arrived, group))
-            now = after(now, own_back)
-        parts = attend_group(now, group, is_anchor=number == 2)
+            now = tick(now, *list(returned.values())[-4:-2])
+        parts = attend_group(now, group, is_anchor=number in (1, 2))
         send_back(parts)
         now = after(now, *parts.values())
-        if number == 2:
-            now = after(now, list(returned.values())[-4])
-            beside = near_part(
-                now, own_picks, queries, keys, values, near, other_heads, near_shift, slots
-            )
-            beside_back = passed_along(after(beside, *those(arrived, groups[3])), "pipe", 1)
+        if number == 0:
+            beside = near_part(now, own_picks, queries, near, near_shift, slots)
             now = after(now, beside)
-        if 2 <= number < len(groups) - 2:
-            ask_for(groups[number + 2], now, *those(arrived, groups[number + 1]))
+        if number == 3:
+            beside_back = passed_along(after(beside, *parts.values()), "pipe", 1)
+    before = passed_along(after(own_picks, now), "pipe", 1)
     now = tick(now)
 
     final = groups[-1][0]
@@ -564,8 +552,9 @@
     pieces = [piece for piece in returned if piece != final]
     places = [HEADS + merged_shifts.index(shift) * slots + first for shift, first, _ in pieces]
     parts = [own_back, beside_back] + [returned[piece] for piece in pieces]
-    mixed, sums = merge(now, before, parts, [0, len(first_heads)] + places, merged_shifts, slots)
-    return finish(now, before, mixed, sums, returned[final], final[0], slots)[None]
+    result, mixed, sums = merge(now, before, parts, [0, HEADS] + places, merged_shifts, slots)
+    result = finish(now, before, result, mixed, sums, returned[final], final[0], slots)
+    return result[None]
 
 
 def travelling_keys(queries, keys, values, picks):

time: 153 us -> 150 us (0.980)
  the two profiles are of different devices: /device:TPU:28 before, /device:TPU:26 now
where the time goes in v8:
time: 150 us; the launch traced here: 148 us
  starting transfers between devices  60.4 us (40%)
  Pallas kernels  50.8 us (34%)
  waiting for transfers between devices  32.5 us (22%)
  local copies, waits for them, and re-layouts  3.38 us (2%)
    ppermute x8, starting transfers between devices, down(): lax.ppermute(value, 'ctx', [(at, at - shift) for at in range(shift, width)])  47.9 us
    ppermute x8, waiting for transfers between devices, up_and_on(): return lax.ppermute(value, ('ctx', 'pipe'), pairs)  31.7 us
    pallas_call x5, Pallas kernels, attend(): call(functools.partial(attend_kernel, group=group, slots=slots), [SCALARS...  19.2 us
    ppermute x8, starting transfers between devices, up_and_on(): return lax.ppermute(value, ('ctx', 'pipe'), pairs)  11.1 us
    pallas_call x1, Pallas kernels, own_part(): call(own_kernel, [SCALARS, IN_VMEM, IN_VMEM, IN_VMEM], jax.ShapeDtypeStru...  8.95 us
    pallas_call x1, Pallas kernels, merge(): call(functools.partial(merge_kernel, places=tuple(places), shifts=shifts,...  8.2 us
    pallas_call x3, Pallas kernels, pack(): call(functools.partial(pack_kernel, jobs=jobs, slots=slots), [SCALARS, SC...  6.14 us
    pallas_call x1, Pallas kernels, near_part(): call(functools.partial(near_kernel, shift=shift, slots=slots), [SCALARS,...  3.44 us
  transfers between devices with their start and end apart: 20, of which 5 were waited for; matrix products, arithmetic and copies ran while one was open for 0% of the time, Pallas kernels for 31%

profile of v8, /device:TPU:26, one launch (start us, length us, event | category | flops | bytes accessed | tf_op | source)
XLA Modules:
  0.0 147.6 jit_solution(13662936545131277784)
XLA Ops:
  0.0 1.6 %copy-done = bf16[1,512,2048]{2,1,0:T(8,128)(2,1)S(1)} copy-done((bf16[1,512,2048]{2,1,0:T(8,128)(2,1)S(1)}, bf16[1,512,2048]{2,1,0:T(8,128)(2,1)}, u32[]{:S(2)}) %copy-start) | copy-done | bytes 2097176
  1.6 1.6 %copy-done.2 = bf16[1,512,2048]{2,1,0:T(8,128)(2,1)S(1)} copy-done((bf16[1,512,2048]{2,1,0:T(8,128)(2,1)S(1)}, bf16[1,512,2048]{2,1,0:T(8,128)(2,1)}, u32[]{:S(2)}) %copy-start.2) | copy-done | bytes 2097176
  3.2 1.4 shard_map.46
  4.6 1.3 collective-permute-start.1
  5.9 0.0 copy-start.1
  5.9 0.0 copy-start.3
  5.9 1.2 shard_map.47
  7.2 4.5 %collective-permute-start = (bf16[4,512,128]{2,1,0:T(8,128)(2,1)S(1)}, bf16[4,512,128]{2,1,0:T(8,128)(2,1)S(1)}, u32[]{:S(2)}, u32[]{:S(2)}) collective-permute-start(bf16[4,512,128]{2,1,0:T(8,128)(2,1)S(1)} %shard_map.47), channel_id=1, source_target_pairs={{16,0},{20,4},{24,8},{28,12},{17,1},{21,5},{25,9},{29,13},{18,2},{... | collective-permute-start | bytes 1572872 | tf_op jit(solution)/shard_map/ppermute | solution.py:471
  11.6 3.5 %shard_map.48 = (bf16[4,512,128]{2,1,0:T(8,128)(2,1)S(1)}, bf16[4,512,128]{2,1,0:T(8,128)(2,1)S(1)}, bf16[2,512,128]{2,1,0:T(8,128)(2,1)}, bf16[2,512,128]{2,1,0...) custom-call(s32[1]{0:T(128)} %bitcast.here_ref, ...), custom_call_target="tpu_custom_call" | custom-call | bytes 5242880 | tf_op jit(solution)/shard_map/pallas_call | solution.py:127
  15.2 9.0 %shard_map.49 = bf16[16,528,128]{2,1,0:T(8,128)(2,1)} custom-call(s32[1]{0:T(128)} %bitcast.here_ref, bf16[512,2048]{1,0:T(8,128)(2,1)S(1)} %bitcast.24, bf16[512,2048]{1,0:T(8,128)(2,1)S(1)} %bitcast.9, bf16[512,2048]{1,0:T(8,128)(2,1)S(1)} %bitcast.16), custom_call_target="tpu_custom_call" | custom-call | flops 2147483648 | bytes 8388608 | tf_op jit(solution)/shard_map/pallas_call | solution.py:266
  24.1 3.4 %collective-permute-start.2 = (bf16[4,512,128]{2,1,0:T(8,128)(2,1)S(1)}, bf16[4,512,128]{2,1,0:T(8,128)(2,1)S(1)}, u32[]{:S(2)}, u32[]{:S(2)}) collective-permute-start(bf16[4,512,128]{2,1,0:T(8,128)(2,1)S(1)} %get-tuple-element.60), channel_id=1, source_target_pairs={{4,0},{8,4},{12,8},{16,12},{20,16},{24,20},{28,24},{5,1},{9,5},{13... | collective-permute-start | bytes 1572872 | tf_op jit(solution)/shard_map/ppermute | solution.py:471
  27.5 0.7 collective-permute-start.3
  28.2 0.1 collective-permute-start.4
  28.3 0.0 collective-permute-done.refs_0_
  28.3 3.5 %shard_map.50 = bf16[4,528,128]{2,1,0:T(8,128)(2,1)} custom-call(s32[1]{0:T(128)} %bitcast.here_ref, s32[8,2,16]{2,1,0:T(2,128)} %bitcast.2.picks_ref, bf16[512,2048]{1,0:T(8,128)(2,1)S(1)} %bitcast.10, bf16[512,2048]{1,0:T(8,128)(2,1)S(1)} %bitcast.17, bf16[4,512,128]{2,1,0:T(8,128)(2,1)S(1)} %collective-permute-done.refs_0_), custom_call_target="tpu_custom_call" | custom-call | flops 536870912 | bytes 2097152 | tf_op jit(solution)/shard_map/pallas_call | solution.py:226
  31.8 1.3 collective-permute-start.9
  33.1 0.0 collective-permute-done.1.near_ref
  33.1 7.8 %collective-permute-start.5 = (bf16[2,512,128]{2,1,0:T(8,128)(2,1)}, bf16[2,512,128]{2,1,0:T(8,128)(2,1)}, u32[]{:S(2)}, u32[]{:S(2)}) collective-permute-start(bf16[2,512,128]{2,1,0:T(8,128)(2,1)} %get-tuple-element.66), channel_id=1, source_target_pairs={{12,0},{16,4},{20,8},{24,12},{28,16},{13,1},{17,5},{21,9},{25,13},... | collective-permute-start | bytes 786440 | tf_op jit(solution)/shard_map/ppermute | solution.py:471
  40.9 3.4 %shard_map.51 = bf16[4,528,128]{2,1,0:T(8,128)(2,1)} custom-call(s32[1]{0:T(128)} %bitcast.here_ref, s32[8,2,16]{2,1,0:T(2,128)} %bitcast.2.picks_ref, bf16[512,2048]{1,0:T(8,128)(2,1)S(1)} %bitcast.25, bf16[8,512,128]{2,1,0:T(8,128)(2,1)S(1)} %collective-permute-done.1.near_ref), custom_call_target="tpu_custom_call" | custom-call | flops 536870912 | bytes 3145728 | tf_op jit(solution)/shard_map/pallas_call | solution.py:292
  44.3 17.8 %collective-permute-start.6 = (bf16[2,512,128]{2,1,0:T(8,128)(2,1)}, bf16[2,512,128]{2,1,0:T(8,128)(2,1)}, u32[]{:S(2)}, u32[]{:S(2)}) collective-permute-start(bf16[2,512,128]{2,1,0:T(8,128)(2,1)} %get-tuple-element.67), channel_id=1, source_target_pairs={{20,0},{24,4},{28,8},{21,1},{25,5},{29,9},{22,2},{26,6},{30,10},{2... | collective-permute-start | bytes 786440 | tf_op jit(solution)/shard_map/ppermute | solution.py:471
  62.2 4.8 %shard_map.52 = (bf16[4,528,128]{2,1,0:T(8,128)(2,1)}, bf16[4,528,128]{2,1,0:T(8,128)(2,1)}) custom-call(s32[1]{0:T(128)} %bitcast.here_ref, s32[8,2,16]{2,1,0:T(2,128)} %bitcast.2.picks_ref, bf16[512,2048]{1,0:T(8,128)(2,1)S(1)} %bitcast.11, bf16[512,2048]{1,0:T(8,128)(2,1)S(1)} %bitcast.18, bf16[4,512,128]{2,1,0:T(8,128)(2,1)S(1)} %collective-permute-done.2.refs_0_, ...), custom_call_target="tpu_custom_call" | custom-call | flops 999999995904 | bytes 4194304 | tf_op jit(solution)/shard_map/pallas_call | solution.py:226
  67.0 1.9 %collective-permute-start.11 = (bf16[4,528,128]{2,1,0:T(8,128)(2,1)}, bf16[4,528,128]{2,1,0:T(8,128)(2,1)}, u32[]{:S(2)}, u32[]{:S(2)}) collective-permute-start(bf16[4,528,128]{2,1,0:T(8,128)(2,1)} %get-tuple-element.62), channel_id=1, source_target_pairs={{0,5},{1,6},{2,7},{3,4},{4,9},{5,10},{6,11},{7,8},{8,13},{9,14},{1... | collective-permute-start | bytes 1622024 | tf_op jit(solution)/shard_map/ppermute | solution.py:479
  68.9 0.0 collective-permute-done.5.refs_0_
  68.9 1.5 collective-permute-start.16
  70.4 0.0 collective-permute-done.6.refs_1_
  70.4 4.5 %collective-permute-start.7 = (bf16[2,512,128]{2,1,0:T(8,128)(2,1)}, bf16[2,512,128]{2,1,0:T(8,128)(2,1)}, u32[]{:S(2)}, u32[]{:S(2)}) collective-permute-start(bf16[2,512,128]{2,1,0:T(8,128)(2,1)} %get-tuple-element.71), channel_id=1, source_target_pairs={{12,0},{16,4},{20,8},{24,12},{28,16},{13,1},{17,5},{21,9},{25,13},... | collective-permute-start | bytes 786440 | tf_op jit(solution)/shard_map/ppermute | solution.py:471
  74.9 0.0 collective-permute-done.4.refs_0_
  74.9 3.1 %collective-permute-start.8 = (bf16[2,512,128]{2,1,0:T(8,128)(2,1)}, bf16[2,512,128]{2,1,0:T(8,128)(2,1)}, u32[]{:S(2)}, u32[]{:S(2)}) collective-permute-start(bf16[2,512,128]{2,1,0:T(8,128)(2,1)} %get-tuple-element.72), channel_id=1, source_target_pairs={{20,0},{24,4},{28,8},{21,1},{25,5},{29,9},{22,2},{26,6},{30,10},{2... | collective-permute-start | bytes 786440 | tf_op jit(solution)/shard_map/ppermute | solution.py:471
  78.1 2.9 %shard_map.53 = (bf16[2,528,128]{2,1,0:T(8,128)(2,1)S(1)}, bf16[2,528,128]{2,1,0:T(8,128)(2,1)S(1)}) custom-call(s32[1]{0:T(128)} %bitcast.here_ref, s32[8,2,16]{2,1,0:T(2,128)} %bitcast.2.picks_ref, bf16[512,2048]{1,0:T(8,128)(2,1)S(1)} %bitcast.12, bf16[512,2048]{1,0:T(8,128)(2,1)S(1)} %bitcast.19, bf16[2,512,128]{2,1,0:T(8,128)(2,1)} %collective-permute-done.5.refs_0_, ...), custom_call_target="tpu_custom_call" | custom-call | flops 999999995904 | bytes 2097152 | tf_op jit(solution)/shard_map/pallas_call | solution.py:226
  81.0 12.5 %collective-permute-done.11.refs_3_ = bf16[4,528,128]{2,1,0:T(8,128)(2,1)} collective-permute-done((bf16[4,528,128]{2,1,0:T(8,128)(2,1)}, bf16[4,528,128]{2,1,0:T(8,128)(2,1)}, u32[]{:S(2)}, u32[]{:S(2)}) %collective-permute-start.11) | collective-permute-done | bytes 540704 | tf_op jit(solution)/shard_map/ppermute | solution.py:479
  93.5 1.3 collective-permute-start.12
  94.8 1.3 collective-permute-start.10
  96.1 3.6 %shard_map.54 = (bf16[2,528,128]{2,1,0:T(8,128)(2,1)}, bf16[2,528,128]{2,1,0:T(8,128)(2,1)}) custom-call(s32[1]{0:T(128)} %bitcast.here_ref, s32[8,2,16]{2,1,0:T(2,128)} %bitcast.2.picks_ref, bf16[512,2048]{1,0:T(8,128)(2,1)S(1)} %bitcast.13, bf16[512,2048]{1,0:T(8,128)(2,1)S(1)} %bitcast.20, bf16[2,512,128]{2,1,0:T(8,128)(2,1)} %collective-permute-done.7.refs_0_, ...), custom_call_target="tpu_custom_call" | custom-call | flops 536870912 | bytes 2097152 | tf_op jit(solution)/shard_map/pallas_call | solution.py:226
  99.7 6.1 %collective-permute-start.13 = (bf16[4,512,128]{2,1,0:T(8,128)(2,1)}, bf16[4,512,128]{2,1,0:T(8,128)(2,1)}, u32[]{:S(2)}, u32[]{:S(2)}) collective-permute-start(bf16[4,512,128]{2,1,0:T(8,128)(2,1)} %get-tuple-element.79), channel_id=1, source_target_pairs={{24,0},{28,4},{25,1},{29,5},{26,2},{30,6},{27,3},{31,7}} | collective-permute-start | bytes 1572872 | tf_op jit(solution)/shard_map/ppermute | solution.py:471
  105.8 1.3 collective-permute-start.17
  107.1 0.1 collective-permute-start.15
  107.2 12.1 %collective-permute-done.10.refs_5_ = bf16[2,528,128]{2,1,0:T(8,128)(2,1)S(1)} collective-permute-done((bf16[2,528,128]{2,1,0:T(8,128)(2,1)S(1)}, bf16[2,528,128]{2,1,0:T(8,128)(2,1)S(1)}, u32[]{:S(2)}, u32[]{:S(2)}) %collective-permute-start.10) | collective-permute-done | bytes 270368 | tf_op jit(solution)/shard_map/ppermute | solution.py:479
  119.3 0.5 shard_map.55.here_ref
  119.8 0.2 copy-done.7
  120.0 1.3 collective-permute-start.18
  121.3 4.4 %shard_map.56 = bf16[4,528,128]{2,1,0:T(8,128)(2,1)} custom-call(s32[1]{0:T(128)} %shard_map.55.here_ref, s32[8,2,16]{2,1,0:T(2,128)} %bitcast.2.picks_ref, bf16[512,2048]{1,0:T(8,128)(2,1)S(1)} %bitcast.14, bf16[512,2048]{1,0:T(8,128)(2,1)S(1)} %bitcast.21, bf16[4,512,128]{2,1,0:T(8,128)(2,1)} %collective-permute-done.13.refs_0_), custom_call_target="tpu_custom_call" | custom-call | flops 536870912 | bytes 2097152 | tf_op jit(solution)/shard_map/pallas_call | solution.py:226
  125.7 1.3 collective-permute-start.19
  127.0 1.2 shard_map.57.here_ref
  128.2 0.9 collective-permute-done.14.picks_ref
  129.1 4.3 %collective-permute-done.18.refs_8_ = bf16[2,528,128]{2,1,0:T(8,128)(2,1)} collective-permute-done((bf16[2,528,128]{2,1,0:T(8,128)(2,1)}, bf16[2,528,128]{2,1,0:T(8,128)(2,1)}, u32[]{:S(2)}, u32[]{:S(2)}) %collective-permute-start.18) | collective-permute-done | bytes 270368 | tf_op jit(solution)/shard_map/ppermute | solution.py:479
  133.4 8.2 %shard_map.58 = (bf16[512,2048]{1,0:T(8,128)(2,1)}, f32[16,512,128]{2,1,0:T(8,128)S(1)}, f32[16,4,128]{2,1,0:T(4,128)S(1)}) custom-call(s32[1]{0:T(128)} %shard_map.57.here_ref, s32[8,2,16]{2,1,0:T(2,128)} %collective-permute-done.14.picks_ref, bf16[16,528,128]{2,1,0:T(8,128)(2,1)} %collective-permute-done.4.refs_0_, ...), custom_call_target="tpu_custom_call" | custom-call | flops 6291456 | bytes 9437184 | tf_op jit(solution)/shard_map/pallas_call | solution.py:364
  141.6 2.7 %collective-permute-done.19.part_ref = bf16[4,528,128]{2,1,0:T(8,128)(2,1)} collective-permute-done((bf16[4,528,128]{2,1,0:T(8,128)(2,1)}, bf16[4,528,128]{2,1,0:T(8,128)(2,1)}, u32[]{:S(2)}, u32[]{:S(2)}) %collective-permute-start.19) | collective-permute-done | bytes 540704 | tf_op jit(solution)/shard_map/ppermute | solution.py:479
  144.3 3.1 %shard_map.59 = bf16[512,2048]{1,0:T(8,128)(2,1)} custom-call(s32[1]{0:T(128)} %shard_map.57.here_ref, s32[8,2,16]{2,1,0:T(2,128)} %collective-permute-done.14.picks_ref, f32[16,512,128]{2,1,0:T(8,128)S(1)} %get-tuple-element.85.mixed_ref, f32[16,4,128]{2,1,0:T(4,128)S(1)} %get-tuple-element.86.sums_ref, ...), custom_call_target="tpu_custom_call", output_to_operand_aliasing={{}: (5, {})} | custom-call | flops 524288 | bytes 2097152 | tf_op jit(solution)/shard_map/pallas_call | solution.py:421
  (24 shorter events, 0.1 us)
Async XLA Ops:
  0.0 1.6 %copy-start = (bf16[1,512,2048]{2,1,0:T(8,128)(2,1)S(1)}, bf16[1,512,2048]{2,1,0:T(8,128)(2,1)}, u32[]{:S(2)}) copy-start(bf16[1,512,2048]{2,1,0:T(8,128)(2,1)} %param.5) | copy-start | bytes 6291460
  1.6 1.6 %copy-start.2 = (bf16[1,512,2048]{2,1,0:T(8,128)(2,1)S(1)}, bf16[1,512,2048]{2,1,0:T(8,128)(2,1)}, u32[]{:S(2)}) copy-start(bf16[1,512,2048]{2,1,0:T(8,128)(2,1)} %param.6) | copy-start | bytes 6291460
  3.2 2.7 %copy-start.4 = (bf16[1,512,2048]{2,1,0:T(8,128)(2,1)S(1)}, bf16[1,512,2048]{2,1,0:T(8,128)(2,1)}, u32[]{:S(2)}) copy-start(bf16[1,512,2048]{2,1,0:T(8,128)(2,1)} %param.4) | copy-start | bytes 6291460
  4.6 28.5 %collective-permute-start.1 = (bf16[8,512,128]{2,1,0:T(8,128)(2,1)S(1)}, bf16[8,512,128]{2,1,0:T(8,128)(2,1)S(1)}, u32[]{:S(2)}, u32[]{:S(2)}) collective-permute-start(bf16[8,512,128]{2,1,0:T(8,128)(2,1)S(1)} %shard_map.46), channel_id=1, source_target_pairs={{0,8},{4,12},{8,16},{12,20},{16,24},{20,28},{1,9},{5,13},{9,17},{1... | collective-permute-start | bytes 3145736 | tf_op jit(solution)/shard_map/ppermute | solution.py:468
  5.9 9.2 %copy-start.1 = (bf16[1,512,2048]{2,1,0:T(8,128)(2,1)S(1)}, bf16[1,512,2048]{2,1,0:T(8,128)(2,1)}, u32[]{:S(2)}) copy-start(bf16[1,512,2048]{2,1,0:T(8,128)(2,1)} %param.5) | copy-start | bytes 6291460
  5.9 9.2 %copy-start.3 = (bf16[1,512,2048]{2,1,0:T(8,128)(2,1)S(1)}, bf16[1,512,2048]{2,1,0:T(8,128)(2,1)}, u32[]{:S(2)}) copy-start(bf16[1,512,2048]{2,1,0:T(8,128)(2,1)} %param.6) | copy-start | bytes 6291460
  7.2 21.1 %collective-permute-start = (bf16[4,512,128]{2,1,0:T(8,128)(2,1)S(1)}, bf16[4,512,128]{2,1,0:T(8,128)(2,1)S(1)}, u32[]{:S(2)}, u32[]{:S(2)}) collective-permute-start(bf16[4,512,128]{2,1,0:T(8,128)(2,1)S(1)} %shard_map.47), channel_id=1, source_target_pairs={{16,0},{20,4},{24,8},{28,12},{17,1},{21,5},{25,9},{29,13},{18,2},{... | collective-permute-start | bytes 1572872 | tf_op jit(solution)/shard_map/ppermute | solution.py:471
  24.1 20.2 %collective-permute-start.2 = (bf16[4,512,128]{2,1,0:T(8,128)(2,1)S(1)}, bf16[4,512,128]{2,1,0:T(8,128)(2,1)S(1)}, u32[]{:S(2)}, u32[]{:S(2)}) collective-permute-start(bf16[4,512,128]{2,1,0:T(8,128)(2,1)S(1)} %get-tuple-element.60), channel_id=1, source_target_pairs={{4,0},{8,4},{12,8},{16,12},{20,16},{24,20},{28,24},{5,1},{9,5},{13... | collective-permute-start | bytes 1572872 | tf_op jit(solution)/shard_map/ppermute | solution.py:471
  27.5 16.8 %collective-permute-start.3 = (bf16[4,512,128]{2,1,0:T(8,128)(2,1)S(1)}, bf16[4,512,128]{2,1,0:T(8,128)(2,1)S(1)}, u32[]{:S(2)}, u32[]{:S(2)}) collective-permute-start(bf16[4,512,128]{2,1,0:T(8,128)(2,1)S(1)} %get-tuple-element.61), channel_id=1, source_target_pairs={{28,0},{29,1},{30,2},{31,3}} | collective-permute-start | bytes 1572872 | tf_op jit(solution)/shard_map/ppermute | solution.py:471
  28.2 46.7 %collective-permute-start.4 = (bf16[16,528,128]{2,1,0:T(8,128)(2,1)}, bf16[16,528,128]{2,1,0:T(8,128)(2,1)}, u32[]{:S(2)}, u32[]{:S(2)}) collective-permute-start(bf16[16,528,128]{2,1,0:T(8,128)(2,1)} %shard_map.49), channel_id=1, source_target_pairs={{0,1},{1,2},{2,3},{3,0},{4,5},{5,6},{6,7},{7,4},{8,9},{9,10},{10,1... | collective-permute-start | bytes 6488072 | tf_op jit(solution)/shard_map/ppermute | solution.py:24
  31.8 49.2 %collective-permute-start.9 = (bf16[4,528,128]{2,1,0:T(8,128)(2,1)}, bf16[4,528,128]{2,1,0:T(8,128)(2,1)}, u32[]{:S(2)}, u32[]{:S(2)}) collective-permute-start(bf16[4,528,128]{2,1,0:T(8,128)(2,1)} %shard_map.50), channel_id=1, source_target_pairs={{0,17},{1,18},{2,19},{3,16},{4,21},{5,22},{6,23},{7,20},{8,25},{9,... | collective-permute-start | bytes 1622024 | tf_op jit(solution)/shard_map/ppermute | solution.py:479
  33.1 35.8 %collective-permute-start.5 = (bf16[2,512,128]{2,1,0:T(8,128)(2,1)}, bf16[2,512,128]{2,1,0:T(8,128)(2,1)}, u32[]{:S(2)}, u32[]{:S(2)}) collective-permute-start(bf16[2,512,128]{2,1,0:T(8,128)(2,1)} %get-tuple-element.66), channel_id=1, source_target_pairs={{12,0},{16,4},{20,8},{24,12},{28,16},{13,1},{17,5},{21,9},{25,13},... | collective-permute-start | bytes 786440 | tf_op jit(solution)/shard_map/ppermute | solution.py:471
  44.3 26.1 %collective-permute-start.6 = (bf16[2,512,128]{2,1,0:T(8,128)(2,1)}, bf16[2,512,128]{2,1,0:T(8,128)(2,1)}, u32[]{:S(2)}, u32[]{:S(2)}) collective-permute-start(bf16[2,512,128]{2,1,0:T(8,128)(2,1)} %get-tuple-element.67), channel_id=1, source_target_pairs={{20,0},{24,4},{28,8},{21,1},{25,5},{29,9},{22,2},{26,6},{30,10},{2... | collective-permute-start | bytes 786440 | tf_op jit(solution)/shard_map/ppermute | solution.py:471
  67.0 26.5 %collective-permute-start.11 = (bf16[4,528,128]{2,1,0:T(8,128)(2,1)}, bf16[4,528,128]{2,1,0:T(8,128)(2,1)}, u32[]{:S(2)}, u32[]{:S(2)}) collective-permute-start(bf16[4,528,128]{2,1,0:T(8,128)(2,1)} %get-tuple-element.62), channel_id=1, source_target_pairs={{0,5},{1,6},{2,7},{3,4},{4,9},{5,10},{6,11},{7,8},{8,13},{9,14},{1... | collective-permute-start | bytes 1622024 | tf_op jit(solution)/shard_map/ppermute | solution.py:479
  68.9 36.9 %collective-permute-start.16 = (bf16[4,528,128]{2,1,0:T(8,128)(2,1)}, bf16[4,528,128]{2,1,0:T(8,128)(2,1)}, u32[]{:S(2)}, u32[]{:S(2)}) collective-permute-start(bf16[4,528,128]{2,1,0:T(8,128)(2,1)} %get-tuple-element.63), channel_id=1, source_target_pairs={{0,29},{1,30},{2,31},{3,28}} | collective-permute-start | bytes 1622024 | tf_op jit(solution)/shard_map/ppermute | solution.py:479
  70.4 25.7 %collective-permute-start.7 = (bf16[2,512,128]{2,1,0:T(8,128)(2,1)}, bf16[2,512,128]{2,1,0:T(8,128)(2,1)}, u32[]{:S(2)}, u32[]{:S(2)}) collective-permute-start(bf16[2,512,128]{2,1,0:T(8,128)(2,1)} %get-tuple-element.71), channel_id=1, source_target_pairs={{12,0},{16,4},{20,8},{24,12},{28,16},{13,1},{17,5},{21,9},{25,13},... | collective-permute-start | bytes 786440 | tf_op jit(solution)/shard_map/ppermute | solution.py:471
  74.9 21.2 %collective-permute-start.8 = (bf16[2,512,128]{2,1,0:T(8,128)(2,1)}, bf16[2,512,128]{2,1,0:T(8,128)(2,1)}, u32[]{:S(2)}, u32[]{:S(2)}) collective-permute-start(bf16[2,512,128]{2,1,0:T(8,128)(2,1)} %get-tuple-element.72), channel_id=1, source_target_pairs={{20,0},{24,4},{28,8},{21,1},{25,5},{29,9},{22,2},{26,6},{30,10},{2... | collective-permute-start | bytes 786440 | tf_op jit(solution)/shard_map/ppermute | solution.py:471
  93.5 13.7 %collective-permute-start.12 = (bf16[2,528,128]{2,1,0:T(8,128)(2,1)S(1)}, bf16[2,528,128]{2,1,0:T(8,128)(2,1)S(1)}, u32[]{:S(2)}, u32[]{:S(2)}) collective-permute-start(bf16[2,528,128]{2,1,0:T(8,128)(2,1)S(1)} %get-tuple-element.77), channel_id=1, source_target_pairs={{0,21},{1,22},{2,23},{3,20},{4,25},{5,26},{6,27},{7,24},{8,29},{9,... | collective-permute-start | bytes 811016 | tf_op jit(solution)/shard_map/ppermute | solution.py:479
  94.8 24.6 %collective-permute-start.10 = (bf16[2,528,128]{2,1,0:T(8,128)(2,1)S(1)}, bf16[2,528,128]{2,1,0:T(8,128)(2,1)S(1)}, u32[]{:S(2)}, u32[]{:S(2)}) collective-permute-start(bf16[2,528,128]{2,1,0:T(8,128)(2,1)S(1)} %get-tuple-element.76), channel_id=1, source_target_pairs={{0,13},{1,14},{2,15},{3,12},{4,17},{5,18},{6,19},{7,16},{8,21},{9,... | collective-permute-start | bytes 811016 | tf_op jit(solution)/shard_map/ppermute | solution.py:479
  99.7 21.6 %collective-permute-start.13 = (bf16[4,512,128]{2,1,0:T(8,128)(2,1)}, bf16[4,512,128]{2,1,0:T(8,128)(2,1)}, u32[]{:S(2)}, u32[]{:S(2)}) collective-permute-start(bf16[4,512,128]{2,1,0:T(8,128)(2,1)} %get-tuple-element.79), channel_id=1, source_target_pairs={{24,0},{28,4},{25,1},{29,5},{26,2},{30,6},{27,3},{31,7}} | collective-permute-start | bytes 1572872 | tf_op jit(solution)/shard_map/ppermute | solution.py:471
  105.8 22.4 %collective-permute-start.17 = (bf16[2,528,128]{2,1,0:T(8,128)(2,1)}, bf16[2,528,128]{2,1,0:T(8,128)(2,1)}, u32[]{:S(2)}, u32[]{:S(2)}) collective-permute-start(bf16[2,528,128]{2,1,0:T(8,128)(2,1)} %get-tuple-element.83), channel_id=1, source_target_pairs={{0,13},{1,14},{2,15},{3,12},{4,17},{5,18},{6,19},{7,16},{8,21},{9,... | collective-permute-start | bytes 811016 | tf_op jit(solution)/shard_map/ppermute | solution.py:479
  107.1 26.3 %collective-permute-start.15 = (bf16[4,528,128]{2,1,0:T(8,128)(2,1)}, bf16[4,528,128]{2,1,0:T(8,128)(2,1)}, u32[]{:S(2)}, u32[]{:S(2)}) collective-permute-start(bf16[4,528,128]{2,1,0:T(8,128)(2,1)} %shard_map.51), channel_id=1, source_target_pairs={{0,1},{1,2},{2,3},{3,0},{4,5},{5,6},{6,7},{7,4},{8,9},{9,10},{10,1... | collective-permute-start | bytes 1622024 | tf_op jit(solution)/shard_map/ppermute | solution.py:24
  107.2 12.7 %copy-start.5 = (bf16[2,528,128]{2,1,0:T(8,128)(2,1)}, bf16[2,528,128]{2,1,0:T(8,128)(2,1)S(1)}, u32[]{:S(2)}) copy-start(bf16[2,528,128]{2,1,0:T(8,128)(2,1)S(1)} %collective-permute-done.12.refs_6_) | copy-start | bytes 811012
  119.3 0.7 copy-start.7
  120.0 13.3 %collective-permute-start.18 = (bf16[2,528,128]{2,1,0:T(8,128)(2,1)}, bf16[2,528,128]{2,1,0:T(8,128)(2,1)}, u32[]{:S(2)}, u32[]{:S(2)}) collective-permute-start(bf16[2,528,128]{2,1,0:T(8,128)(2,1)} %get-tuple-element.84), channel_id=1, source_target_pairs={{0,21},{1,22},{2,23},{3,20},{4,25},{5,26},{6,27},{7,24},{8,29},{9,... | collective-permute-start | bytes 811016 | tf_op jit(solution)/shard_map/ppermute | solution.py:479
  125.7 3.4 %collective-permute-start.14 = (s32[8,2,16]{2,1,0:T(2,128)}, s32[8,2,16]{2,1,0:T(2,128)}, u32[]{:S(2)}, u32[]{:S(2)}) collective-permute-start(s32[8,2,16]{2,1,0:T(2,128)} %bitcast.2.picks_ref), channel_id=1, source_target_pairs={{0,1},{1,2},{2,3},{3,0},{4,5},{5,6},{6,7},{7,4},{8,9},{9,10},{10,1... | collective-permute-start | bytes 3080 | tf_op jit(solution)/shard_map/ppermute | solution.py:24
  125.7 18.6 %collective-permute-start.19 = (bf16[4,528,128]{2,1,0:T(8,128)(2,1)}, bf16[4,528,128]{2,1,0:T(8,128)(2,1)}, u32[]{:S(2)}, u32[]{:S(2)}) collective-permute-start(bf16[4,528,128]{2,1,0:T(8,128)(2,1)} %shard_map.56), channel_id=1, source_target_pairs={{0,25},{1,26},{2,27},{3,24},{4,29},{5,30},{6,31},{7,28}} | collective-permute-start | bytes 1622024 | tf_op jit(solution)/shard_map/ppermute | solution.py:479
  127.0 6.4 %copy-start.6 = (bf16[2,528,128]{2,1,0:T(8,128)(2,1)S(1)}, bf16[2,528,128]{2,1,0:T(8,128)(2,1)}, u32[]{:S(2)}) copy-start(bf16[2,528,128]{2,1,0:T(8,128)(2,1)} %copy-done.5) | copy-start | bytes 811012
  127.0 6.4 %copy-start.8 = (bf16[2,528,128]{2,1,0:T(8,128)(2,1)S(1)}, bf16[2,528,128]{2,1,0:T(8,128)(2,1)}, u32[]{:S(2)}) copy-start(bf16[2,528,128]{2,1,0:T(8,128)(2,1)} %copy-done.7) | copy-start | bytes 811012

commit v9 on v8

--- a/solution.py
+++ b/solution.py
@@ -72,7 +72,7 @@
         [SCALARS],
         jax.ShapeDtypeStruct((1,), jnp.int32),
         SCALARS,
-        flops=HIGH_COST,
+        flops=0,
     )(after(here, *earlier))
 
 
@@ -274,31 +274,34 @@
     )(here, queries, keys, values)
 
 
-def near_kernel(here_ref, picks_ref, query_ref, near_ref, out_ref, heads_ref, *, shift, slots):
+def near_kernel(here_ref, picks_ref, query_ref, *refs, shifts, slots):
+    near_refs, out_ref, heads_ref = refs[: len(shifts)], refs[-2], refs[-1]
     rows = query_ref.shape[0]
     here = here_ref[0]
-    list_heads(heads_ref, 0, picks_ref, here, here - shift, slots)
-    for slot in range(slots):
-        columns = head_columns(jnp.maximum(heads_ref[slot], 0))
-        outputs, lines = attend_rows(
-            query_ref[:, columns], near_ref[2 * slot], with_ones(near_ref[2 * slot + 1]), rows
-        )
-        out_ref[slot, :rows, :] = outputs.astype(jnp.bfloat16)
-        out_ref[slot, rows:, :] = three_parts(lines)
-
-
-def near_part(here, picks, queries, near, shift, slots):
+    for place, (shift, near_ref) in enumerate(zip(shifts, near_refs)):
+        list_heads(heads_ref, 0, picks_ref, here, here - shift, slots)
+        for slot in range(slots):
+            columns = head_columns(jnp.maximum(heads_ref[slot], 0))
+            outputs, lines = attend_rows(
+                query_ref[:, columns], near_ref[2 * slot], with_ones(near_ref[2 * slot + 1]), rows
+            )
+            out_ref[place * slots + slot, :rows, :] = outputs.astype(jnp.bfloat16)
+            out_ref[place * slots + slot, rows:, :] = three_parts(lines)
+
+
+def near_part(here, picks, queries, near, shifts, slots):
     rows = queries.shape[0]
+    total = len(shifts) * slots
     return call(
-        functools.partial(near_kernel, shift=shift, slots=slots),
-        [SCALARS, SCALARS, IN_VMEM, IN_VMEM],
-        jax.ShapeDtypeStruct((slots, rows + STAT_ROWS, HD), jnp.bfloat16),
+        functools.partial(near_kernel, shifts=shifts, slots=slots),
+        [SCALARS, SCALARS, IN_VMEM] + [IN_VMEM] * len(shifts),
+        jax.ShapeDtypeStruct((total, rows + STAT_ROWS, HD), jnp.bfloat16),
         IN_VMEM,
         [pltpu.SMEM((slots + 1,), jnp.int32)],
-        flops=4 * slots * rows * rows * HD,
-        moved=12 * slots * rows * HD,
-        exps=slots * rows * rows,
-    )(here, picks, queries, near)
+        flops=4 * total * rows * rows * HD,
+        moved=12 * total * rows * HD,
+        exps=total * rows * rows,
+    )(here, picks, queries, *near)
 
 
 def find_spots(spots_ref, found_ref, picks_ref, here, shifts, slots):
@@ -381,74 +384,87 @@
     )(here, picks, *parts)
 
 
-def finish_kernel(
-    here_ref, picks_ref, mixed_ref, sums_ref, part_ref, old_ref, out_ref, heads_ref, held, sems, *, shift, slots
-):
-    del old_ref
+def finish_kernel(here_ref, picks_ref, mixed_ref, sums_ref, *refs, shifts, slots):
+    count = len(shifts)
+    parts, out_ref, (heads_ref, held, sems) = refs[:count], refs[count + 1], refs[count + 2 :]
     groups = sums_ref.shape[1]
     rows = groups * LANES
     here = here_ref[0]
-    list_heads(heads_ref, 0, picks_ref, here, here - shift, slots)
-
-    def patch(slot):
-        columns = head_columns(jnp.maximum(heads_ref[slot], 0))
-        return pltpu.make_async_copy(held.at[slot], out_ref.at[:, columns], sems.at[slot])
-
-    for slot in range(slots):
-
-        @pl.when(heads_ref[slot] >= 0)
+    for number, shift in enumerate(shifts):
+        list_heads(heads_ref, number * slots, picks_ref, here, here - shift, slots)
+
+    def slot_of(head, number):
+        found = jnp.int32(-1)
+        for slot in range(slots):
+            found = jnp.where(heads_ref[number * slots + slot] == head, slot, found)
+        return found
+
+    def is_first(head, number):
+        first = head >= 0
+        for earlier in range(number):
+            first = first & (slot_of(head, earlier) < 0)
+        return first
+
+    def patch(place):
+        columns = head_columns(jnp.maximum(heads_ref[place], 0))
+        return pltpu.make_async_copy(held.at[place], out_ref.at[:, columns], sems.at[place])
+
+    places = [(number, number * slots + slot) for number in range(count) for slot in range(slots)]
+    for number, place in places:
+        head = heads_ref[place]
+
+        @pl.when(is_first(head, number))
         def _():
-            head = heads_ref[slot]
-            added = stats_of(part_ref[slot, rows:, :], groups)
-            share = 1.0 / (1.0 + jnp.exp2(sums_ref[head] - added))
+            found = [slot_of(head, later) for later in range(number, count)]
+            spots = [jnp.maximum(spot, 0) for spot in found]
+            sums = [sums_ref[head]]
+            for part, spot, safe in zip(parts[number:], found, spots):
+                added = stats_of(part[safe, rows:, :], groups)
+                sums.append(jnp.where(spot >= 0, added, -jnp.inf))
+            top = functools.reduce(jnp.maximum, sums)
+            shares = [jnp.exp2(part - top) for part in sums]
+            whole = functools.reduce(jnp.add, shares)
             for group in range(groups):
                 span = pl.ds(group * LANES, LANES)
-                old = mixed_ref[head, span, :]
-                new = part_ref[slot, span, :].astype(jnp.float32)
-                mixed = old + (new - old) * down_rows(share[group : group + 1, :])
-                held[slot, span, :] = mixed.astype(jnp.bfloat16)
-            patch(slot).start()
-
-    for slot in range(slots):
-
-        @pl.when(heads_ref[slot] >= 0)
+                before = mixed_ref[head, span, :]
+                mixed = before
+                for part, spot, safe, share in zip(parts[number:], found, spots, shares[1:]):
+                    new = jnp.where(spot >= 0, part[safe, span, :].astype(jnp.float32), 0.0)
+                    weight = down_rows((share / whole)[group : group + 1, :])
+                    mixed = mixed + (new - before) * weight
+                held[place, span, :] = mixed.astype(jnp.bfloat16)
+            patch(place).start()
+
+    for number, place in places:
+
+        @pl.when(is_first(heads_ref[place], number))
         def _():
-            patch(slot).wait()
-
-
-def finish(here, picks, result, mixed, sums, part, shift, slots):
-    heads, rows, _ = mixed.shape
+            patch(place).wait()
+
+
+def finish(here, picks, result, mixed, sums, parts, shifts, slots):
+    rows = mixed.shape[1]
+    total = len(shifts) * slots
     return pl.pallas_call(
-        functools.partial(finish_kernel, shift=shift, slots=slots),
-        in_specs=[SCALARS, SCALARS, IN_VMEM, IN_VMEM, IN_VMEM, IN_HBM],
+        functools.partial(finish_kernel, shifts=shifts, slots=slots),
+        in_specs=[SCALARS, SCALARS] + [IN_VMEM] * (2 + len(parts)) + [IN_HBM],
         out_specs=IN_HBM,
         out_shape=jax.ShapeDtypeStruct(result.shape, result.dtype),
         scratch_shapes=[
-            pltpu.SMEM((slots + 1,), jnp.int32),
-            pltpu.VMEM((slots, rows, HD), jnp.bfloat16),
-            pltpu.SemaphoreType.DMA((slots,)),
+            pltpu.SMEM((total + 1,), jnp.int32),
+            pltpu.VMEM((total, rows, HD), jnp.bfloat16),
+            pltpu.SemaphoreType.DMA((total,)),
         ],
-        input_output_aliases={5: 0},
+        input_output_aliases={4 + len(parts): 0},
         compiler_params=pltpu.CompilerParams(vmem_limit_bytes=VMEM_BYTES),
         cost_estimate=pl.CostEstimate(
-            flops=2 * slots * rows * HD, bytes_accessed=8 * slots * rows * HD, transcendentals=0
+            flops=2 * total * rows * HD, bytes_accessed=8 * total * rows * HD, transcendentals=0
         ),
-    )(here, picks, mixed, sums, part, result)
+    )(here, picks, mixed, sums, *parts, result)
 
 
 def after(value, *earlier):
     return lax.optimization_barrier((value,) + earlier)[0]
-
-
-def groups_in_order(width, slots):
-    middle = width // 2
-    groups = [[(middle, 0, slots)], [(shift, 0, slots) for shift in (1, width - 1)]]
-    for low in range(3, middle):
-        size = max(1, slots // 2)
-        for first in range(0, slots, size):
-            count = min(size, slots - first)
-            groups.append([(low, first, count), (width - low, first, count)])
-    return groups + [[(width - 2, 0, slots)]]
 
 
 def travelling_queries(queries, keys, values, picks):
@@ -459,10 +475,12 @@
     queries, keys, values = queries[0], keys[0], values[0]
     own_picks = picks[0].transpose(0, 2, 1)
 
-    groups = groups_in_order(width, slots)
-    near_shift = 2
-    near_jobs = [(near_shift, 0, slots, True)]
-    query_jobs = [piece + (False,) for group in groups for piece in group]
+    near_shifts = (2, width - 2)
+    middle = width // 2
+    far_shifts = [middle, 1, width - 1]
+    for low in range(middle - 1, 2, -1):
+        far_shifts += [low, width - low]
+    final_shifts = tuple(far_shifts[-2:])
 
     def up(value, shift):
         return lax.ppermute(value, "ctx", [(at, at + shift) for at in range(width - shift)])
@@ -478,83 +496,56 @@
         ]
         return lax.ppermute(value, ("ctx", "pipe"), pairs)
 
-    near_send = pack(here, own_picks, [keys, values], near_jobs, slots)[0]
-    near = up(near_send, near_shift)
-    sends, now = {}, after(here, near_send)
-    for jobs in (query_jobs[:1], query_jobs[1:]):
+    near_jobs = [(shift, 0, slots, True) for shift in near_shifts]
+    near_sends = pack(here, own_picks, [keys, values], near_jobs, slots)
+    near = [up(near_sends[0], near_shifts[0])]
+    before = passed_along(own_picks, "pipe", 1)
+    sends, now = {}, after(here, *near_sends)
+    for shifts in (far_shifts[:1], far_shifts[1:]):
+        jobs = [(shift, 0, slots, False) for shift in shifts]
         packed = pack(now, own_picks, [queries], jobs, slots)
-        sends |= {job[:3]: send for job, send in zip(jobs, packed)}
+        sends |= zip(shifts, packed)
         now = after(now, *packed)
-    arrived = {}
-
-    def attend_group(token, group, is_anchor=False):
-        return dict(
-            zip(
-                group,
-                attend(
-                    token,
-                    own_picks,
-                    keys,
-                    values,
-                    [arrived[piece] for piece in group],
-                    tuple(group),
-                    slots,
-                    is_anchor,
-                ),
-            )
-        )
-
-    def ask_for(group, *earlier):
-        for piece in group:
-            send = after(sends[piece], *earlier) if earlier else sends[piece]
-            arrived[piece] = down(send, piece[0])
-
-    def send_back(parts):
-        for piece, part in parts.items():
-            if len(returned) >= 3:
-                part = after(part, list(returned.values())[-3])
-            returned[piece] = up_and_on(part, piece[0])
-
-    def those(found, group):
-        return [found[piece] for piece in group]
-
-    returned = {}
-    ask_for(groups[0])
-    own = own_part(now, queries, keys, values)
+    arrived, returned = {}, {}
+
+    def ask_for(shift, *earlier):
+        arrived[shift] = down(after(sends[shift], *earlier), shift)
+
+    def work(token, shift, is_anchor=False):
+        return attend(
+            token, own_picks, keys, values, [arrived[shift]], ((shift, 0, slots),), slots, is_anchor
+        )[0]
+
+    four, one, seven, three, five = far_shifts
+    ask_for(four, near_sends[0])
+    own = own_part(after(now, before), queries, keys, values)
     own_back = passed_along(own, "pipe", 1)
-    ask_for(groups[1], own)
-    now = after(here, own)
-    for number, group in enumerate(groups):
-        if number == 0:
-            ask_for(groups[2][:1], now, *those(arrived, group))
-        elif number == 1:
-            ask_for(groups[2][1:], now, *those(arrived, group))
-        elif number + 1 < len(groups):
-            ask_for(groups[number + 1], now, *those(arrived, group))
-        if number == 2:
-            now = after(now, own_back)
-        if number == len(groups) - 1:
-            now = tick(now, *list(returned.values())[-4:-2])
-        parts = attend_group(now, group, is_anchor=number in (1, 2))
-        send_back(parts)
-        now = after(now, *parts.values())
-        if number == 0:
-            beside = near_part(now, own_picks, queries, near, near_shift, slots)
-            now = after(now, beside)
-        if number == 3:
-            beside_back = passed_along(after(beside, *parts.values()), "pipe", 1)
-    before = passed_along(after(own_picks, now), "pipe", 1)
-    now = tick(now)
-
-    final = groups[-1][0]
-    others = [shift for shift in range(1, width) if shift not in (near_shift, final[0])]
-    merged_shifts = (near_shift,) + tuple(others)
-    pieces = [piece for piece in returned if piece != final]
-    places = [HEADS + merged_shifts.index(shift) * slots + first for shift, first, _ in pieces]
-    parts = [own_back, beside_back] + [returned[piece] for piece in pieces]
+    near.append(up(after(near_sends[1], own), near_shifts[1]))
+    ask_for(one, arrived[four], near[0], own)
+    ask_for(seven, arrived[four], near[0], own)
+    part_four = work(after(here, own, near[0]), four, is_anchor=True)
+    returned[four] = up_and_on(after(part_four, own_back), four)
+    part_one = work(after(here, part_four, own_back), one, is_anchor=True)
+    ask_for(three, own_back, part_four, arrived[one])
+    part_seven = work(after(here, part_one, own_back), seven, is_anchor=True)
+    ask_for(five, arrived[one], part_four)
+    returned[one] = up_and_on(after(part_one, *near), one)
+    returned[seven] = up_and_on(after(part_seven, *near), seven)
+    beside = near_part(after(here, part_seven), own_picks, queries, near, near_shifts, slots)
+    part_three = work(after(here, beside, returned[four]), three, is_anchor=True)
+    returned[three] = up_and_on(after(part_three, returned[four]), three)
+    beside_back = passed_along(after(beside, arrived[three]), "pipe", 1)
+    part_five = work(after(here, part_three, returned[one]), five, is_anchor=True)
+    returned[five] = up_and_on(after(part_five, returned[one]), five)
+    now = after(here, part_five)
+
+    merged_shifts = near_shifts + (four, one, seven)
+    places = [HEADS + place * slots for place in range(2, 5)]
+    parts = [own_back, beside_back] + [returned[shift] for shift in (four, one, seven)]
     result, mixed, sums = merge(now, before, parts, [0, HEADS] + places, merged_shifts, slots)
-    result = finish(now, before, result, mixed, sums, returned[final], final[0], slots)
-    return result[None]
+    lasts = [returned[shift] for shift in final_shifts]
+    now = tick(now, sums, returned[three])
+    return finish(now, before, result, mixed, sums, lasts, final_shifts, slots)[None]
 
 
 def travelling_keys(queries, keys, values, picks):
@@ -618,7 +609,7 @@
 
 
 def per_device(queries, keys, values, picks):
-    few_shifts = 8 <= lax.axis_size("ctx") <= 16
+    few_shifts = lax.axis_size("ctx") == 8
     run = travelling_queries if few_shifts else travelling_keys
     return run(queries, keys, values, picks)
 

time: 150 us -> 162 us (1.080)
  the two profiles are of different devices: /device:TPU:26 before, /device:TPU:29 now
where the time goes in v9:
time: 162 us; the launch traced here: 161 us
  waiting for transfers between devices  54.9 us (34%)
  Pallas kernels  51.4 us (32%)
  starting transfers between devices  50.2 us (31%)
  local copies, waits for them, and re-layouts  4.27 us (3%)
    ppermute x5, waiting for transfers between devices, up_and_on(): return lax.ppermute(value, ('ctx', 'pipe'), pairs)  47.1 us
    ppermute x5, starting transfers between devices, down(): lax.ppermute(value, 'ctx', [(at, at - shift) for at in range(shift, width)])  23.6 us
    pallas_call x5, Pallas kernels, attend(): call(functools.partial(attend_kernel, group=group, slots=slots), [SCALARS...  17.7 us
    ppermute x3, starting transfers between devices, passed_along(): return lax.ppermute(value, axis, pairs)  17.4 us
    pallas_call x1, Pallas kernels, own_part(): call(own_kernel, [SCALARS, IN_VMEM, IN_VMEM, IN_VMEM], jax.ShapeDtypeStru...  9.01 us
    pallas_call x1, Pallas kernels, merge(): call(functools.partial(merge_kernel, places=tuple(places), shifts=shifts,...  7.44 us
    pallas_call x3, Pallas kernels, pack(): call(functools.partial(pack_kernel, jobs=jobs, slots=slots), [SCALARS, SC...  7.42 us
    ppermute x5, starting transfers between devices, up_and_on(): return lax.ppermute(value, ('ctx', 'pipe'), pairs)  6.61 us
  transfers between devices with their start and end apart: 15, of which 7 were waited for; matrix products, arithmetic and copies ran while one was open for 0% of the time, Pallas kernels for 28%

profile of v9, /device:TPU:29, one launch (start us, length us, event | category | flops | bytes accessed | tf_op | source)
XLA Modules:
  0.0 161.1 jit_solution(5152872161978025296)
XLA Ops:
  0.0 1.6 copy-done.1
  1.6 1.6 copy-done.2
  3.2 2.9 %shard_map.46 = (bf16[8,512,128]{2,1,0:T(8,128)(2,1)S(1)}, bf16[8,512,128]{2,1,0:T(8,128)(2,1)}) custom-call(s32[1]{0:T(128)} %bitcast.here_ref, s32[8,2,16]{2,1,0:T(2,128)} %bitcast.2.picks_ref, bf16[512,2048]{1,0:T(8,128)(2,1)S(1)} %bitcast.12, bf16[512,2048]{1,0:T(8,128)(2,1)S(1)} %bitcast.19), custom_call_target="tpu_custom_call" | custom-call | bytes 4194304 | tf_op jit(solution)/shard_map/pallas_call | solution.py:127
  6.0 1.3 collective-permute-start.1
  7.3 0.0 copy-done
  7.4 0.0 copy-start.3
  7.4 1.2 shard_map.47
  8.6 3.9 %collective-permute-start.2 = (bf16[4,512,128]{2,1,0:T(8,128)(2,1)S(1)}, bf16[4,512,128]{2,1,0:T(8,128)(2,1)S(1)}, u32[]{:S(2)}, u32[]{:S(2)}) collective-permute-start(bf16[4,512,128]{2,1,0:T(8,128)(2,1)S(1)} %shard_map.47), channel_id=1, source_target_pairs={{16,0},{20,4},{24,8},{28,12},{17,1},{21,5},{25,9},{29,13},{18,2},{... | collective-permute-start | bytes 1572872 | tf_op jit(solution)/shard_map/ppermute | solution.py:489
  12.5 2.4 %collective-permute-start = (s32[8,2,16]{2,1,0:T(2,128)}, s32[8,2,16]{2,1,0:T(2,128)S(1)}, u32[]{:S(2)}, u32[]{:S(2)}) collective-permute-start(s32[8,2,16]{2,1,0:T(2,128)} %bitcast.2.picks_ref), channel_id=1, source_target_pairs={{0,1},{1,2},{2,3},{3,0},{4,5},{5,6},{6,7},{7,4},{8,9},{9,10},{10,1... | collective-permute-start | bytes 3080 | tf_op jit(solution)/shard_map/ppermute | solution.py:24
  14.9 3.3 %shard_map.48 = (bf16[4,512,128]{2,1,0:T(8,128)(2,1)}, bf16[4,512,128]{2,1,0:T(8,128)(2,1)}, bf16[4,512,128]{2,1,0:T(8,128)(2,1)}, bf16[4,512,128]{2,1,0:T(8,128)(2,1)}) custom-call(s32[1]{0:T(128)} %bitcast.here_ref, s32[8,2,16]{2,1,0:T(2,128)} %bitcast.2.picks_ref, bf16[512,2048]{1,0:T(8,128)(2,1)S(1)} %bitcast.9), custom_call_target="tpu_custom_call" | custom-call | bytes 4194304 | tf_op jit(solution)/shard_map/pallas_call | solution.py:127
  18.3 0.0 collective-permute-done.picks_ref
  18.3 9.0 %shard_map.49 = bf16[16,528,128]{2,1,0:T(8,128)(2,1)} custom-call(s32[1]{0:T(128)} %bitcast.here_ref, bf16[512,2048]{1,0:T(8,128)(2,1)S(1)} %bitcast.10, bf16[512,2048]{1,0:T(8,128)(2,1)S(1)} %bitcast.13, bf16[512,2048]{1,0:T(8,128)(2,1)S(1)} %bitcast.20), custom_call_target="tpu_custom_call" | custom-call | flops 2147483648 | bytes 8388608 | tf_op jit(solution)/shard_map/pallas_call | solution.py:266
  27.3 0.0 collective-permute-start.3
  27.3 1.3 collective-permute-start.6
  28.6 0.0 collective-permute-done.2.refs_0_
  28.6 3.5 %collective-permute-done.1.refs_0_ = bf16[8,512,128]{2,1,0:T(8,128)(2,1)S(1)} collective-permute-done((bf16[8,512,128]{2,1,0:T(8,128)(2,1)S(1)}, bf16[8,512,128]{2,1,0:T(8,128)(2,1)S(1)}, u32[]{:S(2)}, u32[]{:S(2)}) %collective-permute-start.1) | collective-permute-done | bytes 1048608 | tf_op jit(solution)/shard_map/ppermute | solution.py:486
  32.1 1.1 copy-done.4
  33.1 2.9 %collective-permute-start.4 = (bf16[4,512,128]{2,1,0:T(8,128)(2,1)}, bf16[4,512,128]{2,1,0:T(8,128)(2,1)}, u32[]{:S(2)}, u32[]{:S(2)}) collective-permute-start(bf16[4,512,128]{2,1,0:T(8,128)(2,1)} %get-tuple-element.51), channel_id=1, source_target_pairs={{4,0},{8,4},{12,8},{16,12},{20,16},{24,20},{28,24},{5,1},{9,5},{13... | collective-permute-start | bytes 1572872 | tf_op jit(solution)/shard_map/ppermute | solution.py:489
  36.1 6.4 %collective-permute-start.5 = (bf16[4,512,128]{2,1,0:T(8,128)(2,1)}, bf16[4,512,128]{2,1,0:T(8,128)(2,1)}, u32[]{:S(2)}, u32[]{:S(2)}) collective-permute-start(bf16[4,512,128]{2,1,0:T(8,128)(2,1)} %get-tuple-element.53), channel_id=1, source_target_pairs={{28,0},{29,1},{30,2},{31,3}} | collective-permute-start | bytes 1572872 | tf_op jit(solution)/shard_map/ppermute | solution.py:489
  42.4 3.5 %shard_map.50 = bf16[4,528,128]{2,1,0:T(8,128)(2,1)} custom-call(s32[1]{0:T(128)} %bitcast.here_ref, s32[8,2,16]{2,1,0:T(2,128)} %bitcast.2.picks_ref, bf16[512,2048]{1,0:T(8,128)(2,1)S(1)} %bitcast.14, bf16[512,2048]{1,0:T(8,128)(2,1)S(1)} %bitcast.21, bf16[4,512,128]{2,1,0:T(8,128)(2,1)S(1)} %collective-permute-done.2.refs_0_), custom_call_target="tpu_custom_call" | custom-call | flops 999999995904 | bytes 2097152 | tf_op jit(solution)/shard_map/pallas_call | solution.py:226
  45.9 0.0 collective-permute-done.4.refs_0_
  45.9 8.4 %collective-permute-start.10 = (bf16[4,512,128]{2,1,0:T(8,128)(2,1)}, bf16[4,512,128]{2,1,0:T(8,128)(2,1)}, u32[]{:S(2)}, u32[]{:S(2)}) collective-permute-start(bf16[4,512,128]{2,1,0:T(8,128)(2,1)} %get-tuple-element.61), channel_id=1, source_target_pairs={{20,0},{24,4},{28,8},{21,1},{25,5},{29,9},{22,2},{26,6},{30,10},{2... | collective-permute-start | bytes 1572872 | tf_op jit(solution)/shard_map/ppermute | solution.py:489
  54.3 0.0 collective-permute-done.3.refs_0_
  54.3 3.8 %shard_map.51 = bf16[4,528,128]{2,1,0:T(8,128)(2,1)} custom-call(s32[1]{0:T(128)} %bitcast.here_ref, s32[8,2,16]{2,1,0:T(2,128)} %bitcast.2.picks_ref, bf16[512,2048]{1,0:T(8,128)(2,1)S(1)} %bitcast.15, bf16[512,2048]{1,0:T(8,128)(2,1)S(1)} %bitcast.22, bf16[4,512,128]{2,1,0:T(8,128)(2,1)} %collective-permute-done.4.refs_0_), custom_call_target="tpu_custom_call" | custom-call | flops 999999995904 | bytes 2097152 | tf_op jit(solution)/shard_map/pallas_call | solution.py:226
  58.1 2.1 %collective-permute-start.8 = (bf16[4,512,128]{2,1,0:T(8,128)(2,1)}, bf16[4,512,128]{2,1,0:T(8,128)(2,1)}, u32[]{:S(2)}, u32[]{:S(2)}) collective-permute-start(bf16[4,512,128]{2,1,0:T(8,128)(2,1)} %get-tuple-element.58), channel_id=1, source_target_pairs={{12,0},{16,4},{20,8},{24,12},{28,16},{13,1},{17,5},{21,9},{25,13},... | collective-permute-start | bytes 1572872 | tf_op jit(solution)/shard_map/ppermute | solution.py:489
  60.1 1.3 collective-permute-start.7
  61.4 0.0 collective-permute-done.5.refs_0_
  61.4 3.8 %shard_map.52 = bf16[4,528,128]{2,1,0:T(8,128)(2,1)} custom-call(s32[1]{0:T(128)} %bitcast.here_ref, s32[8,2,16]{2,1,0:T(2,128)} %bitcast.2.picks_ref, bf16[512,2048]{1,0:T(8,128)(2,1)S(1)} %bitcast.16, bf16[512,2048]{1,0:T(8,128)(2,1)S(1)} %bitcast.23, bf16[4,512,128]{2,1,0:T(8,128)(2,1)} %collective-permute-done.5.refs_0_), custom_call_target="tpu_custom_call" | custom-call | flops 999999995904 | bytes 2097152 | tf_op jit(solution)/shard_map/pallas_call | solution.py:226
  65.3 0.0 collective-permute-done.6.refs_1_
  65.3 1.3 collective-permute-start.12
  66.5 1.5 collective-permute-start.9
  68.0 5.4 %shard_map.53 = bf16[8,528,128]{2,1,0:T(8,128)(2,1)} custom-call(s32[1]{0:T(128)} %bitcast.here_ref, s32[8,2,16]{2,1,0:T(2,128)} %bitcast.2.picks_ref, bf16[512,2048]{1,0:T(8,128)(2,1)S(1)} %bitcast.11, bf16[8,512,128]{2,1,0:T(8,128)(2,1)S(1)} %copy-done.5, bf16[8,512,128]{2,1,0:T(8,128)(2,1)} %collective-permute-done.6.refs_1_), custom_call_target="tpu_custom_call" | custom-call | flops 1073741824 | bytes 6291456 | tf_op jit(solution)/shard_map/pallas_call | solution.py:295
  73.4 0.4 collective-permute-done.8.refs_0_
  73.8 15.0 %collective-permute-start.11 = (bf16[8,528,128]{2,1,0:T(8,128)(2,1)}, bf16[8,528,128]{2,1,0:T(8,128)(2,1)}, u32[]{:S(2)}, u32[]{:S(2)}) collective-permute-start(bf16[8,528,128]{2,1,0:T(8,128)(2,1)} %shard_map.53), channel_id=1, source_target_pairs={{0,1},{1,2},{2,3},{3,0},{4,5},{5,6},{6,7},{7,4},{8,9},{9,10},{10,1... | collective-permute-start | bytes 3244040 | tf_op jit(solution)/shard_map/ppermute | solution.py:24
  88.8 8.9 %collective-permute-done.7.refs_2_ = bf16[4,528,128]{2,1,0:T(8,128)(2,1)} collective-permute-done((bf16[4,528,128]{2,1,0:T(8,128)(2,1)}, bf16[4,528,128]{2,1,0:T(8,128)(2,1)}, u32[]{:S(2)}, u32[]{:S(2)}) %collective-permute-start.7) | collective-permute-done | bytes 540704 | tf_op jit(solution)/shard_map/ppermute | solution.py:497
  97.7 3.7 %shard_map.54 = bf16[4,528,128]{2,1,0:T(8,128)(2,1)} custom-call(s32[1]{0:T(128)} %bitcast.here_ref, s32[8,2,16]{2,1,0:T(2,128)} %bitcast.2.picks_ref, bf16[512,2048]{1,0:T(8,128)(2,1)S(1)} %bitcast.17, bf16[512,2048]{1,0:T(8,128)(2,1)S(1)} %bitcast.24, bf16[4,512,128]{2,1,0:T(8,128)(2,1)} %collective-permute-done.8.refs_0_), custom_call_target="tpu_custom_call" | custom-call | flops 999999995904 | bytes 2097152 | tf_op jit(solution)/shard_map/pallas_call | solution.py:226
  101.4 0.2 collective-permute-done.9.refs_3_
  101.6 1.3 collective-permute-start.13
  102.8 0.0 collective-permute-done.10.refs_0_
  102.9 2.9 %shard_map.55 = bf16[4,528,128]{2,1,0:T(8,128)(2,1)S(1)} custom-call(s32[1]{0:T(128)} %bitcast.here_ref, s32[8,2,16]{2,1,0:T(2,128)} %bitcast.2.picks_ref, bf16[512,2048]{1,0:T(8,128)(2,1)S(1)} %bitcast.18, bf16[512,2048]{1,0:T(8,128)(2,1)S(1)} %bitcast.25, bf16[4,512,128]{2,1,0:T(8,128)(2,1)} %collective-permute-done.10.refs_0_), custom_call_target="tpu_custom_call" | custom-call | flops 999999995904 | bytes 2097152 | tf_op jit(solution)/shard_map/pallas_call | solution.py:226
  105.8 1.3 collective-permute-start.14
  107.1 0.0 collective-permute-done.12.refs_4_
  107.1 4.0 %collective-permute-done.11.refs_1_ = bf16[8,528,128]{2,1,0:T(8,128)(2,1)} collective-permute-done((bf16[8,528,128]{2,1,0:T(8,128)(2,1)}, bf16[8,528,128]{2,1,0:T(8,128)(2,1)}, u32[]{:S(2)}, u32[]{:S(2)}) %collective-permute-start.11) | collective-permute-done | bytes 1081376 | tf_op jit(solution)/shard_map/ppermute | solution.py:24
  111.1 7.4 %shard_map.56 = (bf16[512,2048]{1,0:T(8,128)(2,1)}, f32[16,512,128]{2,1,0:T(8,128)S(1)}, f32[16,4,128]{2,1,0:T(4,128)S(1)}) custom-call(s32[1]{0:T(128)} %bitcast.here_ref, s32[8,2,16]{2,1,0:T(2,128)S(1)} %copy-done.7, bf16[16,528,128]{2,1,0:T(8,128)(2,1)} %collective-permute-done.3.refs_0_, bf16[8,528,128]{2,1,0:T(8,128)(2,1)} %collective-permute-done.11.refs_1_, ...), custom_call_target="tpu_custom_call" | custom-call | flops 6291456 | bytes 8912896 | tf_op jit(solution)/shard_map/pallas_call | solution.py:367
  118.5 3.3 %collective-permute-done.13.refs_0_ = bf16[4,528,128]{2,1,0:T(8,128)(2,1)} collective-permute-done((bf16[4,528,128]{2,1,0:T(8,128)(2,1)}, bf16[4,528,128]{2,1,0:T(8,128)(2,1)}, u32[]{:S(2)}, u32[]{:S(2)}) %collective-permute-start.13) | collective-permute-done | bytes 540704 | tf_op jit(solution)/shard_map/ppermute | solution.py:497
  121.8 0.5 shard_map.57.here_ref
  122.3 34.7 %collective-permute-done.14.refs_1_ = bf16[4,528,128]{2,1,0:T(8,128)(2,1)S(1)} collective-permute-done((bf16[4,528,128]{2,1,0:T(8,128)(2,1)S(1)}, bf16[4,528,128]{2,1,0:T(8,128)(2,1)S(1)}, u32[]{:S(2)}, u32[]{:S(2)}) %collective-permute-start.14) | collective-permute-done | bytes 540704 | tf_op jit(solution)/shard_map/ppermute | solution.py:497
  157.1 3.9 %shard_map.58 = bf16[512,2048]{1,0:T(8,128)(2,1)} custom-call(s32[1]{0:T(128)} %shard_map.57.here_ref, s32[8,2,16]{2,1,0:T(2,128)S(1)} %copy-done.7, f32[16,512,128]{2,1,0:T(8,128)S(1)} %get-tuple-element.68.mixed_ref, f32[16,4,128]{2,1,0:T(4,128)S(1)} %get-tuple-element.65.sums_ref, ...), custom_call_target="tpu_custom_call", output_to_operand_aliasing={{}: (6, {})} | custom-call | flops 1048576 | bytes 4194304 | tf_op jit(solution)/shard_map/pallas_call | solution.py:448
  (11 shorter events, 0.0 us)
Async XLA Ops:
  0.0 1.6 copy-start.1
  1.6 1.6 copy-start.2
  3.2 4.2 %copy-start = (bf16[1,512,2048]{2,1,0:T(8,128)(2,1)S(1)}, bf16[1,512,2048]{2,1,0:T(8,128)(2,1)}, u32[]{:S(2)}) copy-start(bf16[1,512,2048]{2,1,0:T(8,128)(2,1)} %param.4) | copy-start | bytes 6291460
  6.0 26.0 %collective-permute-start.1 = (bf16[8,512,128]{2,1,0:T(8,128)(2,1)S(1)}, bf16[8,512,128]{2,1,0:T(8,128)(2,1)S(1)}, u32[]{:S(2)}, u32[]{:S(2)}) collective-permute-start(bf16[8,512,128]{2,1,0:T(8,128)(2,1)S(1)} %get-tuple-element.38), channel_id=1, source_target_pairs={{0,8},{4,12},{8,16},{12,20},{16,24},{20,28},{1,9},{5,13},{9,17},{1... | collective-permute-start | bytes 3145736 | tf_op jit(solution)/shard_map/ppermute | solution.py:486
  7.4 10.9 %copy-start.3 = (bf16[1,512,2048]{2,1,0:T(8,128)(2,1)S(1)}, bf16[1,512,2048]{2,1,0:T(8,128)(2,1)}, u32[]{:S(2)}) copy-start(bf16[1,512,2048]{2,1,0:T(8,128)(2,1)} %param.6) | copy-start | bytes 6291460
  8.6 20.0 %collective-permute-start.2 = (bf16[4,512,128]{2,1,0:T(8,128)(2,1)S(1)}, bf16[4,512,128]{2,1,0:T(8,128)(2,1)S(1)}, u32[]{:S(2)}, u32[]{:S(2)}) collective-permute-start(bf16[4,512,128]{2,1,0:T(8,128)(2,1)S(1)} %shard_map.47), channel_id=1, source_target_pairs={{16,0},{20,4},{24,8},{28,12},{17,1},{21,5},{25,9},{29,13},{18,2},{... | collective-permute-start | bytes 1572872 | tf_op jit(solution)/shard_map/ppermute | solution.py:489
  12.5 5.7 %collective-permute-start = (s32[8,2,16]{2,1,0:T(2,128)}, s32[8,2,16]{2,1,0:T(2,128)S(1)}, u32[]{:S(2)}, u32[]{:S(2)}) collective-permute-start(s32[8,2,16]{2,1,0:T(2,128)} %bitcast.2.picks_ref), channel_id=1, source_target_pairs={{0,1},{1,2},{2,3},{3,0},{4,5},{5,6},{6,7},{7,4},{8,9},{9,10},{10,1... | collective-permute-start | bytes 3080 | tf_op jit(solution)/shard_map/ppermute | solution.py:24
  18.3 9.0 %copy-start.6 = (s32[8,2,16]{2,1,0:T(2,128)}, s32[8,2,16]{2,1,0:T(2,128)S(1)}, u32[]{:S(2)}) copy-start(s32[8,2,16]{2,1,0:T(2,128)S(1)} %collective-permute-done.picks_ref) | copy-start | bytes 3076
  27.3 27.0 %collective-permute-start.3 = (bf16[16,528,128]{2,1,0:T(8,128)(2,1)}, bf16[16,528,128]{2,1,0:T(8,128)(2,1)}, u32[]{:S(2)}, u32[]{:S(2)}) collective-permute-start(bf16[16,528,128]{2,1,0:T(8,128)(2,1)} %shard_map.49), channel_id=1, source_target_pairs={{0,1},{1,2},{2,3},{3,0},{4,5},{5,6},{6,7},{7,4},{8,9},{9,10},{10,1... | collective-permute-start | bytes 6488072 | tf_op jit(solution)/shard_map/ppermute | solution.py:24
  27.3 38.0 %collective-permute-start.6 = (bf16[8,512,128]{2,1,0:T(8,128)(2,1)}, bf16[8,512,128]{2,1,0:T(8,128)(2,1)}, u32[]{:S(2)}, u32[]{:S(2)}) collective-permute-start(bf16[8,512,128]{2,1,0:T(8,128)(2,1)} %get-tuple-element.55), channel_id=1, source_target_pairs={{0,24},{4,28},{1,25},{5,29},{2,26},{6,30},{3,27},{7,31}} | collective-permute-start | bytes 3145736 | tf_op jit(solution)/shard_map/ppermute | solution.py:486
  32.1 1.1 copy-start.4
  33.1 12.8 %collective-permute-start.4 = (bf16[4,512,128]{2,1,0:T(8,128)(2,1)}, bf16[4,512,128]{2,1,0:T(8,128)(2,1)}, u32[]{:S(2)}, u32[]{:S(2)}) collective-permute-start(bf16[4,512,128]{2,1,0:T(8,128)(2,1)} %get-tuple-element.51), channel_id=1, source_target_pairs={{4,0},{8,4},{12,8},{16,12},{20,16},{24,20},{28,24},{5,1},{9,5},{13... | collective-permute-start | bytes 1572872 | tf_op jit(solution)/shard_map/ppermute | solution.py:489
  36.1 25.4 %collective-permute-start.5 = (bf16[4,512,128]{2,1,0:T(8,128)(2,1)}, bf16[4,512,128]{2,1,0:T(8,128)(2,1)}, u32[]{:S(2)}, u32[]{:S(2)}) collective-permute-start(bf16[4,512,128]{2,1,0:T(8,128)(2,1)} %get-tuple-element.53), channel_id=1, source_target_pairs={{28,0},{29,1},{30,2},{31,3}} | collective-permute-start | bytes 1572872 | tf_op jit(solution)/shard_map/ppermute | solution.py:489
  45.9 56.9 %collective-permute-start.10 = (bf16[4,512,128]{2,1,0:T(8,128)(2,1)}, bf16[4,512,128]{2,1,0:T(8,128)(2,1)}, u32[]{:S(2)}, u32[]{:S(2)}) collective-permute-start(bf16[4,512,128]{2,1,0:T(8,128)(2,1)} %get-tuple-element.61), channel_id=1, source_target_pairs={{20,0},{24,4},{28,8},{21,1},{25,5},{29,9},{22,2},{26,6},{30,10},{2... | collective-permute-start | bytes 1572872 | tf_op jit(solution)/shard_map/ppermute | solution.py:489
  58.1 15.7 %collective-permute-start.8 = (bf16[4,512,128]{2,1,0:T(8,128)(2,1)}, bf16[4,512,128]{2,1,0:T(8,128)(2,1)}, u32[]{:S(2)}, u32[]{:S(2)}) collective-permute-start(bf16[4,512,128]{2,1,0:T(8,128)(2,1)} %get-tuple-element.58), channel_id=1, source_target_pairs={{12,0},{16,4},{20,8},{24,12},{28,16},{13,1},{17,5},{21,9},{25,13},... | collective-permute-start | bytes 1572872 | tf_op jit(solution)/shard_map/ppermute | solution.py:489
  60.1 37.5 %collective-permute-start.7 = (bf16[4,528,128]{2,1,0:T(8,128)(2,1)}, bf16[4,528,128]{2,1,0:T(8,128)(2,1)}, u32[]{:S(2)}, u32[]{:S(2)}) collective-permute-start(bf16[4,528,128]{2,1,0:T(8,128)(2,1)} %shard_map.50), channel_id=1, source_target_pairs={{0,17},{1,18},{2,19},{3,16},{4,21},{5,22},{6,23},{7,20},{8,25},{9,... | collective-permute-start | bytes 1622024 | tf_op jit(solution)/shard_map/ppermute | solution.py:497
  61.4 6.6 %copy-start.5 = (bf16[8,512,128]{2,1,0:T(8,128)(2,1)S(1)}, bf16[8,512,128]{2,1,0:T(8,128)(2,1)}, u32[]{:S(2)}) copy-start(bf16[8,512,128]{2,1,0:T(8,128)(2,1)} %copy-done.4) | copy-start | bytes 3145732
  65.3 41.8 %collective-permute-start.12 = (bf16[4,528,128]{2,1,0:T(8,128)(2,1)}, bf16[4,528,128]{2,1,0:T(8,128)(2,1)}, u32[]{:S(2)}, u32[]{:S(2)}) collective-permute-start(bf16[4,528,128]{2,1,0:T(8,128)(2,1)} %shard_map.52), channel_id=1, source_target_pairs={{0,29},{1,30},{2,31},{3,28}} | collective-permute-start | bytes 1622024 | tf_op jit(solution)/shard_map/ppermute | solution.py:497
  66.5 35.0 %collective-permute-start.9 = (bf16[4,528,128]{2,1,0:T(8,128)(2,1)}, bf16[4,528,128]{2,1,0:T(8,128)(2,1)}, u32[]{:S(2)}, u32[]{:S(2)}) collective-permute-start(bf16[4,528,128]{2,1,0:T(8,128)(2,1)} %shard_map.51), channel_id=1, source_target_pairs={{0,5},{1,6},{2,7},{3,4},{4,9},{5,10},{6,11},{7,8},{8,13},{9,14},{1... | collective-permute-start | bytes 1622024 | tf_op jit(solution)/shard_map/ppermute | solution.py:497
  73.8 37.3 %collective-permute-start.11 = (bf16[8,528,128]{2,1,0:T(8,128)(2,1)}, bf16[8,528,128]{2,1,0:T(8,128)(2,1)}, u32[]{:S(2)}, u32[]{:S(2)}) collective-permute-start(bf16[8,528,128]{2,1,0:T(8,128)(2,1)} %shard_map.53), channel_id=1, source_target_pairs={{0,1},{1,2},{2,3},{3,0},{4,5},{5,6},{6,7},{7,4},{8,9},{9,10},{10,1... | collective-permute-start | bytes 3244040 | tf_op jit(solution)/shard_map/ppermute | solution.py:24
  101.6 20.3 %collective-permute-start.13 = (bf16[4,528,128]{2,1,0:T(8,128)(2,1)}, bf16[4,528,128]{2,1,0:T(8,128)(2,1)}, u32[]{:S(2)}, u32[]{:S(2)}) collective-permute-start(bf16[4,528,128]{2,1,0:T(8,128)(2,1)} %shard_map.54), channel_id=1, source_target_pairs={{0,13},{1,14},{2,15},{3,12},{4,17},{5,18},{6,19},{7,16},{8,21},{9,... | collective-permute-start | bytes 1622024 | tf_op jit(solution)/shard_map/ppermute | solution.py:497
  102.9 8.2 %copy-start.7 = (s32[8,2,16]{2,1,0:T(2,128)S(1)}, s32[8,2,16]{2,1,0:T(2,128)}, u32[]{:S(2)}) copy-start(s32[8,2,16]{2,1,0:T(2,128)} %copy-done.6) | copy-start | bytes 3076
  105.8 51.3 %collective-permute-start.14 = (bf16[4,528,128]{2,1,0:T(8,128)(2,1)S(1)}, bf16[4,528,128]{2,1,0:T(8,128)(2,1)S(1)}, u32[]{:S(2)}, u32[]{:S(2)}) collective-permute-start(bf16[4,528,128]{2,1,0:T(8,128)(2,1)S(1)} %shard_map.55), channel_id=1, source_target_pairs={{0,21},{1,22},{2,23},{3,20},{4,25},{5,26},{6,27},{7,24},{8,29},{9,... | collective-permute-start | bytes 1622024 | tf_op jit(solution)/shard_map/ppermute | solution.py:497

commit v10 on v9

--- a/solution.py
+++ b/solution.py
@@ -477,10 +477,8 @@
 
     near_shifts = (2, width - 2)
     middle = width // 2
-    far_shifts = [middle, 1, width - 1]
-    for low in range(middle - 1, 2, -1):
-        far_shifts += [low, width - low]
-    final_shifts = tuple(far_shifts[-2:])
+    far_shifts = [middle, middle - 1, middle + 1, 1, width - 1]
+    final_shifts = tuple(far_shifts[3:])
 
     def up(value, shift):
         return lax.ppermute(value, "ctx", [(at, at + shift) for at in range(width - shift)])
@@ -516,35 +514,34 @@
             token, own_picks, keys, values, [arrived[shift]], ((shift, 0, slots),), slots, is_anchor
         )[0]
 
-    four, one, seven, three, five = far_shifts
+    four, three, five, one, seven = far_shifts
     ask_for(four, near_sends[0])
     own = own_part(after(now, before), queries, keys, values)
     own_back = passed_along(own, "pipe", 1)
     near.append(up(after(near_sends[1], own), near_shifts[1]))
-    ask_for(one, arrived[four], near[0], own)
-    ask_for(seven, arrived[four], near[0], own)
+    ask_for(three, arrived[four], near[0], own)
+    ask_for(five, arrived[four], near[0], own)
     part_four = work(after(here, own, near[0]), four, is_anchor=True)
-    returned[four] = up_and_on(after(part_four, own_back), four)
-    part_one = work(after(here, part_four, own_back), one, is_anchor=True)
-    ask_for(three, own_back, part_four, arrived[one])
-    part_seven = work(after(here, part_one, own_back), seven, is_anchor=True)
-    ask_for(five, arrived[one], part_four)
-    returned[one] = up_and_on(after(part_one, *near), one)
-    returned[seven] = up_and_on(after(part_seven, *near), seven)
-    beside = near_part(after(here, part_seven), own_picks, queries, near, near_shifts, slots)
-    part_three = work(after(here, beside, returned[four]), three, is_anchor=True)
-    returned[three] = up_and_on(after(part_three, returned[four]), three)
-    beside_back = passed_along(after(beside, arrived[three]), "pipe", 1)
-    part_five = work(after(here, part_three, returned[one]), five, is_anchor=True)
-    returned[five] = up_and_on(after(part_five, returned[one]), five)
-    now = after(here, part_five)
-
-    merged_shifts = near_shifts + (four, one, seven)
-    places = [HEADS + place * slots for place in range(2, 5)]
-    parts = [own_back, beside_back] + [returned[shift] for shift in (four, one, seven)]
+    returned[four] = up_and_on(part_four, four)
+    beside = near_part(after(here, part_four, own_back), own_picks, queries, near, near_shifts, slots)
+    ask_for(one, own_back, part_four, *near)
+    ask_for(seven, own_back, part_four, *near)
+    part_three = work(after(here, beside), three, is_anchor=True)
+    returned[three] = up_and_on(part_three, three)
+    part_five = work(after(here, part_three), five)
+    returned[five] = up_and_on(part_five, five)
+    beside_back = passed_along(beside, "pipe", 1)
+    part_one = work(after(here, part_five, beside_back), one)
+    returned[one] = up_and_on(part_one, one)
+    part_seven = work(after(here, part_one), seven)
+    returned[seven] = up_and_on(part_seven, seven)
+    now = after(here, part_seven)
+
+    merged_shifts = near_shifts + (four, three, five)
+    places = [HEADS + place * slots for place in (2, 3, 4)]
+    parts = [own_back, beside_back, returned[four], returned[three], returned[five]]
     result, mixed, sums = merge(now, before, parts, [0, HEADS] + places, merged_shifts, slots)
     lasts = [returned[shift] for shift in final_shifts]
-    now = tick(now, sums, returned[three])
     return finish(now, before, result, mixed, sums, lasts, final_shifts, slots)[None]
 
 

time: 162 us -> 145 us (0.90)
  starting transfers between devices: 50.2 us -> 38.5 us
  Pallas kernels: 51.4 us -> 47.6 us
    ppermute x5, waiting for transfers between devices: 47.1 us -> 34.5 us  [up_and_on(): return lax.ppermute(value, ('ctx', 'pipe'), pairs)]
    ppermute x3, waiting for transfers between devices: 3.96 us -> 11.8 us  [passed_along(): return lax.ppermute(value, axis, pairs)]
    ppermute x5, starting transfers between devices: 23.6 us -> 16.2 us  [down(): lax.ppermute(value, 'ctx', [(at, at - shift) for at in range(shift, width)])]
    ppermute x3, starting transfers between devices: 17.4 us -> 13.1 us  [passed_along(): return lax.ppermute(value, axis, pairs)]
    ppermute x2, waiting for transfers between devices: 3.48 us -> 7.68 us  [up(): lax.ppermute(value, 'ctx', [(at, at + shift) for at in range(width - shif...]
    pallas_call x5, Pallas kernels: 17.7 us -> 15.3 us  [attend(): call(functools.partial(attend_kernel, group=group, slots=slots), [SCALARS...]
    unnamed x16 -> x18, local copies, waits for them, and re-layouts: 4.27 us -> 4.2 us
  transfers between devices with their start and end apart: 15 -> 15, of which waited for: 7 -> 5; matrix products, arithmetic and copies ran while one was open for 0% -> 0% of each run, Pallas kernels for 28% -> 29%
where the time goes in v10:
time: 145 us
  waiting for transfers between devices  54 us (37%)
  Pallas kernels  47.6 us (33%)
  starting transfers between devices  38.5 us (27%)
  local copies, waits for them, and re-layouts  4.2 us (3%)
    ppermute x5, waiting for transfers between devices, up_and_on(): return lax.ppermute(value, ('ctx', 'pipe'), pairs)  34.5 us
    ppermute x5, starting transfers between devices, down(): lax.ppermute(value, 'ctx', [(at, at - shift) for at in range(shift, width)])  16.2 us
    pallas_call x5, Pallas kernels, attend(): call(functools.partial(attend_kernel, group=group, slots=slots), [SCALARS...  15.3 us
    ppermute x3, starting transfers between devices, passed_along(): return lax.ppermute(value, axis, pairs)  13.1 us
    ppermute x3, waiting for transfers between devices, passed_along(): return lax.ppermute(value, axis, pairs)  11.8 us
    pallas_call x1, Pallas kernels, own_part(): call(own_kernel, [SCALARS, IN_VMEM, IN_VMEM, IN_VMEM], jax.ShapeDtypeStru...  8.95 us
    ppermute x2, waiting for transfers between devices, up(): lax.ppermute(value, 'ctx', [(at, at + shift) for at in range(width - shif...  7.68 us
    pallas_call x3, Pallas kernels, pack(): call(functools.partial(pack_kernel, jobs=jobs, slots=slots), [SCALARS, SC...  7.51 us
  transfers between devices with their start and end apart: 15, of which 5 were waited for; matrix products, arithmetic and copies ran while one was open for 0% of the time, Pallas kernels for 29%

profile of v10, /device:TPU:29, one launch (start us, length us, event | category | flops | bytes accessed | tf_op | source)
XLA Modules:
  0.0 144.7 jit_solution(8674620149060809391)
XLA Ops:
  0.0 1.6 %copy-done = bf16[1,512,2048]{2,1,0:T(8,128)(2,1)S(1)} copy-done((bf16[1,512,2048]{2,1,0:T(8,128)(2,1)S(1)}, bf16[1,512,2048]{2,1,0:T(8,128)(2,1)}, u32[]{:S(2)}) %copy-start) | copy-done | bytes 2097176
  1.6 1.6 %copy-done.2 = bf16[1,512,2048]{2,1,0:T(8,128)(2,1)S(1)} copy-done((bf16[1,512,2048]{2,1,0:T(8,128)(2,1)S(1)}, bf16[1,512,2048]{2,1,0:T(8,128)(2,1)}, u32[]{:S(2)}) %copy-start.2) | copy-done | bytes 2097176
  3.2 2.9 %shard_map.46 = (bf16[8,512,128]{2,1,0:T(8,128)(2,1)S(1)}, bf16[8,512,128]{2,1,0:T(8,128)(2,1)}) custom-call(s32[1]{0:T(128)} %bitcast.here_ref, s32[8,2,16]{2,1,0:T(2,128)} %bitcast.2.picks_ref, bf16[512,2048]{1,0:T(8,128)(2,1)S(1)} %bitcast.8, bf16[512,2048]{1,0:T(8,128)(2,1)S(1)} %bitcast.15), custom_call_target="tpu_custom_call" | custom-call | bytes 4194304 | tf_op jit(solution)/shard_map/pallas_call | solution.py:127
  6.0 1.3 collective-permute-start.1
  7.3 0.0 copy-done.4
  7.4 0.0 copy-start.1
  7.4 0.0 copy-start.3
  7.4 1.2 shard_map.47
  8.6 3.9 %collective-permute-start.2 = (bf16[4,512,128]{2,1,0:T(8,128)(2,1)S(1)}, bf16[4,512,128]{2,1,0:T(8,128)(2,1)S(1)}, u32[]{:S(2)}, u32[]{:S(2)}) collective-permute-start(bf16[4,512,128]{2,1,0:T(8,128)(2,1)S(1)} %shard_map.47), channel_id=1, source_target_pairs={{16,0},{20,4},{24,8},{28,12},{17,1},{21,5},{25,9},{29,13},{18,2},{... | collective-permute-start | bytes 1572872 | tf_op jit(solution)/shard_map/ppermute | solution.py:487
  12.5 2.4 %collective-permute-start = (s32[8,2,16]{2,1,0:T(2,128)}, s32[8,2,16]{2,1,0:T(2,128)S(1)}, u32[]{:S(2)}, u32[]{:S(2)}) collective-permute-start(s32[8,2,16]{2,1,0:T(2,128)} %bitcast.2.picks_ref), channel_id=1, source_target_pairs={{0,1},{1,2},{2,3},{3,0},{4,5},{5,6},{6,7},{7,4},{8,9},{9,10},{10,1... | collective-permute-start | bytes 3080 | tf_op jit(solution)/shard_map/ppermute | solution.py:24
  14.9 3.4 %shard_map.48 = (bf16[4,512,128]{2,1,0:T(8,128)(2,1)}, bf16[4,512,128]{2,1,0:T(8,128)(2,1)}, bf16[4,512,128]{2,1,0:T(8,128)(2,1)}, bf16[4,512,128]{2,1,0:T(8,128)(2,1)}) custom-call(s32[1]{0:T(128)} %bitcast.here_ref, s32[8,2,16]{2,1,0:T(2,128)} %bitcast.2.picks_ref, bf16[512,2048]{1,0:T(8,128)(2,1)S(1)} %bitcast.23), custom_call_target="tpu_custom_call" | custom-call | bytes 4194304 | tf_op jit(solution)/shard_map/pallas_call | solution.py:127
  18.4 0.0 collective-permute-done.picks_ref
  18.4 9.0 %shard_map.49 = bf16[16,528,128]{2,1,0:T(8,128)(2,1)} custom-call(s32[1]{0:T(128)} %bitcast.here_ref, bf16[512,2048]{1,0:T(8,128)(2,1)S(1)} %bitcast.24, bf16[512,2048]{1,0:T(8,128)(2,1)S(1)} %bitcast.9, bf16[512,2048]{1,0:T(8,128)(2,1)S(1)} %bitcast.16), custom_call_target="tpu_custom_call" | custom-call | flops 2147483648 | bytes 8388608 | tf_op jit(solution)/shard_map/pallas_call | solution.py:266
  27.4 0.0 collective-permute-start.3
  27.4 1.3 collective-permute-start.4
  28.6 0.0 collective-permute-done.2.refs_0_
  28.7 3.4 %collective-permute-done.1.refs_0_ = bf16[8,512,128]{2,1,0:T(8,128)(2,1)S(1)} collective-permute-done((bf16[8,512,128]{2,1,0:T(8,128)(2,1)S(1)}, bf16[8,512,128]{2,1,0:T(8,128)(2,1)S(1)}, u32[]{:S(2)}, u32[]{:S(2)}) %collective-permute-start.1) | collective-permute-done | bytes 1048608 | tf_op jit(solution)/shard_map/ppermute | solution.py:484
  32.1 1.0 copy-done.5
  33.1 5.2 %collective-permute-start.5 = (bf16[4,512,128]{2,1,0:T(8,128)(2,1)}, bf16[4,512,128]{2,1,0:T(8,128)(2,1)}, u32[]{:S(2)}, u32[]{:S(2)}) collective-permute-start(bf16[4,512,128]{2,1,0:T(8,128)(2,1)} %get-tuple-element.46), channel_id=1, source_target_pairs={{12,0},{16,4},{20,8},{24,12},{28,16},{13,1},{17,5},{21,9},{25,13},... | collective-permute-start | bytes 1572872 | tf_op jit(solution)/shard_map/ppermute | solution.py:487
  38.2 2.1 %collective-permute-start.6 = (bf16[4,512,128]{2,1,0:T(8,128)(2,1)}, bf16[4,512,128]{2,1,0:T(8,128)(2,1)}, u32[]{:S(2)}, u32[]{:S(2)}) collective-permute-start(bf16[4,512,128]{2,1,0:T(8,128)(2,1)} %get-tuple-element.48), channel_id=1, source_target_pairs={{20,0},{24,4},{28,8},{21,1},{25,5},{29,9},{22,2},{26,6},{30,10},{2... | collective-permute-start | bytes 1572872 | tf_op jit(solution)/shard_map/ppermute | solution.py:487
  40.3 3.6 %shard_map.50 = bf16[4,528,128]{2,1,0:T(8,128)(2,1)} custom-call(s32[1]{0:T(128)} %bitcast.here_ref, s32[8,2,16]{2,1,0:T(2,128)} %bitcast.2.picks_ref, bf16[512,2048]{1,0:T(8,128)(2,1)S(1)} %bitcast.10, bf16[512,2048]{1,0:T(8,128)(2,1)S(1)} %bitcast.17, bf16[4,512,128]{2,1,0:T(8,128)(2,1)S(1)} %collective-permute-done.2.refs_0_), custom_call_target="tpu_custom_call" | custom-call | flops 999999995904 | bytes 2097152 | tf_op jit(solution)/shard_map/pallas_call | solution.py:226
  43.9 1.3 collective-permute-start.10
  45.2 6.2 %collective-permute-done.3.refs_0_ = bf16[16,528,128]{2,1,0:T(8,128)(2,1)} collective-permute-done((bf16[16,528,128]{2,1,0:T(8,128)(2,1)}, bf16[16,528,128]{2,1,0:T(8,128)(2,1)}, u32[]{:S(2)}, u32[]{:S(2)}) %collective-permute-start.3) | collective-permute-done | bytes 2162720 | tf_op jit(solution)/shard_map/ppermute | solution.py:24
  51.4 4.3 %collective-permute-done.4.refs_1_ = bf16[8,512,128]{2,1,0:T(8,128)(2,1)} collective-permute-done((bf16[8,512,128]{2,1,0:T(8,128)(2,1)}, bf16[8,512,128]{2,1,0:T(8,128)(2,1)}, u32[]{:S(2)}, u32[]{:S(2)}) %collective-permute-start.4) | collective-permute-done | bytes 1048608 | tf_op jit(solution)/shard_map/ppermute | solution.py:484
  55.6 5.4 %shard_map.51 = bf16[8,528,128]{2,1,0:T(8,128)(2,1)} custom-call(s32[1]{0:T(128)} %bitcast.here_ref, s32[8,2,16]{2,1,0:T(2,128)} %bitcast.2.picks_ref, bf16[512,2048]{1,0:T(8,128)(2,1)S(1)} %bitcast.25, bf16[8,512,128]{2,1,0:T(8,128)(2,1)S(1)} %copy-done.6, bf16[8,512,128]{2,1,0:T(8,128)(2,1)} %collective-permute-done.4.refs_1_), custom_call_target="tpu_custom_call" | custom-call | flops 1073741824 | bytes 6291456 | tf_op jit(solution)/shard_map/pallas_call | solution.py:295
  61.0 10.8 %collective-permute-start.7 = (bf16[8,528,128]{2,1,0:T(8,128)(2,1)}, bf16[8,528,128]{2,1,0:T(8,128)(2,1)}, u32[]{:S(2)}, u32[]{:S(2)}) collective-permute-start(bf16[8,528,128]{2,1,0:T(8,128)(2,1)} %shard_map.51), channel_id=1, source_target_pairs={{0,1},{1,2},{2,3},{3,0},{4,5},{5,6},{6,7},{7,4},{8,9},{9,10},{10,1... | collective-permute-start | bytes 3244040 | tf_op jit(solution)/shard_map/ppermute | solution.py:24
  71.7 3.0 %collective-permute-start.8 = (bf16[4,512,128]{2,1,0:T(8,128)(2,1)}, bf16[4,512,128]{2,1,0:T(8,128)(2,1)}, u32[]{:S(2)}, u32[]{:S(2)}) collective-permute-start(bf16[4,512,128]{2,1,0:T(8,128)(2,1)} %get-tuple-element.50), channel_id=1, source_target_pairs={{4,0},{8,4},{12,8},{16,12},{20,16},{24,20},{28,24},{5,1},{9,5},{13... | collective-permute-start | bytes 1572872 | tf_op jit(solution)/shard_map/ppermute | solution.py:487
  74.7 0.0 collective-permute-done.5.refs_0_
  74.7 2.1 %collective-permute-start.9 = (bf16[4,512,128]{2,1,0:T(8,128)(2,1)}, bf16[4,512,128]{2,1,0:T(8,128)(2,1)}, u32[]{:S(2)}, u32[]{:S(2)}) collective-permute-start(bf16[4,512,128]{2,1,0:T(8,128)(2,1)} %get-tuple-element.52), channel_id=1, source_target_pairs={{28,0},{29,1},{30,2},{31,3}} | collective-permute-start | bytes 1572872 | tf_op jit(solution)/shard_map/ppermute | solution.py:487
  76.8 2.9 %shard_map.52 = bf16[4,528,128]{2,1,0:T(8,128)(2,1)S(1)} custom-call(s32[1]{0:T(128)} %bitcast.here_ref, s32[8,2,16]{2,1,0:T(2,128)} %bitcast.2.picks_ref, bf16[512,2048]{1,0:T(8,128)(2,1)S(1)} %bitcast.11, bf16[512,2048]{1,0:T(8,128)(2,1)S(1)} %bitcast.18, bf16[4,512,128]{2,1,0:T(8,128)(2,1)} %collective-permute-done.5.refs_0_), custom_call_target="tpu_custom_call" | custom-call | flops 999999995904 | bytes 2097152 | tf_op jit(solution)/shard_map/pallas_call | solution.py:226
  79.7 0.0 collective-permute-done.6.refs_0_
  79.7 1.5 %collective-permute-start.11 = (bf16[4,528,128]{2,1,0:T(8,128)(2,1)S(1)}, bf16[4,528,128]{2,1,0:T(8,128)(2,1)S(1)}, u32[]{:S(2)}, u32[]{:S(2)}) collective-permute-start(bf16[4,528,128]{2,1,0:T(8,128)(2,1)S(1)} %shard_map.52), channel_id=1, source_target_pairs={{0,13},{1,14},{2,15},{3,12},{4,17},{5,18},{6,19},{7,16},{8,21},{9,... | collective-permute-start | bytes 1622024 | tf_op jit(solution)/shard_map/ppermute | solution.py:495
  81.2 2.9 %shard_map.53 = bf16[4,528,128]{2,1,0:T(8,128)(2,1)S(1)} custom-call(s32[1]{0:T(128)} %bitcast.here_ref, s32[8,2,16]{2,1,0:T(2,128)} %bitcast.2.picks_ref, bf16[512,2048]{1,0:T(8,128)(2,1)S(1)} %bitcast.12, bf16[512,2048]{1,0:T(8,128)(2,1)S(1)} %bitcast.19, bf16[4,512,128]{2,1,0:T(8,128)(2,1)} %collective-permute-done.6.refs_0_), custom_call_target="tpu_custom_call" | custom-call | flops 536870912 | bytes 2097152 | tf_op jit(solution)/shard_map/pallas_call | solution.py:226
  84.1 5.7 %collective-permute-done.7.refs_1_ = bf16[8,528,128]{2,1,0:T(8,128)(2,1)} collective-permute-done((bf16[8,528,128]{2,1,0:T(8,128)(2,1)}, bf16[8,528,128]{2,1,0:T(8,128)(2,1)}, u32[]{:S(2)}, u32[]{:S(2)}) %collective-permute-start.7) | collective-permute-done | bytes 1081376 | tf_op jit(solution)/shard_map/ppermute | solution.py:24
  89.8 1.3 collective-permute-start.12
  91.1 0.0 collective-permute-done.8.refs_0_
  91.1 2.9 %shard_map.54 = bf16[4,528,128]{2,1,0:T(8,128)(2,1)S(1)} custom-call(s32[1]{0:T(128)} %bitcast.here_ref, s32[8,2,16]{2,1,0:T(2,128)} %bitcast.2.picks_ref, bf16[512,2048]{1,0:T(8,128)(2,1)S(1)} %bitcast.13, bf16[512,2048]{1,0:T(8,128)(2,1)S(1)} %bitcast.20, bf16[4,512,128]{2,1,0:T(8,128)(2,1)} %collective-permute-done.8.refs_0_), custom_call_target="tpu_custom_call" | custom-call | flops 536870912 | bytes 2097152 | tf_op jit(solution)/shard_map/pallas_call | solution.py:226
  94.0 0.0 collective-permute-done.9.refs_0_
  94.0 2.9 %shard_map.55 = bf16[4,528,128]{2,1,0:T(8,128)(2,1)S(1)} custom-call(s32[1]{0:T(128)} %bitcast.here_ref, s32[8,2,16]{2,1,0:T(2,128)} %bitcast.2.picks_ref, bf16[512,2048]{1,0:T(8,128)(2,1)S(1)} %bitcast.14, bf16[512,2048]{1,0:T(8,128)(2,1)S(1)} %bitcast.21, bf16[4,512,128]{2,1,0:T(8,128)(2,1)} %collective-permute-done.9.refs_0_), custom_call_target="tpu_custom_call" | custom-call | flops 536870912 | bytes 2097152 | tf_op jit(solution)/shard_map/pallas_call | solution.py:226
  97.0 1.3 collective-permute-start.14
  98.3 1.3 collective-permute-start.13
  99.6 0.0 collective-permute-done.10.refs_2_
  99.6 34.5 %collective-permute-done.12.refs_4_ = bf16[4,528,128]{2,1,0:T(8,128)(2,1)S(1)} collective-permute-done((bf16[4,528,128]{2,1,0:T(8,128)(2,1)S(1)}, bf16[4,528,128]{2,1,0:T(8,128)(2,1)S(1)}, u32[]{:S(2)}, u32[]{:S(2)}) %collective-permute-start.12) | collective-permute-done | bytes 540704 | tf_op jit(solution)/shard_map/ppermute | solution.py:495
  134.0 0.0 collective-permute-done.11.refs_3_
  134.0 7.1 %shard_map.56 = (bf16[512,2048]{1,0:T(8,128)(2,1)}, f32[16,512,128]{2,1,0:T(8,128)S(1)}, f32[16,4,128]{2,1,0:T(4,128)S(1)}) custom-call(s32[1]{0:T(128)} %bitcast.here_ref, s32[8,2,16]{2,1,0:T(2,128)S(1)} %copy-done.8, bf16[16,528,128]{2,1,0:T(8,128)(2,1)} %collective-permute-done.3.refs_0_, bf16[8,528,128]{2,1,0:T(8,128)(2,1)} %collective-permute-done.7.refs_1_, ...), custom_call_target="tpu_custom_call" | custom-call | flops 6291456 | bytes 8912896 | tf_op jit(solution)/shard_map/pallas_call | solution.py:367
  141.2 0.0 collective-permute-done.14.refs_1_
  141.2 0.0 collective-permute-done.13.refs_0_
  141.2 3.3 %shard_map.57 = bf16[512,2048]{1,0:T(8,128)(2,1)} custom-call(s32[1]{0:T(128)} %bitcast.here_ref, s32[8,2,16]{2,1,0:T(2,128)S(1)} %copy-done.8, f32[16,512,128]{2,1,0:T(8,128)S(1)} %get-tuple-element.54.mixed_ref, f32[16,4,128]{2,1,0:T(4,128)S(1)} %get-tuple-element.55.sums_ref, ...), custom_call_target="tpu_custom_call", output_to_operand_aliasing={{}: (6, {})} | custom-call | flops 1048576 | bytes 4194304 | tf_op jit(solution)/shard_map/pallas_call | solution.py:448
  (12 shorter events, 0.0 us)
Async XLA Ops:
  0.0 1.6 %copy-start = (bf16[1,512,2048]{2,1,0:T(8,128)(2,1)S(1)}, bf16[1,512,2048]{2,1,0:T(8,128)(2,1)}, u32[]{:S(2)}) copy-start(bf16[1,512,2048]{2,1,0:T(8,128)(2,1)} %param.5) | copy-start | bytes 6291460
  1.6 1.6 %copy-start.2 = (bf16[1,512,2048]{2,1,0:T(8,128)(2,1)S(1)}, bf16[1,512,2048]{2,1,0:T(8,128)(2,1)}, u32[]{:S(2)}) copy-start(bf16[1,512,2048]{2,1,0:T(8,128)(2,1)} %param.6) | copy-start | bytes 6291460
  3.2 4.2 %copy-start.4 = (bf16[1,512,2048]{2,1,0:T(8,128)(2,1)S(1)}, bf16[1,512,2048]{2,1,0:T(8,128)(2,1)}, u32[]{:S(2)}) copy-start(bf16[1,512,2048]{2,1,0:T(8,128)(2,1)} %param.4) | copy-start | bytes 6291460
  6.0 26.0 %collective-permute-start.1 = (bf16[8,512,128]{2,1,0:T(8,128)(2,1)S(1)}, bf16[8,512,128]{2,1,0:T(8,128)(2,1)S(1)}, u32[]{:S(2)}, u32[]{:S(2)}) collective-permute-start(bf16[8,512,128]{2,1,0:T(8,128)(2,1)S(1)} %get-tuple-element.31), channel_id=1, source_target_pairs={{0,8},{4,12},{8,16},{12,20},{16,24},{20,28},{1,9},{5,13},{9,17},{1... | collective-permute-start | bytes 3145736 | tf_op jit(solution)/shard_map/ppermute | solution.py:484
  7.4 11.0 %copy-start.1 = (bf16[1,512,2048]{2,1,0:T(8,128)(2,1)S(1)}, bf16[1,512,2048]{2,1,0:T(8,128)(2,1)}, u32[]{:S(2)}) copy-start(bf16[1,512,2048]{2,1,0:T(8,128)(2,1)} %param.5) | copy-start | bytes 6291460
  7.4 11.0 %copy-start.3 = (bf16[1,512,2048]{2,1,0:T(8,128)(2,1)S(1)}, bf16[1,512,2048]{2,1,0:T(8,128)(2,1)}, u32[]{:S(2)}) copy-start(bf16[1,512,2048]{2,1,0:T(8,128)(2,1)} %param.6) | copy-start | bytes 6291460
  8.6 20.0 %collective-permute-start.2 = (bf16[4,512,128]{2,1,0:T(8,128)(2,1)S(1)}, bf16[4,512,128]{2,1,0:T(8,128)(2,1)S(1)}, u32[]{:S(2)}, u32[]{:S(2)}) collective-permute-start(bf16[4,512,128]{2,1,0:T(8,128)(2,1)S(1)} %shard_map.47), channel_id=1, source_target_pairs={{16,0},{20,4},{24,8},{28,12},{17,1},{21,5},{25,9},{29,13},{18,2},{... | collective-permute-start | bytes 1572872 | tf_op jit(solution)/shard_map/ppermute | solution.py:487
  12.5 5.8 %collective-permute-start = (s32[8,2,16]{2,1,0:T(2,128)}, s32[8,2,16]{2,1,0:T(2,128)S(1)}, u32[]{:S(2)}, u32[]{:S(2)}) collective-permute-start(s32[8,2,16]{2,1,0:T(2,128)} %bitcast.2.picks_ref), channel_id=1, source_target_pairs={{0,1},{1,2},{2,3},{3,0},{4,5},{5,6},{6,7},{7,4},{8,9},{9,10},{10,1... | collective-permute-start | bytes 3080 | tf_op jit(solution)/shard_map/ppermute | solution.py:24
  18.4 9.0 %copy-start.7 = (s32[8,2,16]{2,1,0:T(2,128)}, s32[8,2,16]{2,1,0:T(2,128)S(1)}, u32[]{:S(2)}) copy-start(s32[8,2,16]{2,1,0:T(2,128)S(1)} %collective-permute-done.picks_ref) | copy-start | bytes 3076
  27.4 24.0 %collective-permute-start.3 = (bf16[16,528,128]{2,1,0:T(8,128)(2,1)}, bf16[16,528,128]{2,1,0:T(8,128)(2,1)}, u32[]{:S(2)}, u32[]{:S(2)}) collective-permute-start(bf16[16,528,128]{2,1,0:T(8,128)(2,1)} %shard_map.49), channel_id=1, source_target_pairs={{0,1},{1,2},{2,3},{3,0},{4,5},{5,6},{6,7},{7,4},{8,9},{9,10},{10,1... | collective-permute-start | bytes 6488072 | tf_op jit(solution)/shard_map/ppermute | solution.py:24
  27.4 28.3 %collective-permute-start.4 = (bf16[8,512,128]{2,1,0:T(8,128)(2,1)}, bf16[8,512,128]{2,1,0:T(8,128)(2,1)}, u32[]{:S(2)}, u32[]{:S(2)}) collective-permute-start(bf16[8,512,128]{2,1,0:T(8,128)(2,1)} %get-tuple-element.44), channel_id=1, source_target_pairs={{0,24},{4,28},{1,25},{5,29},{2,26},{6,30},{3,27},{7,31}} | collective-permute-start | bytes 3145736 | tf_op jit(solution)/shard_map/ppermute | solution.py:484
  32.1 1.0 copy-start.5
  33.1 41.6 %collective-permute-start.5 = (bf16[4,512,128]{2,1,0:T(8,128)(2,1)}, bf16[4,512,128]{2,1,0:T(8,128)(2,1)}, u32[]{:S(2)}, u32[]{:S(2)}) collective-permute-start(bf16[4,512,128]{2,1,0:T(8,128)(2,1)} %get-tuple-element.46), channel_id=1, source_target_pairs={{12,0},{16,4},{20,8},{24,12},{28,16},{13,1},{17,5},{21,9},{25,13},... | collective-permute-start | bytes 1572872 | tf_op jit(solution)/shard_map/ppermute | solution.py:487
  38.2 41.5 %collective-permute-start.6 = (bf16[4,512,128]{2,1,0:T(8,128)(2,1)}, bf16[4,512,128]{2,1,0:T(8,128)(2,1)}, u32[]{:S(2)}, u32[]{:S(2)}) collective-permute-start(bf16[4,512,128]{2,1,0:T(8,128)(2,1)} %get-tuple-element.48), channel_id=1, source_target_pairs={{20,0},{24,4},{28,8},{21,1},{25,5},{29,9},{22,2},{26,6},{30,10},{2... | collective-permute-start | bytes 1572872 | tf_op jit(solution)/shard_map/ppermute | solution.py:487
  40.3 15.3 %copy-start.6 = (bf16[8,512,128]{2,1,0:T(8,128)(2,1)S(1)}, bf16[8,512,128]{2,1,0:T(8,128)(2,1)}, u32[]{:S(2)}) copy-start(bf16[8,512,128]{2,1,0:T(8,128)(2,1)} %copy-done.5) | copy-start | bytes 3145732
  43.9 55.7 %collective-permute-start.10 = (bf16[4,528,128]{2,1,0:T(8,128)(2,1)}, bf16[4,528,128]{2,1,0:T(8,128)(2,1)}, u32[]{:S(2)}, u32[]{:S(2)}) collective-permute-start(bf16[4,528,128]{2,1,0:T(8,128)(2,1)} %shard_map.50), channel_id=1, source_target_pairs={{0,17},{1,18},{2,19},{3,16},{4,21},{5,22},{6,23},{7,20},{8,25},{9,... | collective-permute-start | bytes 1622024 | tf_op jit(solution)/shard_map/ppermute | solution.py:495
  61.0 28.8 %collective-permute-start.7 = (bf16[8,528,128]{2,1,0:T(8,128)(2,1)}, bf16[8,528,128]{2,1,0:T(8,128)(2,1)}, u32[]{:S(2)}, u32[]{:S(2)}) collective-permute-start(bf16[8,528,128]{2,1,0:T(8,128)(2,1)} %shard_map.51), channel_id=1, source_target_pairs={{0,1},{1,2},{2,3},{3,0},{4,5},{5,6},{6,7},{7,4},{8,9},{9,10},{10,1... | collective-permute-start | bytes 3244040 | tf_op jit(solution)/shard_map/ppermute | solution.py:24
  71.7 19.3 %collective-permute-start.8 = (bf16[4,512,128]{2,1,0:T(8,128)(2,1)}, bf16[4,512,128]{2,1,0:T(8,128)(2,1)}, u32[]{:S(2)}, u32[]{:S(2)}) collective-permute-start(bf16[4,512,128]{2,1,0:T(8,128)(2,1)} %get-tuple-element.50), channel_id=1, source_target_pairs={{4,0},{8,4},{12,8},{16,12},{20,16},{24,20},{28,24},{5,1},{9,5},{13... | collective-permute-start | bytes 1572872 | tf_op jit(solution)/shard_map/ppermute | solution.py:487
  74.7 19.3 %collective-permute-start.9 = (bf16[4,512,128]{2,1,0:T(8,128)(2,1)}, bf16[4,512,128]{2,1,0:T(8,128)(2,1)}, u32[]{:S(2)}, u32[]{:S(2)}) collective-permute-start(bf16[4,512,128]{2,1,0:T(8,128)(2,1)} %get-tuple-element.52), channel_id=1, source_target_pairs={{28,0},{29,1},{30,2},{31,3}} | collective-permute-start | bytes 1572872 | tf_op jit(solution)/shard_map/ppermute | solution.py:487
  79.7 54.3 %collective-permute-start.11 = (bf16[4,528,128]{2,1,0:T(8,128)(2,1)S(1)}, bf16[4,528,128]{2,1,0:T(8,128)(2,1)S(1)}, u32[]{:S(2)}, u32[]{:S(2)}) collective-permute-start(bf16[4,528,128]{2,1,0:T(8,128)(2,1)S(1)} %shard_map.52), channel_id=1, source_target_pairs={{0,13},{1,14},{2,15},{3,12},{4,17},{5,18},{6,19},{7,16},{8,21},{9,... | collective-permute-start | bytes 1622024 | tf_op jit(solution)/shard_map/ppermute | solution.py:495
  89.8 44.3 %collective-permute-start.12 = (bf16[4,528,128]{2,1,0:T(8,128)(2,1)S(1)}, bf16[4,528,128]{2,1,0:T(8,128)(2,1)S(1)}, u32[]{:S(2)}, u32[]{:S(2)}) collective-permute-start(bf16[4,528,128]{2,1,0:T(8,128)(2,1)S(1)} %shard_map.53), channel_id=1, source_target_pairs={{0,21},{1,22},{2,23},{3,20},{4,25},{5,26},{6,27},{7,24},{8,29},{9,... | collective-permute-start | bytes 1622024 | tf_op jit(solution)/shard_map/ppermute | solution.py:495
  94.0 40.0 %copy-start.8 = (s32[8,2,16]{2,1,0:T(2,128)S(1)}, s32[8,2,16]{2,1,0:T(2,128)}, u32[]{:S(2)}) copy-start(s32[8,2,16]{2,1,0:T(2,128)} %copy-done.7) | copy-start | bytes 3076
  97.0 44.2 %collective-permute-start.14 = (bf16[4,528,128]{2,1,0:T(8,128)(2,1)S(1)}, bf16[4,528,128]{2,1,0:T(8,128)(2,1)S(1)}, u32[]{:S(2)}, u32[]{:S(2)}) collective-permute-start(bf16[4,528,128]{2,1,0:T(8,128)(2,1)S(1)} %shard_map.55), channel_id=1, source_target_pairs={{0,29},{1,30},{2,31},{3,28}} | collective-permute-start | bytes 1622024 | tf_op jit(solution)/shard_map/ppermute | solution.py:495
  98.3 42.9 %collective-permute-start.13 = (bf16[4,528,128]{2,1,0:T(8,128)(2,1)S(1)}, bf16[4,528,128]{2,1,0:T(8,128)(2,1)S(1)}, u32[]{:S(2)}, u32[]{:S(2)}) collective-permute-start(bf16[4,528,128]{2,1,0:T(8,128)(2,1)S(1)} %shard_map.54), channel_id=1, source_target_pairs={{0,5},{1,6},{2,7},{3,4},{4,9},{5,10},{6,11},{7,8},{8,13},{9,14},{1... | collective-permute-start | bytes 1622024 | tf_op jit(solution)/shard_map/ppermute | solution.py:495

commit v11 on v10

--- a/solution.py
+++ b/solution.py
@@ -477,8 +477,8 @@
 
     near_shifts = (2, width - 2)
     middle = width // 2
-    far_shifts = [middle, middle - 1, middle + 1, 1, width - 1]
-    final_shifts = tuple(far_shifts[3:])
+    far_shifts = [middle - 1, middle + 1, middle, 1, width - 1]
+    final_shifts = tuple(far_shifts[2:])
 
     def up(value, shift):
         return lax.ppermute(value, "ctx", [(at, at + shift) for at in range(width - shift)])
@@ -499,7 +499,7 @@
     near = [up(near_sends[0], near_shifts[0])]
     before = passed_along(own_picks, "pipe", 1)
     sends, now = {}, after(here, *near_sends)
-    for shifts in (far_shifts[:1], far_shifts[1:]):
+    for shifts in (far_shifts[:2], far_shifts[2:]):
         jobs = [(shift, 0, slots, False) for shift in shifts]
         packed = pack(now, own_picks, [queries], jobs, slots)
         sends |= zip(shifts, packed)
@@ -514,32 +514,32 @@
             token, own_picks, keys, values, [arrived[shift]], ((shift, 0, slots),), slots, is_anchor
         )[0]
 
-    four, three, five, one, seven = far_shifts
-    ask_for(four, near_sends[0])
+    three, five, four, one, seven = far_shifts
+    ask_for(three, near_sends[0])
+    ask_for(five, near_sends[0])
     own = own_part(after(now, before), queries, keys, values)
     own_back = passed_along(own, "pipe", 1)
     near.append(up(after(near_sends[1], own), near_shifts[1]))
-    ask_for(three, arrived[four], near[0], own)
-    ask_for(five, arrived[four], near[0], own)
-    part_four = work(after(here, own, near[0]), four, is_anchor=True)
+    part_three = work(after(here, own, near[0]), three, is_anchor=True)
+    returned[three] = up_and_on(part_three, three)
+    part_five = work(after(here, part_three), five, is_anchor=True)
+    returned[five] = up_and_on(part_five, five)
+    ask_for(four, arrived[three], arrived[five], near[0])
+    beside = near_part(after(here, part_five, own_back), own_picks, queries, near, near_shifts, slots)
+    ask_for(one, own_back, part_five, *near)
+    ask_for(seven, own_back, part_five, *near)
+    beside_back = passed_along(beside, "pipe", 1)
+    part_four = work(after(here, beside), four, is_anchor=True)
     returned[four] = up_and_on(part_four, four)
-    beside = near_part(after(here, part_four, own_back), own_picks, queries, near, near_shifts, slots)
-    ask_for(one, own_back, part_four, *near)
-    ask_for(seven, own_back, part_four, *near)
-    part_three = work(after(here, beside), three, is_anchor=True)
-    returned[three] = up_and_on(part_three, three)
-    part_five = work(after(here, part_three), five)
-    returned[five] = up_and_on(part_five, five)
-    beside_back = passed_along(beside, "pipe", 1)
-    part_one = work(after(here, part_five, beside_back), one)
+    part_one = work(after(here, part_four, beside_back), one)
     returned[one] = up_and_on(part_one, one)
     part_seven = work(after(here, part_one), seven)
     returned[seven] = up_and_on(part_seven, seven)
     now = after(here, part_seven)
 
-    merged_shifts = near_shifts + (four, three, five)
-    places = [HEADS + place * slots for place in (2, 3, 4)]
-    parts = [own_back, beside_back, returned[four], returned[three], returned[five]]
+    merged_shifts = near_shifts + (three, five)
+    places = [HEADS + place * slots for place in (2, 3)]
+    parts = [own_back, beside_back, returned[three], returned[five]]
     result, mixed, sums = merge(now, before, parts, [0, HEADS] + places, merged_shifts, slots)
     lasts = [returned[shift] for shift in final_shifts]
     return finish(now, before, result, mixed, sums, lasts, final_shifts, slots)[None]

time: 145 us -> 143 us (0.986)
  the two profiles are of different devices: /device:TPU:29 before, /device:TPU:26 now
where the time goes in v11:
time: 143 us; the launch traced here: 141 us
  starting transfers between devices  49.4 us (35%)
  Pallas kernels  49.1 us (34%)
  waiting for transfers between devices  36.9 us (26%)
  local copies, waits for them, and re-layouts  4.91 us (3%)
    ppermute x5, starting transfers between devices, down(): lax.ppermute(value, 'ctx', [(at, at - shift) for at in range(shift, width)])  39.7 us
    ppermute x5, waiting for transfers between devices, up_and_on(): return lax.ppermute(value, ('ctx', 'pipe'), pairs)  17 us
    pallas_call x5, Pallas kernels, attend(): call(functools.partial(attend_kernel, group=group, slots=slots), [SCALARS...  16 us
    ppermute x5, waiting for transfers between devices, down(): lax.ppermute(value, 'ctx', [(at, at - shift) for at in range(shift, width)])  12.5 us
    pallas_call x1, Pallas kernels, own_part(): call(own_kernel, [SCALARS, IN_VMEM, IN_VMEM, IN_VMEM], jax.ShapeDtypeStru...  8.95 us
    pallas_call x3, Pallas kernels, pack(): call(functools.partial(pack_kernel, jobs=jobs, slots=slots), [SCALARS, SC...  7.47 us
    pallas_call x1, Pallas kernels, merge(): call(functools.partial(merge_kernel, places=tuple(places), shifts=shifts,...  7.26 us
    ppermute x5, starting transfers between devices, up_and_on(): return lax.ppermute(value, ('ctx', 'pipe'), pairs)  6.47 us
  transfers between devices with their start and end apart: 15, of which 5 were waited for; matrix products, arithmetic and copies ran while one was open for 0% of the time, Pallas kernels for 30%

profile of v11, /device:TPU:26, one launch (start us, length us, event | category | flops | bytes accessed | tf_op | source)
XLA Modules:
  0.0 140.8 jit_solution(16232336834903080685)
XLA Ops:
  0.0 1.6 %copy-done.1 = bf16[1,512,2048]{2,1,0:T(8,128)(2,1)S(1)} copy-done((bf16[1,512,2048]{2,1,0:T(8,128)(2,1)S(1)}, bf16[1,512,2048]{2,1,0:T(8,128)(2,1)}, u32[]{:S(2)}) %copy-start.1) | copy-done | bytes 2097176
  1.6 1.6 %copy-done.2 = bf16[1,512,2048]{2,1,0:T(8,128)(2,1)S(1)} copy-done((bf16[1,512,2048]{2,1,0:T(8,128)(2,1)S(1)}, bf16[1,512,2048]{2,1,0:T(8,128)(2,1)}, u32[]{:S(2)}) %copy-start.2) | copy-done | bytes 2097176
  3.2 0.7 copy-done.6
  3.9 2.6 %shard_map.46 = (bf16[8,512,128]{2,1,0:T(8,128)(2,1)S(1)}, bf16[8,512,128]{2,1,0:T(8,128)(2,1)}) custom-call(s32[1]{0:T(128)} %bitcast.here_ref, s32[8,2,16]{2,1,0:T(2,128)S(1)} %bitcast.26, bf16[512,2048]{1,0:T(8,128)(2,1)S(1)} %bitcast.12, bf16[512,2048]{1,0:T(8,128)(2,1)S(1)} %bitcast.19), custom_call_target="tpu_custom_call" | custom-call | bytes 4194304 | tf_op jit(solution)/shard_map/pallas_call | solution.py:127
  6.5 1.3 collective-permute-start.1
  7.8 0.0 copy-start.3
  7.8 2.1 %shard_map.47 = (bf16[4,512,128]{2,1,0:T(8,128)(2,1)S(1)}, bf16[4,512,128]{2,1,0:T(8,128)(2,1)}) custom-call(s32[1]{0:T(128)} %bitcast.here_ref, s32[8,2,16]{2,1,0:T(2,128)S(1)} %bitcast.27, bf16[512,2048]{1,0:T(8,128)(2,1)S(1)} %bitcast.8), custom_call_target="tpu_custom_call" | custom-call | bytes 2097152 | tf_op jit(solution)/shard_map/pallas_call | solution.py:127
  9.9 5.4 %collective-permute-start.2 = (bf16[4,512,128]{2,1,0:T(8,128)(2,1)S(1)}, bf16[4,512,128]{2,1,0:T(8,128)(2,1)S(1)}, u32[]{:S(2)}, u32[]{:S(2)}) collective-permute-start(bf16[4,512,128]{2,1,0:T(8,128)(2,1)S(1)} %get-tuple-element.44), channel_id=1, source_target_pairs={{12,0},{16,4},{20,8},{24,12},{28,16},{13,1},{17,5},{21,9},{25,13},... | collective-permute-start | bytes 1572872 | tf_op jit(solution)/shard_map/ppermute | solution.py:487
  15.4 0.1 collective-permute-start
  15.4 2.1 %collective-permute-start.3 = (bf16[4,512,128]{2,1,0:T(8,128)(2,1)}, bf16[4,512,128]{2,1,0:T(8,128)(2,1)}, u32[]{:S(2)}, u32[]{:S(2)}) collective-permute-start(bf16[4,512,128]{2,1,0:T(8,128)(2,1)} %get-tuple-element.46), channel_id=1, source_target_pairs={{20,0},{24,4},{28,8},{21,1},{25,5},{29,9},{22,2},{26,6},{30,10},{2... | collective-permute-start | bytes 1572872 | tf_op jit(solution)/shard_map/ppermute | solution.py:487
  17.6 2.8 %shard_map.48 = (bf16[4,512,128]{2,1,0:T(8,128)(2,1)}, bf16[4,512,128]{2,1,0:T(8,128)(2,1)}, bf16[4,512,128]{2,1,0:T(8,128)(2,1)}) custom-call(s32[1]{0:T(128)} %bitcast.here_ref, s32[8,2,16]{2,1,0:T(2,128)S(1)} %bitcast.29, bf16[512,2048]{1,0:T(8,128)(2,1)S(1)} %bitcast.9), custom_call_target="tpu_custom_call" | custom-call | bytes 3145728 | tf_op jit(solution)/shard_map/pallas_call | solution.py:127
  20.3 0.0 collective-permute-done.picks_ref
  20.4 0.0 copy-done.3
  20.4 8.9 %shard_map.49 = bf16[16,528,128]{2,1,0:T(8,128)(2,1)} custom-call(s32[1]{0:T(128)} %bitcast.here_ref, bf16[512,2048]{1,0:T(8,128)(2,1)S(1)} %bitcast.10, bf16[512,2048]{1,0:T(8,128)(2,1)S(1)} %bitcast.13, bf16[512,2048]{1,0:T(8,128)(2,1)S(1)} %bitcast.20), custom_call_target="tpu_custom_call" | custom-call | flops 2147483648 | bytes 8388608 | tf_op jit(solution)/shard_map/pallas_call | solution.py:266
  29.3 0.6 collective-permute-start.4
  29.9 1.3 collective-permute-start.5
  31.2 2.1 %collective-permute-done.1.refs_0_ = bf16[8,512,128]{2,1,0:T(8,128)(2,1)S(1)} collective-permute-done((bf16[8,512,128]{2,1,0:T(8,128)(2,1)S(1)}, bf16[8,512,128]{2,1,0:T(8,128)(2,1)S(1)}, u32[]{:S(2)}, u32[]{:S(2)}) %collective-permute-start.1) | collective-permute-done | bytes 1048608 | tf_op jit(solution)/shard_map/ppermute | solution.py:484
  33.3 1.0 copy-done.4
  34.3 0.0 collective-permute-done.2.refs_0_
  34.3 3.4 %shard_map.50 = bf16[4,528,128]{2,1,0:T(8,128)(2,1)} custom-call(s32[1]{0:T(128)} %bitcast.here_ref, s32[8,2,16]{2,1,0:T(2,128)S(1)} %bitcast.30, bf16[512,2048]{1,0:T(8,128)(2,1)S(1)} %bitcast.14, bf16[512,2048]{1,0:T(8,128)(2,1)S(1)} %bitcast.21, bf16[4,512,128]{2,1,0:T(8,128)(2,1)S(1)} %collective-permute-done.2.refs_0_), custom_call_target="tpu_custom_call" | custom-call | flops 999999995904 | bytes 2097152 | tf_op jit(solution)/shard_map/pallas_call | solution.py:226
  37.7 1.3 collective-permute-start.10
  38.9 0.0 collective-permute-done.3.refs_0_
  39.0 10.6 %collective-permute-start.6 = (bf16[4,512,128]{2,1,0:T(8,128)(2,1)}, bf16[4,512,128]{2,1,0:T(8,128)(2,1)}, u32[]{:S(2)}, u32[]{:S(2)}) collective-permute-start(bf16[4,512,128]{2,1,0:T(8,128)(2,1)} %get-tuple-element.50), channel_id=1, source_target_pairs={{16,0},{20,4},{24,8},{28,12},{17,1},{21,5},{25,9},{29,13},{18,2},{... | collective-permute-start | bytes 1572872 | tf_op jit(solution)/shard_map/ppermute | solution.py:487
  49.5 3.9 %shard_map.51 = bf16[4,528,128]{2,1,0:T(8,128)(2,1)} custom-call(s32[1]{0:T(128)} %bitcast.here_ref, s32[8,2,16]{2,1,0:T(2,128)S(1)} %bitcast.31, bf16[512,2048]{1,0:T(8,128)(2,1)S(1)} %bitcast.15, bf16[512,2048]{1,0:T(8,128)(2,1)S(1)} %bitcast.22, bf16[4,512,128]{2,1,0:T(8,128)(2,1)} %collective-permute-done.3.refs_0_), custom_call_target="tpu_custom_call" | custom-call | flops 999999995904 | bytes 2097152 | tf_op jit(solution)/shard_map/pallas_call | solution.py:226
  53.4 1.3 collective-permute-start.11
  54.7 1.2 collective-permute-done.4.refs_0_
  55.9 4.1 %collective-permute-done.5.refs_1_ = bf16[8,512,128]{2,1,0:T(8,128)(2,1)} collective-permute-done((bf16[8,512,128]{2,1,0:T(8,128)(2,1)}, bf16[8,512,128]{2,1,0:T(8,128)(2,1)}, u32[]{:S(2)}, u32[]{:S(2)}) %collective-permute-start.5) | collective-permute-done | bytes 1048608 | tf_op jit(solution)/shard_map/ppermute | solution.py:484
  60.0 5.4 %shard_map.52 = bf16[8,528,128]{2,1,0:T(8,128)(2,1)} custom-call(s32[1]{0:T(128)} %bitcast.here_ref, s32[8,2,16]{2,1,0:T(2,128)S(1)} %bitcast.32, bf16[512,2048]{1,0:T(8,128)(2,1)S(1)} %bitcast.11, bf16[8,512,128]{2,1,0:T(8,128)(2,1)S(1)} %copy-done.5, bf16[8,512,128]{2,1,0:T(8,128)(2,1)} %collective-permute-done.5.refs_1_), custom_call_target="tpu_custom_call" | custom-call | flops 1073741824 | bytes 6291456 | tf_op jit(solution)/shard_map/pallas_call | solution.py:295
  65.4 0.0 collective-permute-start.7
  65.4 20.0 %collective-permute-start.8 = (bf16[4,512,128]{2,1,0:T(8,128)(2,1)}, bf16[4,512,128]{2,1,0:T(8,128)(2,1)}, u32[]{:S(2)}, u32[]{:S(2)}) collective-permute-start(bf16[4,512,128]{2,1,0:T(8,128)(2,1)} %get-tuple-element.52), channel_id=1, source_target_pairs={{4,0},{8,4},{12,8},{16,12},{20,16},{24,20},{28,24},{5,1},{9,5},{13... | collective-permute-start | bytes 1572872 | tf_op jit(solution)/shard_map/ppermute | solution.py:487
  85.3 0.0 collective-permute-done.6.refs_0_
  85.3 1.6 %collective-permute-start.9 = (bf16[4,512,128]{2,1,0:T(8,128)(2,1)}, bf16[4,512,128]{2,1,0:T(8,128)(2,1)}, u32[]{:S(2)}, u32[]{:S(2)}) collective-permute-start(bf16[4,512,128]{2,1,0:T(8,128)(2,1)} %get-tuple-element.54), channel_id=1, source_target_pairs={{28,0},{29,1},{30,2},{31,3}} | collective-permute-start | bytes 1572872 | tf_op jit(solution)/shard_map/ppermute | solution.py:487
  87.0 2.9 %shard_map.53 = bf16[4,528,128]{2,1,0:T(8,128)(2,1)S(1)} custom-call(s32[1]{0:T(128)} %bitcast.here_ref, s32[8,2,16]{2,1,0:T(2,128)S(1)} %bitcast.33, bf16[512,2048]{1,0:T(8,128)(2,1)S(1)} %bitcast.16, bf16[512,2048]{1,0:T(8,128)(2,1)S(1)} %bitcast.23, bf16[4,512,128]{2,1,0:T(8,128)(2,1)} %collective-permute-done.6.refs_0_), custom_call_target="tpu_custom_call" | custom-call | flops 999999995904 | bytes 2097152 | tf_op jit(solution)/shard_map/pallas_call | solution.py:226
  89.9 0.0 collective-permute-done.7.refs_1_
  89.9 1.3 collective-permute-start.12
  91.2 12.5 %collective-permute-done.8.refs_0_ = bf16[4,512,128]{2,1,0:T(8,128)(2,1)} collective-permute-done((bf16[4,512,128]{2,1,0:T(8,128)(2,1)}, bf16[4,512,128]{2,1,0:T(8,128)(2,1)}, u32[]{:S(2)}, u32[]{:S(2)}) %collective-permute-start.8) | collective-permute-done | bytes 524320 | tf_op jit(solution)/shard_map/ppermute | solution.py:487
  103.7 2.9 %shard_map.54 = bf16[4,528,128]{2,1,0:T(8,128)(2,1)S(1)} custom-call(s32[1]{0:T(128)} %bitcast.here_ref, s32[8,2,16]{2,1,0:T(2,128)S(1)} %bitcast.34, bf16[512,2048]{1,0:T(8,128)(2,1)S(1)} %bitcast.17, bf16[512,2048]{1,0:T(8,128)(2,1)S(1)} %bitcast.24, bf16[4,512,128]{2,1,0:T(8,128)(2,1)} %collective-permute-done.8.refs_0_), custom_call_target="tpu_custom_call" | custom-call | flops 536870912 | bytes 2097152 | tf_op jit(solution)/shard_map/pallas_call | solution.py:226
  106.6 0.0 collective-permute-done.9.refs_0_
  106.6 2.9 %shard_map.55 = bf16[4,528,128]{2,1,0:T(8,128)(2,1)S(1)} custom-call(s32[1]{0:T(128)} %bitcast.here_ref, s32[8,2,16]{2,1,0:T(2,128)S(1)} %bitcast.35, bf16[512,2048]{1,0:T(8,128)(2,1)S(1)} %bitcast.18, bf16[512,2048]{1,0:T(8,128)(2,1)S(1)} %bitcast.25, bf16[4,512,128]{2,1,0:T(8,128)(2,1)} %collective-permute-done.9.refs_0_), custom_call_target="tpu_custom_call" | custom-call | flops 536870912 | bytes 2097152 | tf_op jit(solution)/shard_map/pallas_call | solution.py:226
  109.6 0.7 collective-permute-start.14
  110.3 1.9 %collective-permute-start.13 = (bf16[4,528,128]{2,1,0:T(8,128)(2,1)S(1)}, bf16[4,528,128]{2,1,0:T(8,128)(2,1)S(1)}, u32[]{:S(2)}, u32[]{:S(2)}) collective-permute-start(bf16[4,528,128]{2,1,0:T(8,128)(2,1)S(1)} %shard_map.54), channel_id=1, source_target_pairs={{0,5},{1,6},{2,7},{3,4},{4,9},{5,10},{6,11},{7,8},{8,13},{9,14},{1... | collective-permute-start | bytes 1622024 | tf_op jit(solution)/shard_map/ppermute | solution.py:495
  112.2 0.0 collective-permute-done.11.refs_3_
  112.2 0.0 collective-permute-done.10.refs_2_
  112.2 7.3 %shard_map.56 = (bf16[512,2048]{1,0:T(8,128)(2,1)}, f32[16,512,128]{2,1,0:T(8,128)S(1)}, f32[16,4,128]{2,1,0:T(4,128)S(1)}) custom-call(s32[1]{0:T(128)} %bitcast.here_ref, s32[8,2,16]{2,1,0:T(2,128)S(1)} %copy-done.9, bf16[16,528,128]{2,1,0:T(8,128)(2,1)} %collective-permute-done.4.refs_0_, bf16[8,528,128]{2,1,0:T(8,128)(2,1)} %collective-permute-done.7.refs_1_, ...), custom_call_target="tpu_custom_call" | custom-call | flops 6291456 | bytes 8388608 | tf_op jit(solution)/shard_map/pallas_call | solution.py:367
  119.5 0.0 collective-permute-done.12.refs_0_
  119.5 0.0 collective-permute-done.14.refs_2_
  119.5 17.0 %collective-permute-done.13.refs_1_ = bf16[4,528,128]{2,1,0:T(8,128)(2,1)S(1)} collective-permute-done((bf16[4,528,128]{2,1,0:T(8,128)(2,1)S(1)}, bf16[4,528,128]{2,1,0:T(8,128)(2,1)S(1)}, u32[]{:S(2)}, u32[]{:S(2)}) %collective-permute-start.13) | collective-permute-done | bytes 540704 | tf_op jit(solution)/shard_map/ppermute | solution.py:495
  136.5 4.1 %shard_map.57 = bf16[512,2048]{1,0:T(8,128)(2,1)} custom-call(s32[1]{0:T(128)} %bitcast.here_ref, s32[8,2,16]{2,1,0:T(2,128)S(1)} %copy-done.9, f32[16,512,128]{2,1,0:T(8,128)S(1)} %get-tuple-element.56.mixed_ref, f32[16,4,128]{2,1,0:T(4,128)S(1)} %get-tuple-element.57.sums_ref, ...), custom_call_target="tpu_custom_call", output_to_operand_aliasing={{}: (7, {})} | custom-call | flops 1572864 | bytes 6291456 | tf_op jit(solution)/shard_map/pallas_call | solution.py:448
  (14 shorter events, 0.0 us)
Async XLA Ops:
  0.0 1.6 %copy-start.1 = (bf16[1,512,2048]{2,1,0:T(8,128)(2,1)S(1)}, bf16[1,512,2048]{2,1,0:T(8,128)(2,1)}, u32[]{:S(2)}) copy-start(bf16[1,512,2048]{2,1,0:T(8,128)(2,1)} %param.5) | copy-start | bytes 6291460
  1.6 1.6 %copy-start.2 = (bf16[1,512,2048]{2,1,0:T(8,128)(2,1)S(1)}, bf16[1,512,2048]{2,1,0:T(8,128)(2,1)}, u32[]{:S(2)}) copy-start(bf16[1,512,2048]{2,1,0:T(8,128)(2,1)} %param.6) | copy-start | bytes 6291460
  3.2 0.7 copy-start.6
  3.9 3.9 %copy-start = (bf16[1,512,2048]{2,1,0:T(8,128)(2,1)S(1)}, bf16[1,512,2048]{2,1,0:T(8,128)(2,1)}, u32[]{:S(2)}) copy-start(bf16[1,512,2048]{2,1,0:T(8,128)(2,1)} %param.4) | copy-start | bytes 6291460
  3.9 3.9 %copy-start.7 = (s32[1,8,16,2]{2,3,1,0:T(2,128)S(1)}, s32[1,8,16,2]{2,3,1,0:T(2,128)}, u32[]{:S(2)}) copy-start(s32[1,8,16,2]{2,3,1,0:T(2,128)} %param.7) | copy-start | bytes 3076
  6.5 26.8 %collective-permute-start.1 = (bf16[8,512,128]{2,1,0:T(8,128)(2,1)S(1)}, bf16[8,512,128]{2,1,0:T(8,128)(2,1)S(1)}, u32[]{:S(2)}, u32[]{:S(2)}) collective-permute-start(bf16[8,512,128]{2,1,0:T(8,128)(2,1)S(1)} %get-tuple-element.32), channel_id=1, source_target_pairs={{0,8},{4,12},{8,16},{12,20},{16,24},{20,28},{1,9},{5,13},{9,17},{1... | collective-permute-start | bytes 3145736 | tf_op jit(solution)/shard_map/ppermute | solution.py:484
  7.8 12.5 %copy-start.3 = (bf16[1,512,2048]{2,1,0:T(8,128)(2,1)S(1)}, bf16[1,512,2048]{2,1,0:T(8,128)(2,1)}, u32[]{:S(2)}) copy-start(bf16[1,512,2048]{2,1,0:T(8,128)(2,1)} %param.6) | copy-start | bytes 6291460
  9.9 24.4 %collective-permute-start.2 = (bf16[4,512,128]{2,1,0:T(8,128)(2,1)S(1)}, bf16[4,512,128]{2,1,0:T(8,128)(2,1)S(1)}, u32[]{:S(2)}, u32[]{:S(2)}) collective-permute-start(bf16[4,512,128]{2,1,0:T(8,128)(2,1)S(1)} %get-tuple-element.44), channel_id=1, source_target_pairs={{12,0},{16,4},{20,8},{24,12},{28,16},{13,1},{17,5},{21,9},{25,13},... | collective-permute-start | bytes 1572872 | tf_op jit(solution)/shard_map/ppermute | solution.py:487
  15.4 5.0 %collective-permute-start = (s32[8,2,16]{2,1,0:T(2,128)S(1)}, s32[8,2,16]{2,1,0:T(2,128)S(1)}, u32[]{:S(2)}, u32[]{:S(2)}) collective-permute-start(s32[8,2,16]{2,1,0:T(2,128)S(1)} %bitcast.28), channel_id=1, source_target_pairs={{0,1},{1,2},{2,3},{3,0},{4,5},{5,6},{6,7},{7,4},{8,9},{9,10},{10,1... | collective-permute-start | bytes 3080 | tf_op jit(solution)/shard_map/ppermute | solution.py:24
  15.4 23.5 %collective-permute-start.3 = (bf16[4,512,128]{2,1,0:T(8,128)(2,1)}, bf16[4,512,128]{2,1,0:T(8,128)(2,1)}, u32[]{:S(2)}, u32[]{:S(2)}) collective-permute-start(bf16[4,512,128]{2,1,0:T(8,128)(2,1)} %get-tuple-element.46), channel_id=1, source_target_pairs={{20,0},{24,4},{28,8},{21,1},{25,5},{29,9},{22,2},{26,6},{30,10},{2... | collective-permute-start | bytes 1572872 | tf_op jit(solution)/shard_map/ppermute | solution.py:487
  20.4 9.0 %copy-start.8 = (s32[8,2,16]{2,1,0:T(2,128)}, s32[8,2,16]{2,1,0:T(2,128)S(1)}, u32[]{:S(2)}) copy-start(s32[8,2,16]{2,1,0:T(2,128)S(1)} %collective-permute-done.picks_ref) | copy-start | bytes 3076
  29.3 26.6 %collective-permute-start.4 = (bf16[16,528,128]{2,1,0:T(8,128)(2,1)}, bf16[16,528,128]{2,1,0:T(8,128)(2,1)}, u32[]{:S(2)}, u32[]{:S(2)}) collective-permute-start(bf16[16,528,128]{2,1,0:T(8,128)(2,1)} %shard_map.49), channel_id=1, source_target_pairs={{0,1},{1,2},{2,3},{3,0},{4,5},{5,6},{6,7},{7,4},{8,9},{9,10},{10,1... | collective-permute-start | bytes 6488072 | tf_op jit(solution)/shard_map/ppermute | solution.py:24
  29.9 30.1 %collective-permute-start.5 = (bf16[8,512,128]{2,1,0:T(8,128)(2,1)}, bf16[8,512,128]{2,1,0:T(8,128)(2,1)}, u32[]{:S(2)}, u32[]{:S(2)}) collective-permute-start(bf16[8,512,128]{2,1,0:T(8,128)(2,1)} %get-tuple-element.48), channel_id=1, source_target_pairs={{0,24},{4,28},{1,25},{5,29},{2,26},{6,30},{3,27},{7,31}} | collective-permute-start | bytes 3145736 | tf_op jit(solution)/shard_map/ppermute | solution.py:484
  33.3 1.0 copy-start.4
  37.7 74.6 %collective-permute-start.10 = (bf16[4,528,128]{2,1,0:T(8,128)(2,1)}, bf16[4,528,128]{2,1,0:T(8,128)(2,1)}, u32[]{:S(2)}, u32[]{:S(2)}) collective-permute-start(bf16[4,528,128]{2,1,0:T(8,128)(2,1)} %shard_map.50), channel_id=1, source_target_pairs={{0,13},{1,14},{2,15},{3,12},{4,17},{5,18},{6,19},{7,16},{8,21},{9,... | collective-permute-start | bytes 1622024 | tf_op jit(solution)/shard_map/ppermute | solution.py:495
  39.0 46.4 %collective-permute-start.6 = (bf16[4,512,128]{2,1,0:T(8,128)(2,1)}, bf16[4,512,128]{2,1,0:T(8,128)(2,1)}, u32[]{:S(2)}, u32[]{:S(2)}) collective-permute-start(bf16[4,512,128]{2,1,0:T(8,128)(2,1)} %get-tuple-element.50), channel_id=1, source_target_pairs={{16,0},{20,4},{24,8},{28,12},{17,1},{21,5},{25,9},{29,13},{18,2},{... | collective-permute-start | bytes 1572872 | tf_op jit(solution)/shard_map/ppermute | solution.py:487
  49.5 10.5 %copy-start.5 = (bf16[8,512,128]{2,1,0:T(8,128)(2,1)S(1)}, bf16[8,512,128]{2,1,0:T(8,128)(2,1)}, u32[]{:S(2)}) copy-start(bf16[8,512,128]{2,1,0:T(8,128)(2,1)} %copy-done.4) | copy-start | bytes 3145732
  53.4 58.8 %collective-permute-start.11 = (bf16[4,528,128]{2,1,0:T(8,128)(2,1)}, bf16[4,528,128]{2,1,0:T(8,128)(2,1)}, u32[]{:S(2)}, u32[]{:S(2)}) collective-permute-start(bf16[4,528,128]{2,1,0:T(8,128)(2,1)} %shard_map.51), channel_id=1, source_target_pairs={{0,21},{1,22},{2,23},{3,20},{4,25},{5,26},{6,27},{7,24},{8,29},{9,... | collective-permute-start | bytes 1622024 | tf_op jit(solution)/shard_map/ppermute | solution.py:495
  65.4 24.6 %collective-permute-start.7 = (bf16[8,528,128]{2,1,0:T(8,128)(2,1)}, bf16[8,528,128]{2,1,0:T(8,128)(2,1)}, u32[]{:S(2)}, u32[]{:S(2)}) collective-permute-start(bf16[8,528,128]{2,1,0:T(8,128)(2,1)} %shard_map.52), channel_id=1, source_target_pairs={{0,1},{1,2},{2,3},{3,0},{4,5},{5,6},{6,7},{7,4},{8,9},{9,10},{10,1... | collective-permute-start | bytes 3244040 | tf_op jit(solution)/shard_map/ppermute | solution.py:24
  65.4 38.3 %collective-permute-start.8 = (bf16[4,512,128]{2,1,0:T(8,128)(2,1)}, bf16[4,512,128]{2,1,0:T(8,128)(2,1)}, u32[]{:S(2)}, u32[]{:S(2)}) collective-permute-start(bf16[4,512,128]{2,1,0:T(8,128)(2,1)} %get-tuple-element.52), channel_id=1, source_target_pairs={{4,0},{8,4},{12,8},{16,12},{20,16},{24,20},{28,24},{5,1},{9,5},{13... | collective-permute-start | bytes 1572872 | tf_op jit(solution)/shard_map/ppermute | solution.py:487
  85.3 21.3 %collective-permute-start.9 = (bf16[4,512,128]{2,1,0:T(8,128)(2,1)}, bf16[4,512,128]{2,1,0:T(8,128)(2,1)}, u32[]{:S(2)}, u32[]{:S(2)}) collective-permute-start(bf16[4,512,128]{2,1,0:T(8,128)(2,1)} %get-tuple-element.54), channel_id=1, source_target_pairs={{28,0},{29,1},{30,2},{31,3}} | collective-permute-start | bytes 1572872 | tf_op jit(solution)/shard_map/ppermute | solution.py:487
  89.9 29.6 %collective-permute-start.12 = (bf16[4,528,128]{2,1,0:T(8,128)(2,1)S(1)}, bf16[4,528,128]{2,1,0:T(8,128)(2,1)S(1)}, u32[]{:S(2)}, u32[]{:S(2)}) collective-permute-start(bf16[4,528,128]{2,1,0:T(8,128)(2,1)S(1)} %shard_map.53), channel_id=1, source_target_pairs={{0,17},{1,18},{2,19},{3,16},{4,21},{5,22},{6,23},{7,20},{8,25},{9,... | collective-permute-start | bytes 1622024 | tf_op jit(solution)/shard_map/ppermute | solution.py:495
  106.6 5.6 %copy-start.9 = (s32[8,2,16]{2,1,0:T(2,128)S(1)}, s32[8,2,16]{2,1,0:T(2,128)}, u32[]{:S(2)}) copy-start(s32[8,2,16]{2,1,0:T(2,128)} %copy-done.8) | copy-start | bytes 3076
  109.6 9.9 %collective-permute-start.14 = (bf16[4,528,128]{2,1,0:T(8,128)(2,1)S(1)}, bf16[4,528,128]{2,1,0:T(8,128)(2,1)S(1)}, u32[]{:S(2)}, u32[]{:S(2)}) collective-permute-start(bf16[4,528,128]{2,1,0:T(8,128)(2,1)S(1)} %shard_map.55), channel_id=1, source_target_pairs={{0,29},{1,30},{2,31},{3,28}} | collective-permute-start | bytes 1622024 | tf_op jit(solution)/shard_map/ppermute | solution.py:495
  110.3 26.3 %collective-permute-start.13 = (bf16[4,528,128]{2,1,0:T(8,128)(2,1)S(1)}, bf16[4,528,128]{2,1,0:T(8,128)(2,1)S(1)}, u32[]{:S(2)}, u32[]{:S(2)}) collective-permute-start(bf16[4,528,128]{2,1,0:T(8,128)(2,1)S(1)} %shard_map.54), channel_id=1, source_target_pairs={{0,5},{1,6},{2,7},{3,4},{4,9},{5,10},{6,11},{7,8},{8,13},{9,14},{1... | collective-permute-start | bytes 1622024 | tf_op jit(solution)/shard_map/ppermute | solution.py:495

commit v12 on v11

--- a/solution.py
+++ b/solution.py
@@ -298,7 +298,7 @@
         jax.ShapeDtypeStruct((total, rows + STAT_ROWS, HD), jnp.bfloat16),
         IN_VMEM,
         [pltpu.SMEM((slots + 1,), jnp.int32)],
-        flops=4 * total * rows * rows * HD,
+        flops=HIGH_COST,
         moved=12 * total * rows * HD,
         exps=total * rows * rows,
     )(here, picks, queries, *near)
@@ -477,7 +477,7 @@
 
     near_shifts = (2, width - 2)
     middle = width // 2
-    far_shifts = [middle - 1, middle + 1, middle, 1, width - 1]
+    far_shifts = [middle - 1, middle + 1, 1, width - 1, middle]
     final_shifts = tuple(far_shifts[2:])
 
     def up(value, shift):
@@ -514,7 +514,7 @@
             token, own_picks, keys, values, [arrived[shift]], ((shift, 0, slots),), slots, is_anchor
         )[0]
 
-    three, five, four, one, seven = far_shifts
+    three, five, one, seven, four = far_shifts
     ask_for(three, near_sends[0])
     ask_for(five, near_sends[0])
     own = own_part(after(now, before), queries, keys, values)
@@ -524,18 +524,18 @@
     returned[three] = up_and_on(part_three, three)
     part_five = work(after(here, part_three), five, is_anchor=True)
     returned[five] = up_and_on(part_five, five)
-    ask_for(four, arrived[three], arrived[five], near[0])
+    ask_for(one, arrived[three], arrived[five], near[0])
     beside = near_part(after(here, part_five, own_back), own_picks, queries, near, near_shifts, slots)
-    ask_for(one, own_back, part_five, *near)
-    ask_for(seven, own_back, part_five, *near)
-    beside_back = passed_along(beside, "pipe", 1)
-    part_four = work(after(here, beside), four, is_anchor=True)
+    ask_for(seven, own_back, part_five)
+    beside_back = passed_along(after(beside, arrived[seven]), "pipe", 1)
+    part_one = work(after(here, beside), one)
+    returned[one] = up_and_on(part_one, one)
+    ask_for(four, arrived[one], beside)
+    part_seven = work(after(here, part_one), seven, is_anchor=True)
+    returned[seven] = up_and_on(part_seven, seven)
+    part_four = work(after(here, part_seven, beside_back), four)
     returned[four] = up_and_on(part_four, four)
-    part_one = work(after(here, part_four, beside_back), one)
-    returned[one] = up_and_on(part_one, one)
-    part_seven = work(after(here, part_one), seven)
-    returned[seven] = up_and_on(part_seven, seven)
-    now = after(here, part_seven)
+    now = after(here, part_four)
 
     merged_shifts = near_shifts + (three, five)
     places = [HEADS + place * slots for place in (2, 3)]

time: 143 us -> 158 us (1.10)
  waiting for transfers between devices: 36.9 us -> 52.3 us
    ppermute x3, waiting for transfers between devices: 1.25 us -> 16 us  [passed_along(): return lax.ppermute(value, axis, pairs)]
    ppermute x5, waiting for transfers between devices: 17 us -> 31 us  [up_and_on(): return lax.ppermute(value, ('ctx', 'pipe'), pairs)]
    ppermute x5, waiting for transfers between devices: 12.5 us -> 1 us  [down(): lax.ppermute(value, 'ctx', [(at, at - shift) for at in range(shift, width)])]
    ppermute x5, starting transfers between devices: 39.7 us -> 28.2 us  [down(): lax.ppermute(value, 'ctx', [(at, at - shift) for at in range(shift, width)])]
    ppermute x5, starting transfers between devices: 6.47 us -> 15.8 us  [up_and_on(): return lax.ppermute(value, ('ctx', 'pipe'), pairs)]
    ppermute x3, starting transfers between devices: 0.68 us -> 2.77 us  [passed_along(): return lax.ppermute(value, axis, pairs)]
    ppermute x2, waiting for transfers between devices: 6.16 us -> 4.3 us  [up(): lax.ppermute(value, 'ctx', [(at, at + shift) for at in range(width - shif...]
    unnamed x20 -> x22, local copies, waits for them, and re-layouts: 4.91 us -> 4.86 us
  transfers between devices with their start and end apart: 15 -> 15, of which waited for: 5 -> 5; matrix products, arithmetic and copies ran while one was open for 0% -> 0% of each run, Pallas kernels for 30% -> 28%
where the time goes in v12:
time: 158 us; the launch traced here: 157 us
  waiting for transfers between devices  52.3 us (33%)
  Pallas kernels  50.1 us (32%)
  starting transfers between devices  49.3 us (31%)
  local copies, waits for them, and re-layouts  4.86 us (3%)
    ppermute x5, waiting for transfers between devices, up_and_on(): return lax.ppermute(value, ('ctx', 'pipe'), pairs)  31 us
    ppermute x5, starting transfers between devices, down(): lax.ppermute(value, 'ctx', [(at, at - shift) for at in range(shift, width)])  28.2 us
    pallas_call x5, Pallas kernels, attend(): call(functools.partial(attend_kernel, group=group, slots=slots), [SCALARS...  16.8 us
    ppermute x3, waiting for transfers between devices, passed_along(): return lax.ppermute(value, axis, pairs)  16 us
    ppermute x5, starting transfers between devices, up_and_on(): return lax.ppermute(value, ('ctx', 'pipe'), pairs)  15.8 us
    pallas_call x1, Pallas kernels, own_part(): call(own_kernel, [SCALARS, IN_VMEM, IN_VMEM, IN_VMEM], jax.ShapeDtypeStru...  9.02 us
    pallas_call x3, Pallas kernels, pack(): call(functools.partial(pack_kernel, jobs=jobs, slots=slots), [SCALARS, SC...  7.44 us
    pallas_call x1, Pallas kernels, merge(): call(functools.partial(merge_kernel, places=tuple(places), shifts=shifts,...  7.28 us
  transfers between devices with their start and end apart: 15, of which 5 were waited for; matrix products, arithmetic and copies ran while one was open for 0% of the time, Pallas kernels for 28%

profile of v12, /device:TPU:26, one launch (start us, length us, event | category | flops | bytes accessed | tf_op | source)
XLA Modules:
  0.0 157.0 jit_solution(4819794687232267291)
XLA Ops:
  0.0 1.6 %copy-done = bf16[1,512,2048]{2,1,0:T(8,128)(2,1)S(1)} copy-done((bf16[1,512,2048]{2,1,0:T(8,128)(2,1)S(1)}, bf16[1,512,2048]{2,1,0:T(8,128)(2,1)}, u32[]{:S(2)}) %copy-start) | copy-done | bytes 2097176
  1.6 1.6 %copy-done.2 = bf16[1,512,2048]{2,1,0:T(8,128)(2,1)S(1)} copy-done((bf16[1,512,2048]{2,1,0:T(8,128)(2,1)S(1)}, bf16[1,512,2048]{2,1,0:T(8,128)(2,1)}, u32[]{:S(2)}) %copy-start.2) | copy-done | bytes 2097176
  3.2 0.7 copy-done.5
  3.9 2.6 %shard_map.46 = (bf16[8,512,128]{2,1,0:T(8,128)(2,1)S(1)}, bf16[8,512,128]{2,1,0:T(8,128)(2,1)}) custom-call(s32[1]{0:T(128)} %bitcast.here_ref, s32[8,2,16]{2,1,0:T(2,128)S(1)} %bitcast.26, bf16[512,2048]{1,0:T(8,128)(2,1)S(1)} %bitcast.8, bf16[512,2048]{1,0:T(8,128)(2,1)S(1)} %bitcast.15), custom_call_target="tpu_custom_call" | custom-call | bytes 4194304 | tf_op jit(solution)/shard_map/pallas_call | solution.py:127
  6.5 1.3 collective-permute-start.1
  7.8 0.0 copy-start.1
  7.8 0.0 copy-start.3
  7.8 2.1 %shard_map.47 = (bf16[4,512,128]{2,1,0:T(8,128)(2,1)S(1)}, bf16[4,512,128]{2,1,0:T(8,128)(2,1)}) custom-call(s32[1]{0:T(128)} %bitcast.here_ref, s32[8,2,16]{2,1,0:T(2,128)S(1)} %bitcast.27, bf16[512,2048]{1,0:T(8,128)(2,1)S(1)} %bitcast.22), custom_call_target="tpu_custom_call" | custom-call | bytes 2097152 | tf_op jit(solution)/shard_map/pallas_call | solution.py:127
  9.9 5.4 %collective-permute-start.2 = (bf16[4,512,128]{2,1,0:T(8,128)(2,1)S(1)}, bf16[4,512,128]{2,1,0:T(8,128)(2,1)S(1)}, u32[]{:S(2)}, u32[]{:S(2)}) collective-permute-start(bf16[4,512,128]{2,1,0:T(8,128)(2,1)S(1)} %get-tuple-element.45), channel_id=1, source_target_pairs={{12,0},{16,4},{20,8},{24,12},{28,16},{13,1},{17,5},{21,9},{25,13},... | collective-permute-start | bytes 1572872 | tf_op jit(solution)/shard_map/ppermute | solution.py:487
  15.3 0.1 collective-permute-start
  15.4 2.1 %collective-permute-start.3 = (bf16[4,512,128]{2,1,0:T(8,128)(2,1)}, bf16[4,512,128]{2,1,0:T(8,128)(2,1)}, u32[]{:S(2)}, u32[]{:S(2)}) collective-permute-start(bf16[4,512,128]{2,1,0:T(8,128)(2,1)} %get-tuple-element.47), channel_id=1, source_target_pairs={{20,0},{24,4},{28,8},{21,1},{25,5},{29,9},{22,2},{26,6},{30,10},{2... | collective-permute-start | bytes 1572872 | tf_op jit(solution)/shard_map/ppermute | solution.py:487
  17.5 2.8 %shard_map.48 = (bf16[4,512,128]{2,1,0:T(8,128)(2,1)}, bf16[4,512,128]{2,1,0:T(8,128)(2,1)}, bf16[4,512,128]{2,1,0:T(8,128)(2,1)}) custom-call(s32[1]{0:T(128)} %bitcast.here_ref, s32[8,2,16]{2,1,0:T(2,128)S(1)} %bitcast.29, bf16[512,2048]{1,0:T(8,128)(2,1)S(1)} %bitcast.23), custom_call_target="tpu_custom_call" | custom-call | bytes 3145728 | tf_op jit(solution)/shard_map/pallas_call | solution.py:127
  20.3 0.0 collective-permute-done.picks_ref
  20.3 9.0 %shard_map.49 = bf16[16,528,128]{2,1,0:T(8,128)(2,1)} custom-call(s32[1]{0:T(128)} %bitcast.here_ref, bf16[512,2048]{1,0:T(8,128)(2,1)S(1)} %bitcast.24, bf16[512,2048]{1,0:T(8,128)(2,1)S(1)} %bitcast.9, bf16[512,2048]{1,0:T(8,128)(2,1)S(1)} %bitcast.16), custom_call_target="tpu_custom_call" | custom-call | flops 2147483648 | bytes 8388608 | tf_op jit(solution)/shard_map/pallas_call | solution.py:266
  29.3 0.6 collective-permute-start.4
  30.0 1.3 collective-permute-start.5
  31.3 2.0 %collective-permute-done.1.refs_0_ = bf16[8,512,128]{2,1,0:T(8,128)(2,1)S(1)} collective-permute-done((bf16[8,512,128]{2,1,0:T(8,128)(2,1)S(1)}, bf16[8,512,128]{2,1,0:T(8,128)(2,1)S(1)}, u32[]{:S(2)}, u32[]{:S(2)}) %collective-permute-start.1) | collective-permute-done | bytes 1048608 | tf_op jit(solution)/shard_map/ppermute | solution.py:484
  33.3 0.9 copy-done.9
  34.2 0.0 collective-permute-done.2.refs_0_
  34.2 3.4 %shard_map.50 = bf16[4,528,128]{2,1,0:T(8,128)(2,1)} custom-call(s32[1]{0:T(128)} %bitcast.here_ref, s32[8,2,16]{2,1,0:T(2,128)S(1)} %bitcast.30, bf16[512,2048]{1,0:T(8,128)(2,1)S(1)} %bitcast.10, bf16[512,2048]{1,0:T(8,128)(2,1)S(1)} %bitcast.17, bf16[4,512,128]{2,1,0:T(8,128)(2,1)S(1)} %collective-permute-done.2.refs_0_), custom_call_target="tpu_custom_call" | custom-call | flops 999999995904 | bytes 2097152 | tf_op jit(solution)/shard_map/pallas_call | solution.py:226
  37.6 1.3 collective-permute-start.10
  38.9 0.0 collective-permute-done.3.refs_0_
  38.9 12.2 %collective-permute-start.6 = (bf16[4,512,128]{2,1,0:T(8,128)(2,1)}, bf16[4,512,128]{2,1,0:T(8,128)(2,1)}, u32[]{:S(2)}, u32[]{:S(2)}) collective-permute-start(bf16[4,512,128]{2,1,0:T(8,128)(2,1)} %get-tuple-element.51), channel_id=1, source_target_pairs={{4,0},{8,4},{12,8},{16,12},{20,16},{24,20},{28,24},{5,1},{9,5},{13... | collective-permute-start | bytes 1572872 | tf_op jit(solution)/shard_map/ppermute | solution.py:487
  51.2 0.0 copy-start.6
  51.2 3.8 %shard_map.51 = bf16[4,528,128]{2,1,0:T(8,128)(2,1)} custom-call(s32[1]{0:T(128)} %bitcast.here_ref, s32[8,2,16]{2,1,0:T(2,128)S(1)} %bitcast.31, bf16[512,2048]{1,0:T(8,128)(2,1)S(1)} %bitcast.11, bf16[512,2048]{1,0:T(8,128)(2,1)S(1)} %bitcast.18, bf16[4,512,128]{2,1,0:T(8,128)(2,1)} %collective-permute-done.3.refs_0_), custom_call_target="tpu_custom_call" | custom-call | flops 999999995904 | bytes 2097152 | tf_op jit(solution)/shard_map/pallas_call | solution.py:226
  55.0 1.3 collective-permute-start.11
  56.3 0.0 collective-permute-done.4.refs_0_
  56.3 1.5 collective-permute-start.7
  57.8 2.3 %collective-permute-done.5.refs_1_ = bf16[8,512,128]{2,1,0:T(8,128)(2,1)} collective-permute-done((bf16[8,512,128]{2,1,0:T(8,128)(2,1)}, bf16[8,512,128]{2,1,0:T(8,128)(2,1)}, u32[]{:S(2)}, u32[]{:S(2)}) %collective-permute-start.5) | collective-permute-done | bytes 1048608 | tf_op jit(solution)/shard_map/ppermute | solution.py:484
  60.1 5.4 %shard_map.52 = bf16[8,528,128]{2,1,0:T(8,128)(2,1)} custom-call(s32[1]{0:T(128)} %bitcast.here_ref, s32[8,2,16]{2,1,0:T(2,128)S(1)} %bitcast.32, bf16[512,2048]{1,0:T(8,128)(2,1)S(1)} %bitcast.25, bf16[8,512,128]{2,1,0:T(8,128)(2,1)S(1)} %copy-done.10, bf16[8,512,128]{2,1,0:T(8,128)(2,1)} %collective-permute-done.5.refs_1_), custom_call_target="tpu_custom_call" | custom-call | flops 999999995904 | bytes 6291456 | tf_op jit(solution)/shard_map/pallas_call | solution.py:295
  65.5 1.0 collective-permute-done.6.refs_0_
  66.4 3.7 %shard_map.53 = bf16[4,528,128]{2,1,0:T(8,128)(2,1)} custom-call(s32[1]{0:T(128)} %bitcast.here_ref, s32[8,2,16]{2,1,0:T(2,128)S(1)} %bitcast.33, bf16[512,2048]{1,0:T(8,128)(2,1)S(1)} %bitcast.12, bf16[512,2048]{1,0:T(8,128)(2,1)S(1)} %bitcast.19, bf16[4,512,128]{2,1,0:T(8,128)(2,1)} %collective-permute-done.6.refs_0_), custom_call_target="tpu_custom_call" | custom-call | flops 536870912 | bytes 2097152 | tf_op jit(solution)/shard_map/pallas_call | solution.py:226
  70.2 11.2 %collective-permute-start.12 = (bf16[4,528,128]{2,1,0:T(8,128)(2,1)}, bf16[4,528,128]{2,1,0:T(8,128)(2,1)}, u32[]{:S(2)}, u32[]{:S(2)}) collective-permute-start(bf16[4,528,128]{2,1,0:T(8,128)(2,1)} %shard_map.53), channel_id=1, source_target_pairs={{0,5},{1,6},{2,7},{3,4},{4,9},{5,10},{6,11},{7,8},{8,13},{9,14},{1... | collective-permute-start | bytes 1622024 | tf_op jit(solution)/shard_map/ppermute | solution.py:495
  81.4 7.0 %collective-permute-start.9 = (bf16[4,512,128]{2,1,0:T(8,128)(2,1)}, bf16[4,512,128]{2,1,0:T(8,128)(2,1)}, u32[]{:S(2)}, u32[]{:S(2)}) collective-permute-start(bf16[4,512,128]{2,1,0:T(8,128)(2,1)} %get-tuple-element.56), channel_id=1, source_target_pairs={{16,0},{20,4},{24,8},{28,12},{17,1},{21,5},{25,9},{29,13},{18,2},{... | collective-permute-start | bytes 1572872 | tf_op jit(solution)/shard_map/ppermute | solution.py:487
  88.4 0.0 collective-permute-done.7.refs_0_
  88.4 2.1 %collective-permute-start.8 = (bf16[8,528,128]{2,1,0:T(8,128)(2,1)}, bf16[8,528,128]{2,1,0:T(8,128)(2,1)}, u32[]{:S(2)}, u32[]{:S(2)}) collective-permute-start(bf16[8,528,128]{2,1,0:T(8,128)(2,1)} %shard_map.52), channel_id=1, source_target_pairs={{0,1},{1,2},{2,3},{3,0},{4,5},{5,6},{6,7},{7,4},{8,9},{9,10},{10,1... | collective-permute-start | bytes 3244040 | tf_op jit(solution)/shard_map/ppermute | solution.py:24
  90.5 2.9 %shard_map.54 = bf16[4,528,128]{2,1,0:T(8,128)(2,1)S(1)} custom-call(s32[1]{0:T(128)} %bitcast.here_ref, s32[8,2,16]{2,1,0:T(2,128)S(1)} %bitcast.34, bf16[512,2048]{1,0:T(8,128)(2,1)S(1)} %bitcast.13, bf16[512,2048]{1,0:T(8,128)(2,1)S(1)} %bitcast.20, bf16[4,512,128]{2,1,0:T(8,128)(2,1)} %collective-permute-done.7.refs_0_), custom_call_target="tpu_custom_call" | custom-call | flops 999999995904 | bytes 2097152 | tf_op jit(solution)/shard_map/pallas_call | solution.py:226
  93.4 16.0 %collective-permute-done.8.refs_1_ = bf16[8,528,128]{2,1,0:T(8,128)(2,1)} collective-permute-done((bf16[8,528,128]{2,1,0:T(8,128)(2,1)}, bf16[8,528,128]{2,1,0:T(8,128)(2,1)}, u32[]{:S(2)}, u32[]{:S(2)}) %collective-permute-start.8) | collective-permute-done | bytes 1081376 | tf_op jit(solution)/shard_map/ppermute | solution.py:24
  109.4 0.7 collective-permute-start.13
  110.1 0.0 collective-permute-done.9.refs_0_
  110.1 2.9 %shard_map.55 = bf16[4,528,128]{2,1,0:T(8,128)(2,1)S(1)} custom-call(s32[1]{0:T(128)} %bitcast.here_ref, s32[8,2,16]{2,1,0:T(2,128)S(1)} %bitcast.35, bf16[512,2048]{1,0:T(8,128)(2,1)S(1)} %bitcast.14, bf16[512,2048]{1,0:T(8,128)(2,1)S(1)} %bitcast.21, bf16[4,512,128]{2,1,0:T(8,128)(2,1)} %collective-permute-done.9.refs_0_), custom_call_target="tpu_custom_call" | custom-call | flops 536870912 | bytes 2097152 | tf_op jit(solution)/shard_map/pallas_call | solution.py:226
  113.0 1.3 collective-permute-start.14
  114.3 0.0 collective-permute-done.11.refs_3_
  114.3 7.3 %shard_map.56 = (bf16[512,2048]{1,0:T(8,128)(2,1)}, f32[16,512,128]{2,1,0:T(8,128)S(1)}, f32[16,4,128]{2,1,0:T(4,128)S(1)}) custom-call(s32[1]{0:T(128)} %bitcast.here_ref, s32[8,2,16]{2,1,0:T(2,128)S(1)} %copy-done.8, bf16[16,528,128]{2,1,0:T(8,128)(2,1)} %collective-permute-done.4.refs_0_, bf16[8,528,128]{2,1,0:T(8,128)(2,1)} %collective-permute-done.8.refs_1_, ...), custom_call_target="tpu_custom_call" | custom-call | flops 6291456 | bytes 8388608 | tf_op jit(solution)/shard_map/pallas_call | solution.py:367
  121.6 0.0 collective-permute-done.12.refs_0_
  121.6 0.0 collective-permute-done.13.refs_1_
  121.6 31.0 %collective-permute-done.14.refs_2_ = bf16[4,528,128]{2,1,0:T(8,128)(2,1)S(1)} collective-permute-done((bf16[4,528,128]{2,1,0:T(8,128)(2,1)S(1)}, bf16[4,528,128]{2,1,0:T(8,128)(2,1)S(1)}, u32[]{:S(2)}, u32[]{:S(2)}) %collective-permute-start.14) | collective-permute-done | bytes 540704 | tf_op jit(solution)/shard_map/ppermute | solution.py:495
  152.6 4.3 %shard_map.57 = bf16[512,2048]{1,0:T(8,128)(2,1)} custom-call(s32[1]{0:T(128)} %bitcast.here_ref, s32[8,2,16]{2,1,0:T(2,128)S(1)} %copy-done.8, f32[16,512,128]{2,1,0:T(8,128)S(1)} %get-tuple-element.58.mixed_ref, f32[16,4,128]{2,1,0:T(4,128)S(1)} %get-tuple-element.59.sums_ref, ...), custom_call_target="tpu_custom_call", output_to_operand_aliasing={{}: (7, {})} | custom-call | flops 1572864 | bytes 6291456 | tf_op jit(solution)/shard_map/pallas_call | solution.py:448
  (16 shorter events, 0.0 us)
Async XLA Ops:
  0.0 1.6 %copy-start = (bf16[1,512,2048]{2,1,0:T(8,128)(2,1)S(1)}, bf16[1,512,2048]{2,1,0:T(8,128)(2,1)}, u32[]{:S(2)}) copy-start(bf16[1,512,2048]{2,1,0:T(8,128)(2,1)} %param.5) | copy-start | bytes 6291460
  1.6 1.6 %copy-start.2 = (bf16[1,512,2048]{2,1,0:T(8,128)(2,1)S(1)}, bf16[1,512,2048]{2,1,0:T(8,128)(2,1)}, u32[]{:S(2)}) copy-start(bf16[1,512,2048]{2,1,0:T(8,128)(2,1)} %param.6) | copy-start | bytes 6291460
  3.2 0.7 copy-start.5
  3.9 3.9 %copy-start.4 = (bf16[1,512,2048]{2,1,0:T(8,128)(2,1)S(1)}, bf16[1,512,2048]{2,1,0:T(8,128)(2,1)}, u32[]{:S(2)}) copy-start(bf16[1,512,2048]{2,1,0:T(8,128)(2,1)} %param.4) | copy-start | bytes 6291460
  6.5 26.8 %collective-permute-start.1 = (bf16[8,512,128]{2,1,0:T(8,128)(2,1)S(1)}, bf16[8,512,128]{2,1,0:T(8,128)(2,1)S(1)}, u32[]{:S(2)}, u32[]{:S(2)}) collective-permute-start(bf16[8,512,128]{2,1,0:T(8,128)(2,1)S(1)} %get-tuple-element.33), channel_id=1, source_target_pairs={{0,8},{4,12},{8,16},{12,20},{16,24},{20,28},{1,9},{5,13},{9,17},{1... | collective-permute-start | bytes 3145736 | tf_op jit(solution)/shard_map/ppermute | solution.py:484
  7.8 12.5 %copy-start.1 = (bf16[1,512,2048]{2,1,0:T(8,128)(2,1)S(1)}, bf16[1,512,2048]{2,1,0:T(8,128)(2,1)}, u32[]{:S(2)}) copy-start(bf16[1,512,2048]{2,1,0:T(8,128)(2,1)} %param.5) | copy-start | bytes 6291460
  7.8 12.5 %copy-start.3 = (bf16[1,512,2048]{2,1,0:T(8,128)(2,1)S(1)}, bf16[1,512,2048]{2,1,0:T(8,128)(2,1)}, u32[]{:S(2)}) copy-start(bf16[1,512,2048]{2,1,0:T(8,128)(2,1)} %param.6) | copy-start | bytes 6291460
  9.9 24.3 %collective-permute-start.2 = (bf16[4,512,128]{2,1,0:T(8,128)(2,1)S(1)}, bf16[4,512,128]{2,1,0:T(8,128)(2,1)S(1)}, u32[]{:S(2)}, u32[]{:S(2)}) collective-permute-start(bf16[4,512,128]{2,1,0:T(8,128)(2,1)S(1)} %get-tuple-element.45), channel_id=1, source_target_pairs={{12,0},{16,4},{20,8},{24,12},{28,16},{13,1},{17,5},{21,9},{25,13},... | collective-permute-start | bytes 1572872 | tf_op jit(solution)/shard_map/ppermute | solution.py:487
  15.3 5.0 %collective-permute-start = (s32[8,2,16]{2,1,0:T(2,128)S(1)}, s32[8,2,16]{2,1,0:T(2,128)S(1)}, u32[]{:S(2)}, u32[]{:S(2)}) collective-permute-start(s32[8,2,16]{2,1,0:T(2,128)S(1)} %bitcast.28), channel_id=1, source_target_pairs={{0,1},{1,2},{2,3},{3,0},{4,5},{5,6},{6,7},{7,4},{8,9},{9,10},{10,1... | collective-permute-start | bytes 3080 | tf_op jit(solution)/shard_map/ppermute | solution.py:24
  15.4 23.5 %collective-permute-start.3 = (bf16[4,512,128]{2,1,0:T(8,128)(2,1)}, bf16[4,512,128]{2,1,0:T(8,128)(2,1)}, u32[]{:S(2)}, u32[]{:S(2)}) collective-permute-start(bf16[4,512,128]{2,1,0:T(8,128)(2,1)} %get-tuple-element.47), channel_id=1, source_target_pairs={{20,0},{24,4},{28,8},{21,1},{25,5},{29,9},{22,2},{26,6},{30,10},{2... | collective-permute-start | bytes 1572872 | tf_op jit(solution)/shard_map/ppermute | solution.py:487
  20.3 9.0 %copy-start.7 = (s32[8,2,16]{2,1,0:T(2,128)}, s32[8,2,16]{2,1,0:T(2,128)S(1)}, u32[]{:S(2)}) copy-start(s32[8,2,16]{2,1,0:T(2,128)S(1)} %collective-permute-done.picks_ref) | copy-start | bytes 3076
  29.3 27.0 %collective-permute-start.4 = (bf16[16,528,128]{2,1,0:T(8,128)(2,1)}, bf16[16,528,128]{2,1,0:T(8,128)(2,1)}, u32[]{:S(2)}, u32[]{:S(2)}) collective-permute-start(bf16[16,528,128]{2,1,0:T(8,128)(2,1)} %shard_map.49), channel_id=1, source_target_pairs={{0,1},{1,2},{2,3},{3,0},{4,5},{5,6},{6,7},{7,4},{8,9},{9,10},{10,1... | collective-permute-start | bytes 6488072 | tf_op jit(solution)/shard_map/ppermute | solution.py:24
  30.0 30.1 %collective-permute-start.5 = (bf16[8,512,128]{2,1,0:T(8,128)(2,1)}, bf16[8,512,128]{2,1,0:T(8,128)(2,1)}, u32[]{:S(2)}, u32[]{:S(2)}) collective-permute-start(bf16[8,512,128]{2,1,0:T(8,128)(2,1)} %get-tuple-element.49), channel_id=1, source_target_pairs={{0,24},{4,28},{1,25},{5,29},{2,26},{6,30},{3,27},{7,31}} | collective-permute-start | bytes 3145736 | tf_op jit(solution)/shard_map/ppermute | solution.py:484
  33.3 1.0 copy-start.9
  37.6 76.7 %collective-permute-start.10 = (bf16[4,528,128]{2,1,0:T(8,128)(2,1)}, bf16[4,528,128]{2,1,0:T(8,128)(2,1)}, u32[]{:S(2)}, u32[]{:S(2)}) collective-permute-start(bf16[4,528,128]{2,1,0:T(8,128)(2,1)} %shard_map.50), channel_id=1, source_target_pairs={{0,13},{1,14},{2,15},{3,12},{4,17},{5,18},{6,19},{7,16},{8,21},{9,... | collective-permute-start | bytes 1622024 | tf_op jit(solution)/shard_map/ppermute | solution.py:495
  38.9 27.5 %collective-permute-start.6 = (bf16[4,512,128]{2,1,0:T(8,128)(2,1)}, bf16[4,512,128]{2,1,0:T(8,128)(2,1)}, u32[]{:S(2)}, u32[]{:S(2)}) collective-permute-start(bf16[4,512,128]{2,1,0:T(8,128)(2,1)} %get-tuple-element.51), channel_id=1, source_target_pairs={{4,0},{8,4},{12,8},{16,12},{20,16},{24,20},{28,24},{5,1},{9,5},{13... | collective-permute-start | bytes 1572872 | tf_op jit(solution)/shard_map/ppermute | solution.py:487
  51.2 8.9 %copy-start.6 = (s32[1,8,16,2]{2,3,1,0:T(2,128)S(1)}, s32[1,8,16,2]{2,3,1,0:T(2,128)}, u32[]{:S(2)}) copy-start(s32[1,8,16,2]{2,3,1,0:T(2,128)} %param.7) | copy-start | bytes 3076
  51.2 8.9 %copy-start.10 = (bf16[8,512,128]{2,1,0:T(8,128)(2,1)S(1)}, bf16[8,512,128]{2,1,0:T(8,128)(2,1)}, u32[]{:S(2)}) copy-start(bf16[8,512,128]{2,1,0:T(8,128)(2,1)} %copy-done.9) | copy-start | bytes 3145732
  55.0 59.3 %collective-permute-start.11 = (bf16[4,528,128]{2,1,0:T(8,128)(2,1)}, bf16[4,528,128]{2,1,0:T(8,128)(2,1)}, u32[]{:S(2)}, u32[]{:S(2)}) collective-permute-start(bf16[4,528,128]{2,1,0:T(8,128)(2,1)} %shard_map.51), channel_id=1, source_target_pairs={{0,21},{1,22},{2,23},{3,20},{4,25},{5,26},{6,27},{7,24},{8,29},{9,... | collective-permute-start | bytes 1622024 | tf_op jit(solution)/shard_map/ppermute | solution.py:495
  56.3 32.1 %collective-permute-start.7 = (bf16[4,512,128]{2,1,0:T(8,128)(2,1)}, bf16[4,512,128]{2,1,0:T(8,128)(2,1)}, u32[]{:S(2)}, u32[]{:S(2)}) collective-permute-start(bf16[4,512,128]{2,1,0:T(8,128)(2,1)} %get-tuple-element.53), channel_id=1, source_target_pairs={{28,0},{29,1},{30,2},{31,3}} | collective-permute-start | bytes 1572872 | tf_op jit(solution)/shard_map/ppermute | solution.py:487
  70.2 51.5 %collective-permute-start.12 = (bf16[4,528,128]{2,1,0:T(8,128)(2,1)}, bf16[4,528,128]{2,1,0:T(8,128)(2,1)}, u32[]{:S(2)}, u32[]{:S(2)}) collective-permute-start(bf16[4,528,128]{2,1,0:T(8,128)(2,1)} %shard_map.53), channel_id=1, source_target_pairs={{0,5},{1,6},{2,7},{3,4},{4,9},{5,10},{6,11},{7,8},{8,13},{9,14},{1... | collective-permute-start | bytes 1622024 | tf_op jit(solution)/shard_map/ppermute | solution.py:495
  81.4 28.7 %collective-permute-start.9 = (bf16[4,512,128]{2,1,0:T(8,128)(2,1)}, bf16[4,512,128]{2,1,0:T(8,128)(2,1)}, u32[]{:S(2)}, u32[]{:S(2)}) collective-permute-start(bf16[4,512,128]{2,1,0:T(8,128)(2,1)} %get-tuple-element.56), channel_id=1, source_target_pairs={{16,0},{20,4},{24,8},{28,12},{17,1},{21,5},{25,9},{29,13},{18,2},{... | collective-permute-start | bytes 1572872 | tf_op jit(solution)/shard_map/ppermute | solution.py:487
  88.4 21.0 %collective-permute-start.8 = (bf16[8,528,128]{2,1,0:T(8,128)(2,1)}, bf16[8,528,128]{2,1,0:T(8,128)(2,1)}, u32[]{:S(2)}, u32[]{:S(2)}) collective-permute-start(bf16[8,528,128]{2,1,0:T(8,128)(2,1)} %shard_map.52), channel_id=1, source_target_pairs={{0,1},{1,2},{2,3},{3,0},{4,5},{5,6},{6,7},{7,4},{8,9},{9,10},{10,1... | collective-permute-start | bytes 3244040 | tf_op jit(solution)/shard_map/ppermute | solution.py:24
  93.4 20.9 %copy-start.8 = (s32[8,2,16]{2,1,0:T(2,128)S(1)}, s32[8,2,16]{2,1,0:T(2,128)}, u32[]{:S(2)}) copy-start(s32[8,2,16]{2,1,0:T(2,128)} %copy-done.7) | copy-start | bytes 3076
  109.4 12.3 %collective-permute-start.13 = (bf16[4,528,128]{2,1,0:T(8,128)(2,1)S(1)}, bf16[4,528,128]{2,1,0:T(8,128)(2,1)S(1)}, u32[]{:S(2)}, u32[]{:S(2)}) collective-permute-start(bf16[4,528,128]{2,1,0:T(8,128)(2,1)S(1)} %shard_map.54), channel_id=1, source_target_pairs={{0,29},{1,30},{2,31},{3,28}} | collective-permute-start | bytes 1622024 | tf_op jit(solution)/shard_map/ppermute | solution.py:495
  113.0 39.6 %collective-permute-start.14 = (bf16[4,528,128]{2,1,0:T(8,128)(2,1)S(1)}, bf16[4,528,128]{2,1,0:T(8,128)(2,1)S(1)}, u32[]{:S(2)}, u32[]{:S(2)}) collective-permute-start(bf16[4,528,128]{2,1,0:T(8,128)(2,1)S(1)} %shard_map.55), channel_id=1, source_target_pairs={{0,17},{1,18},{2,19},{3,16},{4,21},{5,22},{6,23},{7,20},{8,25},{9,... | collective-permute-start | bytes 1622024 | tf_op jit(solution)/shard_map/ppermute | solution.py:495

commit v13 on v11

--- a/solution.py
+++ b/solution.py
@@ -298,7 +298,7 @@
         jax.ShapeDtypeStruct((total, rows + STAT_ROWS, HD), jnp.bfloat16),
         IN_VMEM,
         [pltpu.SMEM((slots + 1,), jnp.int32)],
-        flops=4 * total * rows * rows * HD,
+        flops=HIGH_COST,
         moved=12 * total * rows * HD,
         exps=total * rows * rows,
     )(here, picks, queries, *near)
@@ -524,7 +524,7 @@
     returned[three] = up_and_on(part_three, three)
     part_five = work(after(here, part_three), five, is_anchor=True)
     returned[five] = up_and_on(part_five, five)
-    ask_for(four, arrived[three], arrived[five], near[0])
+    ask_for(four, arrived[three], arrived[five], part_five, own_back, *near)
     beside = near_part(after(here, part_five, own_back), own_picks, queries, near, near_shifts, slots)
     ask_for(one, own_back, part_five, *near)
     ask_for(seven, own_back, part_five, *near)

time: 143 us -> 145 us (1.014)
  waiting for transfers between devices: 36.9 us -> 59.7 us
  starting transfers between devices: 49.4 us -> 28.4 us
    ppermute x5, starting transfers between devices: 39.7 us -> 18.7 us  [down(): lax.ppermute(value, 'ctx', [(at, at - shift) for at in range(shift, width)])]
    ppermute x2, waiting for transfers between devices: 6.16 us -> 18 us  [up(): lax.ppermute(value, 'ctx', [(at, at + shift) for at in range(width - shif...]
    ppermute x5, waiting for transfers between devices: 12.5 us -> 21.1 us  [down(): lax.ppermute(value, 'ctx', [(at, at - shift) for at in range(shift, width)])]
    ppermute x3, waiting for transfers between devices: 1.25 us -> 3.62 us  [passed_along(): return lax.ppermute(value, axis, pairs)]
    unnamed x20 -> x22, local copies, waits for them, and re-layouts: 4.91 us -> 4.91 us
where the time goes in v13:
time: 145 us; the launch traced here: 143 us
  waiting for transfers between devices  59.7 us (41%)
  Pallas kernels  49.1 us (34%)
  starting transfers between devices  28.4 us (20%)
  local copies, waits for them, and re-layouts  4.91 us (3%)
    ppermute x5, waiting for transfers between devices, down(): lax.ppermute(value, 'ctx', [(at, at - shift) for at in range(shift, width)])  21.1 us
    ppermute x5, starting transfers between devices, down(): lax.ppermute(value, 'ctx', [(at, at - shift) for at in range(shift, width)])  18.7 us
    ppermute x2, waiting for transfers between devices, up(): lax.ppermute(value, 'ctx', [(at, at + shift) for at in range(width - shif...  18 us
    ppermute x5, waiting for transfers between devices, up_and_on(): return lax.ppermute(value, ('ctx', 'pipe'), pairs)  16.9 us
    pallas_call x5, Pallas kernels, attend(): call(functools.partial(attend_kernel, group=group, slots=slots), [SCALARS...  16 us
    pallas_call x1, Pallas kernels, own_part(): call(own_kernel, [SCALARS, IN_VMEM, IN_VMEM, IN_VMEM], jax.ShapeDtypeStru...  8.96 us
    pallas_call x3, Pallas kernels, pack(): call(functools.partial(pack_kernel, jobs=jobs, slots=slots), [SCALARS, SC...  7.45 us
    pallas_call x1, Pallas kernels, merge(): call(functools.partial(merge_kernel, places=tuple(places), shifts=shifts,...  7.26 us
  transfers between devices with their start and end apart: 15, of which 5 were waited for; matrix products, arithmetic and copies ran while one was open for 0% of the time, Pallas kernels for 30%

profile of v13, /device:TPU:26, one launch (start us, length us, event | category | flops | bytes accessed | tf_op | source)
XLA Modules:
  0.0 142.6 jit_solution(9504679205758532030)
XLA Ops:
  0.0 1.6 %copy-done = bf16[1,512,2048]{2,1,0:T(8,128)(2,1)S(1)} copy-done((bf16[1,512,2048]{2,1,0:T(8,128)(2,1)S(1)}, bf16[1,512,2048]{2,1,0:T(8,128)(2,1)}, u32[]{:S(2)}) %copy-start) | copy-done | bytes 2097176
  1.6 1.6 %copy-done.2 = bf16[1,512,2048]{2,1,0:T(8,128)(2,1)S(1)} copy-done((bf16[1,512,2048]{2,1,0:T(8,128)(2,1)S(1)}, bf16[1,512,2048]{2,1,0:T(8,128)(2,1)}, u32[]{:S(2)}) %copy-start.2) | copy-done | bytes 2097176
  3.2 0.7 copy-done.5
  3.9 2.6 %shard_map.46 = (bf16[8,512,128]{2,1,0:T(8,128)(2,1)S(1)}, bf16[8,512,128]{2,1,0:T(8,128)(2,1)}) custom-call(s32[1]{0:T(128)} %bitcast.here_ref, s32[8,2,16]{2,1,0:T(2,128)S(1)} %bitcast.26, bf16[512,2048]{1,0:T(8,128)(2,1)S(1)} %bitcast.8, bf16[512,2048]{1,0:T(8,128)(2,1)S(1)} %bitcast.15), custom_call_target="tpu_custom_call" | custom-call | bytes 4194304 | tf_op jit(solution)/shard_map/pallas_call | solution.py:127
  6.5 1.3 collective-permute-start.1
  7.8 0.0 copy-start.1
  7.8 0.0 copy-start.3
  7.8 2.1 %shard_map.47 = (bf16[4,512,128]{2,1,0:T(8,128)(2,1)S(1)}, bf16[4,512,128]{2,1,0:T(8,128)(2,1)}) custom-call(s32[1]{0:T(128)} %bitcast.here_ref, s32[8,2,16]{2,1,0:T(2,128)S(1)} %bitcast.27, bf16[512,2048]{1,0:T(8,128)(2,1)S(1)} %bitcast.22), custom_call_target="tpu_custom_call" | custom-call | bytes 2097152 | tf_op jit(solution)/shard_map/pallas_call | solution.py:127
  9.9 5.4 %collective-permute-start.2 = (bf16[4,512,128]{2,1,0:T(8,128)(2,1)S(1)}, bf16[4,512,128]{2,1,0:T(8,128)(2,1)S(1)}, u32[]{:S(2)}, u32[]{:S(2)}) collective-permute-start(bf16[4,512,128]{2,1,0:T(8,128)(2,1)S(1)} %get-tuple-element.44), channel_id=1, source_target_pairs={{12,0},{16,4},{20,8},{24,12},{28,16},{13,1},{17,5},{21,9},{25,13},... | collective-permute-start | bytes 1572872 | tf_op jit(solution)/shard_map/ppermute | solution.py:487
  15.4 0.1 collective-permute-start
  15.4 2.1 %collective-permute-start.3 = (bf16[4,512,128]{2,1,0:T(8,128)(2,1)}, bf16[4,512,128]{2,1,0:T(8,128)(2,1)}, u32[]{:S(2)}, u32[]{:S(2)}) collective-permute-start(bf16[4,512,128]{2,1,0:T(8,128)(2,1)} %get-tuple-element.46), channel_id=1, source_target_pairs={{20,0},{24,4},{28,8},{21,1},{25,5},{29,9},{22,2},{26,6},{30,10},{2... | collective-permute-start | bytes 1572872 | tf_op jit(solution)/shard_map/ppermute | solution.py:487
  17.6 2.7 %shard_map.48 = (bf16[4,512,128]{2,1,0:T(8,128)(2,1)}, bf16[4,512,128]{2,1,0:T(8,128)(2,1)}, bf16[4,512,128]{2,1,0:T(8,128)(2,1)}) custom-call(s32[1]{0:T(128)} %bitcast.here_ref, s32[8,2,16]{2,1,0:T(2,128)S(1)} %bitcast.29, bf16[512,2048]{1,0:T(8,128)(2,1)S(1)} %bitcast.23), custom_call_target="tpu_custom_call" | custom-call | bytes 3145728 | tf_op jit(solution)/shard_map/pallas_call | solution.py:127
  20.3 0.0 collective-permute-done.picks_ref
  20.4 9.0 %shard_map.49 = bf16[16,528,128]{2,1,0:T(8,128)(2,1)} custom-call(s32[1]{0:T(128)} %bitcast.here_ref, bf16[512,2048]{1,0:T(8,128)(2,1)S(1)} %bitcast.24, bf16[512,2048]{1,0:T(8,128)(2,1)S(1)} %bitcast.9, bf16[512,2048]{1,0:T(8,128)(2,1)S(1)} %bitcast.16), custom_call_target="tpu_custom_call" | custom-call | flops 2147483648 | bytes 8388608 | tf_op jit(solution)/shard_map/pallas_call | solution.py:266
  29.3 0.6 collective-permute-start.4
  29.9 1.3 collective-permute-start.5
  31.2 2.1 %collective-permute-done.1.refs_0_ = bf16[8,512,128]{2,1,0:T(8,128)(2,1)S(1)} collective-permute-done((bf16[8,512,128]{2,1,0:T(8,128)(2,1)S(1)}, bf16[8,512,128]{2,1,0:T(8,128)(2,1)S(1)}, u32[]{:S(2)}, u32[]{:S(2)}) %collective-permute-start.1) | collective-permute-done | bytes 1048608 | tf_op jit(solution)/shard_map/ppermute | solution.py:484
  33.3 1.0 copy-done.9
  34.3 0.0 collective-permute-done.2.refs_0_
  34.3 3.3 %shard_map.50 = bf16[4,528,128]{2,1,0:T(8,128)(2,1)} custom-call(s32[1]{0:T(128)} %bitcast.here_ref, s32[8,2,16]{2,1,0:T(2,128)S(1)} %bitcast.30, bf16[512,2048]{1,0:T(8,128)(2,1)S(1)} %bitcast.10, bf16[512,2048]{1,0:T(8,128)(2,1)S(1)} %bitcast.17, bf16[4,512,128]{2,1,0:T(8,128)(2,1)S(1)} %collective-permute-done.2.refs_0_), custom_call_target="tpu_custom_call" | custom-call | flops 999999995904 | bytes 2097152 | tf_op jit(solution)/shard_map/pallas_call | solution.py:226
  37.6 1.3 collective-permute-start.10
  38.9 0.0 collective-permute-done.3.refs_0_
  38.9 0.0 copy-start.6
  39.0 3.9 %shard_map.51 = bf16[4,528,128]{2,1,0:T(8,128)(2,1)} custom-call(s32[1]{0:T(128)} %bitcast.here_ref, s32[8,2,16]{2,1,0:T(2,128)S(1)} %bitcast.31, bf16[512,2048]{1,0:T(8,128)(2,1)S(1)} %bitcast.11, bf16[512,2048]{1,0:T(8,128)(2,1)S(1)} %bitcast.18, bf16[4,512,128]{2,1,0:T(8,128)(2,1)} %collective-permute-done.3.refs_0_), custom_call_target="tpu_custom_call" | custom-call | flops 999999995904 | bytes 2097152 | tf_op jit(solution)/shard_map/pallas_call | solution.py:226
  42.8 1.3 collective-permute-start.11
  44.1 15.9 %collective-permute-done.5.refs_1_ = bf16[8,512,128]{2,1,0:T(8,128)(2,1)} collective-permute-done((bf16[8,512,128]{2,1,0:T(8,128)(2,1)}, bf16[8,512,128]{2,1,0:T(8,128)(2,1)}, u32[]{:S(2)}, u32[]{:S(2)}) %collective-permute-start.5) | collective-permute-done | bytes 1048608 | tf_op jit(solution)/shard_map/ppermute | solution.py:484
  60.1 0.0 collective-permute-done.4.refs_0_
  60.1 2.1 %collective-permute-start.6 = (bf16[4,512,128]{2,1,0:T(8,128)(2,1)}, bf16[4,512,128]{2,1,0:T(8,128)(2,1)}, u32[]{:S(2)}, u32[]{:S(2)}) collective-permute-start(bf16[4,512,128]{2,1,0:T(8,128)(2,1)} %get-tuple-element.50), channel_id=1, source_target_pairs={{16,0},{20,4},{24,8},{28,12},{17,1},{21,5},{25,9},{29,13},{18,2},{... | collective-permute-start | bytes 1572872 | tf_op jit(solution)/shard_map/ppermute | solution.py:487
  62.1 5.4 %shard_map.52 = bf16[8,528,128]{2,1,0:T(8,128)(2,1)} custom-call(s32[1]{0:T(128)} %bitcast.here_ref, s32[8,2,16]{2,1,0:T(2,128)S(1)} %bitcast.32, bf16[512,2048]{1,0:T(8,128)(2,1)S(1)} %bitcast.25, bf16[8,512,128]{2,1,0:T(8,128)(2,1)S(1)} %copy-done.10, bf16[8,512,128]{2,1,0:T(8,128)(2,1)} %collective-permute-done.5.refs_1_), custom_call_target="tpu_custom_call" | custom-call | flops 999999995904 | bytes 6291456 | tf_op jit(solution)/shard_map/pallas_call | solution.py:295
  67.5 0.0 collective-permute-start.7
  67.5 7.4 %collective-permute-start.8 = (bf16[4,512,128]{2,1,0:T(8,128)(2,1)}, bf16[4,512,128]{2,1,0:T(8,128)(2,1)}, u32[]{:S(2)}, u32[]{:S(2)}) collective-permute-start(bf16[4,512,128]{2,1,0:T(8,128)(2,1)} %get-tuple-element.52), channel_id=1, source_target_pairs={{4,0},{8,4},{12,8},{16,12},{20,16},{24,20},{28,24},{5,1},{9,5},{13... | collective-permute-start | bytes 1572872 | tf_op jit(solution)/shard_map/ppermute | solution.py:487
  74.9 0.0 collective-permute-done.6.refs_0_
  74.9 1.7 %collective-permute-start.9 = (bf16[4,512,128]{2,1,0:T(8,128)(2,1)}, bf16[4,512,128]{2,1,0:T(8,128)(2,1)}, u32[]{:S(2)}, u32[]{:S(2)}) collective-permute-start(bf16[4,512,128]{2,1,0:T(8,128)(2,1)} %get-tuple-element.54), channel_id=1, source_target_pairs={{28,0},{29,1},{30,2},{31,3}} | collective-permute-start | bytes 1572872 | tf_op jit(solution)/shard_map/ppermute | solution.py:487
  76.6 2.9 %shard_map.53 = bf16[4,528,128]{2,1,0:T(8,128)(2,1)S(1)} custom-call(s32[1]{0:T(128)} %bitcast.here_ref, s32[8,2,16]{2,1,0:T(2,128)S(1)} %bitcast.33, bf16[512,2048]{1,0:T(8,128)(2,1)S(1)} %bitcast.12, bf16[512,2048]{1,0:T(8,128)(2,1)S(1)} %bitcast.19, bf16[4,512,128]{2,1,0:T(8,128)(2,1)} %collective-permute-done.6.refs_0_), custom_call_target="tpu_custom_call" | custom-call | flops 999999995904 | bytes 2097152 | tf_op jit(solution)/shard_map/pallas_call | solution.py:226
  79.5 3.6 %collective-permute-done.7.refs_1_ = bf16[8,528,128]{2,1,0:T(8,128)(2,1)} collective-permute-done((bf16[8,528,128]{2,1,0:T(8,128)(2,1)}, bf16[8,528,128]{2,1,0:T(8,128)(2,1)}, u32[]{:S(2)}, u32[]{:S(2)}) %collective-permute-start.7) | collective-permute-done | bytes 1081376 | tf_op jit(solution)/shard_map/ppermute | solution.py:24
  83.1 1.3 collective-permute-start.12
  84.4 21.1 %collective-permute-done.8.refs_0_ = bf16[4,512,128]{2,1,0:T(8,128)(2,1)} collective-permute-done((bf16[4,512,128]{2,1,0:T(8,128)(2,1)}, bf16[4,512,128]{2,1,0:T(8,128)(2,1)}, u32[]{:S(2)}, u32[]{:S(2)}) %collective-permute-start.8) | collective-permute-done | bytes 524320 | tf_op jit(solution)/shard_map/ppermute | solution.py:487
  105.6 2.9 %shard_map.54 = bf16[4,528,128]{2,1,0:T(8,128)(2,1)S(1)} custom-call(s32[1]{0:T(128)} %bitcast.here_ref, s32[8,2,16]{2,1,0:T(2,128)S(1)} %bitcast.34, bf16[512,2048]{1,0:T(8,128)(2,1)S(1)} %bitcast.13, bf16[512,2048]{1,0:T(8,128)(2,1)S(1)} %bitcast.20, bf16[4,512,128]{2,1,0:T(8,128)(2,1)} %collective-permute-done.8.refs_0_), custom_call_target="tpu_custom_call" | custom-call | flops 536870912 | bytes 2097152 | tf_op jit(solution)/shard_map/pallas_call | solution.py:226
  108.5 0.0 collective-permute-done.9.refs_0_
  108.5 2.9 %shard_map.55 = bf16[4,528,128]{2,1,0:T(8,128)(2,1)S(1)} custom-call(s32[1]{0:T(128)} %bitcast.here_ref, s32[8,2,16]{2,1,0:T(2,128)S(1)} %bitcast.35, bf16[512,2048]{1,0:T(8,128)(2,1)S(1)} %bitcast.14, bf16[512,2048]{1,0:T(8,128)(2,1)S(1)} %bitcast.21, bf16[4,512,128]{2,1,0:T(8,128)(2,1)} %collective-permute-done.9.refs_0_), custom_call_target="tpu_custom_call" | custom-call | flops 536870912 | bytes 2097152 | tf_op jit(solution)/shard_map/pallas_call | solution.py:226
  111.4 0.7 collective-permute-start.14
  112.1 1.9 %collective-permute-start.13 = (bf16[4,528,128]{2,1,0:T(8,128)(2,1)S(1)}, bf16[4,528,128]{2,1,0:T(8,128)(2,1)S(1)}, u32[]{:S(2)}, u32[]{:S(2)}) collective-permute-start(bf16[4,528,128]{2,1,0:T(8,128)(2,1)S(1)} %shard_map.54), channel_id=1, source_target_pairs={{0,5},{1,6},{2,7},{3,4},{4,9},{5,10},{6,11},{7,8},{8,13},{9,14},{1... | collective-permute-start | bytes 1622024 | tf_op jit(solution)/shard_map/ppermute | solution.py:495
  114.1 0.0 collective-permute-done.10.refs_2_
  114.1 7.3 %shard_map.56 = (bf16[512,2048]{1,0:T(8,128)(2,1)}, f32[16,512,128]{2,1,0:T(8,128)S(1)}, f32[16,4,128]{2,1,0:T(4,128)S(1)}) custom-call(s32[1]{0:T(128)} %bitcast.here_ref, s32[8,2,16]{2,1,0:T(2,128)S(1)} %copy-done.8, bf16[16,528,128]{2,1,0:T(8,128)(2,1)} %collective-permute-done.4.refs_0_, bf16[8,528,128]{2,1,0:T(8,128)(2,1)} %collective-permute-done.7.refs_1_, ...), custom_call_target="tpu_custom_call" | custom-call | flops 6291456 | bytes 8388608 | tf_op jit(solution)/shard_map/pallas_call | solution.py:367
  121.4 0.0 collective-permute-done.12.refs_0_
  121.4 0.0 collective-permute-done.14.refs_2_
  121.4 16.9 %collective-permute-done.13.refs_1_ = bf16[4,528,128]{2,1,0:T(8,128)(2,1)S(1)} collective-permute-done((bf16[4,528,128]{2,1,0:T(8,128)(2,1)S(1)}, bf16[4,528,128]{2,1,0:T(8,128)(2,1)S(1)}, u32[]{:S(2)}, u32[]{:S(2)}) %collective-permute-start.13) | collective-permute-done | bytes 540704 | tf_op jit(solution)/shard_map/ppermute | solution.py:495
  138.3 4.1 %shard_map.57 = bf16[512,2048]{1,0:T(8,128)(2,1)} custom-call(s32[1]{0:T(128)} %bitcast.here_ref, s32[8,2,16]{2,1,0:T(2,128)S(1)} %copy-done.8, f32[16,512,128]{2,1,0:T(8,128)S(1)} %get-tuple-element.56.mixed_ref, f32[16,4,128]{2,1,0:T(4,128)S(1)} %get-tuple-element.57.sums_ref, ...), custom_call_target="tpu_custom_call", output_to_operand_aliasing={{}: (7, {})} | custom-call | flops 1572864 | bytes 6291456 | tf_op jit(solution)/shard_map/pallas_call | solution.py:448
  (16 shorter events, 0.0 us)
Async XLA Ops:
  0.0 1.6 %copy-start = (bf16[1,512,2048]{2,1,0:T(8,128)(2,1)S(1)}, bf16[1,512,2048]{2,1,0:T(8,128)(2,1)}, u32[]{:S(2)}) copy-start(bf16[1,512,2048]{2,1,0:T(8,128)(2,1)} %param.5) | copy-start | bytes 6291460
  1.6 1.6 %copy-start.2 = (bf16[1,512,2048]{2,1,0:T(8,128)(2,1)S(1)}, bf16[1,512,2048]{2,1,0:T(8,128)(2,1)}, u32[]{:S(2)}) copy-start(bf16[1,512,2048]{2,1,0:T(8,128)(2,1)} %param.6) | copy-start | bytes 6291460
  3.2 0.7 copy-start.5
  3.9 3.9 %copy-start.4 = (bf16[1,512,2048]{2,1,0:T(8,128)(2,1)S(1)}, bf16[1,512,2048]{2,1,0:T(8,128)(2,1)}, u32[]{:S(2)}) copy-start(bf16[1,512,2048]{2,1,0:T(8,128)(2,1)} %param.4) | copy-start | bytes 6291460
  6.5 26.8 %collective-permute-start.1 = (bf16[8,512,128]{2,1,0:T(8,128)(2,1)S(1)}, bf16[8,512,128]{2,1,0:T(8,128)(2,1)S(1)}, u32[]{:S(2)}, u32[]{:S(2)}) collective-permute-start(bf16[8,512,128]{2,1,0:T(8,128)(2,1)S(1)} %get-tuple-element.32), channel_id=1, source_target_pairs={{0,8},{4,12},{8,16},{12,20},{16,24},{20,28},{1,9},{5,13},{9,17},{1... | collective-permute-start | bytes 3145736 | tf_op jit(solution)/shard_map/ppermute | solution.py:484
  7.8 12.5 %copy-start.1 = (bf16[1,512,2048]{2,1,0:T(8,128)(2,1)S(1)}, bf16[1,512,2048]{2,1,0:T(8,128)(2,1)}, u32[]{:S(2)}) copy-start(bf16[1,512,2048]{2,1,0:T(8,128)(2,1)} %param.5) | copy-start | bytes 6291460
  7.8 12.5 %copy-start.3 = (bf16[1,512,2048]{2,1,0:T(8,128)(2,1)S(1)}, bf16[1,512,2048]{2,1,0:T(8,128)(2,1)}, u32[]{:S(2)}) copy-start(bf16[1,512,2048]{2,1,0:T(8,128)(2,1)} %param.6) | copy-start | bytes 6291460
  9.9 24.3 %collective-permute-start.2 = (bf16[4,512,128]{2,1,0:T(8,128)(2,1)S(1)}, bf16[4,512,128]{2,1,0:T(8,128)(2,1)S(1)}, u32[]{:S(2)}, u32[]{:S(2)}) collective-permute-start(bf16[4,512,128]{2,1,0:T(8,128)(2,1)S(1)} %get-tuple-element.44), channel_id=1, source_target_pairs={{12,0},{16,4},{20,8},{24,12},{28,16},{13,1},{17,5},{21,9},{25,13},... | collective-permute-start | bytes 1572872 | tf_op jit(solution)/shard_map/ppermute | solution.py:487
  15.4 5.0 %collective-permute-start = (s32[8,2,16]{2,1,0:T(2,128)S(1)}, s32[8,2,16]{2,1,0:T(2,128)S(1)}, u32[]{:S(2)}, u32[]{:S(2)}) collective-permute-start(s32[8,2,16]{2,1,0:T(2,128)S(1)} %bitcast.28), channel_id=1, source_target_pairs={{0,1},{1,2},{2,3},{3,0},{4,5},{5,6},{6,7},{7,4},{8,9},{9,10},{10,1... | collective-permute-start | bytes 3080 | tf_op jit(solution)/shard_map/ppermute | solution.py:24
  15.4 23.5 %collective-permute-start.3 = (bf16[4,512,128]{2,1,0:T(8,128)(2,1)}, bf16[4,512,128]{2,1,0:T(8,128)(2,1)}, u32[]{:S(2)}, u32[]{:S(2)}) collective-permute-start(bf16[4,512,128]{2,1,0:T(8,128)(2,1)} %get-tuple-element.46), channel_id=1, source_target_pairs={{20,0},{24,4},{28,8},{21,1},{25,5},{29,9},{22,2},{26,6},{30,10},{2... | collective-permute-start | bytes 1572872 | tf_op jit(solution)/shard_map/ppermute | solution.py:487
  20.4 9.0 %copy-start.7 = (s32[8,2,16]{2,1,0:T(2,128)}, s32[8,2,16]{2,1,0:T(2,128)S(1)}, u32[]{:S(2)}) copy-start(s32[8,2,16]{2,1,0:T(2,128)S(1)} %collective-permute-done.picks_ref) | copy-start | bytes 3076
  29.3 30.7 %collective-permute-start.4 = (bf16[16,528,128]{2,1,0:T(8,128)(2,1)}, bf16[16,528,128]{2,1,0:T(8,128)(2,1)}, u32[]{:S(2)}, u32[]{:S(2)}) collective-permute-start(bf16[16,528,128]{2,1,0:T(8,128)(2,1)} %shard_map.49), channel_id=1, source_target_pairs={{0,1},{1,2},{2,3},{3,0},{4,5},{5,6},{6,7},{7,4},{8,9},{9,10},{10,1... | collective-permute-start | bytes 6488072 | tf_op jit(solution)/shard_map/ppermute | solution.py:24
  29.9 30.1 %collective-permute-start.5 = (bf16[8,512,128]{2,1,0:T(8,128)(2,1)}, bf16[8,512,128]{2,1,0:T(8,128)(2,1)}, u32[]{:S(2)}, u32[]{:S(2)}) collective-permute-start(bf16[8,512,128]{2,1,0:T(8,128)(2,1)} %get-tuple-element.48), channel_id=1, source_target_pairs={{0,24},{4,28},{1,25},{5,29},{2,26},{6,30},{3,27},{7,31}} | collective-permute-start | bytes 3145736 | tf_op jit(solution)/shard_map/ppermute | solution.py:484
  33.3 1.0 copy-start.9
  37.6 76.4 %collective-permute-start.10 = (bf16[4,528,128]{2,1,0:T(8,128)(2,1)}, bf16[4,528,128]{2,1,0:T(8,128)(2,1)}, u32[]{:S(2)}, u32[]{:S(2)}) collective-permute-start(bf16[4,528,128]{2,1,0:T(8,128)(2,1)} %shard_map.50), channel_id=1, source_target_pairs={{0,13},{1,14},{2,15},{3,12},{4,17},{5,18},{6,19},{7,16},{8,21},{9,... | collective-permute-start | bytes 1622024 | tf_op jit(solution)/shard_map/ppermute | solution.py:495
  38.9 23.2 %copy-start.6 = (s32[1,8,16,2]{2,3,1,0:T(2,128)S(1)}, s32[1,8,16,2]{2,3,1,0:T(2,128)}, u32[]{:S(2)}) copy-start(s32[1,8,16,2]{2,3,1,0:T(2,128)} %param.7) | copy-start | bytes 3076
  38.9 23.2 %copy-start.10 = (bf16[8,512,128]{2,1,0:T(8,128)(2,1)S(1)}, bf16[8,512,128]{2,1,0:T(8,128)(2,1)}, u32[]{:S(2)}) copy-start(bf16[8,512,128]{2,1,0:T(8,128)(2,1)} %copy-done.9) | copy-start | bytes 3145732
  42.8 71.2 %collective-permute-start.11 = (bf16[4,528,128]{2,1,0:T(8,128)(2,1)}, bf16[4,528,128]{2,1,0:T(8,128)(2,1)}, u32[]{:S(2)}, u32[]{:S(2)}) collective-permute-start(bf16[4,528,128]{2,1,0:T(8,128)(2,1)} %shard_map.51), channel_id=1, source_target_pairs={{0,21},{1,22},{2,23},{3,20},{4,25},{5,26},{6,27},{7,24},{8,29},{9,... | collective-permute-start | bytes 1622024 | tf_op jit(solution)/shard_map/ppermute | solution.py:495
  60.1 14.9 %collective-permute-start.6 = (bf16[4,512,128]{2,1,0:T(8,128)(2,1)}, bf16[4,512,128]{2,1,0:T(8,128)(2,1)}, u32[]{:S(2)}, u32[]{:S(2)}) collective-permute-start(bf16[4,512,128]{2,1,0:T(8,128)(2,1)} %get-tuple-element.50), channel_id=1, source_target_pairs={{16,0},{20,4},{24,8},{28,12},{17,1},{21,5},{25,9},{29,13},{18,2},{... | collective-permute-start | bytes 1572872 | tf_op jit(solution)/shard_map/ppermute | solution.py:487
  67.5 15.6 %collective-permute-start.7 = (bf16[8,528,128]{2,1,0:T(8,128)(2,1)}, bf16[8,528,128]{2,1,0:T(8,128)(2,1)}, u32[]{:S(2)}, u32[]{:S(2)}) collective-permute-start(bf16[8,528,128]{2,1,0:T(8,128)(2,1)} %shard_map.52), channel_id=1, source_target_pairs={{0,1},{1,2},{2,3},{3,0},{4,5},{5,6},{6,7},{7,4},{8,9},{9,10},{10,1... | collective-permute-start | bytes 3244040 | tf_op jit(solution)/shard_map/ppermute | solution.py:24
  67.5 38.1 %collective-permute-start.8 = (bf16[4,512,128]{2,1,0:T(8,128)(2,1)}, bf16[4,512,128]{2,1,0:T(8,128)(2,1)}, u32[]{:S(2)}, u32[]{:S(2)}) collective-permute-start(bf16[4,512,128]{2,1,0:T(8,128)(2,1)} %get-tuple-element.52), channel_id=1, source_target_pairs={{4,0},{8,4},{12,8},{16,12},{20,16},{24,20},{28,24},{5,1},{9,5},{13... | collective-permute-start | bytes 1572872 | tf_op jit(solution)/shard_map/ppermute | solution.py:487
  74.9 33.6 %collective-permute-start.9 = (bf16[4,512,128]{2,1,0:T(8,128)(2,1)}, bf16[4,512,128]{2,1,0:T(8,128)(2,1)}, u32[]{:S(2)}, u32[]{:S(2)}) collective-permute-start(bf16[4,512,128]{2,1,0:T(8,128)(2,1)} %get-tuple-element.54), channel_id=1, source_target_pairs={{28,0},{29,1},{30,2},{31,3}} | collective-permute-start | bytes 1572872 | tf_op jit(solution)/shard_map/ppermute | solution.py:487
  83.1 38.2 %collective-permute-start.12 = (bf16[4,528,128]{2,1,0:T(8,128)(2,1)S(1)}, bf16[4,528,128]{2,1,0:T(8,128)(2,1)S(1)}, u32[]{:S(2)}, u32[]{:S(2)}) collective-permute-start(bf16[4,528,128]{2,1,0:T(8,128)(2,1)S(1)} %shard_map.53), channel_id=1, source_target_pairs={{0,17},{1,18},{2,19},{3,16},{4,21},{5,22},{6,23},{7,20},{8,25},{9,... | collective-permute-start | bytes 1622024 | tf_op jit(solution)/shard_map/ppermute | solution.py:495
  108.5 5.6 %copy-start.8 = (s32[8,2,16]{2,1,0:T(2,128)S(1)}, s32[8,2,16]{2,1,0:T(2,128)}, u32[]{:S(2)}) copy-start(s32[8,2,16]{2,1,0:T(2,128)} %copy-done.7) | copy-start | bytes 3076
  111.4 9.9 %collective-permute-start.14 = (bf16[4,528,128]{2,1,0:T(8,128)(2,1)S(1)}, bf16[4,528,128]{2,1,0:T(8,128)(2,1)S(1)}, u32[]{:S(2)}, u32[]{:S(2)}) collective-permute-start(bf16[4,528,128]{2,1,0:T(8,128)(2,1)S(1)} %shard_map.55), channel_id=1, source_target_pairs={{0,29},{1,30},{2,31},{3,28}} | collective-permute-start | bytes 1622024 | tf_op jit(solution)/shard_map/ppermute | solution.py:495
  112.1 26.2 %collective-permute-start.13 = (bf16[4,528,128]{2,1,0:T(8,128)(2,1)S(1)}, bf16[4,528,128]{2,1,0:T(8,128)(2,1)S(1)}, u32[]{:S(2)}, u32[]{:S(2)}) collective-permute-start(bf16[4,528,128]{2,1,0:T(8,128)(2,1)S(1)} %shard_map.54), channel_id=1, source_target_pairs={{0,5},{1,6},{2,7},{3,4},{4,9},{5,10},{6,11},{7,8},{8,13},{9,14},{1... | collective-permute-start | bytes 1622024 | tf_op jit(solution)/shard_map/ppermute | solution.py:495

commit v14 on v13

--- a/solution.py
+++ b/solution.py
@@ -121,7 +121,7 @@
         copy.wait()
 
 
-def pack(here, picks, sources, jobs, slots):
+def pack(here, picks, sources, jobs, slots, is_anchor=False):
     rows = sources[0].shape[0]
     sizes = [len(sources) * count for _, _, count, _ in jobs]
     return call(
@@ -130,6 +130,7 @@
         [jax.ShapeDtypeStruct((size, rows, HD), jnp.bfloat16) for size in sizes],
         [IN_VMEM] * len(sizes),
         [pltpu.SMEM((len(jobs) * slots + 1,), jnp.int32), pltpu.SemaphoreType.DMA((sum(sizes),))],
+        flops=HIGH_COST if is_anchor else 0,
         moved=4 * rows * HD * sum(sizes),
     )(here, picks, *sources)
 
@@ -496,12 +497,12 @@
 
     near_jobs = [(shift, 0, slots, True) for shift in near_shifts]
     near_sends = pack(here, own_picks, [keys, values], near_jobs, slots)
-    near = [up(near_sends[0], near_shifts[0])]
-    before = passed_along(own_picks, "pipe", 1)
+    near = [up(send, shift) for send, shift in zip(near_sends, near_shifts)]
+    before = passed_along(after(own_picks, near_sends[0]), "pipe", 1)
     sends, now = {}, after(here, *near_sends)
     for shifts in (far_shifts[:2], far_shifts[2:]):
         jobs = [(shift, 0, slots, False) for shift in shifts]
-        packed = pack(now, own_picks, [queries], jobs, slots)
+        packed = pack(now, own_picks, [queries], jobs, slots, is_anchor=len(shifts) > 2)
         sends |= zip(shifts, packed)
         now = after(now, *packed)
     arrived, returned = {}, {}
@@ -519,21 +520,19 @@
     ask_for(five, near_sends[0])
     own = own_part(after(now, before), queries, keys, values)
     own_back = passed_along(own, "pipe", 1)
-    near.append(up(after(near_sends[1], own), near_shifts[1]))
     part_three = work(after(here, own, near[0]), three, is_anchor=True)
     returned[three] = up_and_on(part_three, three)
     part_five = work(after(here, part_three), five, is_anchor=True)
     returned[five] = up_and_on(part_five, five)
-    ask_for(four, arrived[three], arrived[five], part_five, own_back, *near)
+    for shift in (four, one, seven):
+        ask_for(shift, arrived[three], arrived[five], part_five, own_back, *near)
     beside = near_part(after(here, part_five, own_back), own_picks, queries, near, near_shifts, slots)
-    ask_for(one, own_back, part_five, *near)
-    ask_for(seven, own_back, part_five, *near)
-    beside_back = passed_along(beside, "pipe", 1)
     part_four = work(after(here, beside), four, is_anchor=True)
     returned[four] = up_and_on(part_four, four)
-    part_one = work(after(here, part_four, beside_back), one)
+    part_one = work(after(here, part_four), one, is_anchor=True)
     returned[one] = up_and_on(part_one, one)
-    part_seven = work(after(here, part_one), seven)
+    beside_back = passed_along(after(beside, part_one), "pipe", 1)
+    part_seven = work(after(here, part_one), seven, is_anchor=True)
     returned[seven] = up_and_on(part_seven, seven)
     now = after(here, part_seven)
 
@@ -542,6 +541,8 @@
     parts = [own_back, beside_back, returned[three], returned[five]]
     result, mixed, sums = merge(now, before, parts, [0, HEADS] + places, merged_shifts, slots)
     lasts = [returned[shift] for shift in final_shifts]
+    now = tick(now, sums, returned[four])
+    now = tick(now, returned[one])
     return finish(now, before, result, mixed, sums, lasts, final_shifts, slots)[None]
 
 

time: 145 us -> 162 us (1.12)
  waiting for transfers between devices: 59.7 us -> 69.9 us
  Pallas kernels: 49.1 us -> 55.3 us
  starting transfers between devices: 28.4 us -> 32.3 us
  local copies, waits for them, and re-layouts: 4.91 us -> 3.19 us
    ppermute x3, waiting for transfers between devices: 3.62 us -> 17.6 us  [passed_along(): return lax.ppermute(value, axis, pairs)]
    ppermute x5, waiting for transfers between devices: 16.9 us -> 11.5 us  [up_and_on(): return lax.ppermute(value, ('ctx', 'pipe'), pairs)]
    ppermute x5, starting transfers between devices: 18.7 us -> 22.9 us  [down(): lax.ppermute(value, 'ctx', [(at, at - shift) for at in range(shift, width)])]
    ppermute x2, waiting for transfers between devices: 18 us -> 21.3 us  [up(): lax.ppermute(value, 'ctx', [(at, at + shift) for at in range(width - shif...]
    pallas_call x5, Pallas kernels: 16 us -> 17.9 us  [attend(): call(functools.partial(attend_kernel, group=group, slots=slots), [SCALARS...]
    unnamed x22 -> x8, local copies, waits for them, and re-layouts: 4.91 us -> 3.19 us
  transfers between devices with their start and end apart: 15 -> 15, of which waited for: 5 -> 4; matrix products, arithmetic and copies ran while one was open for 0% -> 0% of each run, Pallas kernels for 30% -> 29%
where the time goes in v14:
time: 162 us; the launch traced here: 161 us
  waiting for transfers between devices  69.9 us (43%)
  Pallas kernels  55.3 us (34%)
  starting transfers between devices  32.3 us (20%)
  local copies, waits for them, and re-layouts  3.19 us (2%)
    ppermute x5, starting transfers between devices, down(): lax.ppermute(value, 'ctx', [(at, at - shift) for at in range(shift, width)])  22.9 us
    ppermute x2, waiting for transfers between devices, up(): lax.ppermute(value, 'ctx', [(at, at + shift) for at in range(width - shif...  21.3 us
    ppermute x5, waiting for transfers between devices, down(): lax.ppermute(value, 'ctx', [(at, at - shift) for at in range(shift, width)])  19.6 us
    pallas_call x5, Pallas kernels, attend(): call(functools.partial(attend_kernel, group=group, slots=slots), [SCALARS...  17.9 us
    ppermute x3, waiting for transfers between devices, passed_along(): return lax.ppermute(value, axis, pairs)  17.6 us
    ppermute x5, waiting for transfers between devices, up_and_on(): return lax.ppermute(value, ('ctx', 'pipe'), pairs)  11.5 us
    pallas_call x1, Pallas kernels, own_part(): call(own_kernel, [SCALARS, IN_VMEM, IN_VMEM, IN_VMEM], jax.ShapeDtypeStru...  8.92 us
    pallas_call x3, Pallas kernels, pack(): call(functools.partial(pack_kernel, jobs=jobs, slots=slots), [SCALARS, SC...  8.54 us
  transfers between devices with their start and end apart: 15, of which 4 were waited for; matrix products, arithmetic and copies ran while one was open for 0% of the time, Pallas kernels for 29%

profile of v14, /device:TPU:26, one launch (start us, length us, event | category | flops | bytes accessed | tf_op | source)
XLA Modules:
  0.0 161.0 jit_solution(3165301942030048968)
XLA Ops:
  0.0 1.6 copy-done.1
  1.6 1.6 copy-done.2
  3.2 3.2 %shard_map.46 = (bf16[8,512,128]{2,1,0:T(8,128)(2,1)}, bf16[8,512,128]{2,1,0:T(8,128)(2,1)}) custom-call(s32[1]{0:T(128)} %bitcast.here_ref, s32[8,2,16]{2,1,0:T(2,128)} %bitcast.2.picks_ref, bf16[512,2048]{1,0:T(8,128)(2,1)S(1)} %bitcast.12, bf16[512,2048]{1,0:T(8,128)(2,1)S(1)} %bitcast.19), custom_call_target="tpu_custom_call" | custom-call | bytes 4194304 | tf_op jit(solution)/shard_map/pallas_call | solution.py:127
  6.4 1.3 collective-permute-start.1
  7.7 0.1 collective-permute-start
  7.8 1.3 collective-permute-start.5
  9.1 0.0 copy-done
  9.1 2.4 %shard_map.47 = (bf16[4,512,128]{2,1,0:T(8,128)(2,1)}, bf16[4,512,128]{2,1,0:T(8,128)(2,1)}) custom-call(s32[1]{0:T(128)} %bitcast.here_ref, s32[8,2,16]{2,1,0:T(2,128)} %bitcast.2.picks_ref, bf16[512,2048]{1,0:T(8,128)(2,1)S(1)} %bitcast.8), custom_call_target="tpu_custom_call" | custom-call | bytes 2097152 | tf_op jit(solution)/shard_map/pallas_call | solution.py:127
  11.4 9.1 %collective-permute-start.3 = (bf16[4,512,128]{2,1,0:T(8,128)(2,1)}, bf16[4,512,128]{2,1,0:T(8,128)(2,1)}, u32[]{:S(2)}, u32[]{:S(2)}) collective-permute-start(bf16[4,512,128]{2,1,0:T(8,128)(2,1)} %get-tuple-element.50), channel_id=1, source_target_pairs={{20,0},{24,4},{28,8},{21,1},{25,5},{29,9},{22,2},{26,6},{30,10},{2... | collective-permute-start | bytes 1572872 | tf_op jit(solution)/shard_map/ppermute | solution.py:488
  20.6 2.1 %collective-permute-start.2 = (bf16[4,512,128]{2,1,0:T(8,128)(2,1)}, bf16[4,512,128]{2,1,0:T(8,128)(2,1)}, u32[]{:S(2)}, u32[]{:S(2)}) collective-permute-start(bf16[4,512,128]{2,1,0:T(8,128)(2,1)} %get-tuple-element.48), channel_id=1, source_target_pairs={{12,0},{16,4},{20,8},{24,12},{28,16},{13,1},{17,5},{21,9},{25,13},... | collective-permute-start | bytes 1572872 | tf_op jit(solution)/shard_map/ppermute | solution.py:488
  22.7 3.0 %shard_map.48 = (bf16[4,512,128]{2,1,0:T(8,128)(2,1)}, bf16[4,512,128]{2,1,0:T(8,128)(2,1)}, bf16[4,512,128]{2,1,0:T(8,128)(2,1)}) custom-call(s32[1]{0:T(128)} %bitcast.here_ref, s32[8,2,16]{2,1,0:T(2,128)} %bitcast.2.picks_ref, bf16[512,2048]{1,0:T(8,128)(2,1)S(1)} %bitcast.9), custom_call_target="tpu_custom_call" | custom-call | flops 999999995904 | bytes 3145728 | tf_op jit(solution)/shard_map/pallas_call | solution.py:127
  25.7 0.0 collective-permute-done.picks_ref
  25.7 0.0 copy-done.3
  25.7 8.9 %shard_map.49 = bf16[16,528,128]{2,1,0:T(8,128)(2,1)} custom-call(s32[1]{0:T(128)} %bitcast.here_ref, bf16[512,2048]{1,0:T(8,128)(2,1)S(1)} %bitcast.10, bf16[512,2048]{1,0:T(8,128)(2,1)S(1)} %bitcast.13, bf16[512,2048]{1,0:T(8,128)(2,1)S(1)} %bitcast.20), custom_call_target="tpu_custom_call" | custom-call | flops 2147483648 | bytes 8388608 | tf_op jit(solution)/shard_map/pallas_call | solution.py:267
  34.6 0.1 collective-permute-start.4
  34.7 21.3 %collective-permute-done.1.refs_0_ = bf16[8,512,128]{2,1,0:T(8,128)(2,1)} collective-permute-done((bf16[8,512,128]{2,1,0:T(8,128)(2,1)}, bf16[8,512,128]{2,1,0:T(8,128)(2,1)}, u32[]{:S(2)}, u32[]{:S(2)}) %collective-permute-start.1) | collective-permute-done | bytes 1048608 | tf_op jit(solution)/shard_map/ppermute | solution.py:485
  56.0 0.0 collective-permute-done.2.refs_0_
  56.0 3.8 %shard_map.50 = bf16[4,528,128]{2,1,0:T(8,128)(2,1)} custom-call(s32[1]{0:T(128)} %bitcast.here_ref, s32[8,2,16]{2,1,0:T(2,128)} %bitcast.2.picks_ref, bf16[512,2048]{1,0:T(8,128)(2,1)S(1)} %bitcast.14, bf16[512,2048]{1,0:T(8,128)(2,1)S(1)} %bitcast.21, bf16[4,512,128]{2,1,0:T(8,128)(2,1)} %collective-permute-done.2.refs_0_), custom_call_target="tpu_custom_call" | custom-call | flops 999999995904 | bytes 2097152 | tf_op jit(solution)/shard_map/pallas_call | solution.py:227
  59.7 1.3 collective-permute-start.10
  61.0 0.0 collective-permute-done.3.refs_0_
  61.0 3.7 %shard_map.51 = bf16[4,528,128]{2,1,0:T(8,128)(2,1)} custom-call(s32[1]{0:T(128)} %bitcast.here_ref, s32[8,2,16]{2,1,0:T(2,128)} %bitcast.2.picks_ref, bf16[512,2048]{1,0:T(8,128)(2,1)S(1)} %bitcast.15, bf16[512,2048]{1,0:T(8,128)(2,1)S(1)} %bitcast.22, bf16[4,512,128]{2,1,0:T(8,128)(2,1)} %collective-permute-done.3.refs_0_), custom_call_target="tpu_custom_call" | custom-call | flops 999999995904 | bytes 2097152 | tf_op jit(solution)/shard_map/pallas_call | solution.py:227
  64.8 1.3 collective-permute-start.11
  66.0 0.0 collective-permute-done.5.refs_1_
  66.1 0.0 collective-permute-done.4.refs_0_
  66.1 3.7 %collective-permute-start.6 = (bf16[4,512,128]{2,1,0:T(8,128)(2,1)}, bf16[4,512,128]{2,1,0:T(8,128)(2,1)}, u32[]{:S(2)}, u32[]{:S(2)}) collective-permute-start(bf16[4,512,128]{2,1,0:T(8,128)(2,1)} %get-tuple-element.53), channel_id=1, source_target_pairs={{16,0},{20,4},{24,8},{28,12},{17,1},{21,5},{25,9},{29,13},{18,2},{... | collective-permute-start | bytes 1572872 | tf_op jit(solution)/shard_map/ppermute | solution.py:488
  69.7 5.7 %shard_map.52 = bf16[8,528,128]{2,1,0:T(8,128)(2,1)} custom-call(s32[1]{0:T(128)} %bitcast.here_ref, s32[8,2,16]{2,1,0:T(2,128)} %bitcast.2.picks_ref, bf16[512,2048]{1,0:T(8,128)(2,1)S(1)} %bitcast.11, bf16[8,512,128]{2,1,0:T(8,128)(2,1)} %collective-permute-done.1.refs_0_, bf16[8,512,128]{2,1,0:T(8,128)(2,1)} %collective-permute-done.5.refs_1_), custom_call_target="tpu_custom_call" | custom-call | flops 999999995904 | bytes 6291456 | tf_op jit(solution)/shard_map/pallas_call | solution.py:296
  75.4 6.5 %collective-permute-start.7 = (bf16[4,512,128]{2,1,0:T(8,128)(2,1)}, bf16[4,512,128]{2,1,0:T(8,128)(2,1)}, u32[]{:S(2)}, u32[]{:S(2)}) collective-permute-start(bf16[4,512,128]{2,1,0:T(8,128)(2,1)} %get-tuple-element.55), channel_id=1, source_target_pairs={{4,0},{8,4},{12,8},{16,12},{20,16},{24,20},{28,24},{5,1},{9,5},{13... | collective-permute-start | bytes 1572872 | tf_op jit(solution)/shard_map/ppermute | solution.py:488
  81.9 1.5 collective-permute-start.8
  83.4 0.0 collective-permute-done.6.refs_0_
  83.4 3.8 %shard_map.53 = bf16[4,528,128]{2,1,0:T(8,128)(2,1)} custom-call(s32[1]{0:T(128)} %bitcast.here_ref, s32[8,2,16]{2,1,0:T(2,128)} %bitcast.2.picks_ref, bf16[512,2048]{1,0:T(8,128)(2,1)S(1)} %bitcast.16, bf16[512,2048]{1,0:T(8,128)(2,1)S(1)} %bitcast.23, bf16[4,512,128]{2,1,0:T(8,128)(2,1)} %collective-permute-done.6.refs_0_), custom_call_target="tpu_custom_call" | custom-call | flops 999999995904 | bytes 2097152 | tf_op jit(solution)/shard_map/pallas_call | solution.py:227
  87.2 19.5 %collective-permute-done.7.refs_0_ = bf16[4,512,128]{2,1,0:T(8,128)(2,1)} collective-permute-done((bf16[4,512,128]{2,1,0:T(8,128)(2,1)}, bf16[4,512,128]{2,1,0:T(8,128)(2,1)}, u32[]{:S(2)}, u32[]{:S(2)}) %collective-permute-start.7) | collective-permute-done | bytes 524320 | tf_op jit(solution)/shard_map/ppermute | solution.py:488
  106.7 3.7 %shard_map.54 = bf16[4,528,128]{2,1,0:T(8,128)(2,1)} custom-call(s32[1]{0:T(128)} %bitcast.here_ref, s32[8,2,16]{2,1,0:T(2,128)} %bitcast.2.picks_ref, bf16[512,2048]{1,0:T(8,128)(2,1)S(1)} %bitcast.17, bf16[512,2048]{1,0:T(8,128)(2,1)S(1)} %bitcast.24, bf16[4,512,128]{2,1,0:T(8,128)(2,1)} %collective-permute-done.7.refs_0_), custom_call_target="tpu_custom_call" | custom-call | flops 999999995904 | bytes 2097152 | tf_op jit(solution)/shard_map/pallas_call | solution.py:227
  110.4 1.9 %collective-permute-start.13 = (bf16[4,528,128]{2,1,0:T(8,128)(2,1)}, bf16[4,528,128]{2,1,0:T(8,128)(2,1)}, u32[]{:S(2)}, u32[]{:S(2)}) collective-permute-start(bf16[4,528,128]{2,1,0:T(8,128)(2,1)} %shard_map.54), channel_id=1, source_target_pairs={{0,5},{1,6},{2,7},{3,4},{4,9},{5,10},{6,11},{7,8},{8,13},{9,14},{1... | collective-permute-start | bytes 1622024 | tf_op jit(solution)/shard_map/ppermute | solution.py:496
  112.3 1.3 collective-permute-start.12
  113.6 0.0 collective-permute-done.8.refs_0_
  113.6 0.2 collective-permute-start.9
  113.8 2.9 %shard_map.55 = bf16[4,528,128]{2,1,0:T(8,128)(2,1)S(1)} custom-call(s32[1]{0:T(128)} %bitcast.here_ref, s32[8,2,16]{2,1,0:T(2,128)} %bitcast.2.picks_ref, bf16[512,2048]{1,0:T(8,128)(2,1)S(1)} %bitcast.18, bf16[512,2048]{1,0:T(8,128)(2,1)S(1)} %bitcast.25, bf16[4,512,128]{2,1,0:T(8,128)(2,1)} %collective-permute-done.8.refs_0_), custom_call_target="tpu_custom_call" | custom-call | flops 999999995904 | bytes 2097152 | tf_op jit(solution)/shard_map/pallas_call | solution.py:227
  116.8 0.0 collective-permute-done.11.refs_3_
  116.8 0.7 collective-permute-start.14
  117.5 0.0 collective-permute-done.10.refs_2_
  117.5 17.6 %collective-permute-done.9.refs_1_ = bf16[8,528,128]{2,1,0:T(8,128)(2,1)} collective-permute-done((bf16[8,528,128]{2,1,0:T(8,128)(2,1)}, bf16[8,528,128]{2,1,0:T(8,128)(2,1)}, u32[]{:S(2)}, u32[]{:S(2)}) %collective-permute-start.9) | collective-permute-done | bytes 1081376 | tf_op jit(solution)/shard_map/ppermute | solution.py:24
  135.1 7.4 %shard_map.56 = (bf16[512,2048]{1,0:T(8,128)(2,1)}, f32[16,512,128]{2,1,0:T(8,128)S(1)}, f32[16,4,128]{2,1,0:T(4,128)S(1)}) custom-call(s32[1]{0:T(128)} %bitcast.here_ref, s32[8,2,16]{2,1,0:T(2,128)} %collective-permute-done.picks_ref, bf16[16,528,128]{2,1,0:T(8,128)(2,1)} %collective-permute-done.4.refs_0_, ...), custom_call_target="tpu_custom_call" | custom-call | flops 6291456 | bytes 8388608 | tf_op jit(solution)/shard_map/pallas_call | solution.py:368
  142.5 11.5 %collective-permute-done.12.refs_0_ = bf16[4,528,128]{2,1,0:T(8,128)(2,1)} collective-permute-done((bf16[4,528,128]{2,1,0:T(8,128)(2,1)}, bf16[4,528,128]{2,1,0:T(8,128)(2,1)}, u32[]{:S(2)}, u32[]{:S(2)}) %collective-permute-start.12) | collective-permute-done | bytes 540704 | tf_op jit(solution)/shard_map/ppermute | solution.py:496
  153.9 0.5 shard_map.57.here_ref
  154.5 0.0 collective-permute-done.13.refs_1_
  154.5 1.1 shard_map.58.here_ref
  155.6 0.0 collective-permute-done.14.refs_2_
  155.6 5.3 %shard_map.59 = bf16[512,2048]{1,0:T(8,128)(2,1)} custom-call(s32[1]{0:T(128)} %shard_map.58.here_ref, s32[8,2,16]{2,1,0:T(2,128)} %collective-permute-done.picks_ref, f32[16,512,128]{2,1,0:T(8,128)S(1)} %get-tuple-element.63.mixed_ref, f32[16,4,128]{2,1,0:T(4,128)S(1)} %get-tuple-element.60.sums_ref, ...), custom_call_target="tpu_custom_call", output_to_operand_aliasing={{}: (7, {})} | custom-call | flops 1572864 | bytes 6291456 | tf_op jit(solution)/shard_map/pallas_call | solution.py:449
  (4 shorter events, 0.0 us)
Async XLA Ops:
  0.0 1.6 copy-start.1
  1.6 1.6 copy-start.2
  3.2 5.9 %copy-start = (bf16[1,512,2048]{2,1,0:T(8,128)(2,1)S(1)}, bf16[1,512,2048]{2,1,0:T(8,128)(2,1)}, u32[]{:S(2)}) copy-start(bf16[1,512,2048]{2,1,0:T(8,128)(2,1)} %param.4) | copy-start | bytes 6291460
  6.4 49.6 %collective-permute-start.1 = (bf16[8,512,128]{2,1,0:T(8,128)(2,1)}, bf16[8,512,128]{2,1,0:T(8,128)(2,1)}, u32[]{:S(2)}, u32[]{:S(2)}) collective-permute-start(bf16[8,512,128]{2,1,0:T(8,128)(2,1)} %get-tuple-element.35), channel_id=1, source_target_pairs={{0,8},{4,12},{8,16},{12,20},{16,24},{20,28},{1,9},{5,13},{9,17},{1... | collective-permute-start | bytes 3145736 | tf_op jit(solution)/shard_map/ppermute | solution.py:485
  7.7 18.0 %collective-permute-start = (s32[8,2,16]{2,1,0:T(2,128)}, s32[8,2,16]{2,1,0:T(2,128)}, u32[]{:S(2)}, u32[]{:S(2)}) collective-permute-start(s32[8,2,16]{2,1,0:T(2,128)} %bitcast.2.picks_ref), channel_id=1, source_target_pairs={{0,1},{1,2},{2,3},{3,0},{4,5},{5,6},{6,7},{7,4},{8,9},{9,10},{10,1... | collective-permute-start | bytes 3080 | tf_op jit(solution)/shard_map/ppermute | solution.py:24
  7.8 58.3 %collective-permute-start.5 = (bf16[8,512,128]{2,1,0:T(8,128)(2,1)}, bf16[8,512,128]{2,1,0:T(8,128)(2,1)}, u32[]{:S(2)}, u32[]{:S(2)}) collective-permute-start(bf16[8,512,128]{2,1,0:T(8,128)(2,1)} %get-tuple-element.36), channel_id=1, source_target_pairs={{0,24},{4,28},{1,25},{5,29},{2,26},{6,30},{3,27},{7,31}} | collective-permute-start | bytes 3145736 | tf_op jit(solution)/shard_map/ppermute | solution.py:485
  11.4 49.6 %collective-permute-start.3 = (bf16[4,512,128]{2,1,0:T(8,128)(2,1)}, bf16[4,512,128]{2,1,0:T(8,128)(2,1)}, u32[]{:S(2)}, u32[]{:S(2)}) collective-permute-start(bf16[4,512,128]{2,1,0:T(8,128)(2,1)} %get-tuple-element.50), channel_id=1, source_target_pairs={{20,0},{24,4},{28,8},{21,1},{25,5},{29,9},{22,2},{26,6},{30,10},{2... | collective-permute-start | bytes 1572872 | tf_op jit(solution)/shard_map/ppermute | solution.py:488
  20.6 35.4 %collective-permute-start.2 = (bf16[4,512,128]{2,1,0:T(8,128)(2,1)}, bf16[4,512,128]{2,1,0:T(8,128)(2,1)}, u32[]{:S(2)}, u32[]{:S(2)}) collective-permute-start(bf16[4,512,128]{2,1,0:T(8,128)(2,1)} %get-tuple-element.48), channel_id=1, source_target_pairs={{12,0},{16,4},{20,8},{24,12},{28,16},{13,1},{17,5},{21,9},{25,13},... | collective-permute-start | bytes 1572872 | tf_op jit(solution)/shard_map/ppermute | solution.py:488
  22.7 3.0 %copy-start.3 = (bf16[1,512,2048]{2,1,0:T(8,128)(2,1)S(1)}, bf16[1,512,2048]{2,1,0:T(8,128)(2,1)}, u32[]{:S(2)}) copy-start(bf16[1,512,2048]{2,1,0:T(8,128)(2,1)} %param.6) | copy-start | bytes 6291460
  34.6 31.4 %collective-permute-start.4 = (bf16[16,528,128]{2,1,0:T(8,128)(2,1)}, bf16[16,528,128]{2,1,0:T(8,128)(2,1)}, u32[]{:S(2)}, u32[]{:S(2)}) collective-permute-start(bf16[16,528,128]{2,1,0:T(8,128)(2,1)} %shard_map.49), channel_id=1, source_target_pairs={{0,1},{1,2},{2,3},{3,0},{4,5},{5,6},{6,7},{7,4},{8,9},{9,10},{10,1... | collective-permute-start | bytes 6488072 | tf_op jit(solution)/shard_map/ppermute | solution.py:24
  59.7 57.7 %collective-permute-start.10 = (bf16[4,528,128]{2,1,0:T(8,128)(2,1)}, bf16[4,528,128]{2,1,0:T(8,128)(2,1)}, u32[]{:S(2)}, u32[]{:S(2)}) collective-permute-start(bf16[4,528,128]{2,1,0:T(8,128)(2,1)} %shard_map.50), channel_id=1, source_target_pairs={{0,13},{1,14},{2,15},{3,12},{4,17},{5,18},{6,19},{7,16},{8,21},{9,... | collective-permute-start | bytes 1622024 | tf_op jit(solution)/shard_map/ppermute | solution.py:496
  64.8 52.0 %collective-permute-start.11 = (bf16[4,528,128]{2,1,0:T(8,128)(2,1)}, bf16[4,528,128]{2,1,0:T(8,128)(2,1)}, u32[]{:S(2)}, u32[]{:S(2)}) collective-permute-start(bf16[4,528,128]{2,1,0:T(8,128)(2,1)} %shard_map.51), channel_id=1, source_target_pairs={{0,21},{1,22},{2,23},{3,20},{4,25},{5,26},{6,27},{7,24},{8,29},{9,... | collective-permute-start | bytes 1622024 | tf_op jit(solution)/shard_map/ppermute | solution.py:496
  66.1 17.3 %collective-permute-start.6 = (bf16[4,512,128]{2,1,0:T(8,128)(2,1)}, bf16[4,512,128]{2,1,0:T(8,128)(2,1)}, u32[]{:S(2)}, u32[]{:S(2)}) collective-permute-start(bf16[4,512,128]{2,1,0:T(8,128)(2,1)} %get-tuple-element.53), channel_id=1, source_target_pairs={{16,0},{20,4},{24,8},{28,12},{17,1},{21,5},{25,9},{29,13},{18,2},{... | collective-permute-start | bytes 1572872 | tf_op jit(solution)/shard_map/ppermute | solution.py:488
  75.4 31.3 %collective-permute-start.7 = (bf16[4,512,128]{2,1,0:T(8,128)(2,1)}, bf16[4,512,128]{2,1,0:T(8,128)(2,1)}, u32[]{:S(2)}, u32[]{:S(2)}) collective-permute-start(bf16[4,512,128]{2,1,0:T(8,128)(2,1)} %get-tuple-element.55), channel_id=1, source_target_pairs={{4,0},{8,4},{12,8},{16,12},{20,16},{24,20},{28,24},{5,1},{9,5},{13... | collective-permute-start | bytes 1572872 | tf_op jit(solution)/shard_map/ppermute | solution.py:488
  81.9 31.7 %collective-permute-start.8 = (bf16[4,512,128]{2,1,0:T(8,128)(2,1)}, bf16[4,512,128]{2,1,0:T(8,128)(2,1)}, u32[]{:S(2)}, u32[]{:S(2)}) collective-permute-start(bf16[4,512,128]{2,1,0:T(8,128)(2,1)} %get-tuple-element.57), channel_id=1, source_target_pairs={{28,0},{29,1},{30,2},{31,3}} | collective-permute-start | bytes 1572872 | tf_op jit(solution)/shard_map/ppermute | solution.py:488
  110.4 44.1 %collective-permute-start.13 = (bf16[4,528,128]{2,1,0:T(8,128)(2,1)}, bf16[4,528,128]{2,1,0:T(8,128)(2,1)}, u32[]{:S(2)}, u32[]{:S(2)}) collective-permute-start(bf16[4,528,128]{2,1,0:T(8,128)(2,1)} %shard_map.54), channel_id=1, source_target_pairs={{0,5},{1,6},{2,7},{3,4},{4,9},{5,10},{6,11},{7,8},{8,13},{9,14},{1... | collective-permute-start | bytes 1622024 | tf_op jit(solution)/shard_map/ppermute | solution.py:496
  112.3 41.6 %collective-permute-start.12 = (bf16[4,528,128]{2,1,0:T(8,128)(2,1)}, bf16[4,528,128]{2,1,0:T(8,128)(2,1)}, u32[]{:S(2)}, u32[]{:S(2)}) collective-permute-start(bf16[4,528,128]{2,1,0:T(8,128)(2,1)} %shard_map.53), channel_id=1, source_target_pairs={{0,17},{1,18},{2,19},{3,16},{4,21},{5,22},{6,23},{7,20},{8,25},{9,... | collective-permute-start | bytes 1622024 | tf_op jit(solution)/shard_map/ppermute | solution.py:496
  113.6 21.4 %collective-permute-start.9 = (bf16[8,528,128]{2,1,0:T(8,128)(2,1)}, bf16[8,528,128]{2,1,0:T(8,128)(2,1)}, u32[]{:S(2)}, u32[]{:S(2)}) collective-permute-start(bf16[8,528,128]{2,1,0:T(8,128)(2,1)} %shard_map.52), channel_id=1, source_target_pairs={{0,1},{1,2},{2,3},{3,0},{4,5},{5,6},{6,7},{7,4},{8,9},{9,10},{10,1... | collective-permute-start | bytes 3244040 | tf_op jit(solution)/shard_map/ppermute | solution.py:24
  116.8 38.8 %collective-permute-start.14 = (bf16[4,528,128]{2,1,0:T(8,128)(2,1)S(1)}, bf16[4,528,128]{2,1,0:T(8,128)(2,1)S(1)}, u32[]{:S(2)}, u32[]{:S(2)}) collective-permute-start(bf16[4,528,128]{2,1,0:T(8,128)(2,1)S(1)} %shard_map.55), channel_id=1, source_target_pairs={{0,29},{1,30},{2,31},{3,28}} | collective-permute-start | bytes 1622024 | tf_op jit(solution)/shard_map/ppermute | solution.py:496

commit v15 on v10

--- a/solution.py
+++ b/solution.py
@@ -478,7 +478,7 @@
     near_shifts = (2, width - 2)
     middle = width // 2
     far_shifts = [middle, middle - 1, middle + 1, 1, width - 1]
-    final_shifts = tuple(far_shifts[3:])
+    final_shifts = tuple(far_shifts[1:])
 
     def up(value, shift):
         return lax.ppermute(value, "ctx", [(at, at + shift) for at in range(width - shift)])
@@ -518,7 +518,7 @@
     ask_for(four, near_sends[0])
     own = own_part(after(now, before), queries, keys, values)
     own_back = passed_along(own, "pipe", 1)
-    near.append(up(after(near_sends[1], own), near_shifts[1]))
+    near.append(up(after(near_sends[1], now), near_shifts[1]))
     ask_for(three, arrived[four], near[0], own)
     ask_for(five, arrived[four], near[0], own)
     part_four = work(after(here, own, near[0]), four, is_anchor=True)
@@ -537,9 +537,9 @@
     returned[seven] = up_and_on(part_seven, seven)
     now = after(here, part_seven)
 
-    merged_shifts = near_shifts + (four, three, five)
-    places = [HEADS + place * slots for place in (2, 3, 4)]
-    parts = [own_back, beside_back, returned[four], returned[three], returned[five]]
+    merged_shifts = near_shifts + (four,)
+    places = [HEADS + 2 * slots]
+    parts = [own_back, beside_back, returned[four]]
     result, mixed, sums = merge(now, before, parts, [0, HEADS] + places, merged_shifts, slots)
     lasts = [returned[shift] for shift in final_shifts]
     return finish(now, before, result, mixed, sums, lasts, final_shifts, slots)[None]

time: 145 us -> 151 us (1.041)
  the two profiles are of different devices: /device:TPU:29 before, /device:TPU:26 now
where the time goes in v15:
time: 151 us; the launch traced here: 149 us
  waiting for transfers between devices  60.5 us (40%)
  Pallas kernels  50.2 us (33%)
  starting transfers between devices  33.5 us (22%)
  local copies, waits for them, and re-layouts  4.19 us (3%)
    ppermute x2, waiting for transfers between devices, up(): lax.ppermute(value, 'ctx', [(at, at + shift) for at in range(width - shif...  27.8 us
    ppermute x5, waiting for transfers between devices, up_and_on(): return lax.ppermute(value, ('ctx', 'pipe'), pairs)  25.4 us
    ppermute x5, starting transfers between devices, down(): lax.ppermute(value, 'ctx', [(at, at - shift) for at in range(shift, width)])  19.2 us
    pallas_call x5, Pallas kernels, attend(): call(functools.partial(attend_kernel, group=group, slots=slots), [SCALARS...  15.3 us
    ppermute x5, starting transfers between devices, up_and_on(): return lax.ppermute(value, ('ctx', 'pipe'), pairs)  11 us
    pallas_call x1, Pallas kernels, own_part(): call(own_kernel, [SCALARS, IN_VMEM, IN_VMEM, IN_VMEM], jax.ShapeDtypeStru...  8.95 us
    pallas_call x3, Pallas kernels, pack(): call(functools.partial(pack_kernel, jobs=jobs, slots=slots), [SCALARS, SC...  7.5 us
    ppermute x5, waiting for transfers between devices, down(): lax.ppermute(value, 'ctx', [(at, at - shift) for at in range(shift, width)])  7.31 us
  transfers between devices with their start and end apart: 15, of which 5 were waited for; matrix products, arithmetic and copies ran while one was open for 0% of the time, Pallas kernels for 28%

profile of v15, /device:TPU:26, one launch (start us, length us, event | category | flops | bytes accessed | tf_op | source)
XLA Modules:
  0.0 148.8 jit_solution(2861280284114813934)
XLA Ops:
  0.0 1.6 %copy-done = bf16[1,512,2048]{2,1,0:T(8,128)(2,1)S(1)} copy-done((bf16[1,512,2048]{2,1,0:T(8,128)(2,1)S(1)}, bf16[1,512,2048]{2,1,0:T(8,128)(2,1)}, u32[]{:S(2)}) %copy-start) | copy-done | bytes 2097176
  1.6 1.6 %copy-done.2 = bf16[1,512,2048]{2,1,0:T(8,128)(2,1)S(1)} copy-done((bf16[1,512,2048]{2,1,0:T(8,128)(2,1)S(1)}, bf16[1,512,2048]{2,1,0:T(8,128)(2,1)}, u32[]{:S(2)}) %copy-start.2) | copy-done | bytes 2097176
  3.2 2.9 %shard_map.46 = (bf16[8,512,128]{2,1,0:T(8,128)(2,1)S(1)}, bf16[8,512,128]{2,1,0:T(8,128)(2,1)}) custom-call(s32[1]{0:T(128)} %bitcast.here_ref, s32[8,2,16]{2,1,0:T(2,128)} %bitcast.2.picks_ref, bf16[512,2048]{1,0:T(8,128)(2,1)S(1)} %bitcast.8, bf16[512,2048]{1,0:T(8,128)(2,1)S(1)} %bitcast.15), custom_call_target="tpu_custom_call" | custom-call | bytes 4194304 | tf_op jit(solution)/shard_map/pallas_call | solution.py:127
  6.0 1.3 collective-permute-start.1
  7.4 0.0 copy-start.1
  7.4 0.0 copy-start.3
  7.4 1.2 shard_map.47
  8.6 4.5 %collective-permute-start.2 = (bf16[4,512,128]{2,1,0:T(8,128)(2,1)S(1)}, bf16[4,512,128]{2,1,0:T(8,128)(2,1)S(1)}, u32[]{:S(2)}, u32[]{:S(2)}) collective-permute-start(bf16[4,512,128]{2,1,0:T(8,128)(2,1)S(1)} %shard_map.47), channel_id=1, source_target_pairs={{16,0},{20,4},{24,8},{28,12},{17,1},{21,5},{25,9},{29,13},{18,2},{... | collective-permute-start | bytes 1572872 | tf_op jit(solution)/shard_map/ppermute | solution.py:487
  13.1 0.1 collective-permute-start
  13.2 3.4 %shard_map.48 = (bf16[4,512,128]{2,1,0:T(8,128)(2,1)}, bf16[4,512,128]{2,1,0:T(8,128)(2,1)}, bf16[4,512,128]{2,1,0:T(8,128)(2,1)}, bf16[4,512,128]{2,1,0:T(8,128)(2,1)}) custom-call(s32[1]{0:T(128)} %bitcast.here_ref, s32[8,2,16]{2,1,0:T(2,128)} %bitcast.2.picks_ref, bf16[512,2048]{1,0:T(8,128)(2,1)S(1)} %bitcast.23), custom_call_target="tpu_custom_call" | custom-call | bytes 4194304 | tf_op jit(solution)/shard_map/pallas_call | solution.py:127
  16.6 1.3 collective-permute-start.4
  17.9 0.0 collective-permute-done.picks_ref
  17.9 8.9 %shard_map.49 = bf16[16,528,128]{2,1,0:T(8,128)(2,1)} custom-call(s32[1]{0:T(128)} %bitcast.here_ref, bf16[512,2048]{1,0:T(8,128)(2,1)S(1)} %bitcast.24, bf16[512,2048]{1,0:T(8,128)(2,1)S(1)} %bitcast.9, bf16[512,2048]{1,0:T(8,128)(2,1)S(1)} %bitcast.16), custom_call_target="tpu_custom_call" | custom-call | flops 2147483648 | bytes 8388608 | tf_op jit(solution)/shard_map/pallas_call | solution.py:266
  26.9 0.7 collective-permute-start.3
  27.5 0.0 collective-permute-done.2.refs_0_
  27.5 27.8 %collective-permute-done.1.refs_0_ = bf16[8,512,128]{2,1,0:T(8,128)(2,1)S(1)} collective-permute-done((bf16[8,512,128]{2,1,0:T(8,128)(2,1)S(1)}, bf16[8,512,128]{2,1,0:T(8,128)(2,1)S(1)}, u32[]{:S(2)}, u32[]{:S(2)}) %collective-permute-start.1) | collective-permute-done | bytes 1048608 | tf_op jit(solution)/shard_map/ppermute | solution.py:484
  55.3 1.0 copy-done.5
  56.3 2.1 %collective-permute-start.5 = (bf16[4,512,128]{2,1,0:T(8,128)(2,1)}, bf16[4,512,128]{2,1,0:T(8,128)(2,1)}, u32[]{:S(2)}, u32[]{:S(2)}) collective-permute-start(bf16[4,512,128]{2,1,0:T(8,128)(2,1)} %get-tuple-element.46), channel_id=1, source_target_pairs={{12,0},{16,4},{20,8},{24,12},{28,16},{13,1},{17,5},{21,9},{25,13},... | collective-permute-start | bytes 1572872 | tf_op jit(solution)/shard_map/ppermute | solution.py:487
  58.4 2.1 %collective-permute-start.6 = (bf16[4,512,128]{2,1,0:T(8,128)(2,1)}, bf16[4,512,128]{2,1,0:T(8,128)(2,1)}, u32[]{:S(2)}, u32[]{:S(2)}) collective-permute-start(bf16[4,512,128]{2,1,0:T(8,128)(2,1)} %get-tuple-element.48), channel_id=1, source_target_pairs={{20,0},{24,4},{28,8},{21,1},{25,5},{29,9},{22,2},{26,6},{30,10},{2... | collective-permute-start | bytes 1572872 | tf_op jit(solution)/shard_map/ppermute | solution.py:487
  60.5 3.6 %shard_map.50 = bf16[4,528,128]{2,1,0:T(8,128)(2,1)} custom-call(s32[1]{0:T(128)} %bitcast.here_ref, s32[8,2,16]{2,1,0:T(2,128)} %bitcast.2.picks_ref, bf16[512,2048]{1,0:T(8,128)(2,1)S(1)} %bitcast.10, bf16[512,2048]{1,0:T(8,128)(2,1)S(1)} %bitcast.17, bf16[4,512,128]{2,1,0:T(8,128)(2,1)S(1)} %collective-permute-done.2.refs_0_), custom_call_target="tpu_custom_call" | custom-call | flops 999999995904 | bytes 2097152 | tf_op jit(solution)/shard_map/pallas_call | solution.py:226
  64.1 1.3 collective-permute-start.10
  65.4 0.0 collective-permute-done.3.refs_0_
  65.4 0.0 collective-permute-done.4.refs_1_
  65.4 0.0 copy-done.6
  65.4 5.4 %shard_map.51 = bf16[8,528,128]{2,1,0:T(8,128)(2,1)} custom-call(s32[1]{0:T(128)} %bitcast.here_ref, s32[8,2,16]{2,1,0:T(2,128)} %bitcast.2.picks_ref, bf16[512,2048]{1,0:T(8,128)(2,1)S(1)} %bitcast.25, bf16[8,512,128]{2,1,0:T(8,128)(2,1)S(1)} %copy-done.6, bf16[8,512,128]{2,1,0:T(8,128)(2,1)} %collective-permute-done.4.refs_1_), custom_call_target="tpu_custom_call" | custom-call | flops 1073741824 | bytes 6291456 | tf_op jit(solution)/shard_map/pallas_call | solution.py:295
  70.8 0.0 collective-permute-start.7
  70.8 9.1 %collective-permute-start.8 = (bf16[4,512,128]{2,1,0:T(8,128)(2,1)}, bf16[4,512,128]{2,1,0:T(8,128)(2,1)}, u32[]{:S(2)}, u32[]{:S(2)}) collective-permute-start(bf16[4,512,128]{2,1,0:T(8,128)(2,1)} %get-tuple-element.50), channel_id=1, source_target_pairs={{4,0},{8,4},{12,8},{16,12},{20,16},{24,20},{28,24},{5,1},{9,5},{13... | collective-permute-start | bytes 1572872 | tf_op jit(solution)/shard_map/ppermute | solution.py:487
  79.9 0.0 collective-permute-done.5.refs_0_
  79.9 1.5 collective-permute-start.9
  81.4 2.9 %shard_map.52 = bf16[4,528,128]{2,1,0:T(8,128)(2,1)S(1)} custom-call(s32[1]{0:T(128)} %bitcast.here_ref, s32[8,2,16]{2,1,0:T(2,128)} %bitcast.2.picks_ref, bf16[512,2048]{1,0:T(8,128)(2,1)S(1)} %bitcast.11, bf16[512,2048]{1,0:T(8,128)(2,1)S(1)} %bitcast.18, bf16[4,512,128]{2,1,0:T(8,128)(2,1)} %collective-permute-done.5.refs_0_), custom_call_target="tpu_custom_call" | custom-call | flops 999999995904 | bytes 2097152 | tf_op jit(solution)/shard_map/pallas_call | solution.py:226
  84.3 0.0 collective-permute-done.6.refs_0_
  84.3 1.5 collective-permute-start.11
  85.8 2.9 %shard_map.53 = bf16[4,528,128]{2,1,0:T(8,128)(2,1)S(1)} custom-call(s32[1]{0:T(128)} %bitcast.here_ref, s32[8,2,16]{2,1,0:T(2,128)} %bitcast.2.picks_ref, bf16[512,2048]{1,0:T(8,128)(2,1)S(1)} %bitcast.12, bf16[512,2048]{1,0:T(8,128)(2,1)S(1)} %bitcast.19, bf16[4,512,128]{2,1,0:T(8,128)(2,1)} %collective-permute-done.6.refs_0_), custom_call_target="tpu_custom_call" | custom-call | flops 536870912 | bytes 2097152 | tf_op jit(solution)/shard_map/pallas_call | solution.py:226
  88.7 0.0 collective-permute-done.7.refs_1_
  88.7 1.3 collective-permute-start.12
  90.0 7.3 %collective-permute-done.8.refs_0_ = bf16[4,512,128]{2,1,0:T(8,128)(2,1)} collective-permute-done((bf16[4,512,128]{2,1,0:T(8,128)(2,1)}, bf16[4,512,128]{2,1,0:T(8,128)(2,1)}, u32[]{:S(2)}, u32[]{:S(2)}) %collective-permute-start.8) | collective-permute-done | bytes 524320 | tf_op jit(solution)/shard_map/ppermute | solution.py:487
  97.3 2.9 %shard_map.54 = bf16[4,528,128]{2,1,0:T(8,128)(2,1)S(1)} custom-call(s32[1]{0:T(128)} %bitcast.here_ref, s32[8,2,16]{2,1,0:T(2,128)} %bitcast.2.picks_ref, bf16[512,2048]{1,0:T(8,128)(2,1)S(1)} %bitcast.13, bf16[512,2048]{1,0:T(8,128)(2,1)S(1)} %bitcast.20, bf16[4,512,128]{2,1,0:T(8,128)(2,1)} %collective-permute-done.8.refs_0_), custom_call_target="tpu_custom_call" | custom-call | flops 536870912 | bytes 2097152 | tf_op jit(solution)/shard_map/pallas_call | solution.py:226
  100.2 0.0 collective-permute-done.9.refs_0_
  100.2 2.9 %shard_map.55 = bf16[4,528,128]{2,1,0:T(8,128)(2,1)S(1)} custom-call(s32[1]{0:T(128)} %bitcast.here_ref, s32[8,2,16]{2,1,0:T(2,128)} %bitcast.2.picks_ref, bf16[512,2048]{1,0:T(8,128)(2,1)S(1)} %bitcast.14, bf16[512,2048]{1,0:T(8,128)(2,1)S(1)} %bitcast.21, bf16[4,512,128]{2,1,0:T(8,128)(2,1)} %collective-permute-done.9.refs_0_), custom_call_target="tpu_custom_call" | custom-call | flops 536870912 | bytes 2097152 | tf_op jit(solution)/shard_map/pallas_call | solution.py:226
  103.2 0.7 collective-permute-start.14
  103.9 6.2 %collective-permute-start.13 = (bf16[4,528,128]{2,1,0:T(8,128)(2,1)S(1)}, bf16[4,528,128]{2,1,0:T(8,128)(2,1)S(1)}, u32[]{:S(2)}, u32[]{:S(2)}) collective-permute-start(bf16[4,528,128]{2,1,0:T(8,128)(2,1)S(1)} %shard_map.54), channel_id=1, source_target_pairs={{0,5},{1,6},{2,7},{3,4},{4,9},{5,10},{6,11},{7,8},{8,13},{9,14},{1... | collective-permute-start | bytes 1622024 | tf_op jit(solution)/shard_map/ppermute | solution.py:495
  110.1 0.0 collective-permute-done.10.refs_2_
  110.1 7.1 %shard_map.56 = (bf16[512,2048]{1,0:T(8,128)(2,1)}, f32[16,512,128]{2,1,0:T(8,128)S(1)}, f32[16,4,128]{2,1,0:T(4,128)S(1)}) custom-call(s32[1]{0:T(128)} %bitcast.here_ref, s32[8,2,16]{2,1,0:T(2,128)S(1)} %collective-permute-done.picks_ref, bf16[16,528,128]{2,1,0:T(8,128)(2,1)} %collective-permute-done.3.refs_0_, ...), custom_call_target="tpu_custom_call" | custom-call | flops 6291456 | bytes 7864320 | tf_op jit(solution)/shard_map/pallas_call | solution.py:367
  117.2 3.0 %collective-permute-done.12.refs_1_ = bf16[4,528,128]{2,1,0:T(8,128)(2,1)S(1)} collective-permute-done((bf16[4,528,128]{2,1,0:T(8,128)(2,1)S(1)}, bf16[4,528,128]{2,1,0:T(8,128)(2,1)S(1)}, u32[]{:S(2)}, u32[]{:S(2)}) %collective-permute-start.12) | collective-permute-done | bytes 540704 | tf_op jit(solution)/shard_map/ppermute | solution.py:495
  120.2 7.3 %collective-permute-done.11.refs_0_ = bf16[4,528,128]{2,1,0:T(8,128)(2,1)S(1)} collective-permute-done((bf16[4,528,128]{2,1,0:T(8,128)(2,1)S(1)}, bf16[4,528,128]{2,1,0:T(8,128)(2,1)S(1)}, u32[]{:S(2)}, u32[]{:S(2)}) %collective-permute-start.11) | collective-permute-done | bytes 540704 | tf_op jit(solution)/shard_map/ppermute | solution.py:495
  127.5 0.0 collective-permute-done.14.refs_3_
  127.5 15.1 %collective-permute-done.13.refs_2_ = bf16[4,528,128]{2,1,0:T(8,128)(2,1)S(1)} collective-permute-done((bf16[4,528,128]{2,1,0:T(8,128)(2,1)S(1)}, bf16[4,528,128]{2,1,0:T(8,128)(2,1)S(1)}, u32[]{:S(2)}, u32[]{:S(2)}) %collective-permute-start.13) | collective-permute-done | bytes 540704 | tf_op jit(solution)/shard_map/ppermute | solution.py:495
  142.6 6.0 %shard_map.57 = bf16[512,2048]{1,0:T(8,128)(2,1)} custom-call(s32[1]{0:T(128)} %bitcast.here_ref, s32[8,2,16]{2,1,0:T(2,128)S(1)} %collective-permute-done.picks_ref, f32[16,512,128]{2,1,0:T(8,128)S(1)} %get-tuple-element.54.mixed_ref, f32[16,4,128]{2,1,0:T(4,128)S(1)} %get-tuple-element.55.sums_ref, ...), custom_call_target="tpu_custom_call", output_to_operand_aliasing={{}: (8, {})} | custom-call | flops 2097152 | bytes 8388608 | tf_op jit(solution)/shard_map/pallas_call | solution.py:448
  (8 shorter events, 0.0 us)
Async XLA Ops:
  0.0 1.6 %copy-start = (bf16[1,512,2048]{2,1,0:T(8,128)(2,1)S(1)}, bf16[1,512,2048]{2,1,0:T(8,128)(2,1)}, u32[]{:S(2)}) copy-start(bf16[1,512,2048]{2,1,0:T(8,128)(2,1)} %param.5) | copy-start | bytes 6291460
  1.6 1.6 %copy-start.2 = (bf16[1,512,2048]{2,1,0:T(8,128)(2,1)S(1)}, bf16[1,512,2048]{2,1,0:T(8,128)(2,1)}, u32[]{:S(2)}) copy-start(bf16[1,512,2048]{2,1,0:T(8,128)(2,1)} %param.6) | copy-start | bytes 6291460
  3.2 4.2 %copy-start.4 = (bf16[1,512,2048]{2,1,0:T(8,128)(2,1)S(1)}, bf16[1,512,2048]{2,1,0:T(8,128)(2,1)}, u32[]{:S(2)}) copy-start(bf16[1,512,2048]{2,1,0:T(8,128)(2,1)} %param.4) | copy-start | bytes 6291460
  6.0 49.3 %collective-permute-start.1 = (bf16[8,512,128]{2,1,0:T(8,128)(2,1)S(1)}, bf16[8,512,128]{2,1,0:T(8,128)(2,1)S(1)}, u32[]{:S(2)}, u32[]{:S(2)}) collective-permute-start(bf16[8,512,128]{2,1,0:T(8,128)(2,1)S(1)} %get-tuple-element.31), channel_id=1, source_target_pairs={{0,8},{4,12},{8,16},{12,20},{16,24},{20,28},{1,9},{5,13},{9,17},{1... | collective-permute-start | bytes 3145736 | tf_op jit(solution)/shard_map/ppermute | solution.py:484
  7.4 10.5 %copy-start.1 = (bf16[1,512,2048]{2,1,0:T(8,128)(2,1)S(1)}, bf16[1,512,2048]{2,1,0:T(8,128)(2,1)}, u32[]{:S(2)}) copy-start(bf16[1,512,2048]{2,1,0:T(8,128)(2,1)} %param.5) | copy-start | bytes 6291460
  7.4 10.5 %copy-start.3 = (bf16[1,512,2048]{2,1,0:T(8,128)(2,1)S(1)}, bf16[1,512,2048]{2,1,0:T(8,128)(2,1)}, u32[]{:S(2)}) copy-start(bf16[1,512,2048]{2,1,0:T(8,128)(2,1)} %param.6) | copy-start | bytes 6291460
  8.6 18.9 %collective-permute-start.2 = (bf16[4,512,128]{2,1,0:T(8,128)(2,1)S(1)}, bf16[4,512,128]{2,1,0:T(8,128)(2,1)S(1)}, u32[]{:S(2)}, u32[]{:S(2)}) collective-permute-start(bf16[4,512,128]{2,1,0:T(8,128)(2,1)S(1)} %shard_map.47), channel_id=1, source_target_pairs={{16,0},{20,4},{24,8},{28,12},{17,1},{21,5},{25,9},{29,13},{18,2},{... | collective-permute-start | bytes 1572872 | tf_op jit(solution)/shard_map/ppermute | solution.py:487
  13.1 4.8 %collective-permute-start = (s32[8,2,16]{2,1,0:T(2,128)}, s32[8,2,16]{2,1,0:T(2,128)S(1)}, u32[]{:S(2)}, u32[]{:S(2)}) collective-permute-start(s32[8,2,16]{2,1,0:T(2,128)} %bitcast.2.picks_ref), channel_id=1, source_target_pairs={{0,1},{1,2},{2,3},{3,0},{4,5},{5,6},{6,7},{7,4},{8,9},{9,10},{10,1... | collective-permute-start | bytes 3080 | tf_op jit(solution)/shard_map/ppermute | solution.py:24
  16.6 48.8 %collective-permute-start.4 = (bf16[8,512,128]{2,1,0:T(8,128)(2,1)}, bf16[8,512,128]{2,1,0:T(8,128)(2,1)}, u32[]{:S(2)}, u32[]{:S(2)}) collective-permute-start(bf16[8,512,128]{2,1,0:T(8,128)(2,1)} %get-tuple-element.44), channel_id=1, source_target_pairs={{0,24},{4,28},{1,25},{5,29},{2,26},{6,30},{3,27},{7,31}} | collective-permute-start | bytes 3145736 | tf_op jit(solution)/shard_map/ppermute | solution.py:484
  26.9 38.5 %collective-permute-start.3 = (bf16[16,528,128]{2,1,0:T(8,128)(2,1)}, bf16[16,528,128]{2,1,0:T(8,128)(2,1)}, u32[]{:S(2)}, u32[]{:S(2)}) collective-permute-start(bf16[16,528,128]{2,1,0:T(8,128)(2,1)} %shard_map.49), channel_id=1, source_target_pairs={{0,1},{1,2},{2,3},{3,0},{4,5},{5,6},{6,7},{7,4},{8,9},{9,10},{10,1... | collective-permute-start | bytes 6488072 | tf_op jit(solution)/shard_map/ppermute | solution.py:24
  55.3 1.0 copy-start.5
  56.3 23.6 %collective-permute-start.5 = (bf16[4,512,128]{2,1,0:T(8,128)(2,1)}, bf16[4,512,128]{2,1,0:T(8,128)(2,1)}, u32[]{:S(2)}, u32[]{:S(2)}) collective-permute-start(bf16[4,512,128]{2,1,0:T(8,128)(2,1)} %get-tuple-element.46), channel_id=1, source_target_pairs={{12,0},{16,4},{20,8},{24,12},{28,16},{13,1},{17,5},{21,9},{25,13},... | collective-permute-start | bytes 1572872 | tf_op jit(solution)/shard_map/ppermute | solution.py:487
  58.4 25.9 %collective-permute-start.6 = (bf16[4,512,128]{2,1,0:T(8,128)(2,1)}, bf16[4,512,128]{2,1,0:T(8,128)(2,1)}, u32[]{:S(2)}, u32[]{:S(2)}) collective-permute-start(bf16[4,512,128]{2,1,0:T(8,128)(2,1)} %get-tuple-element.48), channel_id=1, source_target_pairs={{20,0},{24,4},{28,8},{21,1},{25,5},{29,9},{22,2},{26,6},{30,10},{2... | collective-permute-start | bytes 1572872 | tf_op jit(solution)/shard_map/ppermute | solution.py:487
  60.5 4.9 %copy-start.6 = (bf16[8,512,128]{2,1,0:T(8,128)(2,1)S(1)}, bf16[8,512,128]{2,1,0:T(8,128)(2,1)}, u32[]{:S(2)}) copy-start(bf16[8,512,128]{2,1,0:T(8,128)(2,1)} %copy-done.5) | copy-start | bytes 3145732
  64.1 46.0 %collective-permute-start.10 = (bf16[4,528,128]{2,1,0:T(8,128)(2,1)}, bf16[4,528,128]{2,1,0:T(8,128)(2,1)}, u32[]{:S(2)}, u32[]{:S(2)}) collective-permute-start(bf16[4,528,128]{2,1,0:T(8,128)(2,1)} %shard_map.50), channel_id=1, source_target_pairs={{0,17},{1,18},{2,19},{3,16},{4,21},{5,22},{6,23},{7,20},{8,25},{9,... | collective-permute-start | bytes 1622024 | tf_op jit(solution)/shard_map/ppermute | solution.py:495
  70.8 17.9 %collective-permute-start.7 = (bf16[8,528,128]{2,1,0:T(8,128)(2,1)}, bf16[8,528,128]{2,1,0:T(8,128)(2,1)}, u32[]{:S(2)}, u32[]{:S(2)}) collective-permute-start(bf16[8,528,128]{2,1,0:T(8,128)(2,1)} %shard_map.51), channel_id=1, source_target_pairs={{0,1},{1,2},{2,3},{3,0},{4,5},{5,6},{6,7},{7,4},{8,9},{9,10},{10,1... | collective-permute-start | bytes 3244040 | tf_op jit(solution)/shard_map/ppermute | solution.py:24
  70.8 26.5 %collective-permute-start.8 = (bf16[4,512,128]{2,1,0:T(8,128)(2,1)}, bf16[4,512,128]{2,1,0:T(8,128)(2,1)}, u32[]{:S(2)}, u32[]{:S(2)}) collective-permute-start(bf16[4,512,128]{2,1,0:T(8,128)(2,1)} %get-tuple-element.50), channel_id=1, source_target_pairs={{4,0},{8,4},{12,8},{16,12},{20,16},{24,20},{28,24},{5,1},{9,5},{13... | collective-permute-start | bytes 1572872 | tf_op jit(solution)/shard_map/ppermute | solution.py:487
  79.9 20.3 %collective-permute-start.9 = (bf16[4,512,128]{2,1,0:T(8,128)(2,1)}, bf16[4,512,128]{2,1,0:T(8,128)(2,1)}, u32[]{:S(2)}, u32[]{:S(2)}) collective-permute-start(bf16[4,512,128]{2,1,0:T(8,128)(2,1)} %get-tuple-element.52), channel_id=1, source_target_pairs={{28,0},{29,1},{30,2},{31,3}} | collective-permute-start | bytes 1572872 | tf_op jit(solution)/shard_map/ppermute | solution.py:487
  84.3 43.2 %collective-permute-start.11 = (bf16[4,528,128]{2,1,0:T(8,128)(2,1)S(1)}, bf16[4,528,128]{2,1,0:T(8,128)(2,1)S(1)}, u32[]{:S(2)}, u32[]{:S(2)}) collective-permute-start(bf16[4,528,128]{2,1,0:T(8,128)(2,1)S(1)} %shard_map.52), channel_id=1, source_target_pairs={{0,13},{1,14},{2,15},{3,12},{4,17},{5,18},{6,19},{7,16},{8,21},{9,... | collective-permute-start | bytes 1622024 | tf_op jit(solution)/shard_map/ppermute | solution.py:495
  88.7 31.5 %collective-permute-start.12 = (bf16[4,528,128]{2,1,0:T(8,128)(2,1)S(1)}, bf16[4,528,128]{2,1,0:T(8,128)(2,1)S(1)}, u32[]{:S(2)}, u32[]{:S(2)}) collective-permute-start(bf16[4,528,128]{2,1,0:T(8,128)(2,1)S(1)} %shard_map.53), channel_id=1, source_target_pairs={{0,21},{1,22},{2,23},{3,20},{4,25},{5,26},{6,27},{7,24},{8,29},{9,... | collective-permute-start | bytes 1622024 | tf_op jit(solution)/shard_map/ppermute | solution.py:495
  103.2 24.3 %collective-permute-start.14 = (bf16[4,528,128]{2,1,0:T(8,128)(2,1)S(1)}, bf16[4,528,128]{2,1,0:T(8,128)(2,1)S(1)}, u32[]{:S(2)}, u32[]{:S(2)}) collective-permute-start(bf16[4,528,128]{2,1,0:T(8,128)(2,1)S(1)} %shard_map.55), channel_id=1, source_target_pairs={{0,29},{1,30},{2,31},{3,28}} | collective-permute-start | bytes 1622024 | tf_op jit(solution)/shard_map/ppermute | solution.py:495
  103.9 38.7 %collective-permute-start.13 = (bf16[4,528,128]{2,1,0:T(8,128)(2,1)S(1)}, bf16[4,528,128]{2,1,0:T(8,128)(2,1)S(1)}, u32[]{:S(2)}, u32[]{:S(2)}) collective-permute-start(bf16[4,528,128]{2,1,0:T(8,128)(2,1)S(1)} %shard_map.54), channel_id=1, source_target_pairs={{0,5},{1,6},{2,7},{3,4},{4,9},{5,10},{6,11},{7,8},{8,13},{9,14},{1... | collective-permute-start | bytes 1622024 | tf_op jit(solution)/shard_map/ppermute | solution.py:495

commit v16 on v15

--- a/solution.py
+++ b/solution.py
@@ -518,7 +518,7 @@
     ask_for(four, near_sends[0])
     own = own_part(after(now, before), queries, keys, values)
     own_back = passed_along(own, "pipe", 1)
-    near.append(up(after(near_sends[1], now), near_shifts[1]))
+    near.append(up(after(near_sends[1], own), near_shifts[1]))
     ask_for(three, arrived[four], near[0], own)
     ask_for(five, arrived[four], near[0], own)
     part_four = work(after(here, own, near[0]), four, is_anchor=True)

time: 151 us -> 145 us (0.960)
  starting transfers between devices: 33.5 us -> 22 us
  waiting for transfers between devices: 60.5 us -> 66.6 us
    ppermute x3, waiting for transfers between devices: 0.01 us -> 12.9 us  [passed_along(): return lax.ppermute(value, axis, pairs)]
    ppermute x5, waiting for transfers between devices: 7.31 us -> 0.01 us  [down(): lax.ppermute(value, 'ctx', [(at, at - shift) for at in range(shift, width)])]
    ppermute x5, starting transfers between devices: 19.2 us -> 12 us  [down(): lax.ppermute(value, 'ctx', [(at, at - shift) for at in range(shift, width)])]
    ppermute x5, starting transfers between devices: 11 us -> 6.65 us  [up_and_on(): return lax.ppermute(value, ('ctx', 'pipe'), pairs)]
  transfers between devices with their start and end apart: 15 -> 15, of which waited for: 5 -> 5; matrix products, arithmetic and copies ran while one was open for 0% -> 0% of each run, Pallas kernels for 28% -> 29%
where the time goes in v16:
time: 145 us; the launch traced here: 142 us
  waiting for transfers between devices  66.6 us (46%)
  Pallas kernels  49.2 us (34%)
  starting transfers between devices  22 us (15%)
  local copies, waits for them, and re-layouts  4.19 us (3%)
    ppermute x2, waiting for transfers between devices, up(): lax.ppermute(value, 'ctx', [(at, at + shift) for at in range(width - shif...  27 us
    ppermute x5, waiting for transfers between devices, up_and_on(): return lax.ppermute(value, ('ctx', 'pipe'), pairs)  26.8 us
    pallas_call x5, Pallas kernels, attend(): call(functools.partial(attend_kernel, group=group, slots=slots), [SCALARS...  15.3 us
    ppermute x3, waiting for transfers between devices, passed_along(): return lax.ppermute(value, axis, pairs)  12.9 us
    ppermute x5, starting transfers between devices, down(): lax.ppermute(value, 'ctx', [(at, at - shift) for at in range(shift, width)])  12 us
    pallas_call x1, Pallas kernels, own_part(): call(own_kernel, [SCALARS, IN_VMEM, IN_VMEM, IN_VMEM], jax.ShapeDtypeStru...  8.94 us
    pallas_call x3, Pallas kernels, pack(): call(functools.partial(pack_kernel, jobs=jobs, slots=slots), [SCALARS, SC...  7.5 us
    pallas_call x1, Pallas kernels, merge(): call(functools.partial(merge_kernel, places=tuple(places), shifts=shifts,...  7.1 us
  transfers between devices with their start and end apart: 15, of which 5 were waited for; matrix products, arithmetic and copies ran while one was open for 0% of the time, Pallas kernels for 29%

profile of v16, /device:TPU:26, one launch (start us, length us, event | category | flops | bytes accessed | tf_op | source)
XLA Modules:
  0.0 142.4 jit_solution(18011490085981432696)
XLA Ops:
  0.0 1.6 %copy-done = bf16[1,512,2048]{2,1,0:T(8,128)(2,1)S(1)} copy-done((bf16[1,512,2048]{2,1,0:T(8,128)(2,1)S(1)}, bf16[1,512,2048]{2,1,0:T(8,128)(2,1)}, u32[]{:S(2)}) %copy-start) | copy-done | bytes 2097176
  1.6 1.6 %copy-done.2 = bf16[1,512,2048]{2,1,0:T(8,128)(2,1)S(1)} copy-done((bf16[1,512,2048]{2,1,0:T(8,128)(2,1)S(1)}, bf16[1,512,2048]{2,1,0:T(8,128)(2,1)}, u32[]{:S(2)}) %copy-start.2) | copy-done | bytes 2097176
  3.2 2.9 %shard_map.46 = (bf16[8,512,128]{2,1,0:T(8,128)(2,1)S(1)}, bf16[8,512,128]{2,1,0:T(8,128)(2,1)}) custom-call(s32[1]{0:T(128)} %bitcast.here_ref, s32[8,2,16]{2,1,0:T(2,128)} %bitcast.2.picks_ref, bf16[512,2048]{1,0:T(8,128)(2,1)S(1)} %bitcast.8, bf16[512,2048]{1,0:T(8,128)(2,1)S(1)} %bitcast.15), custom_call_target="tpu_custom_call" | custom-call | bytes 4194304 | tf_op jit(solution)/shard_map/pallas_call | solution.py:127
  6.0 1.3 collective-permute-start.1
  7.4 0.0 copy-start.1
  7.4 0.0 copy-start.3
  7.4 1.2 shard_map.47
  8.6 4.5 %collective-permute-start.2 = (bf16[4,512,128]{2,1,0:T(8,128)(2,1)S(1)}, bf16[4,512,128]{2,1,0:T(8,128)(2,1)S(1)}, u32[]{:S(2)}, u32[]{:S(2)}) collective-permute-start(bf16[4,512,128]{2,1,0:T(8,128)(2,1)S(1)} %shard_map.47), channel_id=1, source_target_pairs={{16,0},{20,4},{24,8},{28,12},{17,1},{21,5},{25,9},{29,13},{18,2},{... | collective-permute-start | bytes 1572872 | tf_op jit(solution)/shard_map/ppermute | solution.py:487
  13.1 0.1 collective-permute-start
  13.2 3.4 %shard_map.48 = (bf16[4,512,128]{2,1,0:T(8,128)(2,1)}, bf16[4,512,128]{2,1,0:T(8,128)(2,1)}, bf16[4,512,128]{2,1,0:T(8,128)(2,1)}, bf16[4,512,128]{2,1,0:T(8,128)(2,1)}) custom-call(s32[1]{0:T(128)} %bitcast.here_ref, s32[8,2,16]{2,1,0:T(2,128)} %bitcast.2.picks_ref, bf16[512,2048]{1,0:T(8,128)(2,1)S(1)} %bitcast.23), custom_call_target="tpu_custom_call" | custom-call | bytes 4194304 | tf_op jit(solution)/shard_map/pallas_call | solution.py:127
  16.6 0.0 collective-permute-done.picks_ref
  16.6 0.0 copy-done.1
  16.6 8.9 %shard_map.49 = bf16[16,528,128]{2,1,0:T(8,128)(2,1)} custom-call(s32[1]{0:T(128)} %bitcast.here_ref, bf16[512,2048]{1,0:T(8,128)(2,1)S(1)} %bitcast.24, bf16[512,2048]{1,0:T(8,128)(2,1)S(1)} %bitcast.9, bf16[512,2048]{1,0:T(8,128)(2,1)S(1)} %bitcast.16), custom_call_target="tpu_custom_call" | custom-call | flops 2147483648 | bytes 8388608 | tf_op jit(solution)/shard_map/pallas_call | solution.py:266
  25.6 0.7 collective-permute-start.3
  26.2 1.3 collective-permute-start.4
  27.5 0.0 collective-permute-done.2.refs_0_
  27.5 27.0 %collective-permute-done.1.refs_0_ = bf16[8,512,128]{2,1,0:T(8,128)(2,1)S(1)} collective-permute-done((bf16[8,512,128]{2,1,0:T(8,128)(2,1)S(1)}, bf16[8,512,128]{2,1,0:T(8,128)(2,1)S(1)}, u32[]{:S(2)}, u32[]{:S(2)}) %collective-permute-start.1) | collective-permute-done | bytes 1048608 | tf_op jit(solution)/shard_map/ppermute | solution.py:484
  54.5 1.0 copy-done.5
  55.5 2.1 %collective-permute-start.5 = (bf16[4,512,128]{2,1,0:T(8,128)(2,1)}, bf16[4,512,128]{2,1,0:T(8,128)(2,1)}, u32[]{:S(2)}, u32[]{:S(2)}) collective-permute-start(bf16[4,512,128]{2,1,0:T(8,128)(2,1)} %get-tuple-element.46), channel_id=1, source_target_pairs={{12,0},{16,4},{20,8},{24,12},{28,16},{13,1},{17,5},{21,9},{25,13},... | collective-permute-start | bytes 1572872 | tf_op jit(solution)/shard_map/ppermute | solution.py:487
  57.6 2.1 %collective-permute-start.6 = (bf16[4,512,128]{2,1,0:T(8,128)(2,1)}, bf16[4,512,128]{2,1,0:T(8,128)(2,1)}, u32[]{:S(2)}, u32[]{:S(2)}) collective-permute-start(bf16[4,512,128]{2,1,0:T(8,128)(2,1)} %get-tuple-element.48), channel_id=1, source_target_pairs={{20,0},{24,4},{28,8},{21,1},{25,5},{29,9},{22,2},{26,6},{30,10},{2... | collective-permute-start | bytes 1572872 | tf_op jit(solution)/shard_map/ppermute | solution.py:487
  59.7 3.6 %shard_map.50 = bf16[4,528,128]{2,1,0:T(8,128)(2,1)} custom-call(s32[1]{0:T(128)} %bitcast.here_ref, s32[8,2,16]{2,1,0:T(2,128)} %bitcast.2.picks_ref, bf16[512,2048]{1,0:T(8,128)(2,1)S(1)} %bitcast.10, bf16[512,2048]{1,0:T(8,128)(2,1)S(1)} %bitcast.17, bf16[4,512,128]{2,1,0:T(8,128)(2,1)S(1)} %collective-permute-done.2.refs_0_), custom_call_target="tpu_custom_call" | custom-call | flops 999999995904 | bytes 2097152 | tf_op jit(solution)/shard_map/pallas_call | solution.py:226
  63.3 1.3 collective-permute-start.10
  64.6 0.0 collective-permute-done.3.refs_0_
  64.6 0.0 collective-permute-done.4.refs_1_
  64.6 5.4 %shard_map.51 = bf16[8,528,128]{2,1,0:T(8,128)(2,1)} custom-call(s32[1]{0:T(128)} %bitcast.here_ref, s32[8,2,16]{2,1,0:T(2,128)} %bitcast.2.picks_ref, bf16[512,2048]{1,0:T(8,128)(2,1)S(1)} %bitcast.25, bf16[8,512,128]{2,1,0:T(8,128)(2,1)S(1)} %copy-done.6, bf16[8,512,128]{2,1,0:T(8,128)(2,1)} %collective-permute-done.4.refs_1_), custom_call_target="tpu_custom_call" | custom-call | flops 1073741824 | bytes 6291456 | tf_op jit(solution)/shard_map/pallas_call | solution.py:295
  70.0 0.0 collective-permute-start.7
  70.0 1.9 %collective-permute-start.8 = (bf16[4,512,128]{2,1,0:T(8,128)(2,1)}, bf16[4,512,128]{2,1,0:T(8,128)(2,1)}, u32[]{:S(2)}, u32[]{:S(2)}) collective-permute-start(bf16[4,512,128]{2,1,0:T(8,128)(2,1)} %get-tuple-element.50), channel_id=1, source_target_pairs={{4,0},{8,4},{12,8},{16,12},{20,16},{24,20},{28,24},{5,1},{9,5},{13... | collective-permute-start | bytes 1572872 | tf_op jit(solution)/shard_map/ppermute | solution.py:487
  71.9 0.0 collective-permute-done.5.refs_0_
  71.9 1.5 %collective-permute-start.9 = (bf16[4,512,128]{2,1,0:T(8,128)(2,1)}, bf16[4,512,128]{2,1,0:T(8,128)(2,1)}, u32[]{:S(2)}, u32[]{:S(2)}) collective-permute-start(bf16[4,512,128]{2,1,0:T(8,128)(2,1)} %get-tuple-element.52), channel_id=1, source_target_pairs={{28,0},{29,1},{30,2},{31,3}} | collective-permute-start | bytes 1572872 | tf_op jit(solution)/shard_map/ppermute | solution.py:487
  73.4 2.9 %shard_map.52 = bf16[4,528,128]{2,1,0:T(8,128)(2,1)S(1)} custom-call(s32[1]{0:T(128)} %bitcast.here_ref, s32[8,2,16]{2,1,0:T(2,128)} %bitcast.2.picks_ref, bf16[512,2048]{1,0:T(8,128)(2,1)S(1)} %bitcast.11, bf16[512,2048]{1,0:T(8,128)(2,1)S(1)} %bitcast.18, bf16[4,512,128]{2,1,0:T(8,128)(2,1)} %collective-permute-done.5.refs_0_), custom_call_target="tpu_custom_call" | custom-call | flops 999999995904 | bytes 2097152 | tf_op jit(solution)/shard_map/pallas_call | solution.py:226
  76.3 0.0 collective-permute-done.6.refs_0_
  76.3 1.5 %collective-permute-start.11 = (bf16[4,528,128]{2,1,0:T(8,128)(2,1)S(1)}, bf16[4,528,128]{2,1,0:T(8,128)(2,1)S(1)}, u32[]{:S(2)}, u32[]{:S(2)}) collective-permute-start(bf16[4,528,128]{2,1,0:T(8,128)(2,1)S(1)} %shard_map.52), channel_id=1, source_target_pairs={{0,13},{1,14},{2,15},{3,12},{4,17},{5,18},{6,19},{7,16},{8,21},{9,... | collective-permute-start | bytes 1622024 | tf_op jit(solution)/shard_map/ppermute | solution.py:495
  77.8 2.9 %shard_map.53 = bf16[4,528,128]{2,1,0:T(8,128)(2,1)S(1)} custom-call(s32[1]{0:T(128)} %bitcast.here_ref, s32[8,2,16]{2,1,0:T(2,128)} %bitcast.2.picks_ref, bf16[512,2048]{1,0:T(8,128)(2,1)S(1)} %bitcast.12, bf16[512,2048]{1,0:T(8,128)(2,1)S(1)} %bitcast.19, bf16[4,512,128]{2,1,0:T(8,128)(2,1)} %collective-permute-done.6.refs_0_), custom_call_target="tpu_custom_call" | custom-call | flops 536870912 | bytes 2097152 | tf_op jit(solution)/shard_map/pallas_call | solution.py:226
  80.7 12.8 %collective-permute-done.7.refs_1_ = bf16[8,528,128]{2,1,0:T(8,128)(2,1)} collective-permute-done((bf16[8,528,128]{2,1,0:T(8,128)(2,1)}, bf16[8,528,128]{2,1,0:T(8,128)(2,1)}, u32[]{:S(2)}, u32[]{:S(2)}) %collective-permute-start.7) | collective-permute-done | bytes 1081376 | tf_op jit(solution)/shard_map/ppermute | solution.py:24
  93.6 1.3 collective-permute-start.12
  94.8 0.0 collective-permute-done.8.refs_0_
  94.9 2.9 %shard_map.54 = bf16[4,528,128]{2,1,0:T(8,128)(2,1)S(1)} custom-call(s32[1]{0:T(128)} %bitcast.here_ref, s32[8,2,16]{2,1,0:T(2,128)} %bitcast.2.picks_ref, bf16[512,2048]{1,0:T(8,128)(2,1)S(1)} %bitcast.13, bf16[512,2048]{1,0:T(8,128)(2,1)S(1)} %bitcast.20, bf16[4,512,128]{2,1,0:T(8,128)(2,1)} %collective-permute-done.8.refs_0_), custom_call_target="tpu_custom_call" | custom-call | flops 536870912 | bytes 2097152 | tf_op jit(solution)/shard_map/pallas_call | solution.py:226
  97.8 0.0 collective-permute-done.9.refs_0_
  97.8 2.9 %shard_map.55 = bf16[4,528,128]{2,1,0:T(8,128)(2,1)S(1)} custom-call(s32[1]{0:T(128)} %bitcast.here_ref, s32[8,2,16]{2,1,0:T(2,128)} %bitcast.2.picks_ref, bf16[512,2048]{1,0:T(8,128)(2,1)S(1)} %bitcast.14, bf16[512,2048]{1,0:T(8,128)(2,1)S(1)} %bitcast.21, bf16[4,512,128]{2,1,0:T(8,128)(2,1)} %collective-permute-done.9.refs_0_), custom_call_target="tpu_custom_call" | custom-call | flops 536870912 | bytes 2097152 | tf_op jit(solution)/shard_map/pallas_call | solution.py:226
  100.7 0.7 collective-permute-start.14
  101.4 1.9 %collective-permute-start.13 = (bf16[4,528,128]{2,1,0:T(8,128)(2,1)S(1)}, bf16[4,528,128]{2,1,0:T(8,128)(2,1)S(1)}, u32[]{:S(2)}, u32[]{:S(2)}) collective-permute-start(bf16[4,528,128]{2,1,0:T(8,128)(2,1)S(1)} %shard_map.54), channel_id=1, source_target_pairs={{0,5},{1,6},{2,7},{3,4},{4,9},{5,10},{6,11},{7,8},{8,13},{9,14},{1... | collective-permute-start | bytes 1622024 | tf_op jit(solution)/shard_map/ppermute | solution.py:495
  103.4 0.0 collective-permute-done.10.refs_2_
  103.4 7.1 %shard_map.56 = (bf16[512,2048]{1,0:T(8,128)(2,1)}, f32[16,512,128]{2,1,0:T(8,128)S(1)}, f32[16,4,128]{2,1,0:T(4,128)S(1)}) custom-call(s32[1]{0:T(128)} %bitcast.here_ref, s32[8,2,16]{2,1,0:T(2,128)S(1)} %collective-permute-done.picks_ref, bf16[16,528,128]{2,1,0:T(8,128)(2,1)} %collective-permute-done.3.refs_0_, ...), custom_call_target="tpu_custom_call" | custom-call | flops 6291456 | bytes 7864320 | tf_op jit(solution)/shard_map/pallas_call | solution.py:367
  110.5 3.5 %collective-permute-done.12.refs_1_ = bf16[4,528,128]{2,1,0:T(8,128)(2,1)S(1)} collective-permute-done((bf16[4,528,128]{2,1,0:T(8,128)(2,1)S(1)}, bf16[4,528,128]{2,1,0:T(8,128)(2,1)S(1)}, u32[]{:S(2)}, u32[]{:S(2)}) %collective-permute-start.12) | collective-permute-done | bytes 540704 | tf_op jit(solution)/shard_map/ppermute | solution.py:495
  114.0 3.3 %collective-permute-done.11.refs_0_ = bf16[4,528,128]{2,1,0:T(8,128)(2,1)S(1)} collective-permute-done((bf16[4,528,128]{2,1,0:T(8,128)(2,1)S(1)}, bf16[4,528,128]{2,1,0:T(8,128)(2,1)S(1)}, u32[]{:S(2)}, u32[]{:S(2)}) %collective-permute-start.11) | collective-permute-done | bytes 540704 | tf_op jit(solution)/shard_map/ppermute | solution.py:495
  117.4 0.0 collective-permute-done.14.refs_3_
  117.4 19.9 %collective-permute-done.13.refs_2_ = bf16[4,528,128]{2,1,0:T(8,128)(2,1)S(1)} collective-permute-done((bf16[4,528,128]{2,1,0:T(8,128)(2,1)S(1)}, bf16[4,528,128]{2,1,0:T(8,128)(2,1)S(1)}, u32[]{:S(2)}, u32[]{:S(2)}) %collective-permute-start.13) | collective-permute-done | bytes 540704 | tf_op jit(solution)/shard_map/ppermute | solution.py:495
  137.3 5.0 %shard_map.57 = bf16[512,2048]{1,0:T(8,128)(2,1)} custom-call(s32[1]{0:T(128)} %bitcast.here_ref, s32[8,2,16]{2,1,0:T(2,128)S(1)} %collective-permute-done.picks_ref, f32[16,512,128]{2,1,0:T(8,128)S(1)} %get-tuple-element.54.mixed_ref, f32[16,4,128]{2,1,0:T(4,128)S(1)} %get-tuple-element.55.sums_ref, ...), custom_call_target="tpu_custom_call", output_to_operand_aliasing={{}: (8, {})} | custom-call | flops 2097152 | bytes 8388608 | tf_op jit(solution)/shard_map/pallas_call | solution.py:448
  (8 shorter events, 0.0 us)
Async XLA Ops:
  0.0 1.6 %copy-start = (bf16[1,512,2048]{2,1,0:T(8,128)(2,1)S(1)}, bf16[1,512,2048]{2,1,0:T(8,128)(2,1)}, u32[]{:S(2)}) copy-start(bf16[1,512,2048]{2,1,0:T(8,128)(2,1)} %param.5) | copy-start | bytes 6291460
  1.6 1.6 %copy-start.2 = (bf16[1,512,2048]{2,1,0:T(8,128)(2,1)S(1)}, bf16[1,512,2048]{2,1,0:T(8,128)(2,1)}, u32[]{:S(2)}) copy-start(bf16[1,512,2048]{2,1,0:T(8,128)(2,1)} %param.6) | copy-start | bytes 6291460
  3.2 4.2 %copy-start.4 = (bf16[1,512,2048]{2,1,0:T(8,128)(2,1)S(1)}, bf16[1,512,2048]{2,1,0:T(8,128)(2,1)}, u32[]{:S(2)}) copy-start(bf16[1,512,2048]{2,1,0:T(8,128)(2,1)} %param.4) | copy-start | bytes 6291460
  6.0 48.5 %collective-permute-start.1 = (bf16[8,512,128]{2,1,0:T(8,128)(2,1)S(1)}, bf16[8,512,128]{2,1,0:T(8,128)(2,1)S(1)}, u32[]{:S(2)}, u32[]{:S(2)}) collective-permute-start(bf16[8,512,128]{2,1,0:T(8,128)(2,1)S(1)} %get-tuple-element.31), channel_id=1, source_target_pairs={{0,8},{4,12},{8,16},{12,20},{16,24},{20,28},{1,9},{5,13},{9,17},{1... | collective-permute-start | bytes 3145736 | tf_op jit(solution)/shard_map/ppermute | solution.py:484
  7.4 9.2 %copy-start.1 = (bf16[1,512,2048]{2,1,0:T(8,128)(2,1)S(1)}, bf16[1,512,2048]{2,1,0:T(8,128)(2,1)}, u32[]{:S(2)}) copy-start(bf16[1,512,2048]{2,1,0:T(8,128)(2,1)} %param.5) | copy-start | bytes 6291460
  7.4 9.2 %copy-start.3 = (bf16[1,512,2048]{2,1,0:T(8,128)(2,1)S(1)}, bf16[1,512,2048]{2,1,0:T(8,128)(2,1)}, u32[]{:S(2)}) copy-start(bf16[1,512,2048]{2,1,0:T(8,128)(2,1)} %param.6) | copy-start | bytes 6291460
  8.6 18.9 %collective-permute-start.2 = (bf16[4,512,128]{2,1,0:T(8,128)(2,1)S(1)}, bf16[4,512,128]{2,1,0:T(8,128)(2,1)S(1)}, u32[]{:S(2)}, u32[]{:S(2)}) collective-permute-start(bf16[4,512,128]{2,1,0:T(8,128)(2,1)S(1)} %shard_map.47), channel_id=1, source_target_pairs={{16,0},{20,4},{24,8},{28,12},{17,1},{21,5},{25,9},{29,13},{18,2},{... | collective-permute-start | bytes 1572872 | tf_op jit(solution)/shard_map/ppermute | solution.py:487
  13.1 3.5 %collective-permute-start = (s32[8,2,16]{2,1,0:T(2,128)}, s32[8,2,16]{2,1,0:T(2,128)S(1)}, u32[]{:S(2)}, u32[]{:S(2)}) collective-permute-start(s32[8,2,16]{2,1,0:T(2,128)} %bitcast.2.picks_ref), channel_id=1, source_target_pairs={{0,1},{1,2},{2,3},{3,0},{4,5},{5,6},{6,7},{7,4},{8,9},{9,10},{10,1... | collective-permute-start | bytes 3080 | tf_op jit(solution)/shard_map/ppermute | solution.py:24
  25.6 39.0 %collective-permute-start.3 = (bf16[16,528,128]{2,1,0:T(8,128)(2,1)}, bf16[16,528,128]{2,1,0:T(8,128)(2,1)}, u32[]{:S(2)}, u32[]{:S(2)}) collective-permute-start(bf16[16,528,128]{2,1,0:T(8,128)(2,1)} %shard_map.49), channel_id=1, source_target_pairs={{0,1},{1,2},{2,3},{3,0},{4,5},{5,6},{6,7},{7,4},{8,9},{9,10},{10,1... | collective-permute-start | bytes 6488072 | tf_op jit(solution)/shard_map/ppermute | solution.py:24
  26.2 38.4 %collective-permute-start.4 = (bf16[8,512,128]{2,1,0:T(8,128)(2,1)}, bf16[8,512,128]{2,1,0:T(8,128)(2,1)}, u32[]{:S(2)}, u32[]{:S(2)}) collective-permute-start(bf16[8,512,128]{2,1,0:T(8,128)(2,1)} %get-tuple-element.44), channel_id=1, source_target_pairs={{0,24},{4,28},{1,25},{5,29},{2,26},{6,30},{3,27},{7,31}} | collective-permute-start | bytes 3145736 | tf_op jit(solution)/shard_map/ppermute | solution.py:484
  54.5 1.0 copy-start.5
  55.5 16.4 %collective-permute-start.5 = (bf16[4,512,128]{2,1,0:T(8,128)(2,1)}, bf16[4,512,128]{2,1,0:T(8,128)(2,1)}, u32[]{:S(2)}, u32[]{:S(2)}) collective-permute-start(bf16[4,512,128]{2,1,0:T(8,128)(2,1)} %get-tuple-element.46), channel_id=1, source_target_pairs={{12,0},{16,4},{20,8},{24,12},{28,16},{13,1},{17,5},{21,9},{25,13},... | collective-permute-start | bytes 1572872 | tf_op jit(solution)/shard_map/ppermute | solution.py:487
  57.6 18.7 %collective-permute-start.6 = (bf16[4,512,128]{2,1,0:T(8,128)(2,1)}, bf16[4,512,128]{2,1,0:T(8,128)(2,1)}, u32[]{:S(2)}, u32[]{:S(2)}) collective-permute-start(bf16[4,512,128]{2,1,0:T(8,128)(2,1)} %get-tuple-element.48), channel_id=1, source_target_pairs={{20,0},{24,4},{28,8},{21,1},{25,5},{29,9},{22,2},{26,6},{30,10},{2... | collective-permute-start | bytes 1572872 | tf_op jit(solution)/shard_map/ppermute | solution.py:487
  59.7 4.9 %copy-start.6 = (bf16[8,512,128]{2,1,0:T(8,128)(2,1)S(1)}, bf16[8,512,128]{2,1,0:T(8,128)(2,1)}, u32[]{:S(2)}) copy-start(bf16[8,512,128]{2,1,0:T(8,128)(2,1)} %copy-done.5) | copy-start | bytes 3145732
  63.3 40.1 %collective-permute-start.10 = (bf16[4,528,128]{2,1,0:T(8,128)(2,1)}, bf16[4,528,128]{2,1,0:T(8,128)(2,1)}, u32[]{:S(2)}, u32[]{:S(2)}) collective-permute-start(bf16[4,528,128]{2,1,0:T(8,128)(2,1)} %shard_map.50), channel_id=1, source_target_pairs={{0,17},{1,18},{2,19},{3,16},{4,21},{5,22},{6,23},{7,20},{8,25},{9,... | collective-permute-start | bytes 1622024 | tf_op jit(solution)/shard_map/ppermute | solution.py:495
  70.0 23.6 %collective-permute-start.7 = (bf16[8,528,128]{2,1,0:T(8,128)(2,1)}, bf16[8,528,128]{2,1,0:T(8,128)(2,1)}, u32[]{:S(2)}, u32[]{:S(2)}) collective-permute-start(bf16[8,528,128]{2,1,0:T(8,128)(2,1)} %shard_map.51), channel_id=1, source_target_pairs={{0,1},{1,2},{2,3},{3,0},{4,5},{5,6},{6,7},{7,4},{8,9},{9,10},{10,1... | collective-permute-start | bytes 3244040 | tf_op jit(solution)/shard_map/ppermute | solution.py:24
  70.0 24.9 %collective-permute-start.8 = (bf16[4,512,128]{2,1,0:T(8,128)(2,1)}, bf16[4,512,128]{2,1,0:T(8,128)(2,1)}, u32[]{:S(2)}, u32[]{:S(2)}) collective-permute-start(bf16[4,512,128]{2,1,0:T(8,128)(2,1)} %get-tuple-element.50), channel_id=1, source_target_pairs={{4,0},{8,4},{12,8},{16,12},{20,16},{24,20},{28,24},{5,1},{9,5},{13... | collective-permute-start | bytes 1572872 | tf_op jit(solution)/shard_map/ppermute | solution.py:487
  71.9 25.9 %collective-permute-start.9 = (bf16[4,512,128]{2,1,0:T(8,128)(2,1)}, bf16[4,512,128]{2,1,0:T(8,128)(2,1)}, u32[]{:S(2)}, u32[]{:S(2)}) collective-permute-start(bf16[4,512,128]{2,1,0:T(8,128)(2,1)} %get-tuple-element.52), channel_id=1, source_target_pairs={{28,0},{29,1},{30,2},{31,3}} | collective-permute-start | bytes 1572872 | tf_op jit(solution)/shard_map/ppermute | solution.py:487
  76.3 41.1 %collective-permute-start.11 = (bf16[4,528,128]{2,1,0:T(8,128)(2,1)S(1)}, bf16[4,528,128]{2,1,0:T(8,128)(2,1)S(1)}, u32[]{:S(2)}, u32[]{:S(2)}) collective-permute-start(bf16[4,528,128]{2,1,0:T(8,128)(2,1)S(1)} %shard_map.52), channel_id=1, source_target_pairs={{0,13},{1,14},{2,15},{3,12},{4,17},{5,18},{6,19},{7,16},{8,21},{9,... | collective-permute-start | bytes 1622024 | tf_op jit(solution)/shard_map/ppermute | solution.py:495
  93.6 20.5 %collective-permute-start.12 = (bf16[4,528,128]{2,1,0:T(8,128)(2,1)S(1)}, bf16[4,528,128]{2,1,0:T(8,128)(2,1)S(1)}, u32[]{:S(2)}, u32[]{:S(2)}) collective-permute-start(bf16[4,528,128]{2,1,0:T(8,128)(2,1)S(1)} %shard_map.53), channel_id=1, source_target_pairs={{0,21},{1,22},{2,23},{3,20},{4,25},{5,26},{6,27},{7,24},{8,29},{9,... | collective-permute-start | bytes 1622024 | tf_op jit(solution)/shard_map/ppermute | solution.py:495
  100.7 16.6 %collective-permute-start.14 = (bf16[4,528,128]{2,1,0:T(8,128)(2,1)S(1)}, bf16[4,528,128]{2,1,0:T(8,128)(2,1)S(1)}, u32[]{:S(2)}, u32[]{:S(2)}) collective-permute-start(bf16[4,528,128]{2,1,0:T(8,128)(2,1)S(1)} %shard_map.55), channel_id=1, source_target_pairs={{0,29},{1,30},{2,31},{3,28}} | collective-permute-start | bytes 1622024 | tf_op jit(solution)/shard_map/ppermute | solution.py:495
  101.4 35.8 %collective-permute-start.13 = (bf16[4,528,128]{2,1,0:T(8,128)(2,1)S(1)}, bf16[4,528,128]{2,1,0:T(8,128)(2,1)S(1)}, u32[]{:S(2)}, u32[]{:S(2)}) collective-permute-start(bf16[4,528,128]{2,1,0:T(8,128)(2,1)S(1)} %shard_map.54), channel_id=1, source_target_pairs={{0,5},{1,6},{2,7},{3,4},{4,9},{5,10},{6,11},{7,8},{8,13},{9,14},{1... | collective-permute-start | bytes 1622024 | tf_op jit(solution)/shard_map/ppermute | solution.py:495

commit v17 on v13

--- a/solution.py
+++ b/solution.py
@@ -519,8 +519,8 @@
     ask_for(five, near_sends[0])
     own = own_part(after(now, before), queries, keys, values)
     own_back = passed_along(own, "pipe", 1)
-    near.append(up(after(near_sends[1], own), near_shifts[1]))
-    part_three = work(after(here, own, near[0]), three, is_anchor=True)
+    near.append(up(after(near_sends[1], now), near_shifts[1]))
+    part_three = work(after(here, own), three, is_anchor=True)
     returned[three] = up_and_on(part_three, three)
     part_five = work(after(here, part_three), five, is_anchor=True)
     returned[five] = up_and_on(part_five, five)

time: 145 us -> 153 us (1.055)
  the two profiles are of different devices: /device:TPU:26 before, /device:TPU:18 now
where the time goes in v17:
time: 153 us
  starting transfers between devices  57 us (37%)
  Pallas kernels  49.7 us (32%)
  waiting for transfers between devices  42.1 us (28%)
  local copies, waits for them, and re-layouts  3.91 us (3%)
    ppermute x5, starting transfers between devices, down(): lax.ppermute(value, 'ctx', [(at, at - shift) for at in range(shift, width)])  32 us
    ppermute x5, waiting for transfers between devices, down(): lax.ppermute(value, 'ctx', [(at, at - shift) for at in range(shift, width)])  23 us
    ppermute x5, starting transfers between devices, up_and_on(): return lax.ppermute(value, ('ctx', 'pipe'), pairs)  19.5 us
    pallas_call x5, Pallas kernels, attend(): call(functools.partial(attend_kernel, group=group, slots=slots), [SCALARS...  15.9 us
    ppermute x5, waiting for transfers between devices, up_and_on(): return lax.ppermute(value, ('ctx', 'pipe'), pairs)  12.5 us
    pallas_call x1, Pallas kernels, own_part(): call(own_kernel, [SCALARS, IN_VMEM, IN_VMEM, IN_VMEM], jax.ShapeDtypeStru...  8.95 us
    pallas_call x3, Pallas kernels, pack(): call(functools.partial(pack_kernel, jobs=jobs, slots=slots), [SCALARS, SC...  7.79 us
    pallas_call x1, Pallas kernels, merge(): call(functools.partial(merge_kernel, places=tuple(places), shifts=shifts,...  7.27 us
  transfers between devices with their start and end apart: 15, of which 4 were waited for; matrix products, arithmetic and copies ran while one was open for 0% of the time, Pallas kernels for 26%

profile of v17, /device:TPU:18, one launch (start us, length us, event | category | flops | bytes accessed | tf_op | source)
XLA Modules:
  0.0 153.1 jit_solution(8585102397915092297)
XLA Ops:
  0.0 1.6 %copy-done = bf16[1,512,2048]{2,1,0:T(8,128)(2,1)S(1)} copy-done((bf16[1,512,2048]{2,1,0:T(8,128)(2,1)S(1)}, bf16[1,512,2048]{2,1,0:T(8,128)(2,1)}, u32[]{:S(2)}) %copy-start) | copy-done | bytes 2097176
  1.6 1.6 %copy-done.2 = bf16[1,512,2048]{2,1,0:T(8,128)(2,1)S(1)} copy-done((bf16[1,512,2048]{2,1,0:T(8,128)(2,1)S(1)}, bf16[1,512,2048]{2,1,0:T(8,128)(2,1)}, u32[]{:S(2)}) %copy-start.2) | copy-done | bytes 2097176
  3.2 0.7 copy-done.5
  3.9 3.0 %shard_map.46 = (bf16[8,512,128]{2,1,0:T(8,128)(2,1)}, bf16[8,512,128]{2,1,0:T(8,128)(2,1)}) custom-call(s32[1]{0:T(128)} %bitcast.here_ref, s32[8,2,16]{2,1,0:T(2,128)S(1)} %bitcast.26, bf16[512,2048]{1,0:T(8,128)(2,1)S(1)} %bitcast.8, bf16[512,2048]{1,0:T(8,128)(2,1)S(1)} %bitcast.15), custom_call_target="tpu_custom_call" | custom-call | bytes 4194304 | tf_op jit(solution)/shard_map/pallas_call | solution.py:127
  6.9 0.0 copy-start.1
  6.9 0.0 copy-start.3
  6.9 2.1 %shard_map.47 = (bf16[4,512,128]{2,1,0:T(8,128)(2,1)S(1)}, bf16[4,512,128]{2,1,0:T(8,128)(2,1)}) custom-call(s32[1]{0:T(128)} %bitcast.here_ref, s32[8,2,16]{2,1,0:T(2,128)S(1)} %bitcast.27, bf16[512,2048]{1,0:T(8,128)(2,1)S(1)} %bitcast.22), custom_call_target="tpu_custom_call" | custom-call | bytes 2097152 | tf_op jit(solution)/shard_map/pallas_call | solution.py:127
  9.0 3.2 %collective-permute-start.1 = (bf16[4,512,128]{2,1,0:T(8,128)(2,1)S(1)}, bf16[4,512,128]{2,1,0:T(8,128)(2,1)S(1)}, u32[]{:S(2)}, u32[]{:S(2)}) collective-permute-start(bf16[4,512,128]{2,1,0:T(8,128)(2,1)S(1)} %get-tuple-element.44), channel_id=1, source_target_pairs={{12,0},{16,4},{20,8},{24,12},{28,16},{13,1},{17,5},{21,9},{25,13},... | collective-permute-start | bytes 1572872 | tf_op jit(solution)/shard_map/ppermute | solution.py:487
  12.2 0.1 collective-permute-start
  12.3 3.5 %collective-permute-start.4 = (bf16[8,512,128]{2,1,0:T(8,128)(2,1)}, bf16[8,512,128]{2,1,0:T(8,128)(2,1)}, u32[]{:S(2)}, u32[]{:S(2)}) collective-permute-start(bf16[8,512,128]{2,1,0:T(8,128)(2,1)} %get-tuple-element.32), channel_id=1, source_target_pairs={{0,8},{4,12},{8,16},{12,20},{16,24},{20,28},{1,9},{5,13},{9,17},{1... | collective-permute-start | bytes 3145736 | tf_op jit(solution)/shard_map/ppermute | solution.py:484
  15.8 1.5 collective-permute-start.2
  17.3 2.7 %shard_map.48 = (bf16[4,512,128]{2,1,0:T(8,128)(2,1)}, bf16[4,512,128]{2,1,0:T(8,128)(2,1)}, bf16[4,512,128]{2,1,0:T(8,128)(2,1)}) custom-call(s32[1]{0:T(128)} %bitcast.here_ref, s32[8,2,16]{2,1,0:T(2,128)S(1)} %bitcast.29, bf16[512,2048]{1,0:T(8,128)(2,1)S(1)} %bitcast.23), custom_call_target="tpu_custom_call" | custom-call | bytes 3145728 | tf_op jit(solution)/shard_map/pallas_call | solution.py:127
  20.0 1.6 %collective-permute-start.5 = (bf16[8,512,128]{2,1,0:T(8,128)(2,1)}, bf16[8,512,128]{2,1,0:T(8,128)(2,1)}, u32[]{:S(2)}, u32[]{:S(2)}) collective-permute-start(bf16[8,512,128]{2,1,0:T(8,128)(2,1)} %get-tuple-element.48), channel_id=1, source_target_pairs={{0,24},{4,28},{1,25},{5,29},{2,26},{6,30},{3,27},{7,31}} | collective-permute-start | bytes 3145736 | tf_op jit(solution)/shard_map/ppermute | solution.py:484
  21.6 0.0 collective-permute-done.picks_ref
  21.6 8.9 %shard_map.49 = bf16[16,528,128]{2,1,0:T(8,128)(2,1)} custom-call(s32[1]{0:T(128)} %bitcast.here_ref, bf16[512,2048]{1,0:T(8,128)(2,1)S(1)} %bitcast.24, bf16[512,2048]{1,0:T(8,128)(2,1)S(1)} %bitcast.9, bf16[512,2048]{1,0:T(8,128)(2,1)S(1)} %bitcast.16), custom_call_target="tpu_custom_call" | custom-call | flops 2147483648 | bytes 8388608 | tf_op jit(solution)/shard_map/pallas_call | solution.py:266
  30.6 0.3 collective-permute-start.3
  30.9 14.9 %collective-permute-done.1.refs_0_ = bf16[4,512,128]{2,1,0:T(8,128)(2,1)S(1)} collective-permute-done((bf16[4,512,128]{2,1,0:T(8,128)(2,1)S(1)}, bf16[4,512,128]{2,1,0:T(8,128)(2,1)S(1)}, u32[]{:S(2)}, u32[]{:S(2)}) %collective-permute-start.1) | collective-permute-done | bytes 524320 | tf_op jit(solution)/shard_map/ppermute | solution.py:487
  45.8 3.4 %shard_map.50 = bf16[4,528,128]{2,1,0:T(8,128)(2,1)} custom-call(s32[1]{0:T(128)} %bitcast.here_ref, s32[8,2,16]{2,1,0:T(2,128)S(1)} %bitcast.30, bf16[512,2048]{1,0:T(8,128)(2,1)S(1)} %bitcast.10, bf16[512,2048]{1,0:T(8,128)(2,1)S(1)} %bitcast.17, bf16[4,512,128]{2,1,0:T(8,128)(2,1)S(1)} %collective-permute-done.1.refs_0_), custom_call_target="tpu_custom_call" | custom-call | flops 999999995904 | bytes 2097152 | tf_op jit(solution)/shard_map/pallas_call | solution.py:226
  49.2 1.9 %collective-permute-start.10 = (bf16[4,528,128]{2,1,0:T(8,128)(2,1)}, bf16[4,528,128]{2,1,0:T(8,128)(2,1)}, u32[]{:S(2)}, u32[]{:S(2)}) collective-permute-start(bf16[4,528,128]{2,1,0:T(8,128)(2,1)} %shard_map.50), channel_id=1, source_target_pairs={{0,13},{1,14},{2,15},{3,12},{4,17},{5,18},{6,19},{7,16},{8,21},{9,... | collective-permute-start | bytes 1622024 | tf_op jit(solution)/shard_map/ppermute | solution.py:495
  51.2 0.0 collective-permute-done.2.refs_0_
  51.2 0.0 copy-start.6
  51.2 3.7 %shard_map.51 = bf16[4,528,128]{2,1,0:T(8,128)(2,1)} custom-call(s32[1]{0:T(128)} %bitcast.here_ref, s32[8,2,16]{2,1,0:T(2,128)S(1)} %bitcast.31, bf16[512,2048]{1,0:T(8,128)(2,1)S(1)} %bitcast.11, bf16[512,2048]{1,0:T(8,128)(2,1)S(1)} %bitcast.18, bf16[4,512,128]{2,1,0:T(8,128)(2,1)} %collective-permute-done.2.refs_0_), custom_call_target="tpu_custom_call" | custom-call | flops 999999995904 | bytes 2097152 | tf_op jit(solution)/shard_map/pallas_call | solution.py:226
  54.9 1.5 collective-permute-start.11
  56.4 6.6 %collective-permute-done.4.refs_0_ = bf16[8,512,128]{2,1,0:T(8,128)(2,1)} collective-permute-done((bf16[8,512,128]{2,1,0:T(8,128)(2,1)}, bf16[8,512,128]{2,1,0:T(8,128)(2,1)}, u32[]{:S(2)}, u32[]{:S(2)}) %collective-permute-start.4) | collective-permute-done | bytes 1048608 | tf_op jit(solution)/shard_map/ppermute | solution.py:484
  63.0 0.0 collective-permute-done.5.refs_1_
  63.0 0.0 collective-permute-done.3.refs_0_
  63.0 4.4 %collective-permute-start.6 = (bf16[4,512,128]{2,1,0:T(8,128)(2,1)}, bf16[4,512,128]{2,1,0:T(8,128)(2,1)}, u32[]{:S(2)}, u32[]{:S(2)}) collective-permute-start(bf16[4,512,128]{2,1,0:T(8,128)(2,1)} %get-tuple-element.50), channel_id=1, source_target_pairs={{16,0},{20,4},{24,8},{28,12},{17,1},{21,5},{25,9},{29,13},{18,2},{... | collective-permute-start | bytes 1572872 | tf_op jit(solution)/shard_map/ppermute | solution.py:487
  67.4 5.7 %shard_map.52 = bf16[8,528,128]{2,1,0:T(8,128)(2,1)} custom-call(s32[1]{0:T(128)} %bitcast.here_ref, s32[8,2,16]{2,1,0:T(2,128)S(1)} %bitcast.32, bf16[512,2048]{1,0:T(8,128)(2,1)S(1)} %bitcast.25, bf16[8,512,128]{2,1,0:T(8,128)(2,1)} %collective-permute-done.4.refs_0_, bf16[8,512,128]{2,1,0:T(8,128)(2,1)} %collective-permute-done.5.refs_1_), custom_call_target="tpu_custom_call" | custom-call | flops 999999995904 | bytes 6291456 | tf_op jit(solution)/shard_map/pallas_call | solution.py:295
  73.1 0.0 collective-permute-start.7
  73.1 21.4 %collective-permute-start.8 = (bf16[4,512,128]{2,1,0:T(8,128)(2,1)}, bf16[4,512,128]{2,1,0:T(8,128)(2,1)}, u32[]{:S(2)}, u32[]{:S(2)}) collective-permute-start(bf16[4,512,128]{2,1,0:T(8,128)(2,1)} %get-tuple-element.52), channel_id=1, source_target_pairs={{4,0},{8,4},{12,8},{16,12},{20,16},{24,20},{28,24},{5,1},{9,5},{13... | collective-permute-start | bytes 1572872 | tf_op jit(solution)/shard_map/ppermute | solution.py:487
  94.5 0.0 collective-permute-done.6.refs_0_
  94.6 1.5 collective-permute-start.9
  96.0 2.9 %shard_map.53 = bf16[4,528,128]{2,1,0:T(8,128)(2,1)S(1)} custom-call(s32[1]{0:T(128)} %bitcast.here_ref, s32[8,2,16]{2,1,0:T(2,128)S(1)} %bitcast.33, bf16[512,2048]{1,0:T(8,128)(2,1)S(1)} %bitcast.12, bf16[512,2048]{1,0:T(8,128)(2,1)S(1)} %bitcast.19, bf16[4,512,128]{2,1,0:T(8,128)(2,1)} %collective-permute-done.6.refs_0_), custom_call_target="tpu_custom_call" | custom-call | flops 999999995904 | bytes 2097152 | tf_op jit(solution)/shard_map/pallas_call | solution.py:226
  99.0 0.0 collective-permute-done.7.refs_1_
  99.0 1.3 collective-permute-start.12
  100.3 8.0 %collective-permute-done.8.refs_0_ = bf16[4,512,128]{2,1,0:T(8,128)(2,1)} collective-permute-done((bf16[4,512,128]{2,1,0:T(8,128)(2,1)}, bf16[4,512,128]{2,1,0:T(8,128)(2,1)}, u32[]{:S(2)}, u32[]{:S(2)}) %collective-permute-start.8) | collective-permute-done | bytes 524320 | tf_op jit(solution)/shard_map/ppermute | solution.py:487
  108.3 2.9 %shard_map.54 = bf16[4,528,128]{2,1,0:T(8,128)(2,1)S(1)} custom-call(s32[1]{0:T(128)} %bitcast.here_ref, s32[8,2,16]{2,1,0:T(2,128)S(1)} %bitcast.34, bf16[512,2048]{1,0:T(8,128)(2,1)S(1)} %bitcast.13, bf16[512,2048]{1,0:T(8,128)(2,1)S(1)} %bitcast.20, bf16[4,512,128]{2,1,0:T(8,128)(2,1)} %collective-permute-done.8.refs_0_), custom_call_target="tpu_custom_call" | custom-call | flops 536870912 | bytes 2097152 | tf_op jit(solution)/shard_map/pallas_call | solution.py:226
  111.2 0.0 collective-permute-done.9.refs_0_
  111.2 2.9 %shard_map.55 = bf16[4,528,128]{2,1,0:T(8,128)(2,1)S(1)} custom-call(s32[1]{0:T(128)} %bitcast.here_ref, s32[8,2,16]{2,1,0:T(2,128)S(1)} %bitcast.35, bf16[512,2048]{1,0:T(8,128)(2,1)S(1)} %bitcast.14, bf16[512,2048]{1,0:T(8,128)(2,1)S(1)} %bitcast.21, bf16[4,512,128]{2,1,0:T(8,128)(2,1)} %collective-permute-done.9.refs_0_), custom_call_target="tpu_custom_call" | custom-call | flops 536870912 | bytes 2097152 | tf_op jit(solution)/shard_map/pallas_call | solution.py:226
  114.2 0.7 collective-permute-start.14
  114.9 14.1 %collective-permute-start.13 = (bf16[4,528,128]{2,1,0:T(8,128)(2,1)S(1)}, bf16[4,528,128]{2,1,0:T(8,128)(2,1)S(1)}, u32[]{:S(2)}, u32[]{:S(2)}) collective-permute-start(bf16[4,528,128]{2,1,0:T(8,128)(2,1)S(1)} %shard_map.54), channel_id=1, source_target_pairs={{0,5},{1,6},{2,7},{3,4},{4,9},{5,10},{6,11},{7,8},{8,13},{9,14},{1... | collective-permute-start | bytes 1622024 | tf_op jit(solution)/shard_map/ppermute | solution.py:495
  128.9 0.0 collective-permute-done.11.refs_3_
  129.0 0.0 collective-permute-done.10.refs_2_
  129.0 7.3 %shard_map.56 = (bf16[512,2048]{1,0:T(8,128)(2,1)}, f32[16,512,128]{2,1,0:T(8,128)S(1)}, f32[16,4,128]{2,1,0:T(4,128)S(1)}) custom-call(s32[1]{0:T(128)} %bitcast.here_ref, s32[8,2,16]{2,1,0:T(2,128)S(1)} %copy-done.8, bf16[16,528,128]{2,1,0:T(8,128)(2,1)} %collective-permute-done.3.refs_0_, bf16[8,528,128]{2,1,0:T(8,128)(2,1)} %collective-permute-done.7.refs_1_, ...), custom_call_target="tpu_custom_call" | custom-call | flops 6291456 | bytes 8388608 | tf_op jit(solution)/shard_map/pallas_call | solution.py:367
  136.3 0.0 collective-permute-done.12.refs_0_
  136.3 0.0 collective-permute-done.14.refs_2_
  136.3 12.5 %collective-permute-done.13.refs_1_ = bf16[4,528,128]{2,1,0:T(8,128)(2,1)S(1)} collective-permute-done((bf16[4,528,128]{2,1,0:T(8,128)(2,1)S(1)}, bf16[4,528,128]{2,1,0:T(8,128)(2,1)S(1)}, u32[]{:S(2)}, u32[]{:S(2)}) %collective-permute-start.13) | collective-permute-done | bytes 540704 | tf_op jit(solution)/shard_map/ppermute | solution.py:495
  148.8 4.1 %shard_map.57 = bf16[512,2048]{1,0:T(8,128)(2,1)} custom-call(s32[1]{0:T(128)} %bitcast.here_ref, s32[8,2,16]{2,1,0:T(2,128)S(1)} %copy-done.8, f32[16,512,128]{2,1,0:T(8,128)S(1)} %get-tuple-element.56.mixed_ref, f32[16,4,128]{2,1,0:T(4,128)S(1)} %get-tuple-element.57.sums_ref, ...), custom_call_target="tpu_custom_call", output_to_operand_aliasing={{}: (7, {})} | custom-call | flops 1572864 | bytes 6291456 | tf_op jit(solution)/shard_map/pallas_call | solution.py:448
  (12 shorter events, 0.0 us)
Async XLA Ops:
  0.0 1.6 %copy-start = (bf16[1,512,2048]{2,1,0:T(8,128)(2,1)S(1)}, bf16[1,512,2048]{2,1,0:T(8,128)(2,1)}, u32[]{:S(2)}) copy-start(bf16[1,512,2048]{2,1,0:T(8,128)(2,1)} %param.5) | copy-start | bytes 6291460
  1.6 1.6 %copy-start.2 = (bf16[1,512,2048]{2,1,0:T(8,128)(2,1)S(1)}, bf16[1,512,2048]{2,1,0:T(8,128)(2,1)}, u32[]{:S(2)}) copy-start(bf16[1,512,2048]{2,1,0:T(8,128)(2,1)} %param.6) | copy-start | bytes 6291460
  3.2 0.7 copy-start.5
  3.9 3.0 %copy-start.4 = (bf16[1,512,2048]{2,1,0:T(8,128)(2,1)S(1)}, bf16[1,512,2048]{2,1,0:T(8,128)(2,1)}, u32[]{:S(2)}) copy-start(bf16[1,512,2048]{2,1,0:T(8,128)(2,1)} %param.4) | copy-start | bytes 6291460
  6.9 14.7 %copy-start.1 = (bf16[1,512,2048]{2,1,0:T(8,128)(2,1)S(1)}, bf16[1,512,2048]{2,1,0:T(8,128)(2,1)}, u32[]{:S(2)}) copy-start(bf16[1,512,2048]{2,1,0:T(8,128)(2,1)} %param.5) | copy-start | bytes 6291460
  6.9 14.7 %copy-start.3 = (bf16[1,512,2048]{2,1,0:T(8,128)(2,1)S(1)}, bf16[1,512,2048]{2,1,0:T(8,128)(2,1)}, u32[]{:S(2)}) copy-start(bf16[1,512,2048]{2,1,0:T(8,128)(2,1)} %param.6) | copy-start | bytes 6291460
  9.0 36.8 %collective-permute-start.1 = (bf16[4,512,128]{2,1,0:T(8,128)(2,1)S(1)}, bf16[4,512,128]{2,1,0:T(8,128)(2,1)S(1)}, u32[]{:S(2)}, u32[]{:S(2)}) collective-permute-start(bf16[4,512,128]{2,1,0:T(8,128)(2,1)S(1)} %get-tuple-element.44), channel_id=1, source_target_pairs={{12,0},{16,4},{20,8},{24,12},{28,16},{13,1},{17,5},{21,9},{25,13},... | collective-permute-start | bytes 1572872 | tf_op jit(solution)/shard_map/ppermute | solution.py:487
  12.2 9.4 %collective-permute-start = (s32[8,2,16]{2,1,0:T(2,128)S(1)}, s32[8,2,16]{2,1,0:T(2,128)S(1)}, u32[]{:S(2)}, u32[]{:S(2)}) collective-permute-start(s32[8,2,16]{2,1,0:T(2,128)S(1)} %bitcast.28), channel_id=1, source_target_pairs={{0,1},{1,2},{2,3},{3,0},{4,5},{5,6},{6,7},{7,4},{8,9},{9,10},{10,1... | collective-permute-start | bytes 3080 | tf_op jit(solution)/shard_map/ppermute | solution.py:24
  12.3 50.7 %collective-permute-start.4 = (bf16[8,512,128]{2,1,0:T(8,128)(2,1)}, bf16[8,512,128]{2,1,0:T(8,128)(2,1)}, u32[]{:S(2)}, u32[]{:S(2)}) collective-permute-start(bf16[8,512,128]{2,1,0:T(8,128)(2,1)} %get-tuple-element.32), channel_id=1, source_target_pairs={{0,8},{4,12},{8,16},{12,20},{16,24},{20,28},{1,9},{5,13},{9,17},{1... | collective-permute-start | bytes 3145736 | tf_op jit(solution)/shard_map/ppermute | solution.py:484
  15.8 35.4 %collective-permute-start.2 = (bf16[4,512,128]{2,1,0:T(8,128)(2,1)}, bf16[4,512,128]{2,1,0:T(8,128)(2,1)}, u32[]{:S(2)}, u32[]{:S(2)}) collective-permute-start(bf16[4,512,128]{2,1,0:T(8,128)(2,1)} %get-tuple-element.46), channel_id=1, source_target_pairs={{20,0},{24,4},{28,8},{21,1},{25,5},{29,9},{22,2},{26,6},{30,10},{2... | collective-permute-start | bytes 1572872 | tf_op jit(solution)/shard_map/ppermute | solution.py:487
  20.0 43.0 %collective-permute-start.5 = (bf16[8,512,128]{2,1,0:T(8,128)(2,1)}, bf16[8,512,128]{2,1,0:T(8,128)(2,1)}, u32[]{:S(2)}, u32[]{:S(2)}) collective-permute-start(bf16[8,512,128]{2,1,0:T(8,128)(2,1)} %get-tuple-element.48), channel_id=1, source_target_pairs={{0,24},{4,28},{1,25},{5,29},{2,26},{6,30},{3,27},{7,31}} | collective-permute-start | bytes 3145736 | tf_op jit(solution)/shard_map/ppermute | solution.py:484
  21.6 9.0 %copy-start.7 = (s32[8,2,16]{2,1,0:T(2,128)}, s32[8,2,16]{2,1,0:T(2,128)S(1)}, u32[]{:S(2)}) copy-start(s32[8,2,16]{2,1,0:T(2,128)S(1)} %collective-permute-done.picks_ref) | copy-start | bytes 3076
  30.6 32.4 %collective-permute-start.3 = (bf16[16,528,128]{2,1,0:T(8,128)(2,1)}, bf16[16,528,128]{2,1,0:T(8,128)(2,1)}, u32[]{:S(2)}, u32[]{:S(2)}) collective-permute-start(bf16[16,528,128]{2,1,0:T(8,128)(2,1)} %shard_map.49), channel_id=1, source_target_pairs={{0,1},{1,2},{2,3},{3,0},{4,5},{5,6},{6,7},{7,4},{8,9},{9,10},{10,1... | collective-permute-start | bytes 6488072 | tf_op jit(solution)/shard_map/ppermute | solution.py:24
  49.2 79.7 %collective-permute-start.10 = (bf16[4,528,128]{2,1,0:T(8,128)(2,1)}, bf16[4,528,128]{2,1,0:T(8,128)(2,1)}, u32[]{:S(2)}, u32[]{:S(2)}) collective-permute-start(bf16[4,528,128]{2,1,0:T(8,128)(2,1)} %shard_map.50), channel_id=1, source_target_pairs={{0,13},{1,14},{2,15},{3,12},{4,17},{5,18},{6,19},{7,16},{8,21},{9,... | collective-permute-start | bytes 1622024 | tf_op jit(solution)/shard_map/ppermute | solution.py:495
  51.2 16.3 %copy-start.6 = (s32[1,8,16,2]{2,3,1,0:T(2,128)S(1)}, s32[1,8,16,2]{2,3,1,0:T(2,128)}, u32[]{:S(2)}) copy-start(s32[1,8,16,2]{2,3,1,0:T(2,128)} %param.7) | copy-start | bytes 3076
  54.9 74.0 %collective-permute-start.11 = (bf16[4,528,128]{2,1,0:T(8,128)(2,1)}, bf16[4,528,128]{2,1,0:T(8,128)(2,1)}, u32[]{:S(2)}, u32[]{:S(2)}) collective-permute-start(bf16[4,528,128]{2,1,0:T(8,128)(2,1)} %shard_map.51), channel_id=1, source_target_pairs={{0,21},{1,22},{2,23},{3,20},{4,25},{5,26},{6,27},{7,24},{8,29},{9,... | collective-permute-start | bytes 1622024 | tf_op jit(solution)/shard_map/ppermute | solution.py:495
  63.0 31.5 %collective-permute-start.6 = (bf16[4,512,128]{2,1,0:T(8,128)(2,1)}, bf16[4,512,128]{2,1,0:T(8,128)(2,1)}, u32[]{:S(2)}, u32[]{:S(2)}) collective-permute-start(bf16[4,512,128]{2,1,0:T(8,128)(2,1)} %get-tuple-element.50), channel_id=1, source_target_pairs={{16,0},{20,4},{24,8},{28,12},{17,1},{21,5},{25,9},{29,13},{18,2},{... | collective-permute-start | bytes 1572872 | tf_op jit(solution)/shard_map/ppermute | solution.py:487
  73.1 25.8 %collective-permute-start.7 = (bf16[8,528,128]{2,1,0:T(8,128)(2,1)}, bf16[8,528,128]{2,1,0:T(8,128)(2,1)}, u32[]{:S(2)}, u32[]{:S(2)}) collective-permute-start(bf16[8,528,128]{2,1,0:T(8,128)(2,1)} %shard_map.52), channel_id=1, source_target_pairs={{0,1},{1,2},{2,3},{3,0},{4,5},{5,6},{6,7},{7,4},{8,9},{9,10},{10,1... | collective-permute-start | bytes 3244040 | tf_op jit(solution)/shard_map/ppermute | solution.py:24
  73.1 35.2 %collective-permute-start.8 = (bf16[4,512,128]{2,1,0:T(8,128)(2,1)}, bf16[4,512,128]{2,1,0:T(8,128)(2,1)}, u32[]{:S(2)}, u32[]{:S(2)}) collective-permute-start(bf16[4,512,128]{2,1,0:T(8,128)(2,1)} %get-tuple-element.52), channel_id=1, source_target_pairs={{4,0},{8,4},{12,8},{16,12},{20,16},{24,20},{28,24},{5,1},{9,5},{13... | collective-permute-start | bytes 1572872 | tf_op jit(solution)/shard_map/ppermute | solution.py:487
  94.6 16.7 %collective-permute-start.9 = (bf16[4,512,128]{2,1,0:T(8,128)(2,1)}, bf16[4,512,128]{2,1,0:T(8,128)(2,1)}, u32[]{:S(2)}, u32[]{:S(2)}) collective-permute-start(bf16[4,512,128]{2,1,0:T(8,128)(2,1)} %get-tuple-element.54), channel_id=1, source_target_pairs={{28,0},{29,1},{30,2},{31,3}} | collective-permute-start | bytes 1572872 | tf_op jit(solution)/shard_map/ppermute | solution.py:487
  99.0 37.3 %collective-permute-start.12 = (bf16[4,528,128]{2,1,0:T(8,128)(2,1)S(1)}, bf16[4,528,128]{2,1,0:T(8,128)(2,1)S(1)}, u32[]{:S(2)}, u32[]{:S(2)}) collective-permute-start(bf16[4,528,128]{2,1,0:T(8,128)(2,1)S(1)} %shard_map.53), channel_id=1, source_target_pairs={{0,17},{1,18},{2,19},{3,16},{4,21},{5,22},{6,23},{7,20},{8,25},{9,... | collective-permute-start | bytes 1622024 | tf_op jit(solution)/shard_map/ppermute | solution.py:495
  111.2 17.8 %copy-start.8 = (s32[8,2,16]{2,1,0:T(2,128)S(1)}, s32[8,2,16]{2,1,0:T(2,128)}, u32[]{:S(2)}) copy-start(s32[8,2,16]{2,1,0:T(2,128)} %copy-done.7) | copy-start | bytes 3076
  114.2 22.1 %collective-permute-start.14 = (bf16[4,528,128]{2,1,0:T(8,128)(2,1)S(1)}, bf16[4,528,128]{2,1,0:T(8,128)(2,1)S(1)}, u32[]{:S(2)}, u32[]{:S(2)}) collective-permute-start(bf16[4,528,128]{2,1,0:T(8,128)(2,1)S(1)} %shard_map.55), channel_id=1, source_target_pairs={{0,29},{1,30},{2,31},{3,28}} | collective-permute-start | bytes 1622024 | tf_op jit(solution)/shard_map/ppermute | solution.py:495
  114.9 33.9 %collective-permute-start.13 = (bf16[4,528,128]{2,1,0:T(8,128)(2,1)S(1)}, bf16[4,528,128]{2,1,0:T(8,128)(2,1)S(1)}, u32[]{:S(2)}, u32[]{:S(2)}) collective-permute-start(bf16[4,528,128]{2,1,0:T(8,128)(2,1)S(1)} %shard_map.54), channel_id=1, source_target_pairs={{0,5},{1,6},{2,7},{3,4},{4,9},{5,10},{6,11},{7,8},{8,13},{9,14},{1... | collective-permute-start | bytes 1622024 | tf_op jit(solution)/shard_map/ppermute | solution.py:495

commit v18 on v13

--- a/solution.py
+++ b/solution.py
@@ -524,7 +524,7 @@
     returned[three] = up_and_on(part_three, three)
     part_five = work(after(here, part_three), five, is_anchor=True)
     returned[five] = up_and_on(part_five, five)
-    ask_for(four, arrived[three], arrived[five], part_five, own_back, *near)
+    ask_for(four, arrived[three], arrived[five], part_five, own_back, near[0])
     beside = near_part(after(here, part_five, own_back), own_picks, queries, near, near_shifts, slots)
     ask_for(one, own_back, part_five, *near)
     ask_for(seven, own_back, part_five, *near)

time: 145 us -> 143 us (0.986)
  waiting for transfers between devices: 59.7 us -> 55 us
  starting transfers between devices: 28.4 us -> 30.7 us
    ppermute x2, waiting for transfers between devices: 18 us -> 4.13 us  [up(): lax.ppermute(value, 'ctx', [(at, at + shift) for at in range(width - shif...]
    ppermute x3, waiting for transfers between devices: 3.62 us -> 14.2 us  [passed_along(): return lax.ppermute(value, axis, pairs)]
    ppermute x5, starting transfers between devices: 18.7 us -> 20.8 us  [down(): lax.ppermute(value, 'ctx', [(at, at - shift) for at in range(shift, width)])]
  transfers between devices with their start and end apart: 15 -> 15, of which waited for: 5 -> 7; matrix products, arithmetic and copies ran while one was open for 0% -> 0% of each run, Pallas kernels for 30% -> 30%
where the time goes in v18:
time: 143 us; the launch traced here: 140 us
  waiting for transfers between devices  55 us (38%)
  Pallas kernels  49.1 us (34%)
  starting transfers between devices  30.7 us (21%)
  local copies, waits for them, and re-layouts  4.91 us (3%)
    ppermute x5, starting transfers between devices, down(): lax.ppermute(value, 'ctx', [(at, at - shift) for at in range(shift, width)])  20.8 us
    ppermute x5, waiting for transfers between devices, down(): lax.ppermute(value, 'ctx', [(at, at - shift) for at in range(shift, width)])  19.7 us
    ppermute x5, waiting for transfers between devices, up_and_on(): return lax.ppermute(value, ('ctx', 'pipe'), pairs)  16.9 us
    pallas_call x5, Pallas kernels, attend(): call(functools.partial(attend_kernel, group=group, slots=slots), [SCALARS...  16 us
    ppermute x3, waiting for transfers between devices, passed_along(): return lax.ppermute(value, axis, pairs)  14.2 us
    pallas_call x1, Pallas kernels, own_part(): call(own_kernel, [SCALARS, IN_VMEM, IN_VMEM, IN_VMEM], jax.ShapeDtypeStru...  8.96 us
    pallas_call x3, Pallas kernels, pack(): call(functools.partial(pack_kernel, jobs=jobs, slots=slots), [SCALARS, SC...  7.45 us
    pallas_call x1, Pallas kernels, merge(): call(functools.partial(merge_kernel, places=tuple(places), shifts=shifts,...  7.26 us
  transfers between devices with their start and end apart: 15, of which 7 were waited for; matrix products, arithmetic and copies ran while one was open for 0% of the time, Pallas kernels for 30%

profile of v18, /device:TPU:26, one launch (start us, length us, event | category | flops | bytes accessed | tf_op | source)
XLA Modules:
  0.0 140.1 jit_solution(2285306715759319547)
XLA Ops:
  0.0 1.6 %copy-done = bf16[1,512,2048]{2,1,0:T(8,128)(2,1)S(1)} copy-done((bf16[1,512,2048]{2,1,0:T(8,128)(2,1)S(1)}, bf16[1,512,2048]{2,1,0:T(8,128)(2,1)}, u32[]{:S(2)}) %copy-start) | copy-done | bytes 2097176
  1.6 1.6 %copy-done.2 = bf16[1,512,2048]{2,1,0:T(8,128)(2,1)S(1)} copy-done((bf16[1,512,2048]{2,1,0:T(8,128)(2,1)S(1)}, bf16[1,512,2048]{2,1,0:T(8,128)(2,1)}, u32[]{:S(2)}) %copy-start.2) | copy-done | bytes 2097176
  3.2 0.7 copy-done.5
  3.9 2.6 %shard_map.46 = (bf16[8,512,128]{2,1,0:T(8,128)(2,1)S(1)}, bf16[8,512,128]{2,1,0:T(8,128)(2,1)}) custom-call(s32[1]{0:T(128)} %bitcast.here_ref, s32[8,2,16]{2,1,0:T(2,128)S(1)} %bitcast.26, bf16[512,2048]{1,0:T(8,128)(2,1)S(1)} %bitcast.8, bf16[512,2048]{1,0:T(8,128)(2,1)S(1)} %bitcast.15), custom_call_target="tpu_custom_call" | custom-call | bytes 4194304 | tf_op jit(solution)/shard_map/pallas_call | solution.py:127
  6.5 1.3 collective-permute-start.1
  7.8 0.0 copy-start.1
  7.8 0.0 copy-start.3
  7.8 2.1 %shard_map.47 = (bf16[4,512,128]{2,1,0:T(8,128)(2,1)S(1)}, bf16[4,512,128]{2,1,0:T(8,128)(2,1)}) custom-call(s32[1]{0:T(128)} %bitcast.here_ref, s32[8,2,16]{2,1,0:T(2,128)S(1)} %bitcast.27, bf16[512,2048]{1,0:T(8,128)(2,1)S(1)} %bitcast.22), custom_call_target="tpu_custom_call" | custom-call | bytes 2097152 | tf_op jit(solution)/shard_map/pallas_call | solution.py:127
  9.9 5.4 %collective-permute-start.2 = (bf16[4,512,128]{2,1,0:T(8,128)(2,1)S(1)}, bf16[4,512,128]{2,1,0:T(8,128)(2,1)S(1)}, u32[]{:S(2)}, u32[]{:S(2)}) collective-permute-start(bf16[4,512,128]{2,1,0:T(8,128)(2,1)S(1)} %get-tuple-element.44), channel_id=1, source_target_pairs={{12,0},{16,4},{20,8},{24,12},{28,16},{13,1},{17,5},{21,9},{25,13},... | collective-permute-start | bytes 1572872 | tf_op jit(solution)/shard_map/ppermute | solution.py:487
  15.4 0.1 collective-permute-start
  15.4 2.1 %collective-permute-start.3 = (bf16[4,512,128]{2,1,0:T(8,128)(2,1)}, bf16[4,512,128]{2,1,0:T(8,128)(2,1)}, u32[]{:S(2)}, u32[]{:S(2)}) collective-permute-start(bf16[4,512,128]{2,1,0:T(8,128)(2,1)} %get-tuple-element.46), channel_id=1, source_target_pairs={{20,0},{24,4},{28,8},{21,1},{25,5},{29,9},{22,2},{26,6},{30,10},{2... | collective-permute-start | bytes 1572872 | tf_op jit(solution)/shard_map/ppermute | solution.py:487
  17.6 2.7 %shard_map.48 = (bf16[4,512,128]{2,1,0:T(8,128)(2,1)}, bf16[4,512,128]{2,1,0:T(8,128)(2,1)}, bf16[4,512,128]{2,1,0:T(8,128)(2,1)}) custom-call(s32[1]{0:T(128)} %bitcast.here_ref, s32[8,2,16]{2,1,0:T(2,128)S(1)} %bitcast.29, bf16[512,2048]{1,0:T(8,128)(2,1)S(1)} %bitcast.23), custom_call_target="tpu_custom_call" | custom-call | bytes 3145728 | tf_op jit(solution)/shard_map/pallas_call | solution.py:127
  20.3 0.0 collective-permute-done.picks_ref
  20.4 9.0 %shard_map.49 = bf16[16,528,128]{2,1,0:T(8,128)(2,1)} custom-call(s32[1]{0:T(128)} %bitcast.here_ref, bf16[512,2048]{1,0:T(8,128)(2,1)S(1)} %bitcast.24, bf16[512,2048]{1,0:T(8,128)(2,1)S(1)} %bitcast.9, bf16[512,2048]{1,0:T(8,128)(2,1)S(1)} %bitcast.16), custom_call_target="tpu_custom_call" | custom-call | flops 2147483648 | bytes 8388608 | tf_op jit(solution)/shard_map/pallas_call | solution.py:266
  29.3 0.6 collective-permute-start.4
  29.9 1.3 collective-permute-start.5
  31.2 2.1 %collective-permute-done.1.refs_0_ = bf16[8,512,128]{2,1,0:T(8,128)(2,1)S(1)} collective-permute-done((bf16[8,512,128]{2,1,0:T(8,128)(2,1)S(1)}, bf16[8,512,128]{2,1,0:T(8,128)(2,1)S(1)}, u32[]{:S(2)}, u32[]{:S(2)}) %collective-permute-start.1) | collective-permute-done | bytes 1048608 | tf_op jit(solution)/shard_map/ppermute | solution.py:484
  33.3 1.0 copy-done.9
  34.3 0.0 collective-permute-done.2.refs_0_
  34.3 3.3 %shard_map.50 = bf16[4,528,128]{2,1,0:T(8,128)(2,1)} custom-call(s32[1]{0:T(128)} %bitcast.here_ref, s32[8,2,16]{2,1,0:T(2,128)S(1)} %bitcast.30, bf16[512,2048]{1,0:T(8,128)(2,1)S(1)} %bitcast.10, bf16[512,2048]{1,0:T(8,128)(2,1)S(1)} %bitcast.17, bf16[4,512,128]{2,1,0:T(8,128)(2,1)S(1)} %collective-permute-done.2.refs_0_), custom_call_target="tpu_custom_call" | custom-call | flops 999999995904 | bytes 2097152 | tf_op jit(solution)/shard_map/pallas_call | solution.py:226
  37.6 1.3 collective-permute-start.10
  38.9 0.0 collective-permute-done.3.refs_0_
  38.9 0.0 copy-start.6
  39.0 3.9 %shard_map.51 = bf16[4,528,128]{2,1,0:T(8,128)(2,1)} custom-call(s32[1]{0:T(128)} %bitcast.here_ref, s32[8,2,16]{2,1,0:T(2,128)S(1)} %bitcast.31, bf16[512,2048]{1,0:T(8,128)(2,1)S(1)} %bitcast.11, bf16[512,2048]{1,0:T(8,128)(2,1)S(1)} %bitcast.18, bf16[4,512,128]{2,1,0:T(8,128)(2,1)} %collective-permute-done.3.refs_0_), custom_call_target="tpu_custom_call" | custom-call | flops 999999995904 | bytes 2097152 | tf_op jit(solution)/shard_map/pallas_call | solution.py:226
  42.8 1.3 collective-permute-start.11
  44.1 11.8 %collective-permute-done.4.refs_0_ = bf16[16,528,128]{2,1,0:T(8,128)(2,1)} collective-permute-done((bf16[16,528,128]{2,1,0:T(8,128)(2,1)}, bf16[16,528,128]{2,1,0:T(8,128)(2,1)}, u32[]{:S(2)}, u32[]{:S(2)}) %collective-permute-start.4) | collective-permute-done | bytes 2162720 | tf_op jit(solution)/shard_map/ppermute | solution.py:24
  55.9 2.1 %collective-permute-start.6 = (bf16[4,512,128]{2,1,0:T(8,128)(2,1)}, bf16[4,512,128]{2,1,0:T(8,128)(2,1)}, u32[]{:S(2)}, u32[]{:S(2)}) collective-permute-start(bf16[4,512,128]{2,1,0:T(8,128)(2,1)} %get-tuple-element.50), channel_id=1, source_target_pairs={{16,0},{20,4},{24,8},{28,12},{17,1},{21,5},{25,9},{29,13},{18,2},{... | collective-permute-start | bytes 1572872 | tf_op jit(solution)/shard_map/ppermute | solution.py:487
  58.0 2.1 %collective-permute-done.5.refs_1_ = bf16[8,512,128]{2,1,0:T(8,128)(2,1)} collective-permute-done((bf16[8,512,128]{2,1,0:T(8,128)(2,1)}, bf16[8,512,128]{2,1,0:T(8,128)(2,1)}, u32[]{:S(2)}, u32[]{:S(2)}) %collective-permute-start.5) | collective-permute-done | bytes 1048608 | tf_op jit(solution)/shard_map/ppermute | solution.py:484
  60.1 5.4 %shard_map.52 = bf16[8,528,128]{2,1,0:T(8,128)(2,1)} custom-call(s32[1]{0:T(128)} %bitcast.here_ref, s32[8,2,16]{2,1,0:T(2,128)S(1)} %bitcast.32, bf16[512,2048]{1,0:T(8,128)(2,1)S(1)} %bitcast.25, bf16[8,512,128]{2,1,0:T(8,128)(2,1)S(1)} %copy-done.10, bf16[8,512,128]{2,1,0:T(8,128)(2,1)} %collective-permute-done.5.refs_1_), custom_call_target="tpu_custom_call" | custom-call | flops 999999995904 | bytes 6291456 | tf_op jit(solution)/shard_map/pallas_call | solution.py:295
  65.4 0.0 collective-permute-start.7
  65.4 9.5 %collective-permute-start.8 = (bf16[4,512,128]{2,1,0:T(8,128)(2,1)}, bf16[4,512,128]{2,1,0:T(8,128)(2,1)}, u32[]{:S(2)}, u32[]{:S(2)}) collective-permute-start(bf16[4,512,128]{2,1,0:T(8,128)(2,1)} %get-tuple-element.52), channel_id=1, source_target_pairs={{4,0},{8,4},{12,8},{16,12},{20,16},{24,20},{28,24},{5,1},{9,5},{13... | collective-permute-start | bytes 1572872 | tf_op jit(solution)/shard_map/ppermute | solution.py:487
  74.9 0.0 collective-permute-done.6.refs_0_
  74.9 1.7 %collective-permute-start.9 = (bf16[4,512,128]{2,1,0:T(8,128)(2,1)}, bf16[4,512,128]{2,1,0:T(8,128)(2,1)}, u32[]{:S(2)}, u32[]{:S(2)}) collective-permute-start(bf16[4,512,128]{2,1,0:T(8,128)(2,1)} %get-tuple-element.54), channel_id=1, source_target_pairs={{28,0},{29,1},{30,2},{31,3}} | collective-permute-start | bytes 1572872 | tf_op jit(solution)/shard_map/ppermute | solution.py:487
  76.6 2.9 %shard_map.53 = bf16[4,528,128]{2,1,0:T(8,128)(2,1)S(1)} custom-call(s32[1]{0:T(128)} %bitcast.here_ref, s32[8,2,16]{2,1,0:T(2,128)S(1)} %bitcast.33, bf16[512,2048]{1,0:T(8,128)(2,1)S(1)} %bitcast.12, bf16[512,2048]{1,0:T(8,128)(2,1)S(1)} %bitcast.19, bf16[4,512,128]{2,1,0:T(8,128)(2,1)} %collective-permute-done.6.refs_0_), custom_call_target="tpu_custom_call" | custom-call | flops 999999995904 | bytes 2097152 | tf_op jit(solution)/shard_map/pallas_call | solution.py:226
  79.5 2.4 %collective-permute-done.7.refs_1_ = bf16[8,528,128]{2,1,0:T(8,128)(2,1)} collective-permute-done((bf16[8,528,128]{2,1,0:T(8,128)(2,1)}, bf16[8,528,128]{2,1,0:T(8,128)(2,1)}, u32[]{:S(2)}, u32[]{:S(2)}) %collective-permute-start.7) | collective-permute-done | bytes 1081376 | tf_op jit(solution)/shard_map/ppermute | solution.py:24
  81.9 1.3 collective-permute-start.12
  83.2 19.7 %collective-permute-done.8.refs_0_ = bf16[4,512,128]{2,1,0:T(8,128)(2,1)} collective-permute-done((bf16[4,512,128]{2,1,0:T(8,128)(2,1)}, bf16[4,512,128]{2,1,0:T(8,128)(2,1)}, u32[]{:S(2)}, u32[]{:S(2)}) %collective-permute-start.8) | collective-permute-done | bytes 524320 | tf_op jit(solution)/shard_map/ppermute | solution.py:487
  102.9 2.9 %shard_map.54 = bf16[4,528,128]{2,1,0:T(8,128)(2,1)S(1)} custom-call(s32[1]{0:T(128)} %bitcast.here_ref, s32[8,2,16]{2,1,0:T(2,128)S(1)} %bitcast.34, bf16[512,2048]{1,0:T(8,128)(2,1)S(1)} %bitcast.13, bf16[512,2048]{1,0:T(8,128)(2,1)S(1)} %bitcast.20, bf16[4,512,128]{2,1,0:T(8,128)(2,1)} %collective-permute-done.8.refs_0_), custom_call_target="tpu_custom_call" | custom-call | flops 536870912 | bytes 2097152 | tf_op jit(solution)/shard_map/pallas_call | solution.py:226
  105.8 0.0 collective-permute-done.9.refs_0_
  105.8 2.9 %shard_map.55 = bf16[4,528,128]{2,1,0:T(8,128)(2,1)S(1)} custom-call(s32[1]{0:T(128)} %bitcast.here_ref, s32[8,2,16]{2,1,0:T(2,128)S(1)} %bitcast.35, bf16[512,2048]{1,0:T(8,128)(2,1)S(1)} %bitcast.14, bf16[512,2048]{1,0:T(8,128)(2,1)S(1)} %bitcast.21, bf16[4,512,128]{2,1,0:T(8,128)(2,1)} %collective-permute-done.9.refs_0_), custom_call_target="tpu_custom_call" | custom-call | flops 536870912 | bytes 2097152 | tf_op jit(solution)/shard_map/pallas_call | solution.py:226
  108.8 0.7 collective-permute-start.14
  109.5 2.1 %collective-permute-start.13 = (bf16[4,528,128]{2,1,0:T(8,128)(2,1)S(1)}, bf16[4,528,128]{2,1,0:T(8,128)(2,1)S(1)}, u32[]{:S(2)}, u32[]{:S(2)}) collective-permute-start(bf16[4,528,128]{2,1,0:T(8,128)(2,1)S(1)} %shard_map.54), channel_id=1, source_target_pairs={{0,5},{1,6},{2,7},{3,4},{4,9},{5,10},{6,11},{7,8},{8,13},{9,14},{1... | collective-permute-start | bytes 1622024 | tf_op jit(solution)/shard_map/ppermute | solution.py:495
  111.6 0.0 collective-permute-done.10.refs_2_
  111.6 7.3 %shard_map.56 = (bf16[512,2048]{1,0:T(8,128)(2,1)}, f32[16,512,128]{2,1,0:T(8,128)S(1)}, f32[16,4,128]{2,1,0:T(4,128)S(1)}) custom-call(s32[1]{0:T(128)} %bitcast.here_ref, s32[8,2,16]{2,1,0:T(2,128)S(1)} %copy-done.8, bf16[16,528,128]{2,1,0:T(8,128)(2,1)} %collective-permute-done.4.refs_0_, bf16[8,528,128]{2,1,0:T(8,128)(2,1)} %collective-permute-done.7.refs_1_, ...), custom_call_target="tpu_custom_call" | custom-call | flops 6291456 | bytes 8388608 | tf_op jit(solution)/shard_map/pallas_call | solution.py:367
  118.9 10.5 %collective-permute-done.12.refs_0_ = bf16[4,528,128]{2,1,0:T(8,128)(2,1)S(1)} collective-permute-done((bf16[4,528,128]{2,1,0:T(8,128)(2,1)S(1)}, bf16[4,528,128]{2,1,0:T(8,128)(2,1)S(1)}, u32[]{:S(2)}, u32[]{:S(2)}) %collective-permute-start.12) | collective-permute-done | bytes 540704 | tf_op jit(solution)/shard_map/ppermute | solution.py:495
  129.4 0.0 collective-permute-done.14.refs_2_
  129.4 6.4 %collective-permute-done.13.refs_1_ = bf16[4,528,128]{2,1,0:T(8,128)(2,1)S(1)} collective-permute-done((bf16[4,528,128]{2,1,0:T(8,128)(2,1)S(1)}, bf16[4,528,128]{2,1,0:T(8,128)(2,1)S(1)}, u32[]{:S(2)}, u32[]{:S(2)}) %collective-permute-start.13) | collective-permute-done | bytes 540704 | tf_op jit(solution)/shard_map/ppermute | solution.py:495
  135.8 4.1 %shard_map.57 = bf16[512,2048]{1,0:T(8,128)(2,1)} custom-call(s32[1]{0:T(128)} %bitcast.here_ref, s32[8,2,16]{2,1,0:T(2,128)S(1)} %copy-done.8, f32[16,512,128]{2,1,0:T(8,128)S(1)} %get-tuple-element.56.mixed_ref, f32[16,4,128]{2,1,0:T(4,128)S(1)} %get-tuple-element.57.sums_ref, ...), custom_call_target="tpu_custom_call", output_to_operand_aliasing={{}: (7, {})} | custom-call | flops 1572864 | bytes 6291456 | tf_op jit(solution)/shard_map/pallas_call | solution.py:448
  (16 shorter events, 0.0 us)
Async XLA Ops:
  0.0 1.6 %copy-start = (bf16[1,512,2048]{2,1,0:T(8,128)(2,1)S(1)}, bf16[1,512,2048]{2,1,0:T(8,128)(2,1)}, u32[]{:S(2)}) copy-start(bf16[1,512,2048]{2,1,0:T(8,128)(2,1)} %param.5) | copy-start | bytes 6291460
  1.6 1.6 %copy-start.2 = (bf16[1,512,2048]{2,1,0:T(8,128)(2,1)S(1)}, bf16[1,512,2048]{2,1,0:T(8,128)(2,1)}, u32[]{:S(2)}) copy-start(bf16[1,512,2048]{2,1,0:T(8,128)(2,1)} %param.6) | copy-start | bytes 6291460
  3.2 0.7 copy-start.5
  3.9 3.9 %copy-start.4 = (bf16[1,512,2048]{2,1,0:T(8,128)(2,1)S(1)}, bf16[1,512,2048]{2,1,0:T(8,128)(2,1)}, u32[]{:S(2)}) copy-start(bf16[1,512,2048]{2,1,0:T(8,128)(2,1)} %param.4) | copy-start | bytes 6291460
  6.5 26.8 %collective-permute-start.1 = (bf16[8,512,128]{2,1,0:T(8,128)(2,1)S(1)}, bf16[8,512,128]{2,1,0:T(8,128)(2,1)S(1)}, u32[]{:S(2)}, u32[]{:S(2)}) collective-permute-start(bf16[8,512,128]{2,1,0:T(8,128)(2,1)S(1)} %get-tuple-element.32), channel_id=1, source_target_pairs={{0,8},{4,12},{8,16},{12,20},{16,24},{20,28},{1,9},{5,13},{9,17},{1... | collective-permute-start | bytes 3145736 | tf_op jit(solution)/shard_map/ppermute | solution.py:484
  7.8 12.5 %copy-start.1 = (bf16[1,512,2048]{2,1,0:T(8,128)(2,1)S(1)}, bf16[1,512,2048]{2,1,0:T(8,128)(2,1)}, u32[]{:S(2)}) copy-start(bf16[1,512,2048]{2,1,0:T(8,128)(2,1)} %param.5) | copy-start | bytes 6291460
  7.8 12.5 %copy-start.3 = (bf16[1,512,2048]{2,1,0:T(8,128)(2,1)S(1)}, bf16[1,512,2048]{2,1,0:T(8,128)(2,1)}, u32[]{:S(2)}) copy-start(bf16[1,512,2048]{2,1,0:T(8,128)(2,1)} %param.6) | copy-start | bytes 6291460
  9.9 24.3 %collective-permute-start.2 = (bf16[4,512,128]{2,1,0:T(8,128)(2,1)S(1)}, bf16[4,512,128]{2,1,0:T(8,128)(2,1)S(1)}, u32[]{:S(2)}, u32[]{:S(2)}) collective-permute-start(bf16[4,512,128]{2,1,0:T(8,128)(2,1)S(1)} %get-tuple-element.44), channel_id=1, source_target_pairs={{12,0},{16,4},{20,8},{24,12},{28,16},{13,1},{17,5},{21,9},{25,13},... | collective-permute-start | bytes 1572872 | tf_op jit(solution)/shard_map/ppermute | solution.py:487
  15.4 5.0 %collective-permute-start = (s32[8,2,16]{2,1,0:T(2,128)S(1)}, s32[8,2,16]{2,1,0:T(2,128)S(1)}, u32[]{:S(2)}, u32[]{:S(2)}) collective-permute-start(s32[8,2,16]{2,1,0:T(2,128)S(1)} %bitcast.28), channel_id=1, source_target_pairs={{0,1},{1,2},{2,3},{3,0},{4,5},{5,6},{6,7},{7,4},{8,9},{9,10},{10,1... | collective-permute-start | bytes 3080 | tf_op jit(solution)/shard_map/ppermute | solution.py:24
  15.4 23.5 %collective-permute-start.3 = (bf16[4,512,128]{2,1,0:T(8,128)(2,1)}, bf16[4,512,128]{2,1,0:T(8,128)(2,1)}, u32[]{:S(2)}, u32[]{:S(2)}) collective-permute-start(bf16[4,512,128]{2,1,0:T(8,128)(2,1)} %get-tuple-element.46), channel_id=1, source_target_pairs={{20,0},{24,4},{28,8},{21,1},{25,5},{29,9},{22,2},{26,6},{30,10},{2... | collective-permute-start | bytes 1572872 | tf_op jit(solution)/shard_map/ppermute | solution.py:487
  20.4 9.0 %copy-start.7 = (s32[8,2,16]{2,1,0:T(2,128)}, s32[8,2,16]{2,1,0:T(2,128)S(1)}, u32[]{:S(2)}) copy-start(s32[8,2,16]{2,1,0:T(2,128)S(1)} %collective-permute-done.picks_ref) | copy-start | bytes 3076
  29.3 26.6 %collective-permute-start.4 = (bf16[16,528,128]{2,1,0:T(8,128)(2,1)}, bf16[16,528,128]{2,1,0:T(8,128)(2,1)}, u32[]{:S(2)}, u32[]{:S(2)}) collective-permute-start(bf16[16,528,128]{2,1,0:T(8,128)(2,1)} %shard_map.49), channel_id=1, source_target_pairs={{0,1},{1,2},{2,3},{3,0},{4,5},{5,6},{6,7},{7,4},{8,9},{9,10},{10,1... | collective-permute-start | bytes 6488072 | tf_op jit(solution)/shard_map/ppermute | solution.py:24
  29.9 30.1 %collective-permute-start.5 = (bf16[8,512,128]{2,1,0:T(8,128)(2,1)}, bf16[8,512,128]{2,1,0:T(8,128)(2,1)}, u32[]{:S(2)}, u32[]{:S(2)}) collective-permute-start(bf16[8,512,128]{2,1,0:T(8,128)(2,1)} %get-tuple-element.48), channel_id=1, source_target_pairs={{0,24},{4,28},{1,25},{5,29},{2,26},{6,30},{3,27},{7,31}} | collective-permute-start | bytes 3145736 | tf_op jit(solution)/shard_map/ppermute | solution.py:484
  33.3 1.0 copy-start.9
  37.6 73.9 %collective-permute-start.10 = (bf16[4,528,128]{2,1,0:T(8,128)(2,1)}, bf16[4,528,128]{2,1,0:T(8,128)(2,1)}, u32[]{:S(2)}, u32[]{:S(2)}) collective-permute-start(bf16[4,528,128]{2,1,0:T(8,128)(2,1)} %shard_map.50), channel_id=1, source_target_pairs={{0,13},{1,14},{2,15},{3,12},{4,17},{5,18},{6,19},{7,16},{8,21},{9,... | collective-permute-start | bytes 1622024 | tf_op jit(solution)/shard_map/ppermute | solution.py:495
  38.9 21.1 %copy-start.6 = (s32[1,8,16,2]{2,3,1,0:T(2,128)S(1)}, s32[1,8,16,2]{2,3,1,0:T(2,128)}, u32[]{:S(2)}) copy-start(s32[1,8,16,2]{2,3,1,0:T(2,128)} %param.7) | copy-start | bytes 3076
  38.9 21.1 %copy-start.10 = (bf16[8,512,128]{2,1,0:T(8,128)(2,1)S(1)}, bf16[8,512,128]{2,1,0:T(8,128)(2,1)}, u32[]{:S(2)}) copy-start(bf16[8,512,128]{2,1,0:T(8,128)(2,1)} %copy-done.9) | copy-start | bytes 3145732
  42.8 68.7 %collective-permute-start.11 = (bf16[4,528,128]{2,1,0:T(8,128)(2,1)}, bf16[4,528,128]{2,1,0:T(8,128)(2,1)}, u32[]{:S(2)}, u32[]{:S(2)}) collective-permute-start(bf16[4,528,128]{2,1,0:T(8,128)(2,1)} %shard_map.51), channel_id=1, source_target_pairs={{0,21},{1,22},{2,23},{3,20},{4,25},{5,26},{6,27},{7,24},{8,29},{9,... | collective-permute-start | bytes 1622024 | tf_op jit(solution)/shard_map/ppermute | solution.py:495
  55.9 19.0 %collective-permute-start.6 = (bf16[4,512,128]{2,1,0:T(8,128)(2,1)}, bf16[4,512,128]{2,1,0:T(8,128)(2,1)}, u32[]{:S(2)}, u32[]{:S(2)}) collective-permute-start(bf16[4,512,128]{2,1,0:T(8,128)(2,1)} %get-tuple-element.50), channel_id=1, source_target_pairs={{16,0},{20,4},{24,8},{28,12},{17,1},{21,5},{25,9},{29,13},{18,2},{... | collective-permute-start | bytes 1572872 | tf_op jit(solution)/shard_map/ppermute | solution.py:487
  65.4 16.5 %collective-permute-start.7 = (bf16[8,528,128]{2,1,0:T(8,128)(2,1)}, bf16[8,528,128]{2,1,0:T(8,128)(2,1)}, u32[]{:S(2)}, u32[]{:S(2)}) collective-permute-start(bf16[8,528,128]{2,1,0:T(8,128)(2,1)} %shard_map.52), channel_id=1, source_target_pairs={{0,1},{1,2},{2,3},{3,0},{4,5},{5,6},{6,7},{7,4},{8,9},{9,10},{10,1... | collective-permute-start | bytes 3244040 | tf_op jit(solution)/shard_map/ppermute | solution.py:24
  65.4 37.5 %collective-permute-start.8 = (bf16[4,512,128]{2,1,0:T(8,128)(2,1)}, bf16[4,512,128]{2,1,0:T(8,128)(2,1)}, u32[]{:S(2)}, u32[]{:S(2)}) collective-permute-start(bf16[4,512,128]{2,1,0:T(8,128)(2,1)} %get-tuple-element.52), channel_id=1, source_target_pairs={{4,0},{8,4},{12,8},{16,12},{20,16},{24,20},{28,24},{5,1},{9,5},{13... | collective-permute-start | bytes 1572872 | tf_op jit(solution)/shard_map/ppermute | solution.py:487
  74.9 30.9 %collective-permute-start.9 = (bf16[4,512,128]{2,1,0:T(8,128)(2,1)}, bf16[4,512,128]{2,1,0:T(8,128)(2,1)}, u32[]{:S(2)}, u32[]{:S(2)}) collective-permute-start(bf16[4,512,128]{2,1,0:T(8,128)(2,1)} %get-tuple-element.54), channel_id=1, source_target_pairs={{28,0},{29,1},{30,2},{31,3}} | collective-permute-start | bytes 1572872 | tf_op jit(solution)/shard_map/ppermute | solution.py:487
  81.9 47.5 %collective-permute-start.12 = (bf16[4,528,128]{2,1,0:T(8,128)(2,1)S(1)}, bf16[4,528,128]{2,1,0:T(8,128)(2,1)S(1)}, u32[]{:S(2)}, u32[]{:S(2)}) collective-permute-start(bf16[4,528,128]{2,1,0:T(8,128)(2,1)S(1)} %shard_map.53), channel_id=1, source_target_pairs={{0,17},{1,18},{2,19},{3,16},{4,21},{5,22},{6,23},{7,20},{8,25},{9,... | collective-permute-start | bytes 1622024 | tf_op jit(solution)/shard_map/ppermute | solution.py:495
  105.8 5.8 %copy-start.8 = (s32[8,2,16]{2,1,0:T(2,128)S(1)}, s32[8,2,16]{2,1,0:T(2,128)}, u32[]{:S(2)}) copy-start(s32[8,2,16]{2,1,0:T(2,128)} %copy-done.7) | copy-start | bytes 3076
  108.8 20.6 %collective-permute-start.14 = (bf16[4,528,128]{2,1,0:T(8,128)(2,1)S(1)}, bf16[4,528,128]{2,1,0:T(8,128)(2,1)S(1)}, u32[]{:S(2)}, u32[]{:S(2)}) collective-permute-start(bf16[4,528,128]{2,1,0:T(8,128)(2,1)S(1)} %shard_map.55), channel_id=1, source_target_pairs={{0,29},{1,30},{2,31},{3,28}} | collective-permute-start | bytes 1622024 | tf_op jit(solution)/shard_map/ppermute | solution.py:495
  109.5 26.3 %collective-permute-start.13 = (bf16[4,528,128]{2,1,0:T(8,128)(2,1)S(1)}, bf16[4,528,128]{2,1,0:T(8,128)(2,1)S(1)}, u32[]{:S(2)}, u32[]{:S(2)}) collective-permute-start(bf16[4,528,128]{2,1,0:T(8,128)(2,1)S(1)} %shard_map.54), channel_id=1, source_target_pairs={{0,5},{1,6},{2,7},{3,4},{4,9},{5,10},{6,11},{7,8},{8,13},{9,14},{1... | collective-permute-start | bytes 1622024 | tf_op jit(solution)/shard_map/ppermute | solution.py:495

commit v19 on v18

--- a/solution.py
+++ b/solution.py
@@ -524,16 +524,16 @@
     returned[three] = up_and_on(part_three, three)
     part_five = work(after(here, part_three), five, is_anchor=True)
     returned[five] = up_and_on(part_five, five)
+    ask_for(one, arrived[three], arrived[five], part_five)
     ask_for(four, arrived[three], arrived[five], part_five, own_back, near[0])
     beside = near_part(after(here, part_five, own_back), own_picks, queries, near, near_shifts, slots)
-    ask_for(one, own_back, part_five, *near)
     ask_for(seven, own_back, part_five, *near)
     beside_back = passed_along(beside, "pipe", 1)
-    part_four = work(after(here, beside), four, is_anchor=True)
+    part_one = work(after(here, beside), one, is_anchor=True)
+    returned[one] = up_and_on(part_one, one)
+    part_four = work(after(here, part_one, beside_back), four)
     returned[four] = up_and_on(part_four, four)
-    part_one = work(after(here, part_four, beside_back), one)
-    returned[one] = up_and_on(part_one, one)
-    part_seven = work(after(here, part_one), seven)
+    part_seven = work(after(here, part_four), seven)
     returned[seven] = up_and_on(part_seven, seven)
     now = after(here, part_seven)
 

time: 143 us -> 147 us (1.028); the launches traced: 140 us -> 146 us
  starting transfers between devices: 30.7 us -> 40.9 us
  waiting for transfers between devices: 55 us -> 51.1 us
    ppermute x5, waiting for transfers between devices: 16.9 us -> 35.1 us  [up_and_on(): return lax.ppermute(value, ('ctx', 'pipe'), pairs)]
    ppermute x3, waiting for transfers between devices: 14.2 us -> 0.01 us  [passed_along(): return lax.ppermute(value, axis, pairs)]
    ppermute x5, starting transfers between devices: 20.8 us -> 30.9 us  [down(): lax.ppermute(value, 'ctx', [(at, at - shift) for at in range(shift, width)])]
    ppermute x5, waiting for transfers between devices: 19.7 us -> 10.3 us  [down(): lax.ppermute(value, 'ctx', [(at, at - shift) for at in range(shift, width)])]
    ppermute x2, waiting for transfers between devices: 4.13 us -> 5.7 us  [up(): lax.ppermute(value, 'ctx', [(at, at + shift) for at in range(width - shif...]
  transfers between devices with their start and end apart: 15 -> 15, of which waited for: 7 -> 6; matrix products, arithmetic and copies ran while one was open for 0% -> 0% of each run, Pallas kernels for 30% -> 29%
where the time goes in v19:
time: 147 us; the launch traced here: 146 us
  waiting for transfers between devices  51.1 us (35%)
  Pallas kernels  49.2 us (33%)
  starting transfers between devices  40.9 us (28%)
  local copies, waits for them, and re-layouts  4.91 us (3%)
    ppermute x5, waiting for transfers between devices, up_and_on(): return lax.ppermute(value, ('ctx', 'pipe'), pairs)  35.1 us
    ppermute x5, starting transfers between devices, down(): lax.ppermute(value, 'ctx', [(at, at - shift) for at in range(shift, width)])  30.9 us
    pallas_call x5, Pallas kernels, attend(): call(functools.partial(attend_kernel, group=group, slots=slots), [SCALARS...  16 us
    ppermute x5, waiting for transfers between devices, down(): lax.ppermute(value, 'ctx', [(at, at - shift) for at in range(shift, width)])  10.3 us
    pallas_call x1, Pallas kernels, own_part(): call(own_kernel, [SCALARS, IN_VMEM, IN_VMEM, IN_VMEM], jax.ShapeDtypeStru...  8.96 us
    pallas_call x3, Pallas kernels, pack(): call(functools.partial(pack_kernel, jobs=jobs, slots=slots), [SCALARS, SC...  7.45 us
    pallas_call x1, Pallas kernels, merge(): call(functools.partial(merge_kernel, places=tuple(places), shifts=shifts,...  7.27 us
    ppermute x5, starting transfers between devices, up_and_on(): return lax.ppermute(value, ('ctx', 'pipe'), pairs)  6.66 us
  transfers between devices with their start and end apart: 15, of which 6 were waited for; matrix products, arithmetic and copies ran while one was open for 0% of the time, Pallas kernels for 29%

profile of v19, /device:TPU:26, one launch (start us, length us, event | category | flops | bytes accessed | tf_op | source)
XLA Modules:
  0.0 146.5 jit_solution(11002736652357796790)
XLA Ops:
  0.0 1.6 %copy-done = bf16[1,512,2048]{2,1,0:T(8,128)(2,1)S(1)} copy-done((bf16[1,512,2048]{2,1,0:T(8,128)(2,1)S(1)}, bf16[1,512,2048]{2,1,0:T(8,128)(2,1)}, u32[]{:S(2)}) %copy-start) | copy-done | bytes 2097176
  1.6 1.6 %copy-done.2 = bf16[1,512,2048]{2,1,0:T(8,128)(2,1)S(1)} copy-done((bf16[1,512,2048]{2,1,0:T(8,128)(2,1)S(1)}, bf16[1,512,2048]{2,1,0:T(8,128)(2,1)}, u32[]{:S(2)}) %copy-start.2) | copy-done | bytes 2097176
  3.2 0.7 copy-done.5
  3.9 2.6 %shard_map.46 = (bf16[8,512,128]{2,1,0:T(8,128)(2,1)S(1)}, bf16[8,512,128]{2,1,0:T(8,128)(2,1)}) custom-call(s32[1]{0:T(128)} %bitcast.here_ref, s32[8,2,16]{2,1,0:T(2,128)S(1)} %bitcast.26, bf16[512,2048]{1,0:T(8,128)(2,1)S(1)} %bitcast.8, bf16[512,2048]{1,0:T(8,128)(2,1)S(1)} %bitcast.15), custom_call_target="tpu_custom_call" | custom-call | bytes 4194304 | tf_op jit(solution)/shard_map/pallas_call | solution.py:127
  6.5 1.3 collective-permute-start.1
  7.8 0.0 copy-start.1
  7.8 0.0 copy-start.3
  7.8 2.1 %shard_map.47 = (bf16[4,512,128]{2,1,0:T(8,128)(2,1)S(1)}, bf16[4,512,128]{2,1,0:T(8,128)(2,1)}) custom-call(s32[1]{0:T(128)} %bitcast.here_ref, s32[8,2,16]{2,1,0:T(2,128)S(1)} %bitcast.27, bf16[512,2048]{1,0:T(8,128)(2,1)S(1)} %bitcast.22), custom_call_target="tpu_custom_call" | custom-call | bytes 2097152 | tf_op jit(solution)/shard_map/pallas_call | solution.py:127
  9.9 5.4 %collective-permute-start.2 = (bf16[4,512,128]{2,1,0:T(8,128)(2,1)S(1)}, bf16[4,512,128]{2,1,0:T(8,128)(2,1)S(1)}, u32[]{:S(2)}, u32[]{:S(2)}) collective-permute-start(bf16[4,512,128]{2,1,0:T(8,128)(2,1)S(1)} %get-tuple-element.44), channel_id=1, source_target_pairs={{12,0},{16,4},{20,8},{24,12},{28,16},{13,1},{17,5},{21,9},{25,13},... | collective-permute-start | bytes 1572872 | tf_op jit(solution)/shard_map/ppermute | solution.py:487
  15.4 0.1 collective-permute-start
  15.4 2.1 %collective-permute-start.3 = (bf16[4,512,128]{2,1,0:T(8,128)(2,1)}, bf16[4,512,128]{2,1,0:T(8,128)(2,1)}, u32[]{:S(2)}, u32[]{:S(2)}) collective-permute-start(bf16[4,512,128]{2,1,0:T(8,128)(2,1)} %get-tuple-element.46), channel_id=1, source_target_pairs={{20,0},{24,4},{28,8},{21,1},{25,5},{29,9},{22,2},{26,6},{30,10},{2... | collective-permute-start | bytes 1572872 | tf_op jit(solution)/shard_map/ppermute | solution.py:487
  17.6 2.7 %shard_map.48 = (bf16[4,512,128]{2,1,0:T(8,128)(2,1)}, bf16[4,512,128]{2,1,0:T(8,128)(2,1)}, bf16[4,512,128]{2,1,0:T(8,128)(2,1)}) custom-call(s32[1]{0:T(128)} %bitcast.here_ref, s32[8,2,16]{2,1,0:T(2,128)S(1)} %bitcast.29, bf16[512,2048]{1,0:T(8,128)(2,1)S(1)} %bitcast.23), custom_call_target="tpu_custom_call" | custom-call | bytes 3145728 | tf_op jit(solution)/shard_map/pallas_call | solution.py:127
  20.3 0.0 collective-permute-done.picks_ref
  20.4 9.0 %shard_map.49 = bf16[16,528,128]{2,1,0:T(8,128)(2,1)} custom-call(s32[1]{0:T(128)} %bitcast.here_ref, bf16[512,2048]{1,0:T(8,128)(2,1)S(1)} %bitcast.24, bf16[512,2048]{1,0:T(8,128)(2,1)S(1)} %bitcast.9, bf16[512,2048]{1,0:T(8,128)(2,1)S(1)} %bitcast.16), custom_call_target="tpu_custom_call" | custom-call | flops 2147483648 | bytes 8388608 | tf_op jit(solution)/shard_map/pallas_call | solution.py:266
  29.3 0.6 collective-permute-start.4
  29.9 1.3 collective-permute-start.5
  31.2 2.1 %collective-permute-done.1.refs_0_ = bf16[8,512,128]{2,1,0:T(8,128)(2,1)S(1)} collective-permute-done((bf16[8,512,128]{2,1,0:T(8,128)(2,1)S(1)}, bf16[8,512,128]{2,1,0:T(8,128)(2,1)S(1)}, u32[]{:S(2)}, u32[]{:S(2)}) %collective-permute-start.1) | collective-permute-done | bytes 1048608 | tf_op jit(solution)/shard_map/ppermute | solution.py:484
  33.3 1.0 copy-done.9
  34.3 0.0 collective-permute-done.2.refs_0_
  34.3 3.3 %shard_map.50 = bf16[4,528,128]{2,1,0:T(8,128)(2,1)} custom-call(s32[1]{0:T(128)} %bitcast.here_ref, s32[8,2,16]{2,1,0:T(2,128)S(1)} %bitcast.30, bf16[512,2048]{1,0:T(8,128)(2,1)S(1)} %bitcast.10, bf16[512,2048]{1,0:T(8,128)(2,1)S(1)} %bitcast.17, bf16[4,512,128]{2,1,0:T(8,128)(2,1)S(1)} %collective-permute-done.2.refs_0_), custom_call_target="tpu_custom_call" | custom-call | flops 999999995904 | bytes 2097152 | tf_op jit(solution)/shard_map/pallas_call | solution.py:226
  37.6 1.3 collective-permute-start.10
  38.9 0.0 collective-permute-done.3.refs_0_
  38.9 0.0 copy-start.6
  39.0 3.9 %shard_map.51 = bf16[4,528,128]{2,1,0:T(8,128)(2,1)} custom-call(s32[1]{0:T(128)} %bitcast.here_ref, s32[8,2,16]{2,1,0:T(2,128)S(1)} %bitcast.31, bf16[512,2048]{1,0:T(8,128)(2,1)S(1)} %bitcast.11, bf16[512,2048]{1,0:T(8,128)(2,1)S(1)} %bitcast.18, bf16[4,512,128]{2,1,0:T(8,128)(2,1)} %collective-permute-done.3.refs_0_), custom_call_target="tpu_custom_call" | custom-call | flops 999999995904 | bytes 2097152 | tf_op jit(solution)/shard_map/pallas_call | solution.py:226
  42.8 1.3 collective-permute-start.11
  44.1 12.3 %collective-permute-start.6 = (bf16[4,512,128]{2,1,0:T(8,128)(2,1)}, bf16[4,512,128]{2,1,0:T(8,128)(2,1)}, u32[]{:S(2)}, u32[]{:S(2)}) collective-permute-start(bf16[4,512,128]{2,1,0:T(8,128)(2,1)} %get-tuple-element.50), channel_id=1, source_target_pairs={{4,0},{8,4},{12,8},{16,12},{20,16},{24,20},{28,24},{5,1},{9,5},{13... | collective-permute-start | bytes 1572872 | tf_op jit(solution)/shard_map/ppermute | solution.py:487
  56.4 0.0 collective-permute-done.4.refs_0_
  56.4 3.6 %collective-permute-done.5.refs_1_ = bf16[8,512,128]{2,1,0:T(8,128)(2,1)} collective-permute-done((bf16[8,512,128]{2,1,0:T(8,128)(2,1)}, bf16[8,512,128]{2,1,0:T(8,128)(2,1)}, u32[]{:S(2)}, u32[]{:S(2)}) %collective-permute-start.5) | collective-permute-done | bytes 1048608 | tf_op jit(solution)/shard_map/ppermute | solution.py:484
  60.0 5.4 %shard_map.52 = bf16[8,528,128]{2,1,0:T(8,128)(2,1)} custom-call(s32[1]{0:T(128)} %bitcast.here_ref, s32[8,2,16]{2,1,0:T(2,128)S(1)} %bitcast.32, bf16[512,2048]{1,0:T(8,128)(2,1)S(1)} %bitcast.25, bf16[8,512,128]{2,1,0:T(8,128)(2,1)S(1)} %copy-done.10, bf16[8,512,128]{2,1,0:T(8,128)(2,1)} %collective-permute-done.5.refs_1_), custom_call_target="tpu_custom_call" | custom-call | flops 999999995904 | bytes 6291456 | tf_op jit(solution)/shard_map/pallas_call | solution.py:295
  65.4 0.0 collective-permute-start.7
  65.4 9.5 %collective-permute-start.8 = (bf16[4,512,128]{2,1,0:T(8,128)(2,1)}, bf16[4,512,128]{2,1,0:T(8,128)(2,1)}, u32[]{:S(2)}, u32[]{:S(2)}) collective-permute-start(bf16[4,512,128]{2,1,0:T(8,128)(2,1)} %get-tuple-element.52), channel_id=1, source_target_pairs={{16,0},{20,4},{24,8},{28,12},{17,1},{21,5},{25,9},{29,13},{18,2},{... | collective-permute-start | bytes 1572872 | tf_op jit(solution)/shard_map/ppermute | solution.py:487
  74.9 7.8 %collective-permute-done.6.refs_0_ = bf16[4,512,128]{2,1,0:T(8,128)(2,1)} collective-permute-done((bf16[4,512,128]{2,1,0:T(8,128)(2,1)}, bf16[4,512,128]{2,1,0:T(8,128)(2,1)}, u32[]{:S(2)}, u32[]{:S(2)}) %collective-permute-start.6) | collective-permute-done | bytes 524320 | tf_op jit(solution)/shard_map/ppermute | solution.py:487
  82.8 1.6 %collective-permute-start.9 = (bf16[4,512,128]{2,1,0:T(8,128)(2,1)}, bf16[4,512,128]{2,1,0:T(8,128)(2,1)}, u32[]{:S(2)}, u32[]{:S(2)}) collective-permute-start(bf16[4,512,128]{2,1,0:T(8,128)(2,1)} %get-tuple-element.54), channel_id=1, source_target_pairs={{28,0},{29,1},{30,2},{31,3}} | collective-permute-start | bytes 1572872 | tf_op jit(solution)/shard_map/ppermute | solution.py:487
  84.4 2.9 %shard_map.53 = bf16[4,528,128]{2,1,0:T(8,128)(2,1)S(1)} custom-call(s32[1]{0:T(128)} %bitcast.here_ref, s32[8,2,16]{2,1,0:T(2,128)S(1)} %bitcast.33, bf16[512,2048]{1,0:T(8,128)(2,1)S(1)} %bitcast.12, bf16[512,2048]{1,0:T(8,128)(2,1)S(1)} %bitcast.19, bf16[4,512,128]{2,1,0:T(8,128)(2,1)} %collective-permute-done.6.refs_0_), custom_call_target="tpu_custom_call" | custom-call | flops 999999995904 | bytes 2097152 | tf_op jit(solution)/shard_map/pallas_call | solution.py:226
  87.3 0.0 collective-permute-done.7.refs_1_
  87.3 2.1 %collective-permute-start.13 = (bf16[4,528,128]{2,1,0:T(8,128)(2,1)S(1)}, bf16[4,528,128]{2,1,0:T(8,128)(2,1)S(1)}, u32[]{:S(2)}, u32[]{:S(2)}) collective-permute-start(bf16[4,528,128]{2,1,0:T(8,128)(2,1)S(1)} %shard_map.53), channel_id=1, source_target_pairs={{0,5},{1,6},{2,7},{3,4},{4,9},{5,10},{6,11},{7,8},{8,13},{9,14},{1... | collective-permute-start | bytes 1622024 | tf_op jit(solution)/shard_map/ppermute | solution.py:495
  89.5 2.4 %collective-permute-done.8.refs_0_ = bf16[4,512,128]{2,1,0:T(8,128)(2,1)} collective-permute-done((bf16[4,512,128]{2,1,0:T(8,128)(2,1)}, bf16[4,512,128]{2,1,0:T(8,128)(2,1)}, u32[]{:S(2)}, u32[]{:S(2)}) %collective-permute-start.8) | collective-permute-done | bytes 524320 | tf_op jit(solution)/shard_map/ppermute | solution.py:487
  91.9 2.9 %shard_map.54 = bf16[4,528,128]{2,1,0:T(8,128)(2,1)S(1)} custom-call(s32[1]{0:T(128)} %bitcast.here_ref, s32[8,2,16]{2,1,0:T(2,128)S(1)} %bitcast.34, bf16[512,2048]{1,0:T(8,128)(2,1)S(1)} %bitcast.13, bf16[512,2048]{1,0:T(8,128)(2,1)S(1)} %bitcast.20, bf16[4,512,128]{2,1,0:T(8,128)(2,1)} %collective-permute-done.8.refs_0_), custom_call_target="tpu_custom_call" | custom-call | flops 536870912 | bytes 2097152 | tf_op jit(solution)/shard_map/pallas_call | solution.py:226
  94.8 0.0 collective-permute-done.9.refs_0_
  94.8 2.9 %shard_map.55 = bf16[4,528,128]{2,1,0:T(8,128)(2,1)S(1)} custom-call(s32[1]{0:T(128)} %bitcast.here_ref, s32[8,2,16]{2,1,0:T(2,128)S(1)} %bitcast.35, bf16[512,2048]{1,0:T(8,128)(2,1)S(1)} %bitcast.14, bf16[512,2048]{1,0:T(8,128)(2,1)S(1)} %bitcast.21, bf16[4,512,128]{2,1,0:T(8,128)(2,1)} %collective-permute-done.9.refs_0_), custom_call_target="tpu_custom_call" | custom-call | flops 536870912 | bytes 2097152 | tf_op jit(solution)/shard_map/pallas_call | solution.py:226
  97.8 0.7 collective-permute-start.14
  98.5 1.3 collective-permute-start.12
  99.8 0.0 collective-permute-done.10.refs_2_
  99.8 7.3 %shard_map.56 = (bf16[512,2048]{1,0:T(8,128)(2,1)}, f32[16,512,128]{2,1,0:T(8,128)S(1)}, f32[16,4,128]{2,1,0:T(4,128)S(1)}) custom-call(s32[1]{0:T(128)} %bitcast.here_ref, s32[8,2,16]{2,1,0:T(2,128)S(1)} %copy-done.8, bf16[16,528,128]{2,1,0:T(8,128)(2,1)} %collective-permute-done.4.refs_0_, bf16[8,528,128]{2,1,0:T(8,128)(2,1)} %collective-permute-done.7.refs_1_, ...), custom_call_target="tpu_custom_call" | custom-call | flops 6291456 | bytes 8388608 | tf_op jit(solution)/shard_map/pallas_call | solution.py:367
  107.1 17.0 %collective-permute-done.13.refs_1_ = bf16[4,528,128]{2,1,0:T(8,128)(2,1)S(1)} collective-permute-done((bf16[4,528,128]{2,1,0:T(8,128)(2,1)S(1)}, bf16[4,528,128]{2,1,0:T(8,128)(2,1)S(1)}, u32[]{:S(2)}, u32[]{:S(2)}) %collective-permute-start.13) | collective-permute-done | bytes 540704 | tf_op jit(solution)/shard_map/ppermute | solution.py:495
  124.0 0.0 collective-permute-done.14.refs_2_
  124.0 18.2 %collective-permute-done.12.refs_0_ = bf16[4,528,128]{2,1,0:T(8,128)(2,1)S(1)} collective-permute-done((bf16[4,528,128]{2,1,0:T(8,128)(2,1)S(1)}, bf16[4,528,128]{2,1,0:T(8,128)(2,1)S(1)}, u32[]{:S(2)}, u32[]{:S(2)}) %collective-permute-start.12) | collective-permute-done | bytes 540704 | tf_op jit(solution)/shard_map/ppermute | solution.py:495
  142.2 4.1 %shard_map.57 = bf16[512,2048]{1,0:T(8,128)(2,1)} custom-call(s32[1]{0:T(128)} %bitcast.here_ref, s32[8,2,16]{2,1,0:T(2,128)S(1)} %copy-done.8, f32[16,512,128]{2,1,0:T(8,128)S(1)} %get-tuple-element.56.mixed_ref, f32[16,4,128]{2,1,0:T(4,128)S(1)} %get-tuple-element.57.sums_ref, ...), custom_call_target="tpu_custom_call", output_to_operand_aliasing={{}: (7, {})} | custom-call | flops 1572864 | bytes 6291456 | tf_op jit(solution)/shard_map/pallas_call | solution.py:448
  (16 shorter events, 0.0 us)
Async XLA Ops:
  0.0 1.6 %copy-start = (bf16[1,512,2048]{2,1,0:T(8,128)(2,1)S(1)}, bf16[1,512,2048]{2,1,0:T(8,128)(2,1)}, u32[]{:S(2)}) copy-start(bf16[1,512,2048]{2,1,0:T(8,128)(2,1)} %param.5) | copy-start | bytes 6291460
  1.6 1.6 %copy-start.2 = (bf16[1,512,2048]{2,1,0:T(8,128)(2,1)S(1)}, bf16[1,512,2048]{2,1,0:T(8,128)(2,1)}, u32[]{:S(2)}) copy-start(bf16[1,512,2048]{2,1,0:T(8,128)(2,1)} %param.6) | copy-start | bytes 6291460
  3.2 0.7 copy-start.5
  3.9 3.9 %copy-start.4 = (bf16[1,512,2048]{2,1,0:T(8,128)(2,1)S(1)}, bf16[1,512,2048]{2,1,0:T(8,128)(2,1)}, u32[]{:S(2)}) copy-start(bf16[1,512,2048]{2,1,0:T(8,128)(2,1)} %param.4) | copy-start | bytes 6291460
  6.5 26.8 %collective-permute-start.1 = (bf16[8,512,128]{2,1,0:T(8,128)(2,1)S(1)}, bf16[8,512,128]{2,1,0:T(8,128)(2,1)S(1)}, u32[]{:S(2)}, u32[]{:S(2)}) collective-permute-start(bf16[8,512,128]{2,1,0:T(8,128)(2,1)S(1)} %get-tuple-element.32), channel_id=1, source_target_pairs={{0,8},{4,12},{8,16},{12,20},{16,24},{20,28},{1,9},{5,13},{9,17},{1... | collective-permute-start | bytes 3145736 | tf_op jit(solution)/shard_map/ppermute | solution.py:484
  7.8 12.5 %copy-start.1 = (bf16[1,512,2048]{2,1,0:T(8,128)(2,1)S(1)}, bf16[1,512,2048]{2,1,0:T(8,128)(2,1)}, u32[]{:S(2)}) copy-start(bf16[1,512,2048]{2,1,0:T(8,128)(2,1)} %param.5) | copy-start | bytes 6291460
  7.8 12.5 %copy-start.3 = (bf16[1,512,2048]{2,1,0:T(8,128)(2,1)S(1)}, bf16[1,512,2048]{2,1,0:T(8,128)(2,1)}, u32[]{:S(2)}) copy-start(bf16[1,512,2048]{2,1,0:T(8,128)(2,1)} %param.6) | copy-start | bytes 6291460
  9.9 24.3 %collective-permute-start.2 = (bf16[4,512,128]{2,1,0:T(8,128)(2,1)S(1)}, bf16[4,512,128]{2,1,0:T(8,128)(2,1)S(1)}, u32[]{:S(2)}, u32[]{:S(2)}) collective-permute-start(bf16[4,512,128]{2,1,0:T(8,128)(2,1)S(1)} %get-tuple-element.44), channel_id=1, source_target_pairs={{12,0},{16,4},{20,8},{24,12},{28,16},{13,1},{17,5},{21,9},{25,13},... | collective-permute-start | bytes 1572872 | tf_op jit(solution)/shard_map/ppermute | solution.py:487
  15.4 4.9 %collective-permute-start = (s32[8,2,16]{2,1,0:T(2,128)S(1)}, s32[8,2,16]{2,1,0:T(2,128)S(1)}, u32[]{:S(2)}, u32[]{:S(2)}) collective-permute-start(s32[8,2,16]{2,1,0:T(2,128)S(1)} %bitcast.28), channel_id=1, source_target_pairs={{0,1},{1,2},{2,3},{3,0},{4,5},{5,6},{6,7},{7,4},{8,9},{9,10},{10,1... | collective-permute-start | bytes 3080 | tf_op jit(solution)/shard_map/ppermute | solution.py:24
  15.4 23.5 %collective-permute-start.3 = (bf16[4,512,128]{2,1,0:T(8,128)(2,1)}, bf16[4,512,128]{2,1,0:T(8,128)(2,1)}, u32[]{:S(2)}, u32[]{:S(2)}) collective-permute-start(bf16[4,512,128]{2,1,0:T(8,128)(2,1)} %get-tuple-element.46), channel_id=1, source_target_pairs={{20,0},{24,4},{28,8},{21,1},{25,5},{29,9},{22,2},{26,6},{30,10},{2... | collective-permute-start | bytes 1572872 | tf_op jit(solution)/shard_map/ppermute | solution.py:487
  20.3 9.0 %copy-start.7 = (s32[8,2,16]{2,1,0:T(2,128)}, s32[8,2,16]{2,1,0:T(2,128)S(1)}, u32[]{:S(2)}) copy-start(s32[8,2,16]{2,1,0:T(2,128)S(1)} %collective-permute-done.picks_ref) | copy-start | bytes 3076
  29.3 27.1 %collective-permute-start.4 = (bf16[16,528,128]{2,1,0:T(8,128)(2,1)}, bf16[16,528,128]{2,1,0:T(8,128)(2,1)}, u32[]{:S(2)}, u32[]{:S(2)}) collective-permute-start(bf16[16,528,128]{2,1,0:T(8,128)(2,1)} %shard_map.49), channel_id=1, source_target_pairs={{0,1},{1,2},{2,3},{3,0},{4,5},{5,6},{6,7},{7,4},{8,9},{9,10},{10,1... | collective-permute-start | bytes 6488072 | tf_op jit(solution)/shard_map/ppermute | solution.py:24
  29.9 30.1 %collective-permute-start.5 = (bf16[8,512,128]{2,1,0:T(8,128)(2,1)}, bf16[8,512,128]{2,1,0:T(8,128)(2,1)}, u32[]{:S(2)}, u32[]{:S(2)}) collective-permute-start(bf16[8,512,128]{2,1,0:T(8,128)(2,1)} %get-tuple-element.48), channel_id=1, source_target_pairs={{0,24},{4,28},{1,25},{5,29},{2,26},{6,30},{3,27},{7,31}} | collective-permute-start | bytes 3145736 | tf_op jit(solution)/shard_map/ppermute | solution.py:484
  33.3 1.0 copy-start.9
  37.6 62.1 %collective-permute-start.10 = (bf16[4,528,128]{2,1,0:T(8,128)(2,1)}, bf16[4,528,128]{2,1,0:T(8,128)(2,1)}, u32[]{:S(2)}, u32[]{:S(2)}) collective-permute-start(bf16[4,528,128]{2,1,0:T(8,128)(2,1)} %shard_map.50), channel_id=1, source_target_pairs={{0,13},{1,14},{2,15},{3,12},{4,17},{5,18},{6,19},{7,16},{8,21},{9,... | collective-permute-start | bytes 1622024 | tf_op jit(solution)/shard_map/ppermute | solution.py:495
  38.9 21.1 %copy-start.6 = (s32[1,8,16,2]{2,3,1,0:T(2,128)S(1)}, s32[1,8,16,2]{2,3,1,0:T(2,128)}, u32[]{:S(2)}) copy-start(s32[1,8,16,2]{2,3,1,0:T(2,128)} %param.7) | copy-start | bytes 3076
  38.9 21.1 %copy-start.10 = (bf16[8,512,128]{2,1,0:T(8,128)(2,1)S(1)}, bf16[8,512,128]{2,1,0:T(8,128)(2,1)}, u32[]{:S(2)}) copy-start(bf16[8,512,128]{2,1,0:T(8,128)(2,1)} %copy-done.9) | copy-start | bytes 3145732
  42.8 56.9 %collective-permute-start.11 = (bf16[4,528,128]{2,1,0:T(8,128)(2,1)}, bf16[4,528,128]{2,1,0:T(8,128)(2,1)}, u32[]{:S(2)}, u32[]{:S(2)}) collective-permute-start(bf16[4,528,128]{2,1,0:T(8,128)(2,1)} %shard_map.51), channel_id=1, source_target_pairs={{0,21},{1,22},{2,23},{3,20},{4,25},{5,26},{6,27},{7,24},{8,29},{9,... | collective-permute-start | bytes 1622024 | tf_op jit(solution)/shard_map/ppermute | solution.py:495
  44.1 38.6 %collective-permute-start.6 = (bf16[4,512,128]{2,1,0:T(8,128)(2,1)}, bf16[4,512,128]{2,1,0:T(8,128)(2,1)}, u32[]{:S(2)}, u32[]{:S(2)}) collective-permute-start(bf16[4,512,128]{2,1,0:T(8,128)(2,1)} %get-tuple-element.50), channel_id=1, source_target_pairs={{4,0},{8,4},{12,8},{16,12},{20,16},{24,20},{28,24},{5,1},{9,5},{13... | collective-permute-start | bytes 1572872 | tf_op jit(solution)/shard_map/ppermute | solution.py:487
  65.4 21.9 %collective-permute-start.7 = (bf16[8,528,128]{2,1,0:T(8,128)(2,1)}, bf16[8,528,128]{2,1,0:T(8,128)(2,1)}, u32[]{:S(2)}, u32[]{:S(2)}) collective-permute-start(bf16[8,528,128]{2,1,0:T(8,128)(2,1)} %shard_map.52), channel_id=1, source_target_pairs={{0,1},{1,2},{2,3},{3,0},{4,5},{5,6},{6,7},{7,4},{8,9},{9,10},{10,1... | collective-permute-start | bytes 3244040 | tf_op jit(solution)/shard_map/ppermute | solution.py:24
  65.4 26.5 %collective-permute-start.8 = (bf16[4,512,128]{2,1,0:T(8,128)(2,1)}, bf16[4,512,128]{2,1,0:T(8,128)(2,1)}, u32[]{:S(2)}, u32[]{:S(2)}) collective-permute-start(bf16[4,512,128]{2,1,0:T(8,128)(2,1)} %get-tuple-element.52), channel_id=1, source_target_pairs={{16,0},{20,4},{24,8},{28,12},{17,1},{21,5},{25,9},{29,13},{18,2},{... | collective-permute-start | bytes 1572872 | tf_op jit(solution)/shard_map/ppermute | solution.py:487
  82.8 12.0 %collective-permute-start.9 = (bf16[4,512,128]{2,1,0:T(8,128)(2,1)}, bf16[4,512,128]{2,1,0:T(8,128)(2,1)}, u32[]{:S(2)}, u32[]{:S(2)}) collective-permute-start(bf16[4,512,128]{2,1,0:T(8,128)(2,1)} %get-tuple-element.54), channel_id=1, source_target_pairs={{28,0},{29,1},{30,2},{31,3}} | collective-permute-start | bytes 1572872 | tf_op jit(solution)/shard_map/ppermute | solution.py:487
  87.3 36.7 %collective-permute-start.13 = (bf16[4,528,128]{2,1,0:T(8,128)(2,1)S(1)}, bf16[4,528,128]{2,1,0:T(8,128)(2,1)S(1)}, u32[]{:S(2)}, u32[]{:S(2)}) collective-permute-start(bf16[4,528,128]{2,1,0:T(8,128)(2,1)S(1)} %shard_map.53), channel_id=1, source_target_pairs={{0,5},{1,6},{2,7},{3,4},{4,9},{5,10},{6,11},{7,8},{8,13},{9,14},{1... | collective-permute-start | bytes 1622024 | tf_op jit(solution)/shard_map/ppermute | solution.py:495
  94.8 5.0 %copy-start.8 = (s32[8,2,16]{2,1,0:T(2,128)S(1)}, s32[8,2,16]{2,1,0:T(2,128)}, u32[]{:S(2)}) copy-start(s32[8,2,16]{2,1,0:T(2,128)} %copy-done.7) | copy-start | bytes 3076
  97.8 26.3 %collective-permute-start.14 = (bf16[4,528,128]{2,1,0:T(8,128)(2,1)S(1)}, bf16[4,528,128]{2,1,0:T(8,128)(2,1)S(1)}, u32[]{:S(2)}, u32[]{:S(2)}) collective-permute-start(bf16[4,528,128]{2,1,0:T(8,128)(2,1)S(1)} %shard_map.55), channel_id=1, source_target_pairs={{0,29},{1,30},{2,31},{3,28}} | collective-permute-start | bytes 1622024 | tf_op jit(solution)/shard_map/ppermute | solution.py:495
  98.5 43.7 %collective-permute-start.12 = (bf16[4,528,128]{2,1,0:T(8,128)(2,1)S(1)}, bf16[4,528,128]{2,1,0:T(8,128)(2,1)S(1)}, u32[]{:S(2)}, u32[]{:S(2)}) collective-permute-start(bf16[4,528,128]{2,1,0:T(8,128)(2,1)S(1)} %shard_map.54), channel_id=1, source_target_pairs={{0,17},{1,18},{2,19},{3,16},{4,21},{5,22},{6,23},{7,20},{8,25},{9,... | collective-permute-start | bytes 1622024 | tf_op jit(solution)/shard_map/ppermute | solution.py:495

commit v20 on v18

--- a/solution.py
+++ b/solution.py
@@ -526,16 +526,16 @@
     returned[five] = up_and_on(part_five, five)
     ask_for(four, arrived[three], arrived[five], part_five, own_back, near[0])
     beside = near_part(after(here, part_five, own_back), own_picks, queries, near, near_shifts, slots)
+    ask_for(seven, own_back, part_five, *near)
     ask_for(one, own_back, part_five, *near)
-    ask_for(seven, own_back, part_five, *near)
     beside_back = passed_along(beside, "pipe", 1)
     part_four = work(after(here, beside), four, is_anchor=True)
     returned[four] = up_and_on(part_four, four)
-    part_one = work(after(here, part_four, beside_back), one)
+    part_seven = work(after(here, part_four, beside_back), seven)
+    returned[seven] = up_and_on(part_seven, seven)
+    part_one = work(after(here, part_seven), one)
     returned[one] = up_and_on(part_one, one)
-    part_seven = work(after(here, part_one), seven)
-    returned[seven] = up_and_on(part_seven, seven)
-    now = after(here, part_seven)
+    now = after(here, part_one)
 
     merged_shifts = near_shifts + (three, five)
     places = [HEADS + place * slots for place in (2, 3)]

time: 143 us -> 141 us (0.986)
  waiting for transfers between devices: 55 us -> 37.7 us
  starting transfers between devices: 30.7 us -> 46.7 us
    ppermute x5, starting transfers between devices: 20.8 us -> 37 us  [down(): lax.ppermute(value, 'ctx', [(at, at - shift) for at in range(shift, width)])]
    ppermute x5, waiting for transfers between devices: 19.7 us -> 5.64 us  [down(): lax.ppermute(value, 'ctx', [(at, at - shift) for at in range(shift, width)])]
    ppermute x3, waiting for transfers between devices: 14.2 us -> 11.8 us  [passed_along(): return lax.ppermute(value, axis, pairs)]
  transfers between devices with their start and end apart: 15 -> 15, of which waited for: 7 -> 6; matrix products, arithmetic and copies ran while one was open for 0% -> 0% of each run, Pallas kernels for 30% -> 31%
where the time goes in v20:
time: 141 us; the launch traced here: 139 us
  Pallas kernels  49.1 us (35%)
  starting transfers between devices  46.7 us (33%)
  waiting for transfers between devices  37.7 us (27%)
  local copies, waits for them, and re-layouts  4.91 us (3%)
    ppermute x5, starting transfers between devices, down(): lax.ppermute(value, 'ctx', [(at, at - shift) for at in range(shift, width)])  37 us
    ppermute x5, waiting for transfers between devices, up_and_on(): return lax.ppermute(value, ('ctx', 'pipe'), pairs)  16.1 us
    pallas_call x5, Pallas kernels, attend(): call(functools.partial(attend_kernel, group=group, slots=slots), [SCALARS...  16 us
    ppermute x3, waiting for transfers between devices, passed_along(): return lax.ppermute(value, axis, pairs)  11.8 us
    pallas_call x1, Pallas kernels, own_part(): call(own_kernel, [SCALARS, IN_VMEM, IN_VMEM, IN_VMEM], jax.ShapeDtypeStru...  8.96 us
    pallas_call x3, Pallas kernels, pack(): call(functools.partial(pack_kernel, jobs=jobs, slots=slots), [SCALARS, SC...  7.44 us
    pallas_call x1, Pallas kernels, merge(): call(functools.partial(merge_kernel, places=tuple(places), shifts=shifts,...  7.28 us
    ppermute x5, starting transfers between devices, up_and_on(): return lax.ppermute(value, ('ctx', 'pipe'), pairs)  6.47 us
  transfers between devices with their start and end apart: 15, of which 6 were waited for; matrix products, arithmetic and copies ran while one was open for 0% of the time, Pallas kernels for 31%

profile of v20, /device:TPU:26, one launch (start us, length us, event | category | flops | bytes accessed | tf_op | source)
XLA Modules:
  0.0 138.9 jit_solution(7864749141696953700)
XLA Ops:
  0.0 1.6 %copy-done = bf16[1,512,2048]{2,1,0:T(8,128)(2,1)S(1)} copy-done((bf16[1,512,2048]{2,1,0:T(8,128)(2,1)S(1)}, bf16[1,512,2048]{2,1,0:T(8,128)(2,1)}, u32[]{:S(2)}) %copy-start) | copy-done | bytes 2097176
  1.6 1.6 %copy-done.2 = bf16[1,512,2048]{2,1,0:T(8,128)(2,1)S(1)} copy-done((bf16[1,512,2048]{2,1,0:T(8,128)(2,1)S(1)}, bf16[1,512,2048]{2,1,0:T(8,128)(2,1)}, u32[]{:S(2)}) %copy-start.2) | copy-done | bytes 2097176
  3.2 0.7 copy-done.5
  3.9 2.6 %shard_map.46 = (bf16[8,512,128]{2,1,0:T(8,128)(2,1)S(1)}, bf16[8,512,128]{2,1,0:T(8,128)(2,1)}) custom-call(s32[1]{0:T(128)} %bitcast.here_ref, s32[8,2,16]{2,1,0:T(2,128)S(1)} %bitcast.26, bf16[512,2048]{1,0:T(8,128)(2,1)S(1)} %bitcast.8, bf16[512,2048]{1,0:T(8,128)(2,1)S(1)} %bitcast.15), custom_call_target="tpu_custom_call" | custom-call | bytes 4194304 | tf_op jit(solution)/shard_map/pallas_call | solution.py:127
  6.5 1.3 collective-permute-start.1
  7.8 0.0 copy-start.1
  7.8 0.0 copy-start.3
  7.8 2.1 %shard_map.47 = (bf16[4,512,128]{2,1,0:T(8,128)(2,1)S(1)}, bf16[4,512,128]{2,1,0:T(8,128)(2,1)}) custom-call(s32[1]{0:T(128)} %bitcast.here_ref, s32[8,2,16]{2,1,0:T(2,128)S(1)} %bitcast.27, bf16[512,2048]{1,0:T(8,128)(2,1)S(1)} %bitcast.22), custom_call_target="tpu_custom_call" | custom-call | bytes 2097152 | tf_op jit(solution)/shard_map/pallas_call | solution.py:127
  9.9 5.4 %collective-permute-start.2 = (bf16[4,512,128]{2,1,0:T(8,128)(2,1)S(1)}, bf16[4,512,128]{2,1,0:T(8,128)(2,1)S(1)}, u32[]{:S(2)}, u32[]{:S(2)}) collective-permute-start(bf16[4,512,128]{2,1,0:T(8,128)(2,1)S(1)} %get-tuple-element.44), channel_id=1, source_target_pairs={{12,0},{16,4},{20,8},{24,12},{28,16},{13,1},{17,5},{21,9},{25,13},... | collective-permute-start | bytes 1572872 | tf_op jit(solution)/shard_map/ppermute | solution.py:487
  15.4 0.1 collective-permute-start
  15.4 2.1 %collective-permute-start.3 = (bf16[4,512,128]{2,1,0:T(8,128)(2,1)}, bf16[4,512,128]{2,1,0:T(8,128)(2,1)}, u32[]{:S(2)}, u32[]{:S(2)}) collective-permute-start(bf16[4,512,128]{2,1,0:T(8,128)(2,1)} %get-tuple-element.46), channel_id=1, source_target_pairs={{20,0},{24,4},{28,8},{21,1},{25,5},{29,9},{22,2},{26,6},{30,10},{2... | collective-permute-start | bytes 1572872 | tf_op jit(solution)/shard_map/ppermute | solution.py:487
  17.6 2.7 %shard_map.48 = (bf16[4,512,128]{2,1,0:T(8,128)(2,1)}, bf16[4,512,128]{2,1,0:T(8,128)(2,1)}, bf16[4,512,128]{2,1,0:T(8,128)(2,1)}) custom-call(s32[1]{0:T(128)} %bitcast.here_ref, s32[8,2,16]{2,1,0:T(2,128)S(1)} %bitcast.29, bf16[512,2048]{1,0:T(8,128)(2,1)S(1)} %bitcast.23), custom_call_target="tpu_custom_call" | custom-call | bytes 3145728 | tf_op jit(solution)/shard_map/pallas_call | solution.py:127
  20.3 0.0 collective-permute-done.picks_ref
  20.4 9.0 %shard_map.49 = bf16[16,528,128]{2,1,0:T(8,128)(2,1)} custom-call(s32[1]{0:T(128)} %bitcast.here_ref, bf16[512,2048]{1,0:T(8,128)(2,1)S(1)} %bitcast.24, bf16[512,2048]{1,0:T(8,128)(2,1)S(1)} %bitcast.9, bf16[512,2048]{1,0:T(8,128)(2,1)S(1)} %bitcast.16), custom_call_target="tpu_custom_call" | custom-call | flops 2147483648 | bytes 8388608 | tf_op jit(solution)/shard_map/pallas_call | solution.py:266
  29.3 0.6 collective-permute-start.4
  29.9 1.3 collective-permute-start.5
  31.2 2.1 %collective-permute-done.1.refs_0_ = bf16[8,512,128]{2,1,0:T(8,128)(2,1)S(1)} collective-permute-done((bf16[8,512,128]{2,1,0:T(8,128)(2,1)S(1)}, bf16[8,512,128]{2,1,0:T(8,128)(2,1)S(1)}, u32[]{:S(2)}, u32[]{:S(2)}) %collective-permute-start.1) | collective-permute-done | bytes 1048608 | tf_op jit(solution)/shard_map/ppermute | solution.py:484
  33.3 1.0 copy-done.9
  34.3 0.0 collective-permute-done.2.refs_0_
  34.3 3.3 %shard_map.50 = bf16[4,528,128]{2,1,0:T(8,128)(2,1)} custom-call(s32[1]{0:T(128)} %bitcast.here_ref, s32[8,2,16]{2,1,0:T(2,128)S(1)} %bitcast.30, bf16[512,2048]{1,0:T(8,128)(2,1)S(1)} %bitcast.10, bf16[512,2048]{1,0:T(8,128)(2,1)S(1)} %bitcast.17, bf16[4,512,128]{2,1,0:T(8,128)(2,1)S(1)} %collective-permute-done.2.refs_0_), custom_call_target="tpu_custom_call" | custom-call | flops 999999995904 | bytes 2097152 | tf_op jit(solution)/shard_map/pallas_call | solution.py:226
  37.6 1.3 collective-permute-start.10
  38.9 0.0 collective-permute-done.3.refs_0_
  38.9 0.0 copy-start.6
  39.0 3.9 %shard_map.51 = bf16[4,528,128]{2,1,0:T(8,128)(2,1)} custom-call(s32[1]{0:T(128)} %bitcast.here_ref, s32[8,2,16]{2,1,0:T(2,128)S(1)} %bitcast.31, bf16[512,2048]{1,0:T(8,128)(2,1)S(1)} %bitcast.11, bf16[512,2048]{1,0:T(8,128)(2,1)S(1)} %bitcast.18, bf16[4,512,128]{2,1,0:T(8,128)(2,1)} %collective-permute-done.3.refs_0_), custom_call_target="tpu_custom_call" | custom-call | flops 999999995904 | bytes 2097152 | tf_op jit(solution)/shard_map/pallas_call | solution.py:226
  42.8 1.3 collective-permute-start.11
  44.1 11.8 %collective-permute-done.4.refs_0_ = bf16[16,528,128]{2,1,0:T(8,128)(2,1)} collective-permute-done((bf16[16,528,128]{2,1,0:T(8,128)(2,1)}, bf16[16,528,128]{2,1,0:T(8,128)(2,1)}, u32[]{:S(2)}, u32[]{:S(2)}) %collective-permute-start.4) | collective-permute-done | bytes 2162720 | tf_op jit(solution)/shard_map/ppermute | solution.py:24
  55.9 2.1 %collective-permute-start.6 = (bf16[4,512,128]{2,1,0:T(8,128)(2,1)}, bf16[4,512,128]{2,1,0:T(8,128)(2,1)}, u32[]{:S(2)}, u32[]{:S(2)}) collective-permute-start(bf16[4,512,128]{2,1,0:T(8,128)(2,1)} %get-tuple-element.50), channel_id=1, source_target_pairs={{16,0},{20,4},{24,8},{28,12},{17,1},{21,5},{25,9},{29,13},{18,2},{... | collective-permute-start | bytes 1572872 | tf_op jit(solution)/shard_map/ppermute | solution.py:487
  58.0 2.1 %collective-permute-done.5.refs_1_ = bf16[8,512,128]{2,1,0:T(8,128)(2,1)} collective-permute-done((bf16[8,512,128]{2,1,0:T(8,128)(2,1)}, bf16[8,512,128]{2,1,0:T(8,128)(2,1)}, u32[]{:S(2)}, u32[]{:S(2)}) %collective-permute-start.5) | collective-permute-done | bytes 1048608 | tf_op jit(solution)/shard_map/ppermute | solution.py:484
  60.0 5.4 %shard_map.52 = bf16[8,528,128]{2,1,0:T(8,128)(2,1)} custom-call(s32[1]{0:T(128)} %bitcast.here_ref, s32[8,2,16]{2,1,0:T(2,128)S(1)} %bitcast.32, bf16[512,2048]{1,0:T(8,128)(2,1)S(1)} %bitcast.25, bf16[8,512,128]{2,1,0:T(8,128)(2,1)S(1)} %copy-done.10, bf16[8,512,128]{2,1,0:T(8,128)(2,1)} %collective-permute-done.5.refs_1_), custom_call_target="tpu_custom_call" | custom-call | flops 999999995904 | bytes 6291456 | tf_op jit(solution)/shard_map/pallas_call | solution.py:295
  65.4 0.0 collective-permute-start.7
  65.4 1.5 %collective-permute-start.8 = (bf16[4,512,128]{2,1,0:T(8,128)(2,1)}, bf16[4,512,128]{2,1,0:T(8,128)(2,1)}, u32[]{:S(2)}, u32[]{:S(2)}) collective-permute-start(bf16[4,512,128]{2,1,0:T(8,128)(2,1)} %get-tuple-element.52), channel_id=1, source_target_pairs={{28,0},{29,1},{30,2},{31,3}} | collective-permute-start | bytes 1572872 | tf_op jit(solution)/shard_map/ppermute | solution.py:487
  66.9 0.4 collective-permute-done.6.refs_0_
  67.3 25.9 %collective-permute-start.9 = (bf16[4,512,128]{2,1,0:T(8,128)(2,1)}, bf16[4,512,128]{2,1,0:T(8,128)(2,1)}, u32[]{:S(2)}, u32[]{:S(2)}) collective-permute-start(bf16[4,512,128]{2,1,0:T(8,128)(2,1)} %get-tuple-element.54), channel_id=1, source_target_pairs={{4,0},{8,4},{12,8},{16,12},{20,16},{24,20},{28,24},{5,1},{9,5},{13... | collective-permute-start | bytes 1572872 | tf_op jit(solution)/shard_map/ppermute | solution.py:487
  93.1 2.9 %shard_map.53 = bf16[4,528,128]{2,1,0:T(8,128)(2,1)S(1)} custom-call(s32[1]{0:T(128)} %bitcast.here_ref, s32[8,2,16]{2,1,0:T(2,128)S(1)} %bitcast.33, bf16[512,2048]{1,0:T(8,128)(2,1)S(1)} %bitcast.12, bf16[512,2048]{1,0:T(8,128)(2,1)S(1)} %bitcast.19, bf16[4,512,128]{2,1,0:T(8,128)(2,1)} %collective-permute-done.6.refs_0_), custom_call_target="tpu_custom_call" | custom-call | flops 999999995904 | bytes 2097152 | tf_op jit(solution)/shard_map/pallas_call | solution.py:226
  96.1 0.0 collective-permute-done.7.refs_1_
  96.1 1.3 collective-permute-start.12
  97.4 0.0 collective-permute-done.8.refs_0_
  97.4 2.9 %shard_map.54 = bf16[4,528,128]{2,1,0:T(8,128)(2,1)S(1)} custom-call(s32[1]{0:T(128)} %bitcast.here_ref, s32[8,2,16]{2,1,0:T(2,128)S(1)} %bitcast.34, bf16[512,2048]{1,0:T(8,128)(2,1)S(1)} %bitcast.13, bf16[512,2048]{1,0:T(8,128)(2,1)S(1)} %bitcast.20, bf16[4,512,128]{2,1,0:T(8,128)(2,1)} %collective-permute-done.8.refs_0_), custom_call_target="tpu_custom_call" | custom-call | flops 536870912 | bytes 2097152 | tf_op jit(solution)/shard_map/pallas_call | solution.py:226
  100.3 5.3 %collective-permute-done.9.refs_0_ = bf16[4,512,128]{2,1,0:T(8,128)(2,1)} collective-permute-done((bf16[4,512,128]{2,1,0:T(8,128)(2,1)}, bf16[4,512,128]{2,1,0:T(8,128)(2,1)}, u32[]{:S(2)}, u32[]{:S(2)}) %collective-permute-start.9) | collective-permute-done | bytes 524320 | tf_op jit(solution)/shard_map/ppermute | solution.py:487
  105.6 2.9 %shard_map.55 = bf16[4,528,128]{2,1,0:T(8,128)(2,1)S(1)} custom-call(s32[1]{0:T(128)} %bitcast.here_ref, s32[8,2,16]{2,1,0:T(2,128)S(1)} %bitcast.35, bf16[512,2048]{1,0:T(8,128)(2,1)S(1)} %bitcast.14, bf16[512,2048]{1,0:T(8,128)(2,1)S(1)} %bitcast.21, bf16[4,512,128]{2,1,0:T(8,128)(2,1)} %collective-permute-done.9.refs_0_), custom_call_target="tpu_custom_call" | custom-call | flops 536870912 | bytes 2097152 | tf_op jit(solution)/shard_map/pallas_call | solution.py:226
  108.5 1.9 %collective-permute-start.13 = (bf16[4,528,128]{2,1,0:T(8,128)(2,1)S(1)}, bf16[4,528,128]{2,1,0:T(8,128)(2,1)S(1)}, u32[]{:S(2)}, u32[]{:S(2)}) collective-permute-start(bf16[4,528,128]{2,1,0:T(8,128)(2,1)S(1)} %shard_map.55), channel_id=1, source_target_pairs={{0,5},{1,6},{2,7},{3,4},{4,9},{5,10},{6,11},{7,8},{8,13},{9,14},{1... | collective-permute-start | bytes 1622024 | tf_op jit(solution)/shard_map/ppermute | solution.py:495
  110.5 0.7 collective-permute-start.14
  111.2 0.0 collective-permute-done.10.refs_2_
  111.2 7.3 %shard_map.56 = (bf16[512,2048]{1,0:T(8,128)(2,1)}, f32[16,512,128]{2,1,0:T(8,128)S(1)}, f32[16,4,128]{2,1,0:T(4,128)S(1)}) custom-call(s32[1]{0:T(128)} %bitcast.here_ref, s32[8,2,16]{2,1,0:T(2,128)S(1)} %copy-done.8, bf16[16,528,128]{2,1,0:T(8,128)(2,1)} %collective-permute-done.4.refs_0_, bf16[8,528,128]{2,1,0:T(8,128)(2,1)} %collective-permute-done.7.refs_1_, ...), custom_call_target="tpu_custom_call" | custom-call | flops 6291456 | bytes 8388608 | tf_op jit(solution)/shard_map/pallas_call | solution.py:367
  118.5 0.0 collective-permute-done.12.refs_0_
  118.5 16.1 %collective-permute-done.13.refs_1_ = bf16[4,528,128]{2,1,0:T(8,128)(2,1)S(1)} collective-permute-done((bf16[4,528,128]{2,1,0:T(8,128)(2,1)S(1)}, bf16[4,528,128]{2,1,0:T(8,128)(2,1)S(1)}, u32[]{:S(2)}, u32[]{:S(2)}) %collective-permute-start.13) | collective-permute-done | bytes 540704 | tf_op jit(solution)/shard_map/ppermute | solution.py:495
  134.6 0.0 collective-permute-done.14.refs_2_
  134.6 4.1 %shard_map.57 = bf16[512,2048]{1,0:T(8,128)(2,1)} custom-call(s32[1]{0:T(128)} %bitcast.here_ref, s32[8,2,16]{2,1,0:T(2,128)S(1)} %copy-done.8, f32[16,512,128]{2,1,0:T(8,128)S(1)} %get-tuple-element.56.mixed_ref, f32[16,4,128]{2,1,0:T(4,128)S(1)} %get-tuple-element.57.sums_ref, ...), custom_call_target="tpu_custom_call", output_to_operand_aliasing={{}: (7, {})} | custom-call | flops 1572864 | bytes 6291456 | tf_op jit(solution)/shard_map/pallas_call | solution.py:448
  (16 shorter events, 0.0 us)
Async XLA Ops:
  0.0 1.6 %copy-start = (bf16[1,512,2048]{2,1,0:T(8,128)(2,1)S(1)}, bf16[1,512,2048]{2,1,0:T(8,128)(2,1)}, u32[]{:S(2)}) copy-start(bf16[1,512,2048]{2,1,0:T(8,128)(2,1)} %param.5) | copy-start | bytes 6291460
  1.6 1.6 %copy-start.2 = (bf16[1,512,2048]{2,1,0:T(8,128)(2,1)S(1)}, bf16[1,512,2048]{2,1,0:T(8,128)(2,1)}, u32[]{:S(2)}) copy-start(bf16[1,512,2048]{2,1,0:T(8,128)(2,1)} %param.6) | copy-start | bytes 6291460
  3.2 0.7 copy-start.5
  3.9 3.9 %copy-start.4 = (bf16[1,512,2048]{2,1,0:T(8,128)(2,1)S(1)}, bf16[1,512,2048]{2,1,0:T(8,128)(2,1)}, u32[]{:S(2)}) copy-start(bf16[1,512,2048]{2,1,0:T(8,128)(2,1)} %param.4) | copy-start | bytes 6291460
  6.5 26.8 %collective-permute-start.1 = (bf16[8,512,128]{2,1,0:T(8,128)(2,1)S(1)}, bf16[8,512,128]{2,1,0:T(8,128)(2,1)S(1)}, u32[]{:S(2)}, u32[]{:S(2)}) collective-permute-start(bf16[8,512,128]{2,1,0:T(8,128)(2,1)S(1)} %get-tuple-element.32), channel_id=1, source_target_pairs={{0,8},{4,12},{8,16},{12,20},{16,24},{20,28},{1,9},{5,13},{9,17},{1... | collective-permute-start | bytes 3145736 | tf_op jit(solution)/shard_map/ppermute | solution.py:484
  7.8 12.5 %copy-start.1 = (bf16[1,512,2048]{2,1,0:T(8,128)(2,1)S(1)}, bf16[1,512,2048]{2,1,0:T(8,128)(2,1)}, u32[]{:S(2)}) copy-start(bf16[1,512,2048]{2,1,0:T(8,128)(2,1)} %param.5) | copy-start | bytes 6291460
  7.8 12.5 %copy-start.3 = (bf16[1,512,2048]{2,1,0:T(8,128)(2,1)S(1)}, bf16[1,512,2048]{2,1,0:T(8,128)(2,1)}, u32[]{:S(2)}) copy-start(bf16[1,512,2048]{2,1,0:T(8,128)(2,1)} %param.6) | copy-start | bytes 6291460
  9.9 24.3 %collective-permute-start.2 = (bf16[4,512,128]{2,1,0:T(8,128)(2,1)S(1)}, bf16[4,512,128]{2,1,0:T(8,128)(2,1)S(1)}, u32[]{:S(2)}, u32[]{:S(2)}) collective-permute-start(bf16[4,512,128]{2,1,0:T(8,128)(2,1)S(1)} %get-tuple-element.44), channel_id=1, source_target_pairs={{12,0},{16,4},{20,8},{24,12},{28,16},{13,1},{17,5},{21,9},{25,13},... | collective-permute-start | bytes 1572872 | tf_op jit(solution)/shard_map/ppermute | solution.py:487
  15.4 4.9 %collective-permute-start = (s32[8,2,16]{2,1,0:T(2,128)S(1)}, s32[8,2,16]{2,1,0:T(2,128)S(1)}, u32[]{:S(2)}, u32[]{:S(2)}) collective-permute-start(s32[8,2,16]{2,1,0:T(2,128)S(1)} %bitcast.28), channel_id=1, source_target_pairs={{0,1},{1,2},{2,3},{3,0},{4,5},{5,6},{6,7},{7,4},{8,9},{9,10},{10,1... | collective-permute-start | bytes 3080 | tf_op jit(solution)/shard_map/ppermute | solution.py:24
  15.4 23.5 %collective-permute-start.3 = (bf16[4,512,128]{2,1,0:T(8,128)(2,1)}, bf16[4,512,128]{2,1,0:T(8,128)(2,1)}, u32[]{:S(2)}, u32[]{:S(2)}) collective-permute-start(bf16[4,512,128]{2,1,0:T(8,128)(2,1)} %get-tuple-element.46), channel_id=1, source_target_pairs={{20,0},{24,4},{28,8},{21,1},{25,5},{29,9},{22,2},{26,6},{30,10},{2... | collective-permute-start | bytes 1572872 | tf_op jit(solution)/shard_map/ppermute | solution.py:487
  20.3 9.0 %copy-start.7 = (s32[8,2,16]{2,1,0:T(2,128)}, s32[8,2,16]{2,1,0:T(2,128)S(1)}, u32[]{:S(2)}) copy-start(s32[8,2,16]{2,1,0:T(2,128)S(1)} %collective-permute-done.picks_ref) | copy-start | bytes 3076
  29.3 26.6 %collective-permute-start.4 = (bf16[16,528,128]{2,1,0:T(8,128)(2,1)}, bf16[16,528,128]{2,1,0:T(8,128)(2,1)}, u32[]{:S(2)}, u32[]{:S(2)}) collective-permute-start(bf16[16,528,128]{2,1,0:T(8,128)(2,1)} %shard_map.49), channel_id=1, source_target_pairs={{0,1},{1,2},{2,3},{3,0},{4,5},{5,6},{6,7},{7,4},{8,9},{9,10},{10,1... | collective-permute-start | bytes 6488072 | tf_op jit(solution)/shard_map/ppermute | solution.py:24
  29.9 30.1 %collective-permute-start.5 = (bf16[8,512,128]{2,1,0:T(8,128)(2,1)}, bf16[8,512,128]{2,1,0:T(8,128)(2,1)}, u32[]{:S(2)}, u32[]{:S(2)}) collective-permute-start(bf16[8,512,128]{2,1,0:T(8,128)(2,1)} %get-tuple-element.48), channel_id=1, source_target_pairs={{0,24},{4,28},{1,25},{5,29},{2,26},{6,30},{3,27},{7,31}} | collective-permute-start | bytes 3145736 | tf_op jit(solution)/shard_map/ppermute | solution.py:484
  33.3 1.0 copy-start.9
  37.6 73.5 %collective-permute-start.10 = (bf16[4,528,128]{2,1,0:T(8,128)(2,1)}, bf16[4,528,128]{2,1,0:T(8,128)(2,1)}, u32[]{:S(2)}, u32[]{:S(2)}) collective-permute-start(bf16[4,528,128]{2,1,0:T(8,128)(2,1)} %shard_map.50), channel_id=1, source_target_pairs={{0,13},{1,14},{2,15},{3,12},{4,17},{5,18},{6,19},{7,16},{8,21},{9,... | collective-permute-start | bytes 1622024 | tf_op jit(solution)/shard_map/ppermute | solution.py:495
  38.9 21.1 %copy-start.6 = (s32[1,8,16,2]{2,3,1,0:T(2,128)S(1)}, s32[1,8,16,2]{2,3,1,0:T(2,128)}, u32[]{:S(2)}) copy-start(s32[1,8,16,2]{2,3,1,0:T(2,128)} %param.7) | copy-start | bytes 3076
  38.9 21.1 %copy-start.10 = (bf16[8,512,128]{2,1,0:T(8,128)(2,1)S(1)}, bf16[8,512,128]{2,1,0:T(8,128)(2,1)}, u32[]{:S(2)}) copy-start(bf16[8,512,128]{2,1,0:T(8,128)(2,1)} %copy-done.9) | copy-start | bytes 3145732
  42.8 68.3 %collective-permute-start.11 = (bf16[4,528,128]{2,1,0:T(8,128)(2,1)}, bf16[4,528,128]{2,1,0:T(8,128)(2,1)}, u32[]{:S(2)}, u32[]{:S(2)}) collective-permute-start(bf16[4,528,128]{2,1,0:T(8,128)(2,1)} %shard_map.51), channel_id=1, source_target_pairs={{0,21},{1,22},{2,23},{3,20},{4,25},{5,26},{6,27},{7,24},{8,29},{9,... | collective-permute-start | bytes 1622024 | tf_op jit(solution)/shard_map/ppermute | solution.py:495
  55.9 11.4 %collective-permute-start.6 = (bf16[4,512,128]{2,1,0:T(8,128)(2,1)}, bf16[4,512,128]{2,1,0:T(8,128)(2,1)}, u32[]{:S(2)}, u32[]{:S(2)}) collective-permute-start(bf16[4,512,128]{2,1,0:T(8,128)(2,1)} %get-tuple-element.50), channel_id=1, source_target_pairs={{16,0},{20,4},{24,8},{28,12},{17,1},{21,5},{25,9},{29,13},{18,2},{... | collective-permute-start | bytes 1572872 | tf_op jit(solution)/shard_map/ppermute | solution.py:487
  65.4 30.7 %collective-permute-start.7 = (bf16[8,528,128]{2,1,0:T(8,128)(2,1)}, bf16[8,528,128]{2,1,0:T(8,128)(2,1)}, u32[]{:S(2)}, u32[]{:S(2)}) collective-permute-start(bf16[8,528,128]{2,1,0:T(8,128)(2,1)} %shard_map.52), channel_id=1, source_target_pairs={{0,1},{1,2},{2,3},{3,0},{4,5},{5,6},{6,7},{7,4},{8,9},{9,10},{10,1... | collective-permute-start | bytes 3244040 | tf_op jit(solution)/shard_map/ppermute | solution.py:24
  65.4 32.0 %collective-permute-start.8 = (bf16[4,512,128]{2,1,0:T(8,128)(2,1)}, bf16[4,512,128]{2,1,0:T(8,128)(2,1)}, u32[]{:S(2)}, u32[]{:S(2)}) collective-permute-start(bf16[4,512,128]{2,1,0:T(8,128)(2,1)} %get-tuple-element.52), channel_id=1, source_target_pairs={{28,0},{29,1},{30,2},{31,3}} | collective-permute-start | bytes 1572872 | tf_op jit(solution)/shard_map/ppermute | solution.py:487
  67.3 38.3 %collective-permute-start.9 = (bf16[4,512,128]{2,1,0:T(8,128)(2,1)}, bf16[4,512,128]{2,1,0:T(8,128)(2,1)}, u32[]{:S(2)}, u32[]{:S(2)}) collective-permute-start(bf16[4,512,128]{2,1,0:T(8,128)(2,1)} %get-tuple-element.54), channel_id=1, source_target_pairs={{4,0},{8,4},{12,8},{16,12},{20,16},{24,20},{28,24},{5,1},{9,5},{13... | collective-permute-start | bytes 1572872 | tf_op jit(solution)/shard_map/ppermute | solution.py:487
  96.1 22.4 %collective-permute-start.12 = (bf16[4,528,128]{2,1,0:T(8,128)(2,1)S(1)}, bf16[4,528,128]{2,1,0:T(8,128)(2,1)S(1)}, u32[]{:S(2)}, u32[]{:S(2)}) collective-permute-start(bf16[4,528,128]{2,1,0:T(8,128)(2,1)S(1)} %shard_map.53), channel_id=1, source_target_pairs={{0,17},{1,18},{2,19},{3,16},{4,21},{5,22},{6,23},{7,20},{8,25},{9,... | collective-permute-start | bytes 1622024 | tf_op jit(solution)/shard_map/ppermute | solution.py:495
  100.3 10.9 %copy-start.8 = (s32[8,2,16]{2,1,0:T(2,128)S(1)}, s32[8,2,16]{2,1,0:T(2,128)}, u32[]{:S(2)}) copy-start(s32[8,2,16]{2,1,0:T(2,128)} %copy-done.7) | copy-start | bytes 3076
  108.5 26.1 %collective-permute-start.13 = (bf16[4,528,128]{2,1,0:T(8,128)(2,1)S(1)}, bf16[4,528,128]{2,1,0:T(8,128)(2,1)S(1)}, u32[]{:S(2)}, u32[]{:S(2)}) collective-permute-start(bf16[4,528,128]{2,1,0:T(8,128)(2,1)S(1)} %shard_map.55), channel_id=1, source_target_pairs={{0,5},{1,6},{2,7},{3,4},{4,9},{5,10},{6,11},{7,8},{8,13},{9,14},{1... | collective-permute-start | bytes 1622024 | tf_op jit(solution)/shard_map/ppermute | solution.py:495
  110.5 24.2 %collective-permute-start.14 = (bf16[4,528,128]{2,1,0:T(8,128)(2,1)S(1)}, bf16[4,528,128]{2,1,0:T(8,128)(2,1)S(1)}, u32[]{:S(2)}, u32[]{:S(2)}) collective-permute-start(bf16[4,528,128]{2,1,0:T(8,128)(2,1)S(1)} %shard_map.54), channel_id=1, source_target_pairs={{0,29},{1,30},{2,31},{3,28}} | collective-permute-start | bytes 1622024 | tf_op jit(solution)/shard_map/ppermute | solution.py:495
